TPU v7x, 32 devices: a whole 2x2x4 slice. The times are simulated.
32 devices in a mesh: req: 16 (over z, y, x), seq: 2 (over core).
Axes of the slice: x: 2, y: 2, z: 4, core: 2. Of those that a mesh axis runs over, the one named last changes fastest.
Arguments:
- tokens: bfloat16 [4096, 1536], P(('req', 'seq')), may hold values from -6 to 6
- attn_gain: float32 [1536], replicated, may hold values from 0.5 to 1.5
- w_qkv: bfloat16 [1536, 2560], replicated, may hold values from -80 to 80
- w_out: bfloat16 [1536, 1536], replicated, may hold values from -0.15625 to 0.15625
- k_cache: bfloat16 [16, 2048, 512], P('req', 'seq'), may hold values from -6 to 6
- v_cache: bfloat16 [16, 2048, 512], P('req', 'seq'), may hold values from -7.5 to 7.5
- cache_len: int32 [16], P('req'), may hold values from 1 to 2048, as said below
- ffn_gain: float32 [1536], replicated, may hold values from 0.5 to 1.5
- routes: int32 [4096, 8], P(('req', 'seq')), may hold values from 0 to 39, as said below
- route_scores: float32 [4096, 8], P(('req', 'seq')), may hold values from 0.05 to 1
- replica_slot: int32 [4096, 40], P(('req', 'seq')), may hold values from 0 to 63, as said below
- expert_up: bfloat16 [64, 1536, 1024], P(('req', 'seq')), may hold values from -2 to 2, as said below
- expert_down: bfloat16 [64, 512, 1536], P(('req', 'seq')), may hold values from -2 to 2, as said below
Outputs:
- attended: bfloat16 [4096, 1536], P(('req', 'seq'))
- stream: bfloat16 [4096, 1536], P(('req', 'seq'))
- expert_mix: bfloat16 [4096, 1536], P(('req', 'seq'))
- appended: bfloat16 [4096, 1024], P(('req', 'seq'))
Inputs may be any that keep to these rules, and one draw needn't show every extreme that they name: `routes`: each token names 8 different experts. Each slot hosts one expert, every expert at least one slot; replica_slot[t, e] is a slot hosting expert e. The 128 rows of one device (rows d * 128 to (d + 1) * 128 - 1) send at most 32 of their routes to any one slot (slot replica_slot[t, routes[t, k]]), and each device sends exactly 32 to some slot. `expert_up`: slots hosting the same expert hold equal weights. `expert_down`: slots hosting the same expert hold equal weights. `cache_len`: at least one request has exactly 2048 cached positions.
All inputs are finite; a program needn't handle non-finite values.
Results may differ from a plain program's by a relative error of at most 0.01.
Values may be sent and summed in bfloat16 or wider, within the bound.
No kernel may reach another device: no remote copies, remote signals or barrier semaphores. Data moves between devices by JAX's collectives and lax.ppermute only.
A program may use at most 128 MiB of HBM per device.

v0:
```python
import jax
import jax.numpy as jnp
from jax import lax
from jax.sharding import PartitionSpec as P

HEADS = 24
KV_HEADS = 8
HEAD = 64
KEY_BLOCK = 128


epsilon = 1e-06
residual_scale = 0.22
score_scale = 0.015625
rope_base = 10000.0
neg_big = -1e30


def rms_scale(row_block, gain_vector):
    widened = row_block.astype(jnp.float32)
    mean_square = jnp.mean(widened * widened, axis=-1, keepdims=True)
    return (widened * lax.rsqrt(mean_square + epsilon) * gain_vector).astype(jnp.bfloat16)


def rotate(head_values, positions):
    half_width = head_values.shape[-1] // 2
    frequency = rope_base ** (-jnp.arange(half_width, dtype=jnp.float32) / half_width)
    angles = positions.astype(jnp.float32)[:, None] * frequency[None, :]
    cosine = jnp.cos(angles)[:, None, :]
    sine_part = jnp.sin(angles)[:, None, :]
    lower_half = head_values[..., :half_width]
    upper_half = head_values[..., half_width:]
    return jnp.concatenate(
        [
            lower_half * cosine - upper_half * sine_part,
            upper_half * cosine + lower_half * sine_part,
        ],
        axis=-1,
    )


def project(row_block, gain_vector, w_qkv, positions):
    normed = rms_scale(row_block, gain_vector)
    projected = jnp.dot(normed, w_qkv, preferred_element_type=jnp.float32)
    query_width = HEADS * HEAD
    key_width = KV_HEADS * HEAD
    queries = rotate(projected[:, :query_width].reshape(-1, HEADS, HEAD), positions).astype(
        jnp.bfloat16
    )
    new_keys = rotate(
        projected[:, query_width : query_width + key_width].reshape(-1, KV_HEADS, HEAD), positions
    ).astype(jnp.bfloat16)
    new_values = projected[:, query_width + key_width :].astype(jnp.bfloat16)
    return (queries, new_keys, new_values)


def fold_blocks(carried, queries, key_part, value_part, visible):
    scores = (
        jnp.einsum("rkgh,nbkh->rkgnb", queries, key_part, preferred_element_type=jnp.float32)
        * score_scale
    )
    visible_mask = visible[:, None, None, :, :]
    block_max = jnp.max(jnp.where(visible_mask, scores, neg_big), axis=-1)
    weights = jnp.where(visible_mask, jnp.exp(scores - block_max[..., None]), 0.0).astype(
        jnp.bfloat16
    )
    totals = jnp.sum(weights, axis=-1, dtype=jnp.float32)
    block_sums = jnp.einsum(
        "rkgnb,nbkh->rkgnh", weights, value_part, preferred_element_type=jnp.float32
    )
    best_score, running_total, running_sum = carried
    new_best = jnp.maximum(best_score, jnp.max(block_max, axis=-1))
    old_scale = jnp.exp(best_score - new_best)
    block_scale = jnp.exp(block_max - new_best[..., None])
    running_total = running_total * old_scale + jnp.sum(totals * block_scale, axis=-1)
    running_sum = running_sum * old_scale[..., None] + jnp.sum(
        block_sums * block_scale[..., None], axis=-2
    )
    return (new_best, running_total, running_sum)


def attend_keys(carried, queries, key_rows, value_rows, visible_of):
    block_count = key_rows.shape[0] // KEY_BLOCK
    group_size = 1
    while group_size * 2 * queries.shape[0] <= 1024 and block_count % (group_size * 2) == 0:
        group_size = group_size * 2
    turn_count = block_count // group_size
    shaped_keys = key_rows.reshape(turn_count, group_size, KEY_BLOCK, KV_HEADS, HEAD)
    shaped_values = value_rows.reshape(turn_count, group_size, KEY_BLOCK, KV_HEADS, HEAD)

    def fold_step(running, inputs):
        turn_index, key_part, value_part = inputs
        visible = visible_of(turn_index * group_size * KEY_BLOCK, group_size * KEY_BLOCK)
        visible = visible.reshape(-1, group_size, KEY_BLOCK)
        return (fold_blocks(running, queries, key_part, value_part, visible), None)

    carried, _ = lax.scan(
        fold_step, carried, (jnp.arange(turn_count, dtype=jnp.int32), shaped_keys, shaped_values)
    )
    return carried


def empty_state(row_count):
    group_size = HEADS // KV_HEADS
    return (
        jnp.full((row_count, KV_HEADS, group_size), neg_big, jnp.float32),
        jnp.zeros((row_count, KV_HEADS, group_size), jnp.float32),
        jnp.zeros((row_count, KV_HEADS, group_size, HEAD), jnp.float32),
    )


def flatten_state(carried):
    best_score, running_total, running_sum = carried
    row_count = best_score.shape[0]
    return (
        best_score.reshape(row_count, HEADS),
        running_total.reshape(row_count, HEADS),
        running_sum.reshape(row_count, HEADS * HEAD),
    )


def finish_state(flat_state):
    best_score, running_total, running_sum = flat_state
    row_count = best_score.shape[0]
    shaped = running_sum.reshape(row_count, HEADS, HEAD) / running_total[..., None]
    return shaped.astype(jnp.bfloat16).reshape(row_count, HEADS * HEAD)


def run_experts(buffer, expert_up, expert_down):
    gate_up = jnp.einsum("sjcd,jdf->sjcf", buffer, expert_up, preferred_element_type=jnp.float32)
    hidden_width = expert_down.shape[1]
    active = (jax.nn.silu(gate_up[..., :hidden_width]) * gate_up[..., hidden_width:]).astype(
        jnp.bfloat16
    )
    return jnp.einsum(
        "sjcf,jfd->sjcd", active, expert_down, preferred_element_type=jnp.float32
    ).astype(jnp.bfloat16)


def shards(
    tokens,
    attn_gain,
    w_qkv,
    w_out,
    k_cache,
    v_cache,
    cache_len,
    ffn_gain,
    routes,
    route_scores,
    replica_slot,
    expert_up,
    expert_down,
):
    row_count = tokens.shape[0]
    seq_count = lax.axis_size("seq")
    seq_index = lax.axis_index("seq")
    length = cache_len[0]
    group_size = HEADS // KV_HEADS
    key_width = KV_HEADS * HEAD
    query_index = seq_index * row_count + jnp.arange(row_count, dtype=jnp.int32)
    positions = length + query_index
    queries, new_keys, new_values = project(tokens, attn_gain, w_qkv, positions)
    appended = jnp.concatenate([new_keys.reshape(row_count, -1), new_values], axis=1)
    own_queries = queries.reshape(row_count, KV_HEADS, group_size, HEAD)
    cache_k, cache_v, span_all = (
        lax.all_gather(k_cache, "seq", axis=1, tiled=True),
        lax.all_gather(v_cache, "seq", axis=1, tiled=True),
        lax.all_gather(appended[None], "seq", axis=1, tiled=True),
    )

    def cache_visible(first_key, key_count):
        key_index = first_key + jnp.arange(key_count, dtype=jnp.int32)
        return jnp.broadcast_to((key_index < length)[None, :], (row_count, key_count))

    def span_visible(first_key, key_count):
        key_index = first_key + jnp.arange(key_count, dtype=jnp.int32)
        return key_index[None, :] <= query_index[:, None]

    carried = attend_keys(
        empty_state(row_count),
        own_queries,
        cache_k[0].reshape(-1, KV_HEADS, HEAD),
        cache_v[0].reshape(-1, KV_HEADS, HEAD),
        cache_visible,
    )
    carried = attend_keys(
        carried,
        own_queries,
        span_all[0][:, :key_width].reshape(-1, KV_HEADS, HEAD),
        span_all[0][:, key_width:].reshape(-1, KV_HEADS, HEAD),
        span_visible,
    )
    attended = finish_state(flatten_state(carried))
    stream = (
        tokens.astype(jnp.float32)
        + residual_scale * jnp.dot(attended, w_out, preferred_element_type=jnp.float32)
    ).astype(jnp.bfloat16)
    expert_in = rms_scale(stream, ffn_gain)
    top_count = routes.shape[1]
    route_rows = row_count * top_count
    slots_dev = expert_up.shape[0]
    req_count = lax.axis_size("req")
    device_count = req_count * seq_count
    slot_total = device_count * slots_dev
    capacity = 2 * ((row_count * top_count + slot_total - 1) // slot_total)
    slot_ids = jnp.take_along_axis(replica_slot, routes, axis=1).reshape(-1)
    slot_hot = (slot_ids[:, None] == jnp.arange(slot_total, dtype=jnp.int32)[None, :]).astype(
        jnp.bfloat16
    )
    route_order = jnp.arange(route_rows, dtype=jnp.int32)
    earlier = (route_order[:, None] > route_order[None, :]).astype(jnp.bfloat16)
    before = jnp.dot(earlier, slot_hot, preferred_element_type=jnp.float32)
    slot_rank = jnp.sum(before * slot_hot.astype(jnp.float32), axis=1).astype(jnp.int32)
    position = slot_ids * capacity + slot_rank
    place = jnp.any(
        (jnp.arange(slot_total * capacity, dtype=jnp.int32)[:, None] == position[None, :]).reshape(
            slot_total * capacity, row_count, top_count
        ),
        axis=2,
    ).astype(jnp.bfloat16)
    outgoing = jnp.dot(place, expert_in, preferred_element_type=jnp.float32).astype(jnp.bfloat16)
    outgoing = outgoing.reshape(device_count, slots_dev, capacity, -1)
    returned = lax.all_to_all(
        run_experts(
            lax.all_to_all(outgoing, ("req", "seq"), split_axis=0, concat_axis=0, tiled=True),
            expert_up,
            expert_down,
        ),
        ("req", "seq"),
        split_axis=0,
        concat_axis=0,
        tiled=True,
    )
    flat_back = returned.reshape(slot_total * capacity, -1)
    picked = flat_back[position].reshape(row_count, top_count, -1)
    shares = route_scores / jnp.sum(route_scores, axis=1, keepdims=True)
    expert_mix = jnp.sum(picked.astype(jnp.float32) * shares[:, :, None], axis=1).astype(
        jnp.bfloat16
    )
    return (attended, stream, expert_mix, appended)


def solution(mesh):
    return jax.shard_map(
        shards,
        mesh=mesh,
        in_specs=(
            P(("req", "seq"), None),
            P(),
            P(),
            P(),
            P("req", "seq", None),
            P("req", "seq", None),
            P("req"),
            P(),
            P(("req", "seq"), None),
            P(("req", "seq"), None),
            P(("req", "seq"), None),
            P(("req", "seq"), None, None),
            P(("req", "seq"), None, None),
        ),
        out_specs=(
            P(("req", "seq"), None),
            P(("req", "seq"), None),
            P(("req", "seq"), None),
            P(("req", "seq"), None),
        ),
        check_vma=False,
    )
```

profile of v0, /device:TPU:0, one launch (start us, length us, event | category | flops | bytes accessed | tf_op | source)
XLA Modules:
  0.0 456.7 jit_solution(17008680267217906498)
XLA Ops:
  9.9 4.7 %fusion.54 = f32[128,2560]{1,0:T(8,128)S(1)} fusion(bf16[1536,2560]{1,0:T(8,128)(2,1)} %param.17, bf16[128,1536]{1,0:T(8,128)(2,1)} %param.15, f32[1536]{0:T(1024)} %param.16, f32[128]{0:T(128)S(1)} %add_rsqrt_fusion.1), kind=kOutput, calls=%fused_computation.78 | convolution fusion | flops 1007419392 | bytes 9574912 | tf_op jit(solution)/shard_map/dot_general | solution.py:44
  16.6 7.0 %gather_fusion.1 = s32[1024]{0:T(1024)S(1)} fusion(s32[128,40]{0,1:T(8,128)S(1)} %copy-done.1, s32[1024]{0:T(1024)S(1)} %reshape.267), kind=kCustom, calls=%fused_computation.1 | custom fusion | bytes 16384 | tf_op jit(solution)/shard_map/jit(take_along_axis)/gather | solution.py:207
  44.1 8.1 %fusion.19 = pred[2048,128]{1,0:T(8,128)(4,1)} fusion(s32[128,8]{0,1:T(8,128)S(1)} %fusion.68), kind=kLoop, calls=%fused_computation.32 | loop fusion | flops 3932160 | bytes 266240 | tf_op jit(solution)/shard_map/reduce_or | solution.py:216
  58.1 6.2 %reshape.289 = bf16[2,8,128,8,64]{4,3,2,1,0:T(8,128)(2,1)} reshape(bf16[1,2048,512]{2,1,0:T(8,128)(2,1)} %all-gather.6.cloned.1.call-done) | data formatting | bytes 4194304 | tf_op jit(solution)/shard_map/reshape;reshape;squeeze | solution.py:89
  64.3 5.5 %copy.103 = bf16[2,8,128,8,64]{2,4,1,3,0:T(8,128)(2,1)} copy(bf16[2,8,128,8,64]{4,3,2,1,0:T(8,128)(2,1)} %reshape.289) | data formatting | bytes 4194304
  69.8 6.2 %reshape.288 = bf16[2,8,128,8,64]{4,3,2,1,0:T(8,128)(2,1)} reshape(bf16[1,2048,512]{2,1,0:T(8,128)(2,1)} %all-gather.4.cloned.1.call-done) | data formatting | bytes 4194304 | tf_op jit(solution)/shard_map/reshape;reshape;squeeze | solution.py:88
  76.0 5.5 %copy.102 = bf16[2,8,128,8,64]{2,4,1,3,0:T(8,128)(2,1)} copy(bf16[2,8,128,8,64]{4,3,2,1,0:T(8,128)(2,1)} %reshape.288) | data formatting | bytes 4194304
  82.0 32.0 %while.5 = (s32[]{:T(128)}, f32[128,8,3]{0,2,1:T(4,128)S(1)}, f32[128,8,3]{0,2,1:T(4,128)}, f32[128,8,3,64]{0,3,2,1:T(8,128)}, s32[2]{0:T(128)}, /*index=5*/s32[...) while((s32[]{:T(128)}, f32[128,8,3]{0,2,1:T(4,128)S(1)}, ...), condition=%wide.region_7.8_spmd.clone, body=%wide.region_1.7_spmd.clone.sunk | while | flops 856075264 | bytes 59203896 | solution.py:97
  84.4 4.6 %fusion.82 = (f32[128,8,3,8]{0,2,3,1:T(4,128)S(1)}, f32[8,8,128,128,3]{3,2,4,1,0:T(8,128)S(1)}) fusion(pred[8,128]{1,0:T(8,128)(4,1)S(1)} %add_compare_fusion.2, bf16[128,8,3,64]{0,3,2,1:T(8,128)(2,1)S(1)} %get-tuple-element.378, bf16[2,8,128,8,64]{2,4,1,3,0:T(8,128)(2,1)} %get-tuple-element.377, s32[]{:T(128)S(6)} %copy.156), kind=kOutput, calls=%fused_computation.8.clone.1 | convolution fusion | flops 412065792 | bytes 14124036 | tf_op jit(solution)/shard_map/while/body/eval_jaxpr/rkgh,nbkh->rkgnb/dot_general | solution.py:59
  89.0 4.5 convert_reduce_fusion.3
  93.6 3.2 fusion.84
  100.4 4.6 %fusion.82 = (f32[128,8,3,8]{0,2,3,1:T(4,128)S(1)}, f32[8,8,128,128,3]{3,2,4,1,0:T(8,128)S(1)}) fusion(pred[8,128]{1,0:T(8,128)(4,1)S(1)} %add_compare_fusion.2, bf16[128,8,3,64]{0,3,2,1:T(8,128)(2,1)S(1)} %get-tuple-element.378, bf16[2,8,128,8,64]{2,4,1,3,0:T(8,128)(2,1)} %get-tuple-element.377, s32[]{:T(128)S(6)} %copy.156), kind=kOutput, calls=%fused_computation.8.clone.1 | convolution fusion | flops 412065792 | bytes 14124036 | tf_op jit(solution)/shard_map/while/body/eval_jaxpr/rkgh,nbkh->rkgnb/dot_general | solution.py:59
  105.0 4.5 convert_reduce_fusion.3
  109.6 3.2 fusion.84
  116.3 3.0 fusion.41
  119.5 3.3 fusion.44
  124.8 145.6 %all_to_all.10 = bf16[32,2,32,1536]{3,2,1,0:T(8,128)(2,1)S(1)} all-to-all(bf16[32,2,32,1536]{3,2,1,0:T(8,128)(2,1)S(1)} %bitcast.133), channel_id=1, replica_groups=mesh['req'=16,'seq'=2] {'req','seq'}, dimensions={0} | all-to-all | bytes 12582912 | tf_op jit(solution)/shard_map/all_to_all | solution.py:226
  270.4 8.8 %fusion.26 = f32[32,2,32,1024]{3,2,0,1:T(8,128)} fusion(bf16[2,1536,1024]{2,1,0:T(8,128)(2,1)S(1)} %bitcast.146, bf16[32,2,32,1536]{3,2,1,0:T(8,128)(2,1)S(1)} %all_to_all.10), kind=kOutput, calls=%fused_computation.44 | convolution fusion | flops 6442450944 | bytes 20971520 | tf_op jit(solution)/shard_map/sjcd,jdf->sjcf/dot_general | solution.py:130
  279.2 7.3 %convert_bitcast_fusion = bf16[32,2,32,1536]{3,2,0,1:T(8,128)(2,1)S(1)} fusion(bf16[2,512,1536]{2,1,0:T(8,128)(2,1)S(1)} %copy-done, f32[32,2,32,1024]{3,2,0,1:T(8,128)} %fusion.26), kind=kOutput, calls=%fused_computation.39 | convolution fusion | flops 3230662656 | bytes 17825792 | tf_op jit(solution)/shard_map/sjcf,jfd->sjcd/dot_general | solution.py:135
  286.5 3.1 copy.116
  289.6 3.9 all-to-all-start.1
  298.0 135.5 %all-to-all-done.1 = bf16[32,2,32,1536]{3,2,1,0:T(8,128)(2,1)} async-done(((bf16[32,2,32,1536]{3,2,1,0:T(8,128)(2,1)}), bf16[32,2,32,1536]{3,2,1,0:T(8,128)(2,1)}, u32[]{:S(2)}, u32[]{:S(2)}) %all-to-all-start.1) | async-done | bytes 6291488 | tf_op jit(solution)/shard_map/all_to_all | solution.py:224
  433.5 10.9 %gather_fusion = bf16[1024,1536]{1,0:T(8,128)(2,1)} fusion(bf16[2048,1536]{1,0:T(8,128)(2,1)} %bitcast.22, s32[1024]{0:T(1024)S(1)} %broadcast_clamp_fusion), kind=kCustom, calls=%fused_computation | custom fusion | bytes 6295552 | tf_op jit(solution)/shard_map/gather | solution.py:236
  444.4 5.5 %fusion.20 = bf16[128,1536]{1,0:T(8,128)(2,1)} fusion(bf16[1024,1536]{1,0:T(8,128)(2,1)} %gather_fusion, f32[128,8]{1,0:T(8,128)S(1)} %copy-done.14), kind=kLoop, calls=%fused_computation.35 | loop fusion | flops 4521984 | bytes 3543040 | tf_op jit(solution)/shard_map/reduce_sum | solution.py:238
  (140 shorter events, 46.0 us)
Async XLA Ops:
  7.2 272.0 %copy-start = (bf16[2,512,1536]{2,1,0:T(8,128)(2,1)S(1)}, bf16[2,512,1536]{2,1,0:T(8,128)(2,1)}, u32[]{:S(2)}) copy-start(bf16[2,512,1536]{2,1,0:T(8,128)(2,1)} %param.27) | copy-start | bytes 9437188
  7.2 50.9 %all-gather.6.cloned.1.call-start = ((), (), s32[]{:S(2)}) async-start(), calls=%async_computation.3 | async-start | bytes 3145728 | tf_op jit(solution)/shard_map/all_gather | solution.py:168
  7.9 61.9 %all-gather.4.cloned.1.call-start = ((), (), s32[]{:S(2)}) async-start(), calls=%async_computation.2 | async-start | bytes 3145728 | tf_op jit(solution)/shard_map/all_gather | solution.py:167
  9.8 6.5 %copy-start.22 = (s32[128,8]{0,1:T(8,128)S(1)}, s32[128,8]{0,1:T(8,128)}, u32[]{:S(2)}) copy-start(s32[128,8]{0,1:T(8,128)} %param.23) | copy-start | bytes 12292
  14.5 2.0 copy-start.1
  24.3 3.3 copy-start.19
  34.2 9.2 %copy-start.17 = (s32[1024]{0:T(1024)}, s32[1024]{0:T(1024)S(1)}, u32[]{:S(2)}) copy-start(s32[1024]{0:T(1024)S(1)} %convert_element_type.115) | copy-start | bytes 12292
  89.0 4.6 %copy-start.8 = (bf16[2,8,128,8,64]{2,4,1,3,0:T(8,128)(2,1)S(1)}, bf16[2,8,128,8,64]{2,4,1,3,0:T(8,128)(2,1)}, u32[]{:S(2)}) copy-start(bf16[2,8,128,8,64]{2,4,1,3,0:T(8,128)(2,1)} %get-tuple-element.379) | copy-start | bytes 6291460 | tf_op jit(solution)/shard_map/while
  93.6 3.2 copy-start.12
  93.6 3.2 copy-start.2
  105.0 4.6 %copy-start.8 = (bf16[2,8,128,8,64]{2,4,1,3,0:T(8,128)(2,1)S(1)}, bf16[2,8,128,8,64]{2,4,1,3,0:T(8,128)(2,1)}, u32[]{:S(2)}) copy-start(bf16[2,8,128,8,64]{2,4,1,3,0:T(8,128)(2,1)} %get-tuple-element.379) | copy-start | bytes 6291460 | tf_op jit(solution)/shard_map/while
  109.6 3.2 copy-start.12
  109.6 3.2 copy-start.2
  116.3 3.0 copy-start.4
  116.3 3.2 copy-start.5
  119.3 3.6 copy-start.9
  119.3 3.6 copy-start.23
  122.9 147.5 %slice-start = ((s8[6291456]{0:T(1024)(128)(4,1)}), s8[4194304]{0:T(1024)(128)(4,1)S(1)}, s32[]{:S(2)}) async-start(s8[6291456]{0:T(1024)(128)(4,1)} %bitcast.145), calls=%async_computation.4 | async-start | bytes 8388608
  124.8 145.6 %slice-start.1 = ((s8[6291456]{0:T(1024)(128)(4,1)}), s8[2097152]{0:T(1024)(128)(4,1)S(1)}, s32[]{:S(2)}) async-start(s8[6291456]{0:T(1024)(128)(4,1)} %bitcast.145), calls=%async_computation.5 | async-start | bytes 4194304
  289.6 3.9 copy-start.21
  289.6 5.6 %copy-start.20 = (f32[128,8]{0,1:T(8,128)S(1)}, f32[128,8]{0,1:T(8,128)}, u32[]{:S(2)}) copy-start(f32[128,8]{0,1:T(8,128)} %param.24) | copy-start | bytes 12292
  289.6 7.5 %copy-start.18 = (s32[1024]{0:T(1024)S(1)}, s32[1024]{0:T(1024)}, u32[]{:S(2)}) copy-start(s32[1024]{0:T(1024)} %copy-done.17) | copy-start | bytes 12292
  289.6 143.9 %all-to-all-start.1 = ((bf16[32,2,32,1536]{3,2,1,0:T(8,128)(2,1)}), bf16[32,2,32,1536]{3,2,1,0:T(8,128)(2,1)}, u32[]{:S(2)}, u32[]{:S(2)}) async-start(bf16[32,2,32,1536]{3,2,1,0:T(8,128)(2,1)} %copy.116), calls=%async_computation.1 | async-start | bytes 12582912 | tf_op jit(solution)/shard_map/all_to_all | solution.py:224
  433.5 10.9 %copy-start.14 = (f32[128,8]{1,0:T(8,128)S(1)}, f32[128,8]{1,0:T(8,128)}, u32[]{:S(2)}) copy-start(f32[128,8]{1,0:T(8,128)} %copy.118) | copy-start | bytes 12292
  (10 other events, 11.7 us)
Sparse Core Ops, SparseCore 0:
  9.6 13.2 all-gather.5
  24.4 11.7 all-gather.3
where the time goes:
time: 458 us; the launch traced here: 457 us
  blocking collectives  148 us (32%)
  waiting for transfers between devices  137 us (30%)
  local copies, waits for them, and re-layouts  67.5 us (15%)
  matrix products  46.6 us (10%)
  other arithmetic  37.2 us (8%)
  between operations  15.1 us (3%)
    all_to_all x1, blocking collectives, shards(): lax.all_to_all(outgoing, ('req', 'seq'), split_axis=0, concat_axis=0, til...  146 us
    all_to_all x1, waiting for transfers between devices, shards(): lax.all_to_all(run_experts(lax.all_to_all(outgoing, ('req', 'seq'), split...  135 us
    unnamed x45, local copies, waits for them, and re-layouts  14.8 us
    gather x1, local copies, waits for them, and re-layouts, shards(): picked = flat_back[position].reshape(row_count, top_count, -1)  10.9 us
    dot_general x3, matrix products, fold_blocks(): jnp.einsum('rkgh,nbkh->rkgnb', queries, key_part, preferred_element_type=...  10.8 us
    reduce_sum x3, other arithmetic, fold_blocks(): totals = jnp.sum(weights, axis=-1, dtype=jnp.float32)  10.7 us
    dot_general x3, matrix products, fold_blocks(): jnp.einsum('rkgnb,nbkh->rkgnh', weights, value_part, preferred_element_ty...  9.27 us
  transfers between devices with their start and end apart: 3, of which 1 were waited for; matrix products, arithmetic and copies ran while one was open for 13% of the time, Pallas kernels for 0%

commit v1 on v0

--- a/solution.py
+++ b/solution.py
@@ -126,15 +126,22 @@
     return shaped.astype(jnp.bfloat16).reshape(row_count, HEADS * HEAD)
 
 
-def run_experts(buffer, expert_up, expert_down):
-    gate_up = jnp.einsum("sjcd,jdf->sjcf", buffer, expert_up, preferred_element_type=jnp.float32)
-    hidden_width = expert_down.shape[1]
-    active = (jax.nn.silu(gate_up[..., :hidden_width]) * gate_up[..., hidden_width:]).astype(
-        jnp.bfloat16
-    )
-    return jnp.einsum(
-        "sjcf,jfd->sjcd", active, expert_down, preferred_element_type=jnp.float32
-    ).astype(jnp.bfloat16)
+def route_tables(routes, route_scores, replica_slot, slot_total):
+    row_count = routes.shape[0]
+    experts = jnp.arange(replica_slot.shape[1], dtype=jnp.int32)
+    slot_ids = jnp.sum(
+        jnp.where(routes[:, :, None] == experts, replica_slot[:, None, :], 0), axis=2
+    )
+    shares = route_scores / jnp.sum(route_scores, axis=1, keepdims=True)
+    slots = jnp.arange(slot_total, dtype=jnp.int32)[:, None, None]
+    hot = slot_ids[None] == slots
+    share_of = jnp.sum(jnp.where(hot, shares[None], 0.0), axis=2)
+    here = jnp.any(hot, axis=2).astype(jnp.bfloat16)
+    order = jnp.arange(row_count, dtype=jnp.int32)
+    earlier = (order[:, None] < order[None, :]).astype(jnp.bfloat16)
+    rank = jnp.dot(here, earlier, preferred_element_type=jnp.float32)
+    rank = jnp.where(here > 0, rank, -1.0)
+    return rank, share_of
 
 
 def shards(
@@ -156,6 +163,21 @@
     seq_count = lax.axis_size("seq")
     seq_index = lax.axis_index("seq")
     length = cache_len[0]
+    slots_dev = expert_up.shape[0]
+    req_count = lax.axis_size("req")
+    slot_total = req_count * seq_count * slots_dev
+    swap = [(i, seq_count - 1 - i) for i in range(seq_count)]
+    up_other = lax.ppermute(expert_up, "seq", swap)
+    down_other = lax.ppermute(expert_down, "seq", swap)
+    tables = jnp.stack(route_tables(routes, route_scores, replica_slot, slot_total))
+    tables = lax.all_gather(tables, "req", axis=0).reshape(
+        req_count, 2, req_count, seq_count, slots_dev, row_count
+    )
+    tables = lax.dynamic_index_in_dim(tables, lax.axis_index("req"), 2, keepdims=False)
+    own = lax.dynamic_index_in_dim(tables, seq_index, 2, keepdims=False)
+    other = lax.dynamic_index_in_dim(tables, seq_count - 1 - seq_index, 2, keepdims=False)
+    tables = jnp.concatenate([own, other], axis=2)
+    rank_here, share_here = tables[:, 0], tables[:, 1]
     group_size = HEADS // KV_HEADS
     key_width = KV_HEADS * HEAD
     query_index = seq_index * row_count + jnp.arange(row_count, dtype=jnp.int32)
@@ -197,47 +219,35 @@
         + residual_scale * jnp.dot(attended, w_out, preferred_element_type=jnp.float32)
     ).astype(jnp.bfloat16)
     expert_in = rms_scale(stream, ffn_gain)
-    top_count = routes.shape[1]
-    route_rows = row_count * top_count
     slots_dev = expert_up.shape[0]
     req_count = lax.axis_size("req")
-    device_count = req_count * seq_count
-    slot_total = device_count * slots_dev
-    capacity = 2 * ((row_count * top_count + slot_total - 1) // slot_total)
-    slot_ids = jnp.take_along_axis(replica_slot, routes, axis=1).reshape(-1)
-    slot_hot = (slot_ids[:, None] == jnp.arange(slot_total, dtype=jnp.int32)[None, :]).astype(
+    slot_total = req_count * seq_count * slots_dev
+    capacity = 2 * ((row_count * routes.shape[1] + slot_total - 1) // slot_total)
+    up_all = jnp.concatenate([expert_up, up_other], axis=0)
+    down_all = jnp.concatenate([expert_down, down_other], axis=0)
+    rows_in = lax.all_gather(expert_in, "req", axis=0)
+    pick = (rank_here[:, :, None, :] == jnp.arange(capacity, dtype=jnp.float32)[:, None]).astype(
         jnp.bfloat16
     )
-    route_order = jnp.arange(route_rows, dtype=jnp.int32)
-    earlier = (route_order[:, None] > route_order[None, :]).astype(jnp.bfloat16)
-    before = jnp.dot(earlier, slot_hot, preferred_element_type=jnp.float32)
-    slot_rank = jnp.sum(before * slot_hot.astype(jnp.float32), axis=1).astype(jnp.int32)
-    position = slot_ids * capacity + slot_rank
-    place = jnp.any(
-        (jnp.arange(slot_total * capacity, dtype=jnp.int32)[:, None] == position[None, :]).reshape(
-            slot_total * capacity, row_count, top_count
-        ),
-        axis=2,
-    ).astype(jnp.bfloat16)
-    outgoing = jnp.dot(place, expert_in, preferred_element_type=jnp.float32).astype(jnp.bfloat16)
-    outgoing = outgoing.reshape(device_count, slots_dev, capacity, -1)
-    returned = lax.all_to_all(
-        run_experts(
-            lax.all_to_all(outgoing, ("req", "seq"), split_axis=0, concat_axis=0, tiled=True),
-            expert_up,
-            expert_down,
-        ),
-        ("req", "seq"),
-        split_axis=0,
-        concat_axis=0,
-        tiled=True,
-    )
-    flat_back = returned.reshape(slot_total * capacity, -1)
-    picked = flat_back[position].reshape(row_count, top_count, -1)
-    shares = route_scores / jnp.sum(route_scores, axis=1, keepdims=True)
-    expert_mix = jnp.sum(picked.astype(jnp.float32) * shares[:, :, None], axis=1).astype(
-        jnp.bfloat16
-    )
+    share_rows = jnp.sum(pick.astype(jnp.float32) * share_here[:, :, None, :], axis=-1)
+    share_rows = jnp.swapaxes(share_rows, 0, 1)
+    gathered = jnp.einsum(
+        "ijct,itd->jicd", pick, rows_in, preferred_element_type=jnp.float32
+    ).astype(jnp.bfloat16)
+    gate_up = jnp.einsum("jicd,jdf->jicf", gathered, up_all, preferred_element_type=jnp.float32)
+    hidden_width = expert_down.shape[1]
+    active = (
+        jax.nn.silu(gate_up[..., :hidden_width])
+        * gate_up[..., hidden_width:]
+        * share_rows[..., None]
+    ).astype(jnp.bfloat16)
+    outputs = jnp.einsum(
+        "jicf,jfd->jicd", active, down_all, preferred_element_type=jnp.float32
+    ).astype(jnp.bfloat16)
+    partial = jnp.einsum(
+        "ijct,jicd->itd", pick, outputs, preferred_element_type=jnp.float32
+    ).astype(jnp.bfloat16)
+    expert_mix = lax.psum_scatter(partial, "req", scatter_dimension=0)
     return (attended, stream, expert_mix, appended)
 
 

time: 458 us -> 381 us (0.83)
  blocking collectives: 148 us -> 2.42 us
  waiting for transfers between devices: 137 us -> 240 us
  local copies, waits for them, and re-layouts: 67.5 us -> 31.9 us
  matrix products: 46.6 us -> 64.7 us
  other arithmetic: 37.2 us -> 23.6 us
    all_to_all x1 -> x0, blocking collectives: 146 us -> none  [shards(): lax.all_to_all(outgoing, ('req', 'seq'), split_axis=0, concat_axis=0, til...]
    reduce_scatter x0 -> x1, waiting for transfers between devices: none -> 143 us  [shards(): expert_mix = lax.psum_scatter(partial, 'req', scatter_dimension=0)]
    all_to_all x1 -> x0, waiting for transfers between devices: 135 us -> none  [shards(): lax.all_to_all(run_experts(lax.all_to_all(outgoing, ('req', 'seq'), split...]
    all_gather x0 -> x2, waiting for transfers between devices: none -> 86.2 us  [the longest x1 86.2 us: shards(): rows_in = lax.all_gather(expert_in, 'req', axis=0)]
    gather x6 -> x0, local copies, waits for them, and re-layouts: 18.3 us -> none  [the longest x1 10.9 us: shards(): picked = flat_back[position].reshape(row_count, top_count, -1)]
    dot_general x4 -> x3, matrix products: 18.5 us -> 30.5 us  [the longest x1 18.9 us: shards(): jnp.einsum('jicd,jdf->jicf', gathered, up_all, preferred_element_type=jnp...]
    dot_general x3, matrix products: 9.27 us -> 18.6 us  [fold_blocks(): jnp.einsum('rkgnb,nbkh->rkgnh', weights, value_part, preferred_element_ty...]
    ppermute x0 -> x2, waiting for transfers between devices: none -> 8.74 us  [the longest x1 8.74 us: shards(): up_other = lax.ppermute(expert_up, 'seq', swap)]
  transfers between devices with their start and end apart: 3 -> 7, of which waited for: 1 -> 3; matrix products, arithmetic and copies ran while one was open for 13% -> 28% of each run, Pallas kernels for 0% -> 0%
where the time goes in v1:
time: 381 us; the launch traced here: 380 us
  waiting for transfers between devices  240 us (63%)
  matrix products  64.7 us (17%)
  local copies, waits for them, and re-layouts  31.9 us (8%)
  other arithmetic  23.6 us (6%)
  between operations  14.8 us (4%)
    reduce_scatter x1, waiting for transfers between devices, shards(): expert_mix = lax.psum_scatter(partial, 'req', scatter_dimension=0)  143 us
    all_gather x1, waiting for transfers between devices, shards(): rows_in = lax.all_gather(expert_in, 'req', axis=0)  86.2 us
    dot_general x1, matrix products, shards(): jnp.einsum('jicd,jdf->jicf', gathered, up_all, preferred_element_type=jnp...  18.9 us
    dot_general x3, matrix products, fold_blocks(): jnp.einsum('rkgnb,nbkh->rkgnh', weights, value_part, preferred_element_ty...  18.6 us
    unnamed x17, local copies, waits for them, and re-layouts  12.8 us
    reduce_sum x3, other arithmetic, fold_blocks(): totals = jnp.sum(weights, axis=-1, dtype=jnp.float32)  11.6 us
    dot_general x1, matrix products, shards(): jnp.einsum('ijct,jicd->itd', pick, outputs, preferred_element_type=jnp.fl...  11.5 us
    ppermute x1, waiting for transfers between devices, shards(): up_other = lax.ppermute(expert_up, 'seq', swap)  8.74 us
  transfers between devices with their start and end apart: 7, of which 3 were waited for; matrix products, arithmetic and copies ran while one was open for 28% of the time, Pallas kernels for 0%

profile of v1, /device:TPU:0, one launch (start us, length us, event | category | flops | bytes accessed | tf_op | source)
XLA Modules:
  0.0 379.6 jit_solution(12890986667288845805)
XLA Ops:
  13.1 4.7 %fusion.60 = f32[128,2560]{1,0:T(8,128)S(1)} fusion(bf16[1536,2560]{1,0:T(8,128)(2,1)} %param.17, bf16[128,1536]{1,0:T(8,128)(2,1)} %param.15, f32[1536]{0:T(1024)} %param.16, f32[128]{0:T(128)S(1)} %add_rsqrt_fusion.1), kind=kOutput, calls=%fused_computation.82 | convolution fusion | flops 1007419392 | bytes 9574912 | tf_op jit(solution)/shard_map/dot_general | solution.py:44
  19.1 2.4 all-gather
  24.1 1.7 copy-done.2
  25.8 1.8 convert_reduce_fusion.1
  27.6 6.2 %reshape.186 = bf16[2,8,128,8,64]{4,3,2,1,0:T(8,128)(2,1)} reshape(bf16[1,2048,512]{2,1,0:T(8,128)(2,1)} %all-gather.8.cloned.1.call-done) | data formatting | bytes 4194304 | tf_op jit(solution)/shard_map/reshape;reshape;squeeze | solution.py:88
  33.8 4.7 %copy.102 = bf16[2,8,128,8,64]{2,4,1,3,0:T(8,128)(2,1)S(1)} copy(bf16[2,8,128,8,64]{4,3,2,1,0:T(8,128)(2,1)} %reshape.186) | data formatting | bytes 4194304
  38.6 6.2 %reshape.187 = bf16[2,8,128,8,64]{4,3,2,1,0:T(8,128)(2,1)} reshape(bf16[1,2048,512]{2,1,0:T(8,128)(2,1)} %all-gather.10.cloned.1.call-done) | data formatting | bytes 4194304 | tf_op jit(solution)/shard_map/reshape;reshape;squeeze | solution.py:89
  44.8 5.5 %copy.103 = bf16[2,8,128,8,64]{2,4,1,3,0:T(8,128)(2,1)} copy(bf16[2,8,128,8,64]{4,3,2,1,0:T(8,128)(2,1)} %reshape.187) | data formatting | bytes 4194304
  50.9 40.9 %while.5 = (s32[]{:T(128)}, f32[128,8,3]{0,2,1:T(4,128)S(1)}, f32[128,8,3]{0,2,1:T(4,128)}, f32[128,8,3,64]{0,3,2,1:T(8,128)S(1)}, s32[2]{0:T(128)}, /*index=5*/...) while((s32[]{:T(128)}, f32[128,8,3]{0,2,1:T(4,128)S(1)}, ...), condition=%wide.region_7.8_spmd.clone, body=%wide.region_1.7_spmd.clone.sunk | while | flops 856075264 | bytes 94794512 | solution.py:97
  50.9 1.3 dynamic_slice.59
  53.6 3.5 fusion.92
  57.1 4.9 %convert_reduce_fusion.3 = (f32[128,8,3,8]{0,2,3,1:T(4,128)S(1)}, f32[128,8,3]{0,2,1:T(4,128)}) fusion(f32[128,8,3,8]{0,2,3,1:T(4,128)S(1)} %get-tuple-element.343, f32[8,8,128,128,3]{3,2,4,1,0:T(8,128)S(1)} %get-tuple-element.344, pred[8,128]{1,0:T(8,128)(4,1)S(1)} %add_compare_fusion.2), kind=kLoop, calls=%fused_computation.5.clone.1 | loop fusion | flops 25138176 | bytes 12792832 | tf_op jit(solution)/shard_map/while/body/eval_jaxpr/reduce_sum | solution.py:67
  62.8 7.9 %fusion.94 = f32[128,8,3,64]{0,3,2,1:T(8,128)S(1)} fusion(f32[128,8,3,8]{0,2,3,1:T(4,128)S(1)} %get-tuple-element.349, bf16[2,8,128,8,64]{2,4,1,3,0:T(8,128)(2,1)} %get-tuple-element.383, s32[]{:T(128)} %get-tuple-element.363, f32[8,8,128,128,3]{3,2,4,1,0:T(8,128)} %copy-done, f32[128,8,3,8]{0,2,3,1:T(4,128)S(1)} %get-tuple-element.343, ...), kind=kOutput, calls=%fused_computation.9.clone.1 | convolution fusion | flops 418185216 | bytes 14616064 | tf_op jit(solution)/shard_map/while/body/eval_jaxpr/rkgnb,nbkh->rkgnh/dot_general | solution.py:68
  71.4 1.3 dynamic_slice.59
  74.1 3.5 fusion.92
  77.6 4.9 %convert_reduce_fusion.3 = (f32[128,8,3,8]{0,2,3,1:T(4,128)S(1)}, f32[128,8,3]{0,2,1:T(4,128)}) fusion(f32[128,8,3,8]{0,2,3,1:T(4,128)S(1)} %get-tuple-element.343, f32[8,8,128,128,3]{3,2,4,1,0:T(8,128)S(1)} %get-tuple-element.344, pred[8,128]{1,0:T(8,128)(4,1)S(1)} %add_compare_fusion.2), kind=kLoop, calls=%fused_computation.5.clone.1 | loop fusion | flops 25138176 | bytes 12792832 | tf_op jit(solution)/shard_map/while/body/eval_jaxpr/reduce_sum | solution.py:67
  83.3 7.8 %fusion.94 = f32[128,8,3,64]{0,3,2,1:T(8,128)S(1)} fusion(f32[128,8,3,8]{0,2,3,1:T(4,128)S(1)} %get-tuple-element.349, bf16[2,8,128,8,64]{2,4,1,3,0:T(8,128)(2,1)} %get-tuple-element.383, s32[]{:T(128)} %get-tuple-element.363, f32[8,8,128,128,3]{3,2,4,1,0:T(8,128)} %copy-done, f32[128,8,3,8]{0,2,3,1:T(4,128)S(1)} %get-tuple-element.343, ...), kind=kOutput, calls=%fused_computation.9.clone.1 | convolution fusion | flops 418185216 | bytes 14616064 | tf_op jit(solution)/shard_map/while/body/eval_jaxpr/rkgnb,nbkh->rkgnh/dot_general | solution.py:68
  94.1 2.9 fusion.44
  97.3 3.3 fusion.48
  103.6 8.7 %collective-permute-done = bf16[2,1536,1024]{2,1,0:T(8,128)(2,1)} collective-permute-done((bf16[2,1536,1024]{2,1,0:T(8,128)(2,1)}, bf16[2,1536,1024]{2,1,0:T(8,128)(2,1)}, u32[]{:S(2)}, u32[]{:S(2)}) %collective-permute-start) | collective-permute-done | bytes 6291488 | tf_op jit(solution)/shard_map/ppermute | solution.py:170
  112.3 86.2 %all-gather.14.cloned.1.call-done = bf16[2048,1536]{1,0:T(8,128)(2,1)} async-done(((bf16[128,1536]{1,0:T(8,128)(2,1)}), bf16[2048,1536]{1,0:T(8,128)(2,1)}) %all-gather.14.cloned.1.call-update) | async-done | bytes 6291472 | tf_op jit(solution)/shard_map/all_gather | solution.py:228
  198.5 18.9 %fusion.19 = f32[4,16,32,1024]{3,2,1,0:T(8,128)} fusion(bf16[2,1536,1024]{2,1,0:T(8,128)(2,1)} %collective-permute-done, bf16[2,1536,1024]{2,1,0:T(8,128)(2,1)} %param.26, bf16[16,128,1536,1]{2,1,0,3:T(8,128)(2,1)} %bitcast.154, f32[16,4,128]{2,1,0:T(4,128)S(1)} %copy.113), kind=kOutput, calls=%fused_computation.30 | convolution fusion | flops 7257456640 | bytes 27295744 | tf_op jit(solution)/shard_map/jicd,jdf->jicf/dot_general | solution.py:237
  217.4 11.5 %bitcast_convert_fusion = bf16[16,128,1536]{2,1,0:T(8,128)(2,1)} fusion(bf16[2,512,1536]{2,1,0:T(8,128)(2,1)} %collective-permute-done.1, bf16[2,512,1536]{2,1,0:T(8,128)(2,1)} %param.27, f32[16,4,128]{2,1,0:T(4,128)S(1)} %copy.113, f32[4,16,32,1024]{3,2,1,0:T(8,128)} %fusion.19, f32[4,16,32]{2,1,0:T(8,128)S(1)} %copy.116), kind=kOutput, calls=%fused_computation.33 | convolution fusion | flops 4043571200 | bytes 21012480 | tf_op jit(solution)/shard_map/ijct,jicd->itd/dot_general | solution.py:247
  229.9 143.2 %reduce-scatter.2.cloned.1.call-done = bf16[1,128,1536]{2,1,0:T(8,128)(2,1)} async-done(((bf16[16,128,1536]{2,1,0:T(8,128)(2,1)}), bf16[1,128,1536]{2,1,0:T(8,128)(2,1)}) %reduce-scatter.2.cloned.1.call-update) | async-done | bytes 393232 | tf_op jit(solution)/shard_map/reduce_scatter | solution.py:250
  (106 shorter events, 20.1 us)
Async XLA Ops:
  7.2 20.4 %all-gather.8.cloned.1.call-start = ((), (), s32[]{:S(2)}) async-start(), calls=%async_computation.1 | async-start | bytes 3145728 | tf_op jit(solution)/shard_map/all_gather | solution.py:189
  7.9 30.7 %all-gather.10.cloned.1.call-start = ((), (), s32[]{:S(2)}) async-start(), calls=%async_computation.2 | async-start | bytes 3145728 | tf_op jit(solution)/shard_map/all_gather | solution.py:190
  8.6 93.7 %all-gather.12.cloned.1.call-start = ((), (), s32[]{:S(2)}) async-start(), calls=%async_computation.4 | async-start | bytes 1114112 | tf_op jit(solution)/shard_map/all_gather | solution.py:173
  11.8 186.7 %all-gather.14.cloned.1.call-start = ((), (), s32[]{:S(2)}) async-start(), calls=%async_computation.5 | async-start | bytes 6684672 | tf_op jit(solution)/shard_map/all_gather | solution.py:228
  19.1 2.5 copy-start.4
  23.4 10.4 %copy-start.8 = (pred[128,2,128]{0,2,1:T(8,128)(4,1)}, pred[128,2,128]{0,2,1:T(8,128)(4,1)S(1)}, u32[]{:S(2)}) copy-start(pred[128,2,128]{0,2,1:T(8,128)(4,1)S(1)} %broadcast_compare_fusion) | copy-start | bytes 98308
  24.1 1.7 copy-start.2
  24.1 9.7 %copy-start.9 = (f32[128,8,3,2]{0,2,3,1:T(4,128)}, f32[128,8,3,2]{0,2,3,1:T(4,128)S(1)}, u32[]{:S(2)}) copy-start(f32[128,8,3,2]{0,2,3,1:T(4,128)S(1)} %get-tuple-element.272) | copy-start | bytes 73732
  53.6 3.5 copy-start.7
  57.1 4.9 %copy-start = (f32[8,8,128,128,3]{3,2,4,1,0:T(8,128)}, f32[8,8,128,128,3]{3,2,4,1,0:T(8,128)S(1)}, u32[]{:S(2)}) copy-start(f32[8,8,128,128,3]{3,2,4,1,0:T(8,128)S(1)} %get-tuple-element.344) | copy-start | bytes 37748740 | tf_op jit(solution)/shard_map/while
  62.8 7.9 %copy-start.5 = (f32[128,8,3]{0,2,1:T(4,128)S(1)}, f32[128,8,3]{0,2,1:T(4,128)}, u32[]{:S(2)}) copy-start(f32[128,8,3]{0,2,1:T(4,128)} %get-tuple-element.365) | copy-start | bytes 36868 | tf_op jit(solution)/shard_map/while
  70.8 0.6 copy-start.6
  74.0 3.5 copy-start.7
  77.6 4.9 %copy-start = (f32[8,8,128,128,3]{3,2,4,1,0:T(8,128)}, f32[8,8,128,128,3]{3,2,4,1,0:T(8,128)S(1)}, u32[]{:S(2)}) copy-start(f32[8,8,128,128,3]{3,2,4,1,0:T(8,128)S(1)} %get-tuple-element.344) | copy-start | bytes 37748740 | tf_op jit(solution)/shard_map/while
  83.3 7.9 %copy-start.5 = (f32[128,8,3]{0,2,1:T(4,128)S(1)}, f32[128,8,3]{0,2,1:T(4,128)}, u32[]{:S(2)}) copy-start(f32[128,8,3]{0,2,1:T(4,128)} %get-tuple-element.365) | copy-start | bytes 36868 | tf_op jit(solution)/shard_map/while
  91.2 0.6 copy-start.6
  91.8 5.5 %copy-start.1 = (bf16[128,1536]{1,0:T(8,128)(2,1)S(1)}, bf16[128,1536]{1,0:T(8,128)(2,1)}, u32[]{:S(2)}) copy-start(bf16[128,1536]{1,0:T(8,128)(2,1)} %param.15) | copy-start | bytes 1179652
  97.0 3.5 copy-start.10
  100.5 116.9 %copy-start.3 = (bf16[128,1536]{1,0:T(8,128)(2,1)}, bf16[128,1536]{1,0:T(8,128)(2,1)S(1)}, u32[]{:S(2)}) copy-start(bf16[128,1536]{1,0:T(8,128)(2,1)S(1)} %get-tuple-element.275) | copy-start | bytes 1179652
  101.5 271.6 %reduce-scatter.2.cloned.1.call-start = ((), (), s32[]{:S(2)}) async-start(), calls=%async_computation.3 | async-start | bytes 6684672 | tf_op jit(solution)/shard_map/reduce_scatter | solution.py:250
  101.8 10.6 %collective-permute-start = (bf16[2,1536,1024]{2,1,0:T(8,128)(2,1)}, bf16[2,1536,1024]{2,1,0:T(8,128)(2,1)}, u32[]{:S(2)}, u32[]{:S(2)}) collective-permute-start(bf16[2,1536,1024]{2,1,0:T(8,128)(2,1)} %param.26), channel_id=1, source_target_pairs={{0,1},{1,0},{2,3},{3,2},{4,5},{5,4},{6,7},{7,6},{8,9},{9,8},{10,11... | collective-permute-start | bytes 18874376 | tf_op jit(solution)/shard_map/ppermute | solution.py:170
  102.2 115.2 %collective-permute-start.1 = (bf16[2,512,1536]{2,1,0:T(8,128)(2,1)}, bf16[2,512,1536]{2,1,0:T(8,128)(2,1)}, u32[]{:S(2)}, u32[]{:S(2)}) collective-permute-start(bf16[2,512,1536]{2,1,0:T(8,128)(2,1)} %param.27), channel_id=1, source_target_pairs={{0,1},{1,0},{2,3},{3,2},{4,5},{5,4},{6,7},{7,6},{8,9},{9,8},{10,11... | collective-permute-start | bytes 9437192 | tf_op jit(solution)/shard_map/ppermute | solution.py:171
Sparse Core Ops, SparseCore 0:
  9.5 13.3 all-gather.7
  24.5 12.0 all-gather.9
  39.9 56.4 all-gather.11
  101.6 96.8 all-gather.13
  229.1 143.9 reduce-scatter.1

commit v2 on v0

v2 whole, which is shorter than its diff:
```python
import functools
import math

import jax
import jax.numpy as jnp
from jax import lax
from jax.experimental import pallas as pl
from jax.experimental.pallas import tpu as pltpu
from jax.sharding import PartitionSpec as P

HEADS = 24
KV_HEADS = 8
HEAD = 64
GROUP = HEADS // KV_HEADS
LANES = 128
PAIR = 2 * GROUP * HEAD

epsilon = 1e-06
residual_scale = 0.22
score_scale = 0.015625
rope_base = 10000.0
neg_big = -1e30

BOTH = ("req", "seq")


def vmem_spec():
    return pl.BlockSpec(memory_space=pltpu.VMEM)


def params(mebibytes):
    return pltpu.CompilerParams(vmem_limit_bytes=mebibytes * 2**20)


def qkv_kernel(own_ref, other_ref, gain_ref, cos_ref, sin_ref, w_ref, q_ref, kv_ref, kvo_ref, normed):
    step = pl.program_id(0)
    rows = own_ref.shape[0]
    width = w_ref.shape[1]

    @pl.when(step == 0)
    def _():
        for index, ref in enumerate((own_ref, other_ref)):
            wide = ref[...].astype(jnp.float32)
            mean_square = jnp.mean(wide * wide, axis=-1, keepdims=True)
            normed[index * rows : (index + 1) * rows] = (
                wide * lax.rsqrt(mean_square + epsilon) * gain_ref[...]
            ).astype(jnp.bfloat16)

    def rotated(x, row_slice):
        lane = lax.broadcasted_iota(jnp.int32, x.shape, 1)
        low = (lane & (HEAD - 1)) < HEAD // 2
        swapped = jnp.where(
            low, pltpu.roll(x, width - HEAD // 2, 1), pltpu.roll(x, HEAD // 2, 1)
        )
        times = width // LANES
        cosine = jnp.concatenate([cos_ref[row_slice]] * times, axis=1)
        sine = jnp.concatenate([sin_ref[row_slice]] * times, axis=1)
        return x * cosine + swapped * sine

    @pl.when(step < 3)
    def _():
        x = jnp.dot(normed[:rows], w_ref[...], preferred_element_type=jnp.float32)
        q_ref[...] = (rotated(x, slice(0, rows)) * score_scale).astype(jnp.bfloat16)

    @pl.when(step == 3)
    def _():
        x = jnp.dot(normed[...], w_ref[...], preferred_element_type=jnp.float32)
        x = rotated(x, slice(0, 2 * rows)).astype(jnp.bfloat16)
        kv_ref[...] = x[:rows]
        kvo_ref[...] = x[rows:]

    @pl.when(step == 4)
    def _():
        x = jnp.dot(normed[...], w_ref[...], preferred_element_type=jnp.float32)
        x = x.astype(jnp.bfloat16)
        kv_ref[...] = x[:rows]
        kvo_ref[...] = x[rows:]


def project(own, other, gain, cosine, sine, w_qkv):
    rows, width = own.shape
    tile = KV_HEADS * HEAD
    return pl.pallas_call(
        qkv_kernel,
        grid=(5,),
        in_specs=[vmem_spec()] * 5 + [pl.BlockSpec((width, tile), lambda i: (0, i))],
        out_specs=[
            pl.BlockSpec((rows, tile), lambda i: (0, jnp.minimum(i, 2))),
            pl.BlockSpec((rows, tile), lambda i: (0, jnp.maximum(i - 3, 0))),
            pl.BlockSpec((rows, tile), lambda i: (0, jnp.maximum(i - 3, 0))),
        ],
        out_shape=[
            jax.ShapeDtypeStruct((rows, HEADS * HEAD), jnp.bfloat16),
            jax.ShapeDtypeStruct((rows, 2 * tile), jnp.bfloat16),
            jax.ShapeDtypeStruct((rows, 2 * tile), jnp.bfloat16),
        ],
        scratch_shapes=[pltpu.VMEM((2 * rows, width), jnp.bfloat16)],
        compiler_params=params(24),
        cost_estimate=pl.CostEstimate(
            flops=2 * rows * width * 3584, bytes_accessed=9_500_000, transcendentals=0
        ),
        name="project_rows",
    )(own, other, gain[None], cosine, sine, w_qkv)


def attend_kernel(
    first_row,
    place_ref,
    q_ref,
    kc_ref,
    kco_ref,
    vc_ref,
    vco_ref,
    ks_ref,
    kso_ref,
    vs_ref,
    vso_ref,
    w_out_ref,
    tokens_ref,
    gain_ref,
    attended_ref,
    stream_ref,
    expert_in_ref,
    keys,
    values,
    wide_q,
    total,
):
    step = pl.program_id(0)
    rows = q_ref.shape[0]
    cached = kc_ref.shape[1]
    span = ks_ref.shape[0]
    seq_index = place_ref[0]
    length = place_ref[1]

    @pl.when(step == 0)
    def _():
        position = lax.broadcasted_iota(jnp.int32, (cached, LANES), 0)
        for index, half in enumerate((seq_index, 1 - seq_index)):
            visible = position + half * cached < length
            keys[index * cached : (index + 1) * cached, LANES:] = jnp.where(
                visible, 0.0, neg_big
            ).astype(jnp.bfloat16)
        key = lax.broadcasted_iota(jnp.int32, (span, LANES), 0)
        row = lax.broadcasted_iota(jnp.int32, (span, LANES), 1)
        keys[2 * cached : 2 * cached + span, LANES:] = jnp.where(key <= row, 0.0, neg_big).astype(
            jnp.bfloat16
        )
        keys[2 * cached + span :, LANES:] = jnp.where(
            jnp.zeros((span, LANES), jnp.int32) < seq_index, 0.0, neg_big
        ).astype(jnp.bfloat16)
        values[:, LANES:] = jnp.ones((values.shape[0], LANES), jnp.bfloat16)
        row = lax.broadcasted_iota(jnp.int32, (rows, LANES), 0) + first_row
        lane = lax.broadcasted_iota(jnp.int32, (rows, LANES), 1)
        chosen = jnp.where(row == lane, 1.0, 0.0).astype(jnp.bfloat16)
        for head in range(2 * GROUP):
            wide_q[head * rows : (head + 1) * rows, LANES:] = chosen

    for ref, parts in ((keys, (kc_ref, kco_ref)), (values, (vc_ref, vco_ref))):
        for index, part in enumerate(parts):
            ref[index * cached : (index + 1) * cached, :LANES] = part[0]
    for ref, parts in ((keys, (ks_ref, kso_ref)), (values, (vs_ref, vso_ref))):
        for index, part in enumerate(parts):
            start = 2 * cached + index * span
            ref[start : start + span, :LANES] = part[...]

    low = lax.broadcasted_iota(jnp.int32, (rows, LANES), 1) < HEAD
    tiles = [q_ref[:, i * LANES : (i + 1) * LANES].astype(jnp.float32) for i in range(3)]
    parts = [
        jnp.where(low, tiles[0], 0.0),
        jnp.where(low, pltpu.roll(tiles[0], HEAD, 1), 0.0),
        jnp.where(low, tiles[1], 0.0),
        jnp.where(low, 0.0, tiles[1]),
        jnp.where(low, 0.0, pltpu.roll(tiles[2], HEAD, 1)),
        jnp.where(low, 0.0, tiles[2]),
    ]
    for head, part in enumerate(parts):
        wide_q[head * rows : (head + 1) * rows, :LANES] = part.astype(jnp.bfloat16)

    heads = []
    for head in range(2 * GROUP):
        scores = lax.dot_general(
            wide_q[head * rows : (head + 1) * rows],
            keys[...],
            (((1,), (1,)), ((), ())),
            preferred_element_type=jnp.float32,
        )
        best = jnp.max(scores, axis=-1, keepdims=True)
        weights = jnp.exp(scores - best).astype(jnp.bfloat16)
        sums = jnp.dot(weights, values[...], preferred_element_type=jnp.float32)
        heads.append(sums[:, :LANES] / sums[:, LANES:])
    merged = jnp.concatenate(
        [
            jnp.where(low, heads[0], pltpu.roll(heads[1], HEAD, 1)),
            jnp.where(low, heads[2], heads[3]),
            jnp.where(low, pltpu.roll(heads[4], HEAD, 1), heads[5]),
        ],
        axis=1,
    ).astype(jnp.bfloat16)
    attended_ref[...] = merged
    product = jnp.dot(merged, w_out_ref[...], preferred_element_type=jnp.float32)

    @pl.when(step == 0)
    def _():
        total[...] = product

    @pl.when(step > 0)
    def _():
        total[...] += product

    @pl.when(step == pl.num_programs(0) - 1)
    def _():
        stream = (tokens_ref[...].astype(jnp.float32) + residual_scale * total[...]).astype(
            jnp.bfloat16
        )
        stream_ref[...] = stream
        wide = stream.astype(jnp.float32)
        mean_square = jnp.mean(wide * wide, axis=-1, keepdims=True)
        expert_in_ref[...] = (wide * lax.rsqrt(mean_square + epsilon) * gain_ref[...]).astype(
            jnp.bfloat16
        )


def attend(place, queries, caches, spans, w_out, tokens, gain, first_row, rows):
    k_cache, k_other, v_cache, v_other = caches
    own_span, other_span = spans
    cached = k_cache.shape[1]
    span = own_span.shape[0]
    width = tokens.shape[1]
    pairs = KV_HEADS // 2
    part = first_row // rows
    key_count = 2 * cached + 2 * span
    cache_spec = pl.BlockSpec((1, cached, LANES), lambda j: (0, 0, j))
    key_spec = pl.BlockSpec((span, LANES), lambda j: (0, j))
    value_spec = pl.BlockSpec((span, LANES), lambda j: (0, pairs + j))
    return pl.pallas_call(
        functools.partial(attend_kernel, first_row),
        grid=(pairs,),
        in_specs=[
            pl.BlockSpec(memory_space=pltpu.SMEM),
            pl.BlockSpec((rows, PAIR), lambda j: (part, j)),
            cache_spec,
            cache_spec,
            cache_spec,
            cache_spec,
            key_spec,
            key_spec,
            value_spec,
            value_spec,
            pl.BlockSpec((PAIR, width), lambda j: (j, 0)),
            pl.BlockSpec((rows, width), lambda j: (part, 0)),
            vmem_spec(),
        ],
        out_specs=[
            pl.BlockSpec((rows, PAIR), lambda j: (0, j)),
            pl.BlockSpec((rows, width), lambda j: (0, 0)),
            pl.BlockSpec((rows, width), lambda j: (0, 0)),
        ],
        out_shape=[
            jax.ShapeDtypeStruct((rows, HEADS * HEAD), jnp.bfloat16),
            jax.ShapeDtypeStruct((rows, width), jnp.bfloat16),
            jax.ShapeDtypeStruct((rows, width), jnp.bfloat16),
        ],
        scratch_shapes=[
            pltpu.VMEM((key_count, 2 * LANES), jnp.bfloat16),
            pltpu.VMEM((key_count, 2 * LANES), jnp.bfloat16),
            pltpu.VMEM((2 * GROUP * rows, 2 * LANES), jnp.bfloat16),
            pltpu.VMEM((rows, width), jnp.float32),
        ],
        compiler_params=params(40),
        cost_estimate=pl.CostEstimate(
            flops=8 * HEADS * rows * key_count * LANES,
            bytes_accessed=10_000_000,
            transcendentals=HEADS * rows * key_count,
        ),
        name="attend_rows",
    )(
        place,
        queries,
        k_cache,
        k_other,
        v_cache,
        v_other,
        own_span,
        other_span,
        own_span,
        other_span,
        w_out,
        tokens,
        gain[None],
    )


def expert_kernel(sources, capacity, slot_ref, *refs):
    row_refs = refs[:sources]
    table_ref, up_ref, up_other_ref, down_ref, down_other_ref = refs[sources : sources + 5]
    out_refs = refs[sources + 5 : 2 * sources + 5]
    held, pick, share_rows = refs[2 * sources + 5 :]
    step = pl.program_id(0)
    slots = held.shape[0]
    own_slots = slots // 2
    tokens = row_refs[0].shape[0]
    hidden = down_ref.shape[1]
    top = table_ref.shape[1] // 2

    @pl.when(step == 0)
    def _():
        hot_rows, share_lines = [], []
        for source in range(sources):
            ids = table_ref[source, :top]
            shares = table_ref[source, top:]
            for slot in range(slots):
                match = ids == slot_ref[slot].astype(jnp.float32)
                hot_rows.append(
                    jnp.max(jnp.where(match, 1.0, 0.0), axis=0, keepdims=True)
                )
                share_lines.append(
                    jnp.sum(jnp.where(match, shares, 0.0), axis=0, keepdims=True)
                )
        hot = jnp.concatenate(hot_rows, axis=0)
        earlier = jnp.where(
            lax.broadcasted_iota(jnp.int32, (tokens, tokens), 0)
            < lax.broadcasted_iota(jnp.int32, (tokens, tokens), 1),
            1.0,
            0.0,
        ).astype(jnp.bfloat16)
        rank = jnp.dot(hot.astype(jnp.bfloat16), earlier, preferred_element_type=jnp.float32)
        rank = jnp.where(hot > 0.0, rank, -1.0)
        place = lax.broadcasted_iota(jnp.int32, (capacity, tokens), 0).astype(jnp.float32)
        for source in range(sources):
            picks = []
            for slot in range(slots):
                line = source * slots + slot
                chosen = jnp.where(place == rank[line : line + 1], 1.0, 0.0)
                share_rows[slot, source * capacity : (source + 1) * capacity] = jnp.sum(
                    chosen * share_lines[line], axis=1, keepdims=True
                )
                picks.append(chosen)
            picked = jnp.concatenate(picks, axis=0)
            pick[source] = jnp.transpose(picked).astype(jnp.bfloat16)
            rows = jnp.dot(
                picked.astype(jnp.bfloat16),
                row_refs[source][...],
                preferred_element_type=jnp.float32,
            ).astype(jnp.bfloat16)
            for slot in range(slots):
                held[slot, source * capacity : (source + 1) * capacity] = rows[
                    slot * capacity : (slot + 1) * capacity
                ]

    def run(up, down):
        gate_up = jnp.dot(held[step], up[0], preferred_element_type=jnp.float32)
        active = (
            jax.nn.silu(gate_up[:, :hidden]) * gate_up[:, hidden:] * share_rows[step]
        ).astype(jnp.bfloat16)
        held[step] = jnp.dot(active, down[0], preferred_element_type=jnp.float32).astype(
            jnp.bfloat16
        )

    @pl.when(step < own_slots)
    def _():
        run(up_ref, down_ref)

    @pl.when(step >= own_slots)
    def _():
        run(up_other_ref, down_other_ref)

    @pl.when(step == slots - 1)
    def _():
        for source in range(sources):
            rows = jnp.concatenate(
                [
                    held[slot, source * capacity : (source + 1) * capacity]
                    for slot in range(slots)
                ],
                axis=0,
            )
            out_refs[source][...] = jnp.dot(
                pick[source], rows, preferred_element_type=jnp.float32
            ).astype(jnp.bfloat16)


def run_experts(slot_ids, rows, tables, ups, downs, capacity):
    sources = len(rows)
    tokens, width = rows[0].shape
    own_slots, _, double = ups[0].shape
    hidden = double // 2
    slots = 2 * own_slots

    def own(j):
        return (jnp.minimum(j, own_slots - 1), 0, 0)

    def other(j):
        return (jnp.maximum(j - own_slots, 0), 0, 0)

    return pl.pallas_call(
        functools.partial(expert_kernel, sources, capacity),
        grid=(slots,),
        in_specs=[pl.BlockSpec(memory_space=pltpu.SMEM)]
        + [vmem_spec()] * (sources + 1)
        + [
            pl.BlockSpec((1, width, double), own),
            pl.BlockSpec((1, width, double), other),
            pl.BlockSpec((1, hidden, width), own),
            pl.BlockSpec((1, hidden, width), other),
        ],
        out_specs=[vmem_spec()] * sources,
        out_shape=[jax.ShapeDtypeStruct((tokens, width), jnp.bfloat16)] * sources,
        scratch_shapes=[
            pltpu.VMEM((slots, sources * capacity, width), jnp.bfloat16),
            pltpu.VMEM((sources, tokens, slots * capacity), jnp.bfloat16),
            pltpu.VMEM((slots, sources * capacity, 1), jnp.float32),
        ],
        compiler_params=params(48),
        cost_estimate=pl.CostEstimate(
            flops=6 * slots * sources * capacity * width * hidden,
            bytes_accessed=26_000_000,
            transcendentals=slots * sources * capacity * hidden,
        ),
        name="run_experts",
    )(slot_ids, *rows, tables, ups[0], ups[1], downs[0], downs[1])


def chip_shape(chips):
    depth = 4 if chips % 4 == 0 else 1
    plane = chips // depth
    side = math.isqrt(plane)
    while plane % side:
        side -= 1
    return depth, plane // side, side


def make_shift(chips, cores):
    depth, tall, wide = chip_shape(chips)
    swap = tall == wide
    sizes = {"z": depth, "a": tall, "b": wide}

    def pairs(role, offset):
        out = []
        for z in range(depth):
            for y in range(tall):
                for x in range(wide):
                    for core in range(cores):
                        axis = role
                        if swap and core % 2 == 1:
                            axis = {"z": "z", "a": "b", "b": "a"}[role]
                        to_z, to_y, to_x = z, y, x
                        if axis == "z":
                            to_z = (z + offset) % depth
                        elif axis == "a":
                            to_y = (y + offset) % tall
                        else:
                            to_x = (x + offset) % wide
                        source = ((z * tall + y) * wide + x) * cores + core
                        target = ((to_z * tall + to_y) * wide + to_x) * cores + core
                        out.append((source, target))
        return out

    def shift(value, role, offset):
        return lax.ppermute(value, BOTH, pairs(role, offset % sizes[role]))

    return shift, sizes


def gather_blocks(value, shift, sizes):
    line = [value] + [shift(value, "z", k) for k in range(1, sizes["z"])]
    plane = [line] + [[shift(v, "a", j) for v in line] for j in range(1, sizes["a"])]
    return [plane] + [
        [[shift(v, "b", k) for v in row] for row in plane] for k in range(1, sizes["b"])
    ]


def gather_stacked(value, shift, sizes):
    stacked = value[None]
    for role in ("z", "a", "b"):
        stacked = jnp.concatenate(
            [stacked] + [shift(stacked, role, k) for k in range(1, sizes[role])], axis=0
        )
    return stacked


def add_all(terms):
    total = terms[0].astype(jnp.float32)
    for term in terms[1:]:
        total = total + term.astype(jnp.float32)
    return total.astype(terms[0].dtype)


def scatter_blocks(blocks, shift, sizes):
    plane = [
        [
            add_all(
                [blocks[0][j][i]]
                + [shift(blocks[k][j][i], "b", -k) for k in range(1, sizes["b"])]
            )
            for i in range(sizes["z"])
        ]
        for j in range(sizes["a"])
    ]
    line = [
        add_all([plane[0][i]] + [shift(plane[j][i], "a", -j) for j in range(1, sizes["a"])])
        for i in range(sizes["z"])
    ]
    return add_all([line[0]] + [shift(line[i], "z", -i) for i in range(1, sizes["z"])])


def rope_tables(positions):
    half = HEAD // 2
    frequency = rope_base ** (-jnp.arange(half, dtype=jnp.float32) / half)
    angles = positions.astype(jnp.float32)[:, None] * frequency[None, :]
    cosine, sine = jnp.cos(angles), jnp.sin(angles)
    return (
        jnp.concatenate([cosine] * 4, axis=1),
        jnp.concatenate([-sine, sine, -sine, sine], axis=1),
    )


def shards(
    tokens,
    attn_gain,
    w_qkv,
    w_out,
    k_cache,
    v_cache,
    cache_len,
    ffn_gain,
    routes,
    route_scores,
    replica_slot,
    expert_up,
    expert_down,
):
    row_count, top_count = routes.shape
    chips, cores = lax.axis_size("req"), lax.axis_size("seq")
    seq_index = lax.axis_index("seq")
    length = cache_len[0]
    slots_dev = expert_up.shape[0]
    slot_total = chips * cores * slots_dev
    capacity = 2 * ((row_count * top_count + slot_total - 1) // slot_total)
    shift, sizes = make_shift(chips, cores)

    def swap(value):
        return lax.ppermute(value, "seq", [(0, 1), (1, 0)])

    other_tokens = swap(tokens)
    k_other, v_other = swap(k_cache), swap(v_cache)

    experts = jnp.arange(replica_slot.shape[1], dtype=jnp.int32)
    slot_of = jnp.sum(
        jnp.where(routes[:, :, None] == experts, replica_slot[:, None, :], 0), axis=2
    )
    shares = route_scores / jnp.sum(route_scores, axis=1, keepdims=True)
    table = jnp.concatenate([slot_of.astype(jnp.float32), shares], axis=1).T
    tables = gather_stacked(table, shift, sizes)

    row_index = jnp.arange(row_count, dtype=jnp.int32)
    cosine, sine = rope_tables(
        length
        + jnp.concatenate(
            [seq_index * row_count + row_index, (1 - seq_index) * row_count + row_index]
        )
    )
    queries, appended, other_span = project(tokens, other_tokens, attn_gain, cosine, sine, w_qkv)
    place = jnp.stack([seq_index, length]).astype(jnp.int32)
    attended, stream, expert_in = attend(
        place,
        queries,
        (k_cache, k_other, v_cache, v_other),
        (appended, other_span),
        w_out,
        tokens,
        ffn_gain,
        0,
        row_count,
    )
    up_other, down_other = swap(expert_up), swap(expert_down)
    chip_slots = jnp.arange(slots_dev, dtype=jnp.int32)
    core_base = lax.axis_index("req") * cores
    slot_ids = jnp.concatenate(
        [
            (core_base + seq_index) * slots_dev + chip_slots,
            (core_base + 1 - seq_index) * slots_dev + chip_slots,
        ]
    ).astype(jnp.int32)
    blocks = gather_blocks(expert_in, shift, sizes)
    in_group = sizes["a"] * sizes["z"]
    results = []
    for index, plane in enumerate(blocks):
        flat = run_experts(
            slot_ids,
            [value for line in plane for value in line],
            tables[index * in_group : (index + 1) * in_group],
            (expert_up, up_other),
            (expert_down, down_other),
            capacity,
        )
        results.append(
            [flat[j * sizes["z"] : (j + 1) * sizes["z"]] for j in range(sizes["a"])]
        )
    expert_mix = scatter_blocks(results, shift, sizes)
    return (attended, stream, expert_mix, appended)


def solution(mesh):
    return jax.shard_map(
        shards,
        mesh=mesh,
        in_specs=(
            P(("req", "seq"), None),
            P(),
            P(),
            P(),
            P("req", "seq", None),
            P("req", "seq", None),
            P("req"),
            P(),
            P(("req", "seq"), None),
            P(("req", "seq"), None),
            P(("req", "seq"), None),
            P(("req", "seq"), None, None),
            P(("req", "seq"), None, None),
        ),
        out_specs=(
            P(("req", "seq"), None),
            P(("req", "seq"), None),
            P(("req", "seq"), None),
            P(("req", "seq"), None),
        ),
        check_vma=False,
    )
```

time: 458 us -> 242 us (0.53)
  blocking collectives: 148 us -> 0 us
  Pallas kernels: 0 us -> 54.2 us
  local copies, waits for them, and re-layouts: 67.5 us -> 13.3 us
  starting transfers between devices: 3.94 us -> 51.6 us
  matrix products: 46.6 us -> 0 us
  other arithmetic: 37.2 us -> 5.07 us
  waiting for transfers between devices: 137 us -> 116 us
  between operations: 15.1 us -> 1.58 us
    all_to_all x1 -> x0, blocking collectives: 146 us -> none  [shards(): lax.all_to_all(outgoing, ('req', 'seq'), split_axis=0, concat_axis=0, til...]
    all_to_all x1 -> x0, waiting for transfers between devices: 135 us -> none  [shards(): lax.all_to_all(run_experts(lax.all_to_all(outgoing, ('req', 'seq'), split...]
    ppermute x0 -> x40, waiting for transfers between devices: none -> 116 us  [the longest x35 116 us: shift(): return lax.ppermute(value, BOTH, pairs(role, offset % sizes[role]))]
    pallas_call x0 -> x4, Pallas kernels: none -> 54.2 us  [the longest x2 25.8 us: run_experts(): pl.pallas_call(functools.partial(expert_kernel, sources, capacity), grid=...]
    ppermute x0 -> x40, starting transfers between devices: none -> 51.6 us  [the longest x35 50.5 us: shift(): return lax.ppermute(value, BOTH, pairs(role, offset % sizes[role]))]
    dot_general x12 -> x0, matrix products: 46.6 us -> none  [the longest x3 10.8 us: fold_blocks(): jnp.einsum('rkgh,nbkh->rkgnb', queries, key_part, preferred_element_type=...]
    gather x6 -> x0, local copies, waits for them, and re-layouts: 18.3 us -> none  [the longest x1 10.9 us: shards(): picked = flat_back[position].reshape(row_count, top_count, -1)]
    reduce_sum x8 -> x1, other arithmetic: 18.3 us -> 0.76 us  [shards(): jnp.sum(jnp.where(routes[:, :, None] == experts, replica_slot[:, None, :]...]
  transfers between devices with their start and end apart: 3 -> 40, of which waited for: 1 -> 18; matrix products, arithmetic and copies ran while one was open for 13% -> 2% of each run, Pallas kernels for 0% -> 17%
where the time goes in v2:
time: 242 us; the launch traced here: 241 us
  waiting for transfers between devices  116 us (48%)
  Pallas kernels  54.2 us (22%)
  starting transfers between devices  51.6 us (21%)
  local copies, waits for them, and re-layouts  13.3 us (5%)
  other arithmetic  5.07 us (2%)
    ppermute x35, waiting for transfers between devices, shift(): return lax.ppermute(value, BOTH, pairs(role, offset % sizes[role]))  116 us
    ppermute x35, starting transfers between devices, shift(): return lax.ppermute(value, BOTH, pairs(role, offset % sizes[role]))  50.5 us
    pallas_call x2, Pallas kernels, run_experts(): pl.pallas_call(functools.partial(expert_kernel, sources, capacity), grid=...  25.8 us
    pallas_call x1, Pallas kernels, attend(): pl.pallas_call(functools.partial(attend_kernel, first_row), grid=(pairs,)...  23.5 us
    unnamed x37, local copies, waits for them, and re-layouts  11.9 us
  transfers between devices with their start and end apart: 40, of which 18 were waited for; matrix products, arithmetic and copies ran while one was open for 2% of the time, Pallas kernels for 17%

profile of v2, /device:TPU:0, one launch (start us, length us, event | category | flops | bytes accessed | tf_op | source)
XLA Modules:
  0.0 241.4 jit_solution(3086807635667562758)
XLA Ops:
  3.3 2.6 %collective-permute-start.10 = (f32[1,16,128]{2,1,0:T(8,128)S(1)}, f32[1,16,128]{2,1,0:T(8,128)S(1)}, u32[]{:S(2)}, u32[]{:S(2)}) collective-permute-start(f32[1,16,128]{2,1,0:T(8,128)S(1)} %maximum_bitcast_fusion), channel_id=1, source_target_pairs={{0,8},{1,9},{2,10},{3,11},{4,12},{5,13},{6,14},{7,15},{8,16},{9,17... | collective-permute-start | bytes 24584 | tf_op jit(solution)/shard_map/ppermute | solution.py:460
  6.0 2.6 %collective-permute-start.11 = (f32[1,16,128]{2,1,0:T(8,128)S(1)}, f32[1,16,128]{2,1,0:T(8,128)S(1)}, u32[]{:S(2)}, u32[]{:S(2)}) collective-permute-start(f32[1,16,128]{2,1,0:T(8,128)S(1)} %maximum_bitcast_fusion), channel_id=1, source_target_pairs={{0,16},{1,17},{2,18},{3,19},{4,20},{5,21},{6,22},{7,23},{8,24},{9,... | collective-permute-start | bytes 24584 | tf_op jit(solution)/shard_map/ppermute | solution.py:460
  12.1 2.3 collective-permute-done.12
  19.9 3.2 %copy-done = bf16[1536,2560]{1,0:T(8,128)(2,1)S(1)} copy-done((bf16[1536,2560]{1,0:T(8,128)(2,1)S(1)}, bf16[1536,2560]{1,0:T(8,128)(2,1)}, u32[]{:S(2)}) %copy-start) | copy-done | bytes 7864344
  24.1 4.8 %project_rows.1 = (bf16[128,1536]{1,0:T(8,128)(2,1)S(1)}, bf16[128,1024]{1,0:T(8,128)(2,1)}, bf16[128,1024]{1,0:T(8,128)(2,1)S(1)}) custom-call(bf16[128,1536]{1,0:T(8,128)(2,1)S(1)} %copy-done.1, bf16[128,1536]{1,0:T(8,128)(2,1)S(1)} %collective-permute-done.other_ref, f32[1,1536]{1,0:T(1,128)S(1)} %broadcast_in_dim.27.gain_ref, ...), custom_call_target="tpu_custom_call" | custom-call | flops 1409286144 | bytes 9500000 | tf_op jit(solution)/shard_map/project_rows/pallas_call | solution.py:83
  30.0 23.5 %attend_rows.1 = (bf16[128,1536]{1,0:T(8,128)(2,1)}, bf16[128,1536]{1,0:T(8,128)(2,1)}, bf16[128,1536]{1,0:T(8,128)(2,1)S(1)}) custom-call(s32[2]{0:T(128)S(1)} %pad_add_fusion.place_ref, bf16[128,1536]{1,0:T(8,128)(2,1)S(1)} %get-tuple-element.26.q_ref, bf16[1,1024,512]{2,1,0:T(8,128)(2,1)S(1)} %copy-done.14, ...), custom_call_target="tpu_custom_call" | custom-call | flops 7247757312 | bytes 10000000 | tf_op jit(solution)/shard_map/attend_rows/pallas_call | solution.py:236
  53.7 3.5 %collective-permute-start.4 = (bf16[128,1536]{1,0:T(8,128)(2,1)S(1)}, bf16[128,1536]{1,0:T(8,128)(2,1)S(1)}, u32[]{:S(2)}, u32[]{:S(2)}) collective-permute-start(bf16[128,1536]{1,0:T(8,128)(2,1)S(1)} %get-tuple-element.31.refs_0_), channel_id=1, source_target_pairs={{0,16},{1,17},{2,18},{3,19},{4,20},{5,21},{6,22},{7,23},{8,24},{9,... | collective-permute-start | bytes 1179656 | tf_op jit(solution)/shard_map/ppermute | solution.py:460
  57.9 9.4 %collective-permute-done.3.refs_1_ = bf16[128,1536]{1,0:T(8,128)(2,1)S(1)} collective-permute-done((bf16[128,1536]{1,0:T(8,128)(2,1)S(1)}, bf16[128,1536]{1,0:T(8,128)(2,1)S(1)}, u32[]{:S(2)}, u32[]{:S(2)}) %collective-permute-start.3) | collective-permute-done | bytes 393248 | tf_op jit(solution)/shard_map/ppermute | solution.py:460
  68.9 14.6 %collective-permute-done.4.refs_2_ = bf16[128,1536]{1,0:T(8,128)(2,1)S(1)} collective-permute-done((bf16[128,1536]{1,0:T(8,128)(2,1)S(1)}, bf16[128,1536]{1,0:T(8,128)(2,1)S(1)}, u32[]{:S(2)}, u32[]{:S(2)}) %collective-permute-start.4) | collective-permute-done | bytes 393248 | tf_op jit(solution)/shard_map/ppermute | solution.py:460
  86.4 9.1 %collective-permute-done.16.refs_0_ = bf16[128,1536]{1,0:T(8,128)(2,1)S(1)} collective-permute-done((bf16[128,1536]{1,0:T(8,128)(2,1)S(1)}, bf16[128,1536]{1,0:T(8,128)(2,1)S(1)}, u32[]{:S(2)}, u32[]{:S(2)}) %collective-permute-start.16) | collective-permute-done | bytes 393248 | tf_op jit(solution)/shard_map/ppermute | solution.py:460
  97.5 2.4 collective-permute-done.8.refs_6_
  101.3 7.2 %collective-permute-done.9.refs_7_ = bf16[128,1536]{1,0:T(8,128)(2,1)} collective-permute-done((bf16[128,1536]{1,0:T(8,128)(2,1)S(1)}, bf16[128,1536]{1,0:T(8,128)(2,1)}, u32[]{:S(2)}, u32[]{:S(2)}) %collective-permute-start.9) | collective-permute-done | bytes 393248 | tf_op jit(solution)/shard_map/ppermute | solution.py:460
  113.5 2.7 %collective-permute-done.19.refs_3_ = bf16[128,1536]{1,0:T(8,128)(2,1)S(1)} collective-permute-done((bf16[128,1536]{1,0:T(8,128)(2,1)S(1)}, bf16[128,1536]{1,0:T(8,128)(2,1)S(1)}, u32[]{:S(2)}, u32[]{:S(2)}) %collective-permute-start.19) | collective-permute-done | bytes 393248 | tf_op jit(solution)/shard_map/ppermute | solution.py:460
  124.7 4.2 %collective-permute-done.22.refs_6_ = bf16[128,1536]{1,0:T(8,128)(2,1)} collective-permute-done((bf16[128,1536]{1,0:T(8,128)(2,1)S(1)}, bf16[128,1536]{1,0:T(8,128)(2,1)}, u32[]{:S(2)}, u32[]{:S(2)}) %collective-permute-start.22) | collective-permute-done | bytes 393248 | tf_op jit(solution)/shard_map/ppermute | solution.py:460
  128.9 4.2 %collective-permute-done.23.refs_7_ = bf16[128,1536]{1,0:T(8,128)(2,1)} collective-permute-done((bf16[128,1536]{1,0:T(8,128)(2,1)}, bf16[128,1536]{1,0:T(8,128)(2,1)}, u32[]{:S(2)}, u32[]{:S(2)}) %collective-permute-start.23) | collective-permute-done | bytes 393248 | tf_op jit(solution)/shard_map/ppermute | solution.py:460
  137.0 13.1 %run_experts.3 = (bf16[128,1536]{1,0:T(8,128)(2,1)S(1)}, bf16[128,1536]{1,0:T(8,128)(2,1)S(1)}, bf16[128,1536]{1,0:T(8,128)(2,1)S(1)}, bf16[128,1536]{1,0:T(8,12...) custom-call(s32[4]{0:T(128)S(1)} %pad_add_fusion.1.slot_ref, ...), custom_call_target="tpu_custom_call" | custom-call | flops 4831838208 | bytes 26000000 | tf_op jit(solution)/shard_map/run_experts/pallas_call | solution.py:396
  155.6 12.8 %run_experts.2 = (bf16[128,1536]{1,0:T(8,128)(2,1)S(1)}, bf16[128,1536]{1,0:T(8,128)(2,1)S(1)}, bf16[128,1536]{1,0:T(8,128)(2,1)S(1)}, bf16[128,1536]{1,0:T(8,12...) custom-call(s32[4]{0:T(128)S(1)} %pad_add_fusion.1.slot_ref, ...), custom_call_target="tpu_custom_call" | custom-call | flops 4831838208 | bytes 26000000 | tf_op jit(solution)/shard_map/run_experts/pallas_call | solution.py:396
  172.0 7.0 %collective-permute-done.37 = bf16[128,1536]{1,0:T(8,128)(2,1)S(1)} collective-permute-done((bf16[128,1536]{1,0:T(8,128)(2,1)S(1)}, bf16[128,1536]{1,0:T(8,128)(2,1)S(1)}, u32[]{:S(2)}, u32[]{:S(2)}) %collective-permute-start.37) | collective-permute-done | bytes 393248 | tf_op jit(solution)/shard_map/ppermute | solution.py:460
  181.2 8.6 %collective-permute-done.30 = bf16[128,1536]{1,0:T(8,128)(2,1)S(1)} collective-permute-done((bf16[128,1536]{1,0:T(8,128)(2,1)S(1)}, bf16[128,1536]{1,0:T(8,128)(2,1)S(1)}, u32[]{:S(2)}, u32[]{:S(2)}) %collective-permute-start.30) | collective-permute-done | bytes 393248 | tf_op jit(solution)/shard_map/ppermute | solution.py:460
  192.1 6.2 %collective-permute-done.34 = bf16[128,1536]{1,0:T(8,128)(2,1)S(1)} collective-permute-done((bf16[128,1536]{1,0:T(8,128)(2,1)S(1)}, bf16[128,1536]{1,0:T(8,128)(2,1)S(1)}, u32[]{:S(2)}, u32[]{:S(2)}) %collective-permute-start.34) | collective-permute-done | bytes 393248 | tf_op jit(solution)/shard_map/ppermute | solution.py:460
  198.2 7.5 %collective-permute-start.31 = (bf16[128,1536]{1,0:T(8,128)(2,1)S(1)}, bf16[128,1536]{1,0:T(8,128)(2,1)S(1)}, u32[]{:S(2)}, u32[]{:S(2)}) collective-permute-start(bf16[128,1536]{1,0:T(8,128)(2,1)S(1)} %add_convert_fusion.7), channel_id=1, source_target_pairs={{0,24},{1,25},{2,26},{3,27},{4,28},{5,29},{6,30},{7,31},{8,0},{9,1... | collective-permute-start | bytes 1179656 | tf_op jit(solution)/shard_map/ppermute | solution.py:460
  206.1 2.4 %collective-permute-start.39 = (bf16[128,1536]{1,0:T(8,128)(2,1)S(1)}, bf16[128,1536]{1,0:T(8,128)(2,1)S(1)}, u32[]{:S(2)}, u32[]{:S(2)}) collective-permute-start(bf16[128,1536]{1,0:T(8,128)(2,1)S(1)} %add_convert_fusion.1), channel_id=1, source_target_pairs={{0,8},{1,9},{2,10},{3,11},{4,12},{5,13},{6,14},{7,15},{8,16},{9,17... | collective-permute-start | bytes 1179656 | tf_op jit(solution)/shard_map/ppermute | solution.py:460
  208.5 5.6 %collective-permute-done.31 = bf16[128,1536]{1,0:T(8,128)(2,1)S(1)} collective-permute-done((bf16[128,1536]{1,0:T(8,128)(2,1)S(1)}, bf16[128,1536]{1,0:T(8,128)(2,1)S(1)}, u32[]{:S(2)}, u32[]{:S(2)}) %collective-permute-start.31) | collective-permute-done | bytes 393248 | tf_op jit(solution)/shard_map/ppermute | solution.py:460
  214.1 26.2 %collective-permute-done.35 = bf16[128,1536]{1,0:T(8,128)(2,1)S(1)} collective-permute-done((bf16[128,1536]{1,0:T(8,128)(2,1)S(1)}, bf16[128,1536]{1,0:T(8,128)(2,1)S(1)}, u32[]{:S(2)}, u32[]{:S(2)}) %collective-permute-start.35) | collective-permute-done | bytes 393248 | tf_op jit(solution)/shard_map/ppermute | solution.py:460
  (124 shorter events, 54.2 us)
Async XLA Ops:
  0.6 132.5 %collective-permute-start.14 = (bf16[2,1536,1024]{2,1,0:T(8,128)(2,1)}, bf16[2,1536,1024]{2,1,0:T(8,128)(2,1)}, u32[]{:S(2)}, u32[]{:S(2)}) collective-permute-start(bf16[2,1536,1024]{2,1,0:T(8,128)(2,1)} %refs_9_.3), channel_id=1, source_target_pairs={{0,1},{1,0},{2,3},{3,2},{4,5},{5,4},{6,7},{7,6},{8,9},{9,8},{10,11... | collective-permute-start | bytes 18874376 | tf_op jit(solution)/shard_map/ppermute | solution.py:543
  8.5 20.4 %collective-permute-start.1 = (bf16[1,1024,512]{2,1,0:T(8,128)(2,1)}, bf16[1,1024,512]{2,1,0:T(8,128)(2,1)S(1)}, u32[]{:S(2)}, u32[]{:S(2)}) collective-permute-start(bf16[1,1024,512]{2,1,0:T(8,128)(2,1)} %kc_ref.1), channel_id=1, source_target_pairs={{0,1},{1,0},{2,3},{3,2},{4,5},{5,4},{6,7},{7,6},{8,9},{9,8},{10,11... | collective-permute-start | bytes 3145736 | tf_op jit(solution)/shard_map/ppermute | solution.py:543
  8.6 20.4 %collective-permute-start.2 = (bf16[1,1024,512]{2,1,0:T(8,128)(2,1)}, bf16[1,1024,512]{2,1,0:T(8,128)(2,1)S(1)}, u32[]{:S(2)}, u32[]{:S(2)}) collective-permute-start(bf16[1,1024,512]{2,1,0:T(8,128)(2,1)} %vc_ref.1), channel_id=1, source_target_pairs={{0,1},{1,0},{2,3},{3,2},{4,5},{5,4},{6,7},{7,6},{8,9},{9,8},{10,11... | collective-permute-start | bytes 3145736 | tf_op jit(solution)/shard_map/ppermute | solution.py:543
  18.3 114.9 %collective-permute-start.15 = (bf16[2,512,1536]{2,1,0:T(8,128)(2,1)}, bf16[2,512,1536]{2,1,0:T(8,128)(2,1)}, u32[]{:S(2)}, u32[]{:S(2)}) collective-permute-start(bf16[2,512,1536]{2,1,0:T(8,128)(2,1)} %refs_11_.3), channel_id=1, source_target_pairs={{0,1},{1,0},{2,3},{3,2},{4,5},{5,4},{6,7},{7,6},{8,9},{9,8},{10,11... | collective-permute-start | bytes 9437192 | tf_op jit(solution)/shard_map/ppermute | solution.py:543
  18.3 38.8 %collective-permute-start.24 = (f32[8,16,128]{2,1,0:T(8,128)S(1)}, f32[8,16,128]{2,1,0:T(8,128)S(1)}, u32[]{:S(2)}, u32[]{:S(2)}) collective-permute-start(f32[8,16,128]{2,1,0:T(8,128)S(1)} %constant_dynamic-update-slice_fusion.refs_8_), channel_id=1, source_target_pairs={{0,2},{1,5},{2,0},{3,7},{4,6},{5,1},{6,4},{7,3},{8,10},{9,13},{10,... | collective-permute-start | bytes 196616 | tf_op jit(solution)/shard_map/ppermute | solution.py:460
  53.4 13.9 %collective-permute-start.3 = (bf16[128,1536]{1,0:T(8,128)(2,1)S(1)}, bf16[128,1536]{1,0:T(8,128)(2,1)S(1)}, u32[]{:S(2)}, u32[]{:S(2)}) collective-permute-start(bf16[128,1536]{1,0:T(8,128)(2,1)S(1)} %get-tuple-element.31.refs_0_), channel_id=1, source_target_pairs={{0,8},{1,9},{2,10},{3,11},{4,12},{5,13},{6,14},{7,15},{8,16},{9,17... | collective-permute-start | bytes 1179656 | tf_op jit(solution)/shard_map/ppermute | solution.py:460
  53.7 29.8 %collective-permute-start.4 = (bf16[128,1536]{1,0:T(8,128)(2,1)S(1)}, bf16[128,1536]{1,0:T(8,128)(2,1)S(1)}, u32[]{:S(2)}, u32[]{:S(2)}) collective-permute-start(bf16[128,1536]{1,0:T(8,128)(2,1)S(1)} %get-tuple-element.31.refs_0_), channel_id=1, source_target_pairs={{0,16},{1,17},{2,18},{3,19},{4,20},{5,21},{6,22},{7,23},{8,24},{9,... | collective-permute-start | bytes 1179656 | tf_op jit(solution)/shard_map/ppermute | solution.py:460
  57.8 26.5 %collective-permute-start.5 = (bf16[128,1536]{1,0:T(8,128)(2,1)S(1)}, bf16[128,1536]{1,0:T(8,128)(2,1)S(1)}, u32[]{:S(2)}, u32[]{:S(2)}) collective-permute-start(bf16[128,1536]{1,0:T(8,128)(2,1)S(1)} %get-tuple-element.31.refs_0_), channel_id=1, source_target_pairs={{0,24},{1,25},{2,26},{3,27},{4,28},{5,29},{6,30},{7,31},{8,0},{9,1... | collective-permute-start | bytes 1179656 | tf_op jit(solution)/shard_map/ppermute | solution.py:460
  67.3 18.2 %collective-permute-start.6 = (bf16[128,1536]{1,0:T(8,128)(2,1)S(1)}, bf16[128,1536]{1,0:T(8,128)(2,1)S(1)}, u32[]{:S(2)}, u32[]{:S(2)}) collective-permute-start(bf16[128,1536]{1,0:T(8,128)(2,1)S(1)} %get-tuple-element.31.refs_0_), channel_id=1, source_target_pairs={{0,4},{1,3},{2,6},{3,1},{4,0},{5,7},{6,2},{7,5},{8,12},{9,11},{10,... | collective-permute-start | bytes 1179656 | tf_op jit(solution)/shard_map/ppermute | solution.py:460
  85.5 14.4 %collective-permute-start.8 = (bf16[128,1536]{1,0:T(8,128)(2,1)S(1)}, bf16[128,1536]{1,0:T(8,128)(2,1)S(1)}, u32[]{:S(2)}, u32[]{:S(2)}) collective-permute-start(bf16[128,1536]{1,0:T(8,128)(2,1)S(1)} %collective-permute-done.4.refs_2_), channel_id=1, source_target_pairs={{0,4},{1,3},{2,6},{3,1},{4,0},{5,7},{6,2},{7,5},{8,12},{9,11},{10,... | collective-permute-start | bytes 1179656 | tf_op jit(solution)/shard_map/ppermute | solution.py:460
  95.5 12.9 %collective-permute-start.9 = (bf16[128,1536]{1,0:T(8,128)(2,1)S(1)}, bf16[128,1536]{1,0:T(8,128)(2,1)}, u32[]{:S(2)}, u32[]{:S(2)}) collective-permute-start(bf16[128,1536]{1,0:T(8,128)(2,1)S(1)} %collective-permute-done.5.refs_3_), channel_id=1, source_target_pairs={{0,4},{1,3},{2,6},{3,1},{4,0},{5,7},{6,2},{7,5},{8,12},{9,11},{10,... | collective-permute-start | bytes 1179656 | tf_op jit(solution)/shard_map/ppermute | solution.py:460
  96.0 13.8 %collective-permute-start.17 = (bf16[128,1536]{1,0:T(8,128)(2,1)S(1)}, bf16[128,1536]{1,0:T(8,128)(2,1)S(1)}, u32[]{:S(2)}, u32[]{:S(2)}) collective-permute-start(bf16[128,1536]{1,0:T(8,128)(2,1)S(1)} %collective-permute-done.3.refs_1_), channel_id=1, source_target_pairs={{0,2},{1,5},{2,0},{3,7},{4,6},{5,1},{6,4},{7,3},{8,10},{9,13},{10,... | collective-permute-start | bytes 1179656 | tf_op jit(solution)/shard_map/ppermute | solution.py:460
  150.1 18.3 %collective-permute-start.26 = (bf16[128,1536]{1,0:T(8,128)(2,1)S(1)}, bf16[128,1536]{1,0:T(8,128)(2,1)S(1)}, u32[]{:S(2)}, u32[]{:S(2)}) collective-permute-start(bf16[128,1536]{1,0:T(8,128)(2,1)S(1)} %get-tuple-element.35), channel_id=1, source_target_pairs={{0,2},{1,5},{2,0},{3,7},{4,6},{5,1},{6,4},{7,3},{8,10},{9,13},{10,... | collective-permute-start | bytes 1179656 | tf_op jit(solution)/shard_map/ppermute | solution.py:460
  151.5 17.7 %collective-permute-start.29 = (bf16[128,1536]{1,0:T(8,128)(2,1)S(1)}, bf16[128,1536]{1,0:T(8,128)(2,1)S(1)}, u32[]{:S(2)}, u32[]{:S(2)}) collective-permute-start(bf16[128,1536]{1,0:T(8,128)(2,1)S(1)} %get-tuple-element.39), channel_id=1, source_target_pairs={{0,2},{1,5},{2,0},{3,7},{4,6},{5,1},{6,4},{7,3},{8,10},{9,13},{10,... | collective-permute-start | bytes 1179656 | tf_op jit(solution)/shard_map/ppermute | solution.py:460
  152.2 27.7 %collective-permute-start.28 = (bf16[128,1536]{1,0:T(8,128)(2,1)S(1)}, bf16[128,1536]{1,0:T(8,128)(2,1)S(1)}, u32[]{:S(2)}, u32[]{:S(2)}) collective-permute-start(bf16[128,1536]{1,0:T(8,128)(2,1)S(1)} %get-tuple-element.37), channel_id=1, source_target_pairs={{0,2},{1,5},{2,0},{3,7},{4,6},{5,1},{6,4},{7,3},{8,10},{9,13},{10,... | collective-permute-start | bytes 1179656 | tf_op jit(solution)/shard_map/ppermute | solution.py:460
  153.5 17.2 %collective-permute-start.33 = (bf16[128,1536]{1,0:T(8,128)(2,1)S(1)}, bf16[128,1536]{1,0:T(8,128)(2,1)S(1)}, u32[]{:S(2)}, u32[]{:S(2)}) collective-permute-start(bf16[128,1536]{1,0:T(8,128)(2,1)S(1)} %get-tuple-element.43), channel_id=1, source_target_pairs={{0,2},{1,5},{2,0},{3,7},{4,6},{5,1},{6,4},{7,3},{8,10},{9,13},{10,... | collective-permute-start | bytes 1179656 | tf_op jit(solution)/shard_map/ppermute | solution.py:460
  154.2 36.3 %collective-permute-start.32 = (bf16[128,1536]{1,0:T(8,128)(2,1)S(1)}, bf16[128,1536]{1,0:T(8,128)(2,1)S(1)}, u32[]{:S(2)}, u32[]{:S(2)}) collective-permute-start(bf16[128,1536]{1,0:T(8,128)(2,1)S(1)} %get-tuple-element.41), channel_id=1, source_target_pairs={{0,2},{1,5},{2,0},{3,7},{4,6},{5,1},{6,4},{7,3},{8,10},{9,13},{10,... | collective-permute-start | bytes 1179656 | tf_op jit(solution)/shard_map/ppermute | solution.py:460
  169.2 36.7 %collective-permute-start.36 = (bf16[128,1536]{1,0:T(8,128)(2,1)S(1)}, bf16[128,1536]{1,0:T(8,128)(2,1)S(1)}, u32[]{:S(2)}, u32[]{:S(2)}) collective-permute-start(bf16[128,1536]{1,0:T(8,128)(2,1)S(1)} %get-tuple-element.45), channel_id=1, source_target_pairs={{0,2},{1,5},{2,0},{3,7},{4,6},{5,1},{6,4},{7,3},{8,10},{9,13},{10,... | collective-permute-start | bytes 1179656 | tf_op jit(solution)/shard_map/ppermute | solution.py:460
  170.7 37.8 %collective-permute-start.25 = (bf16[128,1536]{1,0:T(8,128)(2,1)S(1)}, bf16[128,1536]{1,0:T(8,128)(2,1)S(1)}, u32[]{:S(2)}, u32[]{:S(2)}) collective-permute-start(bf16[128,1536]{1,0:T(8,128)(2,1)S(1)} %get-tuple-element.33), channel_id=1, source_target_pairs={{0,2},{1,5},{2,0},{3,7},{4,6},{5,1},{6,4},{7,3},{8,10},{9,13},{10,... | collective-permute-start | bytes 1179656 | tf_op jit(solution)/shard_map/ppermute | solution.py:460
  179.9 28.6 %collective-permute-start.27 = (bf16[128,1536]{1,0:T(8,128)(2,1)S(1)}, bf16[128,1536]{1,0:T(8,128)(2,1)S(1)}, u32[]{:S(2)}, u32[]{:S(2)}) collective-permute-start(bf16[128,1536]{1,0:T(8,128)(2,1)S(1)} %add_convert_fusion.11), channel_id=1, source_target_pairs={{0,4},{1,3},{2,6},{3,1},{4,0},{5,7},{6,2},{7,5},{8,12},{9,11},{10,... | collective-permute-start | bytes 1179656 | tf_op jit(solution)/shard_map/ppermute | solution.py:460
  190.5 15.4 %collective-permute-start.38 = (bf16[128,1536]{1,0:T(8,128)(2,1)S(1)}, bf16[128,1536]{1,0:T(8,128)(2,1)S(1)}, u32[]{:S(2)}, u32[]{:S(2)}) collective-permute-start(bf16[128,1536]{1,0:T(8,128)(2,1)S(1)} %add_convert_fusion.2), channel_id=1, source_target_pairs={{0,4},{1,3},{2,6},{3,1},{4,0},{5,7},{6,2},{7,5},{8,12},{9,11},{10,... | collective-permute-start | bytes 1179656 | tf_op jit(solution)/shard_map/ppermute | solution.py:460
  198.2 15.9 %collective-permute-start.31 = (bf16[128,1536]{1,0:T(8,128)(2,1)S(1)}, bf16[128,1536]{1,0:T(8,128)(2,1)S(1)}, u32[]{:S(2)}, u32[]{:S(2)}) collective-permute-start(bf16[128,1536]{1,0:T(8,128)(2,1)S(1)} %add_convert_fusion.7), channel_id=1, source_target_pairs={{0,24},{1,25},{2,26},{3,27},{4,28},{5,29},{6,30},{7,31},{8,0},{9,1... | collective-permute-start | bytes 1179656 | tf_op jit(solution)/shard_map/ppermute | solution.py:460
  205.9 34.5 %collective-permute-start.35 = (bf16[128,1536]{1,0:T(8,128)(2,1)S(1)}, bf16[128,1536]{1,0:T(8,128)(2,1)S(1)}, u32[]{:S(2)}, u32[]{:S(2)}) collective-permute-start(bf16[128,1536]{1,0:T(8,128)(2,1)S(1)} %add_convert_fusion.4), channel_id=1, source_target_pairs={{0,16},{1,17},{2,18},{3,19},{4,20},{5,21},{6,22},{7,23},{8,24},{9,... | collective-permute-start | bytes 1179656 | tf_op jit(solution)/shard_map/ppermute | solution.py:460
  206.1 34.2 %collective-permute-start.39 = (bf16[128,1536]{1,0:T(8,128)(2,1)S(1)}, bf16[128,1536]{1,0:T(8,128)(2,1)S(1)}, u32[]{:S(2)}, u32[]{:S(2)}) collective-permute-start(bf16[128,1536]{1,0:T(8,128)(2,1)S(1)} %add_convert_fusion.1), channel_id=1, source_target_pairs={{0,8},{1,9},{2,10},{3,11},{4,12},{5,13},{6,14},{7,15},{8,16},{9,17... | collective-permute-start | bytes 1179656 | tf_op jit(solution)/shard_map/ppermute | solution.py:460
  (33 other events, 255.9 us)

commit v3 on v2

--- a/solution.py
+++ b/solution.py
@@ -95,7 +95,7 @@
             jax.ShapeDtypeStruct((rows, 2 * tile), jnp.bfloat16),
         ],
         scratch_shapes=[pltpu.VMEM((2 * rows, width), jnp.bfloat16)],
-        compiler_params=params(24),
+        compiler_params=params(56),
         cost_estimate=pl.CostEstimate(
             flops=2 * rows * width * 3584, bytes_accessed=9_500_000, transcendentals=0
         ),
@@ -103,29 +103,8 @@
     )(own, other, gain[None], cosine, sine, w_qkv)
 
 
-def attend_kernel(
-    first_row,
-    place_ref,
-    q_ref,
-    kc_ref,
-    kco_ref,
-    vc_ref,
-    vco_ref,
-    ks_ref,
-    kso_ref,
-    vs_ref,
-    vso_ref,
-    w_out_ref,
-    tokens_ref,
-    gain_ref,
-    attended_ref,
-    stream_ref,
-    expert_in_ref,
-    keys,
-    values,
-    wide_q,
-    total,
-):
+def attend_kernel(first_row, extra, place_ref, q_ref, kc_ref, kco_ref, vc_ref, vco_ref, ks_ref, kso_ref, vs_ref, vso_ref, w_out_ref, tokens_ref, gain_ref, *refs):
+    attended_ref, stream_ref, expert_in_ref, keys, values, wide_q, total = refs[extra:]
     step = pl.program_id(0)
     rows = q_ref.shape[0]
     cached = kc_ref.shape[1]
@@ -178,9 +157,10 @@
         wide_q[head * rows : (head + 1) * rows, :LANES] = part.astype(jnp.bfloat16)
 
     heads = []
-    for head in range(2 * GROUP):
+    batch = GROUP * rows
+    for first in range(0, 2 * GROUP * rows, batch):
         scores = lax.dot_general(
-            wide_q[head * rows : (head + 1) * rows],
+            wide_q[first : first + batch],
             keys[...],
             (((1,), (1,)), ((), ())),
             preferred_element_type=jnp.float32,
@@ -188,7 +168,8 @@
         best = jnp.max(scores, axis=-1, keepdims=True)
         weights = jnp.exp(scores - best).astype(jnp.bfloat16)
         sums = jnp.dot(weights, values[...], preferred_element_type=jnp.float32)
-        heads.append(sums[:, :LANES] / sums[:, LANES:])
+        mean = sums[:, :LANES] / sums[:, LANES:]
+        heads += [mean[i : i + rows] for i in range(0, batch, rows)]
     merged = jnp.concatenate(
         [
             jnp.where(low, heads[0], pltpu.roll(heads[1], HEAD, 1)),
@@ -221,20 +202,20 @@
         )
 
 
-def attend(place, queries, caches, spans, w_out, tokens, gain, first_row, rows):
+def attend(place, queries, caches, spans, w_out, tokens, gain, first_row, rows, filled, after):
     k_cache, k_other, v_cache, v_other = caches
     own_span, other_span = spans
     cached = k_cache.shape[1]
-    span = own_span.shape[0]
-    width = tokens.shape[1]
+    span, width = tokens.shape
     pairs = KV_HEADS // 2
     part = first_row // rows
     key_count = 2 * cached + 2 * span
     cache_spec = pl.BlockSpec((1, cached, LANES), lambda j: (0, 0, j))
     key_spec = pl.BlockSpec((span, LANES), lambda j: (0, j))
     value_spec = pl.BlockSpec((span, LANES), lambda j: (0, pairs + j))
+    extra = [*filled, *after]
     return pl.pallas_call(
-        functools.partial(attend_kernel, first_row),
+        functools.partial(attend_kernel, first_row, len(extra)),
         grid=(pairs,),
         in_specs=[
             pl.BlockSpec(memory_space=pltpu.SMEM),
@@ -250,26 +231,28 @@
             pl.BlockSpec((PAIR, width), lambda j: (j, 0)),
             pl.BlockSpec((rows, width), lambda j: (part, 0)),
             vmem_spec(),
-        ],
+        ]
+        + [pl.BlockSpec(memory_space=pl.ANY)] * len(extra),
         out_specs=[
-            pl.BlockSpec((rows, PAIR), lambda j: (0, j)),
-            pl.BlockSpec((rows, width), lambda j: (0, 0)),
+            pl.BlockSpec((rows, PAIR), lambda j: (part, j)),
+            pl.BlockSpec((rows, width), lambda j: (part, 0)),
             pl.BlockSpec((rows, width), lambda j: (0, 0)),
         ],
         out_shape=[
-            jax.ShapeDtypeStruct((rows, HEADS * HEAD), jnp.bfloat16),
-            jax.ShapeDtypeStruct((rows, width), jnp.bfloat16),
+            jax.ShapeDtypeStruct((span, HEADS * HEAD), jnp.bfloat16),
+            jax.ShapeDtypeStruct((span, width), jnp.bfloat16),
             jax.ShapeDtypeStruct((rows, width), jnp.bfloat16),
         ],
+        input_output_aliases={13 + i: i for i in range(len(filled))},
         scratch_shapes=[
             pltpu.VMEM((key_count, 2 * LANES), jnp.bfloat16),
             pltpu.VMEM((key_count, 2 * LANES), jnp.bfloat16),
             pltpu.VMEM((2 * GROUP * rows, 2 * LANES), jnp.bfloat16),
             pltpu.VMEM((rows, width), jnp.float32),
         ],
-        compiler_params=params(40),
+        compiler_params=params(36),
         cost_estimate=pl.CostEstimate(
-            flops=8 * HEADS * rows * key_count * LANES,
+            flops=16 * HEADS * rows * key_count * LANES,
             bytes_accessed=10_000_000,
             transcendentals=HEADS * rows * key_count,
         ),
@@ -288,60 +271,92 @@
         w_out,
         tokens,
         gain[None],
+        *extra,
     )
 
 
-def expert_kernel(sources, capacity, slot_ref, *refs):
-    row_refs = refs[:sources]
-    table_ref, up_ref, up_other_ref, down_ref, down_other_ref = refs[sources : sources + 5]
-    out_refs = refs[sources + 5 : 2 * sources + 5]
-    held, pick, share_rows = refs[2 * sources + 5 :]
-    step = pl.program_id(0)
-    slots = held.shape[0]
-    own_slots = slots // 2
-    tokens = row_refs[0].shape[0]
-    hidden = down_ref.shape[1]
-    top = table_ref.shape[1] // 2
-
-    @pl.when(step == 0)
-    def _():
+def plan_kernel(groups, capacity, slot_ref, chip_ref, table_ref, *out_refs):
+    slots = slot_ref.shape[0]
+    chips, height, tokens = table_ref.shape
+    top = height // 2
+    in_group = chips // groups
+    earlier = jnp.where(
+        lax.broadcasted_iota(jnp.int32, (tokens, tokens), 0)
+        < lax.broadcasted_iota(jnp.int32, (tokens, tokens), 1),
+        1.0,
+        0.0,
+    ).astype(jnp.bfloat16)
+    place = lax.broadcasted_iota(jnp.int32, (capacity, tokens), 0).astype(jnp.float32)
+    for group in range(groups):
+        pick_ref, back_ref, share_ref = out_refs[3 * group : 3 * group + 3]
         hot_rows, share_lines = [], []
-        for source in range(sources):
-            ids = table_ref[source, :top]
-            shares = table_ref[source, top:]
+        for source in range(in_group):
+            entry = table_ref[chip_ref[group * in_group + source]]
             for slot in range(slots):
-                match = ids == slot_ref[slot].astype(jnp.float32)
-                hot_rows.append(
-                    jnp.max(jnp.where(match, 1.0, 0.0), axis=0, keepdims=True)
-                )
+                match = entry[:top] == slot_ref[slot].astype(jnp.float32)
+                hot_rows.append(jnp.max(jnp.where(match, 1.0, 0.0), axis=0, keepdims=True))
                 share_lines.append(
-                    jnp.sum(jnp.where(match, shares, 0.0), axis=0, keepdims=True)
+                    jnp.sum(jnp.where(match, entry[top:], 0.0), axis=0, keepdims=True)
                 )
         hot = jnp.concatenate(hot_rows, axis=0)
-        earlier = jnp.where(
-            lax.broadcasted_iota(jnp.int32, (tokens, tokens), 0)
-            < lax.broadcasted_iota(jnp.int32, (tokens, tokens), 1),
-            1.0,
-            0.0,
-        ).astype(jnp.bfloat16)
         rank = jnp.dot(hot.astype(jnp.bfloat16), earlier, preferred_element_type=jnp.float32)
         rank = jnp.where(hot > 0.0, rank, -1.0)
-        place = lax.broadcasted_iota(jnp.int32, (capacity, tokens), 0).astype(jnp.float32)
-        for source in range(sources):
+        for source in range(in_group):
             picks = []
             for slot in range(slots):
                 line = source * slots + slot
                 chosen = jnp.where(place == rank[line : line + 1], 1.0, 0.0)
-                share_rows[slot, source * capacity : (source + 1) * capacity] = jnp.sum(
+                share_ref[slot, source * capacity : (source + 1) * capacity] = jnp.sum(
                     chosen * share_lines[line], axis=1, keepdims=True
                 )
                 picks.append(chosen)
             picked = jnp.concatenate(picks, axis=0)
-            pick[source] = jnp.transpose(picked).astype(jnp.bfloat16)
+            pick_ref[source] = picked.astype(jnp.bfloat16)
+            back_ref[source] = jnp.transpose(picked).astype(jnp.bfloat16)
+
+
+def plan_routes(slot_ids, chip_ids, tables, groups, capacity):
+    chips, _, tokens = tables.shape
+    slots = slot_ids.shape[0]
+    in_group = chips // groups
+    flat = pl.pallas_call(
+        functools.partial(plan_kernel, groups, capacity),
+        in_specs=[pl.BlockSpec(memory_space=pltpu.SMEM)] * 2 + [vmem_spec()],
+        out_specs=[vmem_spec()] * (3 * groups),
+        out_shape=[
+            jax.ShapeDtypeStruct((in_group, slots * capacity, tokens), jnp.bfloat16),
+            jax.ShapeDtypeStruct((in_group, tokens, slots * capacity), jnp.bfloat16),
+            jax.ShapeDtypeStruct((slots, in_group * capacity, 1), jnp.float32),
+        ]
+        * groups,
+        compiler_params=params(24),
+        cost_estimate=pl.CostEstimate(
+            flops=5_000_000_000, bytes_accessed=2_000_000, transcendentals=0
+        ),
+        name="plan_routes",
+    )(slot_ids, chip_ids, tables)
+    return [flat[3 * i : 3 * i + 3] for i in range(groups)]
+
+
+def expert_kernel(in_cuts, out_cuts, extra, *refs):
+    row_refs = refs[: len(in_cuts)]
+    rest = refs[len(in_cuts) :]
+    pick_ref, back_ref, share_ref, up_ref, up_other_ref, down_ref, down_other_ref = rest[:7]
+    out_refs = rest[7 + extra : 7 + extra + len(out_cuts)]
+    held = rest[-1]
+    step = pl.program_id(0)
+    slots = held.shape[0]
+    own_slots = slots // 2
+    sources = pick_ref.shape[0]
+    capacity = held.shape[1] // sources
+    hidden = down_ref.shape[1]
+
+    @pl.when(step == 0)
+    def _():
+        for source in range(sources):
+            rows = jnp.concatenate([ref[source] for ref in row_refs], axis=0)
             rows = jnp.dot(
-                picked.astype(jnp.bfloat16),
-                row_refs[source][...],
-                preferred_element_type=jnp.float32,
+                pick_ref[source], rows, preferred_element_type=jnp.float32
             ).astype(jnp.bfloat16)
             for slot in range(slots):
                 held[slot, source * capacity : (source + 1) * capacity] = rows[
@@ -351,7 +366,7 @@
     def run(up, down):
         gate_up = jnp.dot(held[step], up[0], preferred_element_type=jnp.float32)
         active = (
-            jax.nn.silu(gate_up[:, :hidden]) * gate_up[:, hidden:] * share_rows[step]
+            jax.nn.silu(gate_up[:, :hidden]) * gate_up[:, hidden:] * share_ref[step]
         ).astype(jnp.bfloat16)
         held[step] = jnp.dot(active, down[0], preferred_element_type=jnp.float32).astype(
             jnp.bfloat16
@@ -375,17 +390,19 @@
                 ],
                 axis=0,
             )
-            out_refs[source][...] = jnp.dot(
-                pick[source], rows, preferred_element_type=jnp.float32
-            ).astype(jnp.bfloat16)
-
-
-def run_experts(slot_ids, rows, tables, ups, downs, capacity):
-    sources = len(rows)
-    tokens, width = rows[0].shape
+            mixed = jnp.dot(back_ref[source], rows, preferred_element_type=jnp.float32)
+            start = 0
+            for ref, count in zip(out_refs, out_cuts):
+                ref[source] = mixed[start : start + count].astype(jnp.bfloat16)
+                start += count
+
+
+def run_experts(rows, plan, ups, downs, out_cuts, after):
+    sources, _, width = rows[0].shape
     own_slots, _, double = ups[0].shape
     hidden = double // 2
     slots = 2 * own_slots
+    places = plan[2].shape[1]
 
     def own(j):
         return (jnp.minimum(j, own_slots - 1), 0, 0)
@@ -394,31 +411,29 @@
         return (jnp.maximum(j - own_slots, 0), 0, 0)
 
     return pl.pallas_call(
-        functools.partial(expert_kernel, sources, capacity),
+        functools.partial(
+            expert_kernel, tuple(r.shape[1] for r in rows), tuple(out_cuts), len(after)
+        ),
         grid=(slots,),
-        in_specs=[pl.BlockSpec(memory_space=pltpu.SMEM)]
-        + [vmem_spec()] * (sources + 1)
+        in_specs=[vmem_spec()] * (len(rows) + 3)
         + [
             pl.BlockSpec((1, width, double), own),
             pl.BlockSpec((1, width, double), other),
             pl.BlockSpec((1, hidden, width), own),
             pl.BlockSpec((1, hidden, width), other),
-        ],
-        out_specs=[vmem_spec()] * sources,
-        out_shape=[jax.ShapeDtypeStruct((tokens, width), jnp.bfloat16)] * sources,
-        scratch_shapes=[
-            pltpu.VMEM((slots, sources * capacity, width), jnp.bfloat16),
-            pltpu.VMEM((sources, tokens, slots * capacity), jnp.bfloat16),
-            pltpu.VMEM((slots, sources * capacity, 1), jnp.float32),
-        ],
-        compiler_params=params(48),
+        ]
+        + [pl.BlockSpec(memory_space=pl.ANY)] * len(after),
+        out_specs=[vmem_spec()] * len(out_cuts),
+        out_shape=[jax.ShapeDtypeStruct((sources, c, width), jnp.bfloat16) for c in out_cuts],
+        scratch_shapes=[pltpu.VMEM((slots, places, width), jnp.bfloat16)],
+        compiler_params=params(44),
         cost_estimate=pl.CostEstimate(
-            flops=6 * slots * sources * capacity * width * hidden,
+            flops=6 * slots * places * width * hidden,
             bytes_accessed=26_000_000,
-            transcendentals=slots * sources * capacity * hidden,
+            transcendentals=slots * places * hidden,
         ),
         name="run_experts",
-    )(slot_ids, *rows, tables, ups[0], ups[1], downs[0], downs[1])
+    )(*rows, *plan, ups[0], ups[1], downs[0], downs[1], *after)
 
 
 def chip_shape(chips):
@@ -462,21 +477,13 @@
     return shift, sizes
 
 
-def gather_blocks(value, shift, sizes):
-    line = [value] + [shift(value, "z", k) for k in range(1, sizes["z"])]
-    plane = [line] + [[shift(v, "a", j) for v in line] for j in range(1, sizes["a"])]
-    return [plane] + [
-        [[shift(v, "b", k) for v in row] for row in plane] for k in range(1, sizes["b"])
-    ]
-
-
-def gather_stacked(value, shift, sizes):
+def gather_planes(value, shift, sizes):
     stacked = value[None]
-    for role in ("z", "a", "b"):
+    for role in ("z", "a"):
         stacked = jnp.concatenate(
             [stacked] + [shift(stacked, role, k) for k in range(1, sizes[role])], axis=0
         )
-    return stacked
+    return [stacked] + [shift(stacked, "b", k) for k in range(1, sizes["b"])]
 
 
 def add_all(terms):
@@ -486,22 +493,30 @@
     return total.astype(terms[0].dtype)
 
 
-def scatter_blocks(blocks, shift, sizes):
-    plane = [
-        [
-            add_all(
-                [blocks[0][j][i]]
-                + [shift(blocks[k][j][i], "b", -k) for k in range(1, sizes["b"])]
-            )
-            for i in range(sizes["z"])
-        ]
-        for j in range(sizes["a"])
-    ]
-    line = [
-        add_all([plane[0][i]] + [shift(plane[j][i], "a", -j) for j in range(1, sizes["a"])])
-        for i in range(sizes["z"])
-    ]
-    return add_all([line[0]] + [shift(line[i], "z", -i) for i in range(1, sizes["z"])])
+def scatter_planes(planes, shift, sizes):
+    deep = sizes["z"]
+    terms = [planes[0]] + [shift(planes[k], "b", -k) for k in range(1, sizes["b"])]
+
+    def part(j):
+        return [term[j * deep : (j + 1) * deep] for term in terms]
+
+    arrived = [shift(add_all(part(j)), "a", -j) for j in range(1, sizes["a"])]
+    line = part(0) + arrived
+    moved = [shift(add_all([t[i] for t in line]), "z", -i) for i in range(1, deep)]
+    return add_all([add_all([t[0] for t in line])] + moved)
+
+
+def source_chips(chip, core, chips):
+    depth, tall, wide = chip_shape(chips)
+    index = jnp.arange(chips, dtype=jnp.int32)
+    back_z, back_a, back_b = index % depth, index // depth % tall, index // (depth * tall)
+    back_y, back_x = back_a, back_b
+    if tall == wide:
+        back_y = jnp.where(core == 0, back_a, back_b)
+        back_x = jnp.where(core == 0, back_b, back_a)
+    z, y, x = chip // (tall * wide), chip // wide % tall, chip % wide
+    z, y, x = (z - back_z) % depth, (y - back_y) % tall, (x - back_x) % wide
+    return ((z * tall + y) * wide + x).astype(jnp.int32)
 
 
 def rope_tables(positions):
@@ -545,13 +560,23 @@
     other_tokens = swap(tokens)
     k_other, v_other = swap(k_cache), swap(v_cache)
 
+    up_other, down_other = swap(expert_up), swap(expert_down)
     experts = jnp.arange(replica_slot.shape[1], dtype=jnp.int32)
     slot_of = jnp.sum(
         jnp.where(routes[:, :, None] == experts, replica_slot[:, None, :], 0), axis=2
     )
     shares = route_scores / jnp.sum(route_scores, axis=1, keepdims=True)
     table = jnp.concatenate([slot_of.astype(jnp.float32), shares], axis=1).T
-    tables = gather_stacked(table, shift, sizes)
+    tables = lax.all_gather(table, "req", axis=0)
+    chip = lax.axis_index("req")
+    chip_slots = jnp.arange(slots_dev, dtype=jnp.int32)
+    slot_ids = jnp.concatenate(
+        [
+            (chip * cores + seq_index) * slots_dev + chip_slots,
+            (chip * cores + 1 - seq_index) * slots_dev + chip_slots,
+        ]
+    ).astype(jnp.int32)
+    plans = plan_routes(slot_ids, source_chips(chip, seq_index, chips), tables, sizes["b"], capacity)
 
     row_index = jnp.arange(row_count, dtype=jnp.int32)
     cosine, sine = rope_tables(
@@ -562,42 +587,39 @@
     )
     queries, appended, other_span = project(tokens, other_tokens, attn_gain, cosine, sine, w_qkv)
     place = jnp.stack([seq_index, length]).astype(jnp.int32)
-    attended, stream, expert_in = attend(
-        place,
-        queries,
-        (k_cache, k_other, v_cache, v_other),
-        (appended, other_span),
-        w_out,
-        tokens,
-        ffn_gain,
-        0,
-        row_count,
+    half = row_count // 2
+    filled, halves = [], []
+    for index in range(2):
+        attended, stream, expert_in = attend(
+            place,
+            queries,
+            (k_cache, k_other, v_cache, v_other),
+            (appended, other_span),
+            w_out,
+            tokens,
+            ffn_gain,
+            index * half,
+            half,
+            filled,
+            [up_other, down_other] if index else [],
+        )
+        filled = [attended, stream]
+        halves.append(gather_planes(expert_in, shift, sizes))
+    results = []
+    for index in range(sizes["b"]):
+        results.append(
+            run_experts(
+                [planes[index] for planes in halves],
+                plans[index],
+                (expert_up, up_other),
+                (expert_down, down_other),
+                (half, row_count - half),
+                results[-1][:1] if results else [],
+            )
+        )
+    expert_mix = jnp.concatenate(
+        [scatter_planes([r[i] for r in results], shift, sizes) for i in range(2)], axis=0
     )
-    up_other, down_other = swap(expert_up), swap(expert_down)
-    chip_slots = jnp.arange(slots_dev, dtype=jnp.int32)
-    core_base = lax.axis_index("req") * cores
-    slot_ids = jnp.concatenate(
-        [
-            (core_base + seq_index) * slots_dev + chip_slots,
-            (core_base + 1 - seq_index) * slots_dev + chip_slots,
-        ]
-    ).astype(jnp.int32)
-    blocks = gather_blocks(expert_in, shift, sizes)
-    in_group = sizes["a"] * sizes["z"]
-    results = []
-    for index, plane in enumerate(blocks):
-        flat = run_experts(
-            slot_ids,
-            [value for line in plane for value in line],
-            tables[index * in_group : (index + 1) * in_group],
-            (expert_up, up_other),
-            (expert_down, down_other),
-            capacity,
-        )
-        results.append(
-            [flat[j * sizes["z"] : (j + 1) * sizes["z"]] for j in range(sizes["a"])]
-        )
-    expert_mix = scatter_blocks(results, shift, sizes)
     return (attended, stream, expert_mix, appended)
 
 

time: 242 us -> 265 us (1.095)
  blocking collectives: 0 us -> 51.3 us
  starting transfers between devices: 51.6 us -> 24 us
  local copies, waits for them, and re-layouts: 13.3 us -> 7.47 us
  Pallas kernels: 54.2 us -> 59.9 us
    all_gather x0 -> x1, blocking collectives: none -> 51.3 us  [shards(): tables = lax.all_gather(table, 'req', axis=0)]
    ppermute x35 -> x20, starting transfers between devices: 50.5 us -> 22.5 us  [shift(): return lax.ppermute(value, BOTH, pairs(role, offset % sizes[role]))]
    unnamed x37 -> x26, local copies, waits for them, and re-layouts: 11.9 us -> 5.37 us
    ppermute x35 -> x20, waiting for transfers between devices: 116 us -> 110 us  [shift(): return lax.ppermute(value, BOTH, pairs(role, offset % sizes[role]))]
    ppermute x5, waiting for transfers between devices: 0.01 us -> 3.76 us  [swap(): return lax.ppermute(value, 'seq', [(0, 1), (1, 0)])]
    pallas_call x3 -> x5, Pallas kernels: 49.3 us -> 52.5 us  [the longest x2 26.1 us: attend(): pl.pallas_call(functools.partial(attend_kernel, first_row, len(extra)), g...]
  transfers between devices with their start and end apart: 40 -> 25, of which waited for: 18 -> 10; matrix products, arithmetic and copies ran while one was open for 2% -> 3% of each run, Pallas kernels for 17% -> 18%
where the time goes in v3:
time: 265 us
  waiting for transfers between devices  114 us (43%)
  Pallas kernels  59.9 us (23%)
  blocking collectives  51.3 us (19%)
  starting transfers between devices  24 us (9%)
  local copies, waits for them, and re-layouts  7.47 us (3%)
  other arithmetic  5.93 us (2%)
    ppermute x20, waiting for transfers between devices, shift(): return lax.ppermute(value, BOTH, pairs(role, offset % sizes[role]))  110 us
    all_gather x1, blocking collectives, shards(): tables = lax.all_gather(table, 'req', axis=0)  51.3 us
    pallas_call x2, Pallas kernels, attend(): pl.pallas_call(functools.partial(attend_kernel, first_row, len(extra)), g...  26.1 us
    pallas_call x2, Pallas kernels, run_experts(): pl.pallas_call(functools.partial(expert_kernel, tuple((r.shape[1] for r i...  25.2 us
    ppermute x20, starting transfers between devices, shift(): return lax.ppermute(value, BOTH, pairs(role, offset % sizes[role]))  22.5 us
    pallas_call x1, Pallas kernels, project(): pl.pallas_call(qkv_kernel, grid=(5,), in_specs=[vmem_spec()] * 5 + [pl.Bl...  7.39 us
    unnamed x26, local copies, waits for them, and re-layouts  5.37 us
  transfers between devices with their start and end apart: 25, of which 10 were waited for; matrix products, arithmetic and copies ran while one was open for 3% of the time, Pallas kernels for 18%

profile of v3, /device:TPU:0, one launch (start us, length us, event | category | flops | bytes accessed | tf_op | source)
XLA Modules:
  0.0 264.6 jit_solution(5837124572990143085)
XLA Ops:
  8.7 3.7 %collective-permute-done.other_ref = bf16[128,1536]{1,0:T(8,128)(2,1)} collective-permute-done((bf16[128,1536]{1,0:T(8,128)(2,1)}, bf16[128,1536]{1,0:T(8,128)(2,1)}, u32[]{:S(2)}, u32[]{:S(2)}) %collective-permute-start) | collective-permute-done | bytes 393248 | tf_op jit(solution)/shard_map/ppermute | solution.py:558
  12.4 7.4 %project_rows.1 = (bf16[128,1536]{1,0:T(8,128)(2,1)}, bf16[128,1024]{1,0:T(8,128)(2,1)}, bf16[128,1024]{1,0:T(8,128)(2,1)}) custom-call(bf16[128,1536]{1,0:T(8,128)(2,1)} %tokens_ref.3, bf16[128,1536]{1,0:T(8,128)(2,1)} %collective-permute-done.other_ref, f32[1,1536]{1,0:T(1,128)} %broadcast_in_dim.31.gain_ref, f32[256,128]{1,0:T(8,128)} %pad_maximum_fusion.3.cos_ref, ...), custom_call_target="tpu_custom_call" | custom-call | flops 1409286144 | bytes 9500000 | tf_op jit(solution)/shard_map/project_rows/pallas_call | solution.py:83
  19.8 2.3 copy-done.2
  25.1 12.8 %attend_rows.2 = (bf16[128,1536]{1,0:T(8,128)(2,1)}, bf16[128,1536]{1,0:T(8,128)(2,1)}, bf16[64,1536]{1,0:T(8,128)(2,1)S(1)}) custom-call(s32[2]{0:T(128)S(1)} %pad_add_fusion.place_ref, bf16[128,1536]{1,0:T(8,128)(2,1)S(1)} %copy-done.5, bf16[1,1024,512]{2,1,0:T(8,128)(2,1)S(1)} %copy-done.3, bf16[1,1024,512]{2,1,0:T(8,128)(2,1)} %collective-permute-done.1.kco_ref, ...), custom_call_target="tpu_custom_call" | custom-call | flops 7247757312 | bytes 10000000 | tf_op jit(solution)/shard_map/attend_rows/pallas_call | solution.py:217
  37.9 5.0 %collective-permute-start.7 = (bf16[1,64,1536]{2,1,0:T(8,128)(2,1)S(1)}, bf16[1,64,1536]{2,1,0:T(8,128)(2,1)S(1)}, u32[]{:S(2)}, u32[]{:S(2)}) collective-permute-start(bf16[1,64,1536]{2,1,0:T(8,128)(2,1)S(1)} %bitcast.36), channel_id=1, source_target_pairs={{0,24},{1,25},{2,26},{3,27},{4,28},{5,29},{6,30},{7,31},{8,0},{9,1... | collective-permute-start | bytes 589832 | tf_op jit(solution)/shard_map/ppermute | solution.py:475
  43.9 4.3 %collective-permute-done.7 = bf16[1,64,1536]{2,1,0:T(8,128)(2,1)S(1)} collective-permute-done((bf16[1,64,1536]{2,1,0:T(8,128)(2,1)S(1)}, bf16[1,64,1536]{2,1,0:T(8,128)(2,1)S(1)}, u32[]{:S(2)}, u32[]{:S(2)}) %collective-permute-start.7) | collective-permute-done | bytes 196640 | tf_op jit(solution)/shard_map/ppermute | solution.py:475
  48.2 11.6 %collective-permute-done.6 = bf16[1,64,1536]{2,1,0:T(8,128)(2,1)S(1)} collective-permute-done((bf16[1,64,1536]{2,1,0:T(8,128)(2,1)S(1)}, bf16[1,64,1536]{2,1,0:T(8,128)(2,1)S(1)}, u32[]{:S(2)}, u32[]{:S(2)}) %collective-permute-start.6) | collective-permute-done | bytes 196640 | tf_op jit(solution)/shard_map/ppermute | solution.py:475
  60.0 1.6 collective-permute-start.8
  61.7 13.3 %attend_rows.3 = (bf16[128,1536]{1,0:T(8,128)(2,1)}, bf16[128,1536]{1,0:T(8,128)(2,1)}, bf16[64,1536]{1,0:T(8,128)(2,1)S(1)}) custom-call(s32[2]{0:T(128)S(1)} %pad_add_fusion.place_ref, bf16[128,1536]{1,0:T(8,128)(2,1)S(1)} %copy-done.5, bf16[1,1024,512]{2,1,0:T(8,128)(2,1)S(1)} %copy-done.3, ...), custom_call_target="tpu_custom_call", output_to_operand_aliasing={{0}: (13, {}), {1}: (14, {})} | custom-call | flops 7247757312 | bytes 10000000 | tf_op jit(solution)/shard_map/attend_rows/pallas_call | solution.py:217
  75.3 2.6 collective-permute-start.10
  77.9 1.9 collective-permute-start.9
  81.5 13.0 %collective-permute-done.10 = bf16[1,64,1536]{2,1,0:T(8,128)(2,1)S(1)} collective-permute-done((bf16[1,64,1536]{2,1,0:T(8,128)(2,1)S(1)}, bf16[1,64,1536]{2,1,0:T(8,128)(2,1)S(1)}, u32[]{:S(2)}, u32[]{:S(2)}) %collective-permute-start.10) | collective-permute-done | bytes 196640 | tf_op jit(solution)/shard_map/ppermute | solution.py:475
  96.3 10.4 %collective-permute-done.12 = bf16[4,64,1536]{2,1,0:T(8,128)(2,1)S(1)} collective-permute-done((bf16[4,64,1536]{2,1,0:T(8,128)(2,1)S(1)}, bf16[4,64,1536]{2,1,0:T(8,128)(2,1)S(1)}, u32[]{:S(2)}, u32[]{:S(2)}) %collective-permute-start.12) | collective-permute-done | bytes 786464 | tf_op jit(solution)/shard_map/ppermute | solution.py:475
  107.3 51.3 %all-gather = f32[256,128]{1,0:T(8,128)S(1)} all-gather(f32[16,128]{1,0:T(8,128)S(1)} %maximum_bitcast_fusion), channel_id=2, replica_groups=mesh['req'=16,'seq'=2] {'req'}, dimensions={0}, use_global_device_ids=true | all-gather | bytes 139264 | tf_op jit(solution)/shard_map/all_gather | solution.py:570
  160.0 12.6 %run_experts.2 = (bf16[8,64,1536]{2,1,0:T(8,128)(2,1)S(1)}, bf16[8,64,1536]{2,1,0:T(8,128)(2,1)S(1)}) custom-call(bf16[8,64,1536]{2,1,0:T(8,128)(2,1)S(1)} %constant_dynamic-update-slice_fusion.refs_0_, bf16[8,64,1536]{2,1,0:T(8,128)(2,1)S(1)} %constant_dynamic-update-slice_fusion.5.refs_1_, bf16[8,128,128]{2,1,0:T(8,128)(2,1)S(1)} %get-tuple-element.32.refs_2_, ...), custom_call_target="tpu_custom_call" | custom-call | flops 4831838208 | bytes 26000000 | tf_op jit(solution)/shard_map/run_experts/pallas_call | solution.py:413
  172.6 12.6 %run_experts.3 = (bf16[8,64,1536]{2,1,0:T(8,128)(2,1)S(1)}, bf16[8,64,1536]{2,1,0:T(8,128)(2,1)S(1)}) custom-call(bf16[8,64,1536]{2,1,0:T(8,128)(2,1)S(1)} %collective-permute-done.13.refs_0_, bf16[8,64,1536]{2,1,0:T(8,128)(2,1)S(1)} %collective-permute-done.14.refs_1_, bf16[8,128,128]{2,1,0:T(8,128)(2,1)S(1)} %get-tuple-element.36.refs_2_, ...), custom_call_target="tpu_custom_call" | custom-call | flops 4831838208 | bytes 26000000 | tf_op jit(solution)/shard_map/run_experts/pallas_call | solution.py:413
  185.2 2.0 collective-permute-start.20
  187.2 32.6 %collective-permute-done.15 = bf16[8,64,1536]{2,1,0:T(8,128)(2,1)S(1)} collective-permute-done((bf16[8,64,1536]{2,1,0:T(8,128)(2,1)S(1)}, bf16[8,64,1536]{2,1,0:T(8,128)(2,1)S(1)}, u32[]{:S(2)}, u32[]{:S(2)}) %collective-permute-start.15) | collective-permute-done | bytes 1572896 | tf_op jit(solution)/shard_map/ppermute | solution.py:475
  220.1 19.2 %collective-permute-done.20 = bf16[8,64,1536]{2,1,0:T(8,128)(2,1)S(1)} collective-permute-done((bf16[8,64,1536]{2,1,0:T(8,128)(2,1)S(1)}, bf16[8,64,1536]{2,1,0:T(8,128)(2,1)S(1)}, u32[]{:S(2)}, u32[]{:S(2)}) %collective-permute-start.20) | collective-permute-done | bytes 1572896 | tf_op jit(solution)/shard_map/ppermute | solution.py:475
  239.9 2.0 collective-permute-start.19
  241.9 9.7 %collective-permute-done.21 = bf16[4,64,1536]{2,1,0:T(8,128)(2,1)S(1)} collective-permute-done((bf16[4,64,1536]{2,1,0:T(8,128)(2,1)S(1)}, bf16[4,64,1536]{2,1,0:T(8,128)(2,1)S(1)}, u32[]{:S(2)}, u32[]{:S(2)}) %collective-permute-start.21) | collective-permute-done | bytes 786464 | tf_op jit(solution)/shard_map/ppermute | solution.py:475
  251.9 2.0 collective-permute-start.24
  254.1 5.7 %collective-permute-done.22 = bf16[64,1536]{1,0:T(8,128)(2,1)S(1)} collective-permute-done((bf16[64,1536]{1,0:T(8,128)(2,1)S(1)}, bf16[64,1536]{1,0:T(8,128)(2,1)S(1)}, u32[]{:S(2)}, u32[]{:S(2)}) %collective-permute-start.22) | collective-permute-done | bytes 196640 | tf_op jit(solution)/shard_map/ppermute | solution.py:475
  259.7 3.9 %collective-permute-done.23 = bf16[64,1536]{1,0:T(8,128)(2,1)S(1)} collective-permute-done((bf16[64,1536]{1,0:T(8,128)(2,1)S(1)}, bf16[64,1536]{1,0:T(8,128)(2,1)S(1)}, u32[]{:S(2)}, u32[]{:S(2)}) %collective-permute-start.23) | collective-permute-done | bytes 196640 | tf_op jit(solution)/shard_map/ppermute | solution.py:475
  (87 shorter events, 19.3 us)
Async XLA Ops:
  0.6 61.0 %collective-permute-start.3 = (bf16[2,1536,1024]{2,1,0:T(8,128)(2,1)}, bf16[2,1536,1024]{2,1,0:T(8,128)(2,1)}, u32[]{:S(2)}, u32[]{:S(2)}) collective-permute-start(bf16[2,1536,1024]{2,1,0:T(8,128)(2,1)} %refs_5_.3), channel_id=1, source_target_pairs={{0,1},{1,0},{2,3},{3,2},{4,5},{5,4},{6,7},{7,6},{8,9},{9,8},{10,11... | collective-permute-start | bytes 18874376 | tf_op jit(solution)/shard_map/ppermute | solution.py:558
  1.1 11.3 %collective-permute-start = (bf16[128,1536]{1,0:T(8,128)(2,1)}, bf16[128,1536]{1,0:T(8,128)(2,1)}, u32[]{:S(2)}, u32[]{:S(2)}) collective-permute-start(bf16[128,1536]{1,0:T(8,128)(2,1)} %tokens_ref.3), channel_id=1, source_target_pairs={{0,1},{1,0},{2,3},{3,2},{4,5},{5,4},{6,7},{7,6},{8,9},{9,8},{10,11... | collective-permute-start | bytes 1179656 | tf_op jit(solution)/shard_map/ppermute | solution.py:558
  1.2 18.6 %collective-permute-start.1 = (bf16[1,1024,512]{2,1,0:T(8,128)(2,1)}, bf16[1,1024,512]{2,1,0:T(8,128)(2,1)}, u32[]{:S(2)}, u32[]{:S(2)}) collective-permute-start(bf16[1,1024,512]{2,1,0:T(8,128)(2,1)} %kc_ref.3), channel_id=1, source_target_pairs={{0,1},{1,0},{2,3},{3,2},{4,5},{5,4},{6,7},{7,6},{8,9},{9,8},{10,11... | collective-permute-start | bytes 3145736 | tf_op jit(solution)/shard_map/ppermute | solution.py:558
  1.7 18.1 %collective-permute-start.2 = (bf16[1,1024,512]{2,1,0:T(8,128)(2,1)}, bf16[1,1024,512]{2,1,0:T(8,128)(2,1)}, u32[]{:S(2)}, u32[]{:S(2)}) collective-permute-start(bf16[1,1024,512]{2,1,0:T(8,128)(2,1)} %vc_ref.3), channel_id=1, source_target_pairs={{0,1},{1,0},{2,3},{3,2},{4,5},{5,4},{6,7},{7,6},{8,9},{9,8},{10,11... | collective-permute-start | bytes 3145736 | tf_op jit(solution)/shard_map/ppermute | solution.py:558
  1.7 59.9 %collective-permute-start.4 = (bf16[2,512,1536]{2,1,0:T(8,128)(2,1)}, bf16[2,512,1536]{2,1,0:T(8,128)(2,1)S(1)}, u32[]{:S(2)}, u32[]{:S(2)}) collective-permute-start(bf16[2,512,1536]{2,1,0:T(8,128)(2,1)} %refs_7_.3), channel_id=1, source_target_pairs={{0,1},{1,0},{2,3},{3,2},{4,5},{5,4},{6,7},{7,6},{8,9},{9,8},{10,11... | collective-permute-start | bytes 9437192 | tf_op jit(solution)/shard_map/ppermute | solution.py:558
  37.9 10.3 %collective-permute-start.7 = (bf16[1,64,1536]{2,1,0:T(8,128)(2,1)S(1)}, bf16[1,64,1536]{2,1,0:T(8,128)(2,1)S(1)}, u32[]{:S(2)}, u32[]{:S(2)}) collective-permute-start(bf16[1,64,1536]{2,1,0:T(8,128)(2,1)S(1)} %bitcast.36), channel_id=1, source_target_pairs={{0,24},{1,25},{2,26},{3,27},{4,28},{5,29},{6,30},{7,31},{8,0},{9,1... | collective-permute-start | bytes 589832 | tf_op jit(solution)/shard_map/ppermute | solution.py:475
  42.9 17.0 %collective-permute-start.6 = (bf16[1,64,1536]{2,1,0:T(8,128)(2,1)S(1)}, bf16[1,64,1536]{2,1,0:T(8,128)(2,1)S(1)}, u32[]{:S(2)}, u32[]{:S(2)}) collective-permute-start(bf16[1,64,1536]{2,1,0:T(8,128)(2,1)S(1)} %bitcast.37), channel_id=1, source_target_pairs={{0,16},{1,17},{2,18},{3,19},{4,20},{5,21},{6,22},{7,23},{8,24},{9,... | collective-permute-start | bytes 589832 | tf_op jit(solution)/shard_map/ppermute | solution.py:475
  42.9 17.0 %collective-permute-start.5 = (bf16[1,64,1536]{2,1,0:T(8,128)(2,1)S(1)}, bf16[1,64,1536]{2,1,0:T(8,128)(2,1)S(1)}, u32[]{:S(2)}, u32[]{:S(2)}) collective-permute-start(bf16[1,64,1536]{2,1,0:T(8,128)(2,1)S(1)} %bitcast.38), channel_id=1, source_target_pairs={{0,8},{1,9},{2,10},{3,11},{4,12},{5,13},{6,14},{7,15},{8,16},{9,17... | collective-permute-start | bytes 589832 | tf_op jit(solution)/shard_map/ppermute | solution.py:475
  60.0 19.9 %collective-permute-start.8 = (bf16[4,64,1536]{2,1,0:T(8,128)(2,1)S(1)}, bf16[4,64,1536]{2,1,0:T(8,128)(2,1)S(1)}, u32[]{:S(2)}, u32[]{:S(2)}) collective-permute-start(bf16[4,64,1536]{2,1,0:T(8,128)(2,1)S(1)} %pad_maximum_fusion), channel_id=1, source_target_pairs={{0,4},{1,3},{2,6},{3,1},{4,0},{5,7},{6,2},{7,5},{8,12},{9,11},{10,... | collective-permute-start | bytes 2359304 | tf_op jit(solution)/shard_map/ppermute | solution.py:475
  75.3 19.2 %collective-permute-start.10 = (bf16[1,64,1536]{2,1,0:T(8,128)(2,1)S(1)}, bf16[1,64,1536]{2,1,0:T(8,128)(2,1)S(1)}, u32[]{:S(2)}, u32[]{:S(2)}) collective-permute-start(bf16[1,64,1536]{2,1,0:T(8,128)(2,1)S(1)} %bitcast.33), channel_id=1, source_target_pairs={{0,16},{1,17},{2,18},{3,19},{4,20},{5,21},{6,22},{7,23},{8,24},{9,... | collective-permute-start | bytes 589832 | tf_op jit(solution)/shard_map/ppermute | solution.py:475
  77.9 16.6 %collective-permute-start.9 = (bf16[1,64,1536]{2,1,0:T(8,128)(2,1)S(1)}, bf16[1,64,1536]{2,1,0:T(8,128)(2,1)S(1)}, u32[]{:S(2)}, u32[]{:S(2)}) collective-permute-start(bf16[1,64,1536]{2,1,0:T(8,128)(2,1)S(1)} %bitcast.34), channel_id=1, source_target_pairs={{0,8},{1,9},{2,10},{3,11},{4,12},{5,13},{6,14},{7,15},{8,16},{9,17... | collective-permute-start | bytes 589832 | tf_op jit(solution)/shard_map/ppermute | solution.py:475
  79.9 92.6 %collective-permute-start.13 = (bf16[8,64,1536]{2,1,0:T(8,128)(2,1)S(1)}, bf16[8,64,1536]{2,1,0:T(8,128)(2,1)S(1)}, u32[]{:S(2)}, u32[]{:S(2)}) collective-permute-start(bf16[8,64,1536]{2,1,0:T(8,128)(2,1)S(1)} %constant_dynamic-update-slice_fusion.refs_0_), channel_id=1, source_target_pairs={{0,2},{1,5},{2,0},{3,7},{4,6},{5,1},{6,4},{7,3},{8,10},{9,13},{10,... | collective-permute-start | bytes 4718600 | tf_op jit(solution)/shard_map/ppermute | solution.py:475
  94.6 12.1 %collective-permute-start.12 = (bf16[4,64,1536]{2,1,0:T(8,128)(2,1)S(1)}, bf16[4,64,1536]{2,1,0:T(8,128)(2,1)S(1)}, u32[]{:S(2)}, u32[]{:S(2)}) collective-permute-start(bf16[4,64,1536]{2,1,0:T(8,128)(2,1)S(1)} %pad_maximum_fusion.1), channel_id=1, source_target_pairs={{0,4},{1,3},{2,6},{3,1},{4,0},{5,7},{6,2},{7,5},{8,12},{9,11},{10,... | collective-permute-start | bytes 2359304 | tf_op jit(solution)/shard_map/ppermute | solution.py:475
  106.7 65.8 %collective-permute-start.14 = (bf16[8,64,1536]{2,1,0:T(8,128)(2,1)S(1)}, bf16[8,64,1536]{2,1,0:T(8,128)(2,1)S(1)}, u32[]{:S(2)}, u32[]{:S(2)}) collective-permute-start(bf16[8,64,1536]{2,1,0:T(8,128)(2,1)S(1)} %constant_dynamic-update-slice_fusion.5.refs_1_), channel_id=1, source_target_pairs={{0,2},{1,5},{2,0},{3,7},{4,6},{5,1},{6,4},{7,3},{8,10},{9,13},{10,... | collective-permute-start | bytes 4718600 | tf_op jit(solution)/shard_map/ppermute | solution.py:475
  185.2 34.7 %collective-permute-start.15 = (bf16[8,64,1536]{2,1,0:T(8,128)(2,1)S(1)}, bf16[8,64,1536]{2,1,0:T(8,128)(2,1)S(1)}, u32[]{:S(2)}, u32[]{:S(2)}) collective-permute-start(bf16[8,64,1536]{2,1,0:T(8,128)(2,1)S(1)} %get-tuple-element.39), channel_id=1, source_target_pairs={{0,2},{1,5},{2,0},{3,7},{4,6},{5,1},{6,4},{7,3},{8,10},{9,13},{10,... | collective-permute-start | bytes 4718600 | tf_op jit(solution)/shard_map/ppermute | solution.py:475
  185.2 54.1 %collective-permute-start.20 = (bf16[8,64,1536]{2,1,0:T(8,128)(2,1)S(1)}, bf16[8,64,1536]{2,1,0:T(8,128)(2,1)S(1)}, u32[]{:S(2)}, u32[]{:S(2)}) collective-permute-start(bf16[8,64,1536]{2,1,0:T(8,128)(2,1)S(1)} %get-tuple-element.41), channel_id=1, source_target_pairs={{0,2},{1,5},{2,0},{3,7},{4,6},{5,1},{6,4},{7,3},{8,10},{9,13},{10,... | collective-permute-start | bytes 4718600 | tf_op jit(solution)/shard_map/ppermute | solution.py:475
  220.0 19.6 %collective-permute-start.16 = (bf16[4,64,1536]{2,1,0:T(8,128)(2,1)S(1)}, bf16[4,64,1536]{2,1,0:T(8,128)(2,1)S(1)}, u32[]{:S(2)}, u32[]{:S(2)}) collective-permute-start(bf16[4,64,1536]{2,1,0:T(8,128)(2,1)S(1)} %add_convert_fusion.1), channel_id=1, source_target_pairs={{0,4},{1,3},{2,6},{3,1},{4,0},{5,7},{6,2},{7,5},{8,12},{9,11},{10,... | collective-permute-start | bytes 2359304 | tf_op jit(solution)/shard_map/ppermute | solution.py:475
  239.5 12.1 %collective-permute-start.21 = (bf16[4,64,1536]{2,1,0:T(8,128)(2,1)S(1)}, bf16[4,64,1536]{2,1,0:T(8,128)(2,1)S(1)}, u32[]{:S(2)}, u32[]{:S(2)}) collective-permute-start(bf16[4,64,1536]{2,1,0:T(8,128)(2,1)S(1)} %add_convert_fusion), channel_id=1, source_target_pairs={{0,4},{1,3},{2,6},{3,1},{4,0},{5,7},{6,2},{7,5},{8,12},{9,11},{10,... | collective-permute-start | bytes 2359304 | tf_op jit(solution)/shard_map/ppermute | solution.py:475
  239.9 14.0 %collective-permute-start.17 = (bf16[64,1536]{1,0:T(8,128)(2,1)S(1)}, bf16[64,1536]{1,0:T(8,128)(2,1)S(1)}, u32[]{:S(2)}, u32[]{:S(2)}) collective-permute-start(bf16[64,1536]{1,0:T(8,128)(2,1)S(1)} %get-tuple-element.42), channel_id=1, source_target_pairs={{0,24},{1,25},{2,26},{3,27},{4,28},{5,29},{6,30},{7,31},{8,0},{9,1... | collective-permute-start | bytes 589832 | tf_op jit(solution)/shard_map/ppermute | solution.py:475
  239.9 14.0 %collective-permute-start.19 = (bf16[64,1536]{1,0:T(8,128)(2,1)S(1)}, bf16[64,1536]{1,0:T(8,128)(2,1)S(1)}, u32[]{:S(2)}, u32[]{:S(2)}) collective-permute-start(bf16[64,1536]{1,0:T(8,128)(2,1)S(1)} %get-tuple-element.43), channel_id=1, source_target_pairs={{0,8},{1,9},{2,10},{3,11},{4,12},{5,13},{6,14},{7,15},{8,16},{9,17... | collective-permute-start | bytes 589832 | tf_op jit(solution)/shard_map/ppermute | solution.py:475
  241.9 12.0 %collective-permute-start.18 = (bf16[64,1536]{1,0:T(8,128)(2,1)S(1)}, bf16[64,1536]{1,0:T(8,128)(2,1)S(1)}, u32[]{:S(2)}, u32[]{:S(2)}) collective-permute-start(bf16[64,1536]{1,0:T(8,128)(2,1)S(1)} %get-tuple-element.44), channel_id=1, source_target_pairs={{0,16},{1,17},{2,18},{3,19},{4,20},{5,21},{6,22},{7,23},{8,24},{9,... | collective-permute-start | bytes 589832 | tf_op jit(solution)/shard_map/ppermute | solution.py:475
  251.8 7.9 %collective-permute-start.22 = (bf16[64,1536]{1,0:T(8,128)(2,1)S(1)}, bf16[64,1536]{1,0:T(8,128)(2,1)S(1)}, u32[]{:S(2)}, u32[]{:S(2)}) collective-permute-start(bf16[64,1536]{1,0:T(8,128)(2,1)S(1)} %get-tuple-element.45), channel_id=1, source_target_pairs={{0,24},{1,25},{2,26},{3,27},{4,28},{5,29},{6,30},{7,31},{8,0},{9,1... | collective-permute-start | bytes 589832 | tf_op jit(solution)/shard_map/ppermute | solution.py:475
  251.9 7.9 %collective-permute-start.24 = (bf16[64,1536]{1,0:T(8,128)(2,1)S(1)}, bf16[64,1536]{1,0:T(8,128)(2,1)S(1)}, u32[]{:S(2)}, u32[]{:S(2)}) collective-permute-start(bf16[64,1536]{1,0:T(8,128)(2,1)S(1)} %get-tuple-element.46), channel_id=1, source_target_pairs={{0,8},{1,9},{2,10},{3,11},{4,12},{5,13},{6,14},{7,15},{8,16},{9,17... | collective-permute-start | bytes 589832 | tf_op jit(solution)/shard_map/ppermute | solution.py:475
  253.9 9.8 %collective-permute-start.23 = (bf16[64,1536]{1,0:T(8,128)(2,1)S(1)}, bf16[64,1536]{1,0:T(8,128)(2,1)S(1)}, u32[]{:S(2)}, u32[]{:S(2)}) collective-permute-start(bf16[64,1536]{1,0:T(8,128)(2,1)S(1)} %get-tuple-element.47), channel_id=1, source_target_pairs={{0,16},{1,17},{2,18},{3,19},{4,20},{5,21},{6,22},{7,23},{8,24},{9,... | collective-permute-start | bytes 589832 | tf_op jit(solution)/shard_map/ppermute | solution.py:475
  (10 other events, 71.3 us)

commit v4 on v3

--- a/solution.py
+++ b/solution.py
@@ -32,7 +32,8 @@
     return pltpu.CompilerParams(vmem_limit_bytes=mebibytes * 2**20)
 
 
-def qkv_kernel(own_ref, other_ref, gain_ref, cos_ref, sin_ref, w_ref, q_ref, kv_ref, kvo_ref, normed):
+def qkv_kernel(own_ref, other_ref, gain_ref, cos_ref, sin_ref, w_ref, *refs):
+    q_ref, kv_ref, kvo_ref, normed = refs[-4:]
     step = pl.program_id(0)
     rows = own_ref.shape[0]
     width = w_ref.shape[1]
@@ -43,7 +44,7 @@
             wide = ref[...].astype(jnp.float32)
             mean_square = jnp.mean(wide * wide, axis=-1, keepdims=True)
             normed[index * rows : (index + 1) * rows] = (
-                wide * lax.rsqrt(mean_square + epsilon) * gain_ref[...]
+                wide * lax.rsqrt(mean_square + epsilon) * gain_ref[...][None, :]
             ).astype(jnp.bfloat16)
 
     def rotated(x, row_slice):
@@ -77,13 +78,15 @@
         kvo_ref[...] = x[rows:]
 
 
-def project(own, other, gain, cosine, sine, w_qkv):
+def project(own, other, gain, cosine, sine, w_qkv, after):
     rows, width = own.shape
     tile = KV_HEADS * HEAD
     return pl.pallas_call(
         qkv_kernel,
         grid=(5,),
-        in_specs=[vmem_spec()] * 5 + [pl.BlockSpec((width, tile), lambda i: (0, i))],
+        in_specs=[vmem_spec()] * 5
+        + [pl.BlockSpec((width, tile), lambda i: (0, i))]
+        + [pl.BlockSpec(memory_space=pl.ANY)] * len(after),
         out_specs=[
             pl.BlockSpec((rows, tile), lambda i: (0, jnp.minimum(i, 2))),
             pl.BlockSpec((rows, tile), lambda i: (0, jnp.maximum(i - 3, 0))),
@@ -95,12 +98,12 @@
             jax.ShapeDtypeStruct((rows, 2 * tile), jnp.bfloat16),
         ],
         scratch_shapes=[pltpu.VMEM((2 * rows, width), jnp.bfloat16)],
-        compiler_params=params(56),
+        compiler_params=params(24),
         cost_estimate=pl.CostEstimate(
             flops=2 * rows * width * 3584, bytes_accessed=9_500_000, transcendentals=0
         ),
         name="project_rows",
-    )(own, other, gain[None], cosine, sine, w_qkv)
+    )(own, other, gain, cosine, sine, w_qkv, *after)
 
 
 def attend_kernel(first_row, extra, place_ref, q_ref, kc_ref, kco_ref, vc_ref, vco_ref, ks_ref, kso_ref, vs_ref, vso_ref, w_out_ref, tokens_ref, gain_ref, *refs):
@@ -197,7 +200,7 @@
         stream_ref[...] = stream
         wide = stream.astype(jnp.float32)
         mean_square = jnp.mean(wide * wide, axis=-1, keepdims=True)
-        expert_in_ref[...] = (wide * lax.rsqrt(mean_square + epsilon) * gain_ref[...]).astype(
+        expert_in_ref[...] = (wide * lax.rsqrt(mean_square + epsilon) * gain_ref[...][None, :]).astype(
             jnp.bfloat16
         )
 
@@ -250,7 +253,7 @@
             pltpu.VMEM((2 * GROUP * rows, 2 * LANES), jnp.bfloat16),
             pltpu.VMEM((rows, width), jnp.float32),
         ],
-        compiler_params=params(36),
+        compiler_params=params(40),
         cost_estimate=pl.CostEstimate(
             flops=16 * HEADS * rows * key_count * LANES,
             bytes_accessed=10_000_000,
@@ -270,15 +273,14 @@
         other_span,
         w_out,
         tokens,
-        gain[None],
+        gain,
         *extra,
     )
 
 
-def plan_kernel(groups, capacity, slot_ref, chip_ref, table_ref, *out_refs):
+def plan_kernel(groups, capacity, top, slot_ref, chip_ref, table_ref, *out_refs):
     slots = slot_ref.shape[0]
-    chips, height, tokens = table_ref.shape
-    top = height // 2
+    chips, _, tokens = table_ref.shape
     in_group = chips // groups
     earlier = jnp.where(
         lax.broadcasted_iota(jnp.int32, (tokens, tokens), 0)
@@ -296,7 +298,7 @@
                 match = entry[:top] == slot_ref[slot].astype(jnp.float32)
                 hot_rows.append(jnp.max(jnp.where(match, 1.0, 0.0), axis=0, keepdims=True))
                 share_lines.append(
-                    jnp.sum(jnp.where(match, entry[top:], 0.0), axis=0, keepdims=True)
+                    jnp.sum(jnp.where(match, entry[top : 2 * top], 0.0), axis=0, keepdims=True)
                 )
         hot = jnp.concatenate(hot_rows, axis=0)
         rank = jnp.dot(hot.astype(jnp.bfloat16), earlier, preferred_element_type=jnp.float32)
@@ -315,12 +317,12 @@
             back_ref[source] = jnp.transpose(picked).astype(jnp.bfloat16)
 
 
-def plan_routes(slot_ids, chip_ids, tables, groups, capacity):
+def plan_routes(slot_ids, chip_ids, tables, groups, capacity, top):
     chips, _, tokens = tables.shape
     slots = slot_ids.shape[0]
     in_group = chips // groups
     flat = pl.pallas_call(
-        functools.partial(plan_kernel, groups, capacity),
+        functools.partial(plan_kernel, groups, capacity, top),
         in_specs=[pl.BlockSpec(memory_space=pltpu.SMEM)] * 2 + [vmem_spec()],
         out_specs=[vmem_spec()] * (3 * groups),
         out_shape=[
@@ -338,23 +340,28 @@
     return [flat[3 * i : 3 * i + 3] for i in range(groups)]
 
 
-def expert_kernel(in_cuts, out_cuts, extra, *refs):
-    row_refs = refs[: len(in_cuts)]
-    rest = refs[len(in_cuts) :]
+def expert_kernel(pieces, halves, out_cuts, extra, *refs):
+    row_refs = refs[: pieces * halves]
+    rest = refs[pieces * halves :]
     pick_ref, back_ref, share_ref, up_ref, up_other_ref, down_ref, down_other_ref = rest[:7]
-    out_refs = rest[7 + extra : 7 + extra + len(out_cuts)]
+    out_refs = rest[7 + extra : 7 + extra + pieces * len(out_cuts)]
     held = rest[-1]
     step = pl.program_id(0)
     slots = held.shape[0]
     own_slots = slots // 2
     sources = pick_ref.shape[0]
+    deep = sources // pieces
     capacity = held.shape[1] // sources
     hidden = down_ref.shape[1]
 
     @pl.when(step == 0)
     def _():
         for source in range(sources):
-            rows = jnp.concatenate([ref[source] for ref in row_refs], axis=0)
+            piece = source // deep
+            rows = jnp.concatenate(
+                [ref[source % deep] for ref in row_refs[piece * halves : (piece + 1) * halves]],
+                axis=0,
+            )
             rows = jnp.dot(
                 pick_ref[source], rows, preferred_element_type=jnp.float32
             ).astype(jnp.bfloat16)
@@ -392,13 +399,15 @@
             )
             mixed = jnp.dot(back_ref[source], rows, preferred_element_type=jnp.float32)
             start = 0
-            for ref, count in zip(out_refs, out_cuts):
-                ref[source] = mixed[start : start + count].astype(jnp.bfloat16)
+            for index, count in enumerate(out_cuts):
+                ref = out_refs[source // deep * len(out_cuts) + index]
+                ref[source % deep] = mixed[start : start + count].astype(jnp.bfloat16)
                 start += count
 
 
 def run_experts(rows, plan, ups, downs, out_cuts, after):
-    sources, _, width = rows[0].shape
+    pieces, halves = len(rows), len(rows[0])
+    deep, _, width = rows[0][0].shape
     own_slots, _, double = ups[0].shape
     hidden = double // 2
     slots = 2 * own_slots
@@ -410,12 +419,10 @@
     def other(j):
         return (jnp.maximum(j - own_slots, 0), 0, 0)
 
-    return pl.pallas_call(
-        functools.partial(
-            expert_kernel, tuple(r.shape[1] for r in rows), tuple(out_cuts), len(after)
-        ),
+    flat = pl.pallas_call(
+        functools.partial(expert_kernel, pieces, halves, tuple(out_cuts), len(after)),
         grid=(slots,),
-        in_specs=[vmem_spec()] * (len(rows) + 3)
+        in_specs=[vmem_spec()] * (pieces * halves + 3)
         + [
             pl.BlockSpec((1, width, double), own),
             pl.BlockSpec((1, width, double), other),
@@ -423,17 +430,37 @@
             pl.BlockSpec((1, hidden, width), other),
         ]
         + [pl.BlockSpec(memory_space=pl.ANY)] * len(after),
-        out_specs=[vmem_spec()] * len(out_cuts),
-        out_shape=[jax.ShapeDtypeStruct((sources, c, width), jnp.bfloat16) for c in out_cuts],
+        out_specs=[vmem_spec()] * (pieces * len(out_cuts)),
+        out_shape=[jax.ShapeDtypeStruct((deep, c, width), jnp.bfloat16) for c in out_cuts]
+        * pieces,
         scratch_shapes=[pltpu.VMEM((slots, places, width), jnp.bfloat16)],
         compiler_params=params(44),
         cost_estimate=pl.CostEstimate(
-            flops=6 * slots * places * width * hidden,
+            flops=10 * slots * places * width * hidden,
             bytes_accessed=26_000_000,
             transcendentals=slots * places * hidden,
         ),
         name="run_experts",
-    )(*rows, *plan, ups[0], ups[1], downs[0], downs[1], *after)
+    )(*[r for piece in rows for r in piece], *plan, ups[0], ups[1], downs[0], downs[1], *after)
+    count = len(out_cuts)
+    return [flat[i * count : (i + 1) * count] for i in range(pieces)]
+
+
+def stack_kernel(count, *refs):
+    out_ref = refs[-1]
+    for index in range(count):
+        out_ref[index] = refs[index][...]
+
+
+def stack_rows(parts, after):
+    return pl.pallas_call(
+        functools.partial(stack_kernel, len(parts)),
+        in_specs=[vmem_spec()] * len(parts) + [pl.BlockSpec(memory_space=pl.ANY)] * len(after),
+        out_specs=vmem_spec(),
+        out_shape=jax.ShapeDtypeStruct((len(parts), *parts[0].shape), parts[0].dtype),
+        compiler_params=params(16),
+        name="stack_rows",
+    )(*parts, *after)
 
 
 def chip_shape(chips):
@@ -477,13 +504,13 @@
     return shift, sizes
 
 
-def gather_planes(value, shift, sizes):
-    stacked = value[None]
-    for role in ("z", "a"):
-        stacked = jnp.concatenate(
-            [stacked] + [shift(stacked, role, k) for k in range(1, sizes[role])], axis=0
-        )
-    return [stacked] + [shift(stacked, "b", k) for k in range(1, sizes["b"])]
+def gather_line(value, shift, sizes):
+    return [value] + [shift(value, "z", k) for k in range(1, sizes["z"])]
+
+
+def gather_planes(line, shift, sizes):
+    plane = [line] + [shift(line, "a", j) for j in range(1, sizes["a"])]
+    return [plane] + [[shift(v, "b", k) for v in plane] for k in range(1, sizes["b"])]
 
 
 def add_all(terms):
@@ -494,16 +521,15 @@
 
 
 def scatter_planes(planes, shift, sizes):
-    deep = sizes["z"]
-    terms = [planes[0]] + [shift(planes[k], "b", -k) for k in range(1, sizes["b"])]
-
-    def part(j):
-        return [term[j * deep : (j + 1) * deep] for term in terms]
-
-    arrived = [shift(add_all(part(j)), "a", -j) for j in range(1, sizes["a"])]
-    line = part(0) + arrived
-    moved = [shift(add_all([t[i] for t in line]), "z", -i) for i in range(1, deep)]
-    return add_all([add_all([t[0] for t in line])] + moved)
+    tall = sizes["a"]
+    arrived = {}
+    for j in range(tall - 1, -1, -1):
+        arrived[j] = [planes[0][j]] + [shift(planes[k][j], "b", -k) for k in range(1, sizes["b"])]
+    line = [shift(add_all(arrived[j]), "a", -j) for j in range(1, tall)] + arrived[0]
+    moved = [
+        shift(add_all([t[i] for t in line]), "z", -i) for i in range(1, sizes["z"])
+    ]
+    return add_all([t[0] for t in line] + moved)
 
 
 def source_chips(chip, core, chips):
@@ -559,14 +585,13 @@
 
     other_tokens = swap(tokens)
     k_other, v_other = swap(k_cache), swap(v_cache)
-
-    up_other, down_other = swap(expert_up), swap(expert_down)
     experts = jnp.arange(replica_slot.shape[1], dtype=jnp.int32)
     slot_of = jnp.sum(
         jnp.where(routes[:, :, None] == experts, replica_slot[:, None, :], 0), axis=2
     )
     shares = route_scores / jnp.sum(route_scores, axis=1, keepdims=True)
     table = jnp.concatenate([slot_of.astype(jnp.float32), shares], axis=1).T
+    table = jnp.pad(table, ((0, row_count - table.shape[0]), (0, 0)))
     tables = lax.all_gather(table, "req", axis=0)
     chip = lax.axis_index("req")
     chip_slots = jnp.arange(slots_dev, dtype=jnp.int32)
@@ -576,7 +601,7 @@
             (chip * cores + 1 - seq_index) * slots_dev + chip_slots,
         ]
     ).astype(jnp.int32)
-    plans = plan_routes(slot_ids, source_chips(chip, seq_index, chips), tables, sizes["b"], capacity)
+    plans = plan_routes(slot_ids, source_chips(chip, seq_index, chips), tables, sizes["b"], capacity, top_count)
 
     row_index = jnp.arange(row_count, dtype=jnp.int32)
     cosine, sine = rope_tables(
@@ -585,10 +610,14 @@
             [seq_index * row_count + row_index, (1 - seq_index) * row_count + row_index]
         )
     )
-    queries, appended, other_span = project(tokens, other_tokens, attn_gain, cosine, sine, w_qkv)
+    queries, appended, other_span = project(
+        tokens, other_tokens, attn_gain, cosine, sine, w_qkv, [k_other, v_other]
+    )
     place = jnp.stack([seq_index, length]).astype(jnp.int32)
+    later_up, later_down, _ = lax.optimization_barrier((expert_up, expert_down, appended))
+    up_other, down_other = swap(later_up), swap(later_down)
     half = row_count // 2
-    filled, halves = [], []
+    filled, lines = [], []
     for index in range(2):
         attended, stream, expert_in = attend(
             place,
@@ -604,21 +633,27 @@
             [up_other, down_other] if index else [],
         )
         filled = [attended, stream]
-        halves.append(gather_planes(expert_in, shift, sizes))
+        lines.append(gather_line(expert_in, shift, sizes))
+    halves = [gather_planes(stack_rows(line, [expert_in]), shift, sizes) for line in lines]
+    cut = row_count // 2
     results = []
     for index in range(sizes["b"]):
         results.append(
             run_experts(
-                [planes[index] for planes in halves],
+                [[planes[index][j] for planes in halves] for j in range(sizes["a"])],
                 plans[index],
                 (expert_up, up_other),
                 (expert_down, down_other),
-                (half, row_count - half),
-                results[-1][:1] if results else [],
+                (cut, row_count - cut),
+                results[-1][0][:1] if results else [],
             )
         )
     expert_mix = jnp.concatenate(
-        [scatter_planes([r[i] for r in results], shift, sizes) for i in range(2)], axis=0
+        [
+            scatter_planes([[piece[i] for piece in r] for r in results], shift, sizes)
+            for i in range(2)
+        ],
+        axis=0,
     )
     return (attended, stream, expert_mix, appended)
 

time: 265 us -> 232 us (0.88)
  blocking collectives: 51.3 us -> 0 us
  between operations: 1.68 us -> 14.9 us
  starting transfers between devices: 24 us -> 36.5 us
  waiting for transfers between devices: 114 us -> 107 us
  local copies, waits for them, and re-layouts: 7.47 us -> 12.5 us
  other arithmetic: 5.93 us -> 3.01 us
    all_gather x1 -> x0, blocking collectives: 51.3 us -> none  [shards(): tables = lax.all_gather(table, 'req', axis=0)]
    ppermute x20 -> x24, starting transfers between devices: 22.5 us -> 35 us  [shift(): return lax.ppermute(value, BOTH, pairs(role, offset % sizes[role]))]
    unnamed x26, local copies, waits for them, and re-layouts: 5.37 us -> 11.9 us
    ppermute x20 -> x24, waiting for transfers between devices: 110 us -> 105 us  [shift(): return lax.ppermute(value, BOTH, pairs(role, offset % sizes[role]))]
    pallas_call x3 -> x5, Pallas kernels: 26.4 us -> 27.3 us  [the longest x2 26 us: run_experts(): pl.pallas_call(functools.partial(expert_kernel, pieces, halves, tuple(out...]
  transfers between devices with their start and end apart: 25 -> 30, of which waited for: 10 -> 13; matrix products, arithmetic and copies ran while one was open for 3% -> 1% of each run, Pallas kernels for 18% -> 17%
where the time goes in v4:
time: 232 us
  waiting for transfers between devices  107 us (46%)
  Pallas kernels  57.6 us (25%)
  starting transfers between devices  36.5 us (16%)
  between operations  14.9 us (6%)
  local copies, waits for them, and re-layouts  12.5 us (5%)
  other arithmetic  3.01 us (1%)
    ppermute x24, waiting for transfers between devices, shift(): return lax.ppermute(value, BOTH, pairs(role, offset % sizes[role]))  105 us
    ppermute x24, starting transfers between devices, shift(): return lax.ppermute(value, BOTH, pairs(role, offset % sizes[role]))  35 us
    pallas_call x2, Pallas kernels, run_experts(): pl.pallas_call(functools.partial(expert_kernel, pieces, halves, tuple(out...  26 us
    pallas_call x2, Pallas kernels, attend(): pl.pallas_call(functools.partial(attend_kernel, first_row, len(extra)), g...  25.5 us
    unnamed x26, local copies, waits for them, and re-layouts  11.9 us
    pallas_call x1, Pallas kernels, project(): pl.pallas_call(qkv_kernel, grid=(5,), in_specs=[vmem_spec()] * 5 + [pl.Bl...  4.87 us
  transfers between devices with their start and end apart: 30, of which 13 were waited for; matrix products, arithmetic and copies ran while one was open for 1% of the time, Pallas kernels for 17%

profile of v4, /device:TPU:0, one launch (start us, length us, event | category | flops | bytes accessed | tf_op | source)
XLA Modules:
  0.0 231.9 jit_solution(3953929696641008730)
XLA Ops:
  12.3 3.2 %copy-done = bf16[1536,2560]{1,0:T(8,128)(2,1)S(1)} copy-done((bf16[1536,2560]{1,0:T(8,128)(2,1)S(1)}, bf16[1536,2560]{1,0:T(8,128)(2,1)}, u32[]{:S(2)}) %copy-start) | copy-done | bytes 7864344
  17.2 4.9 %project_rows.1 = (bf16[128,1536]{1,0:T(8,128)(2,1)S(1)}, bf16[128,1024]{1,0:T(8,128)(2,1)}, bf16[128,1024]{1,0:T(8,128)(2,1)S(1)}) custom-call(bf16[128,1536]{1,0:T(8,128)(2,1)S(1)} %copy-done.1, bf16[128,1536]{1,0:T(8,128)(2,1)S(1)} %collective-permute-done.other_ref, f32[1536]{0:T(1024)S(1)} %copy-done.3, f32[256,128]{1,0:T(8,128)S(1)} %pad_maximum_fusion.1.cos_ref, ...), custom_call_target="tpu_custom_call" | custom-call | flops 1409286144 | bytes 9500000 | tf_op jit(solution)/shard_map/project_rows/pallas_call | solution.py:84
  29.2 12.7 %attend_rows.2 = (bf16[128,1536]{1,0:T(8,128)(2,1)}, bf16[128,1536]{1,0:T(8,128)(2,1)}, bf16[64,1536]{1,0:T(8,128)(2,1)S(1)}) custom-call(s32[2]{0:T(128)S(1)} %pad_add_fusion.place_ref, bf16[128,1536]{1,0:T(8,128)(2,1)S(1)} %get-tuple-element.29.q_ref, bf16[1,1024,512]{2,1,0:T(8,128)(2,1)S(1)} %copy-done.5, ...), custom_call_target="tpu_custom_call" | custom-call | flops 7247757312 | bytes 10000000 | tf_op jit(solution)/shard_map/attend_rows/pallas_call | solution.py:220
  41.9 2.9 %collective-permute-start.5 = (bf16[64,1536]{1,0:T(8,128)(2,1)S(1)}, bf16[64,1536]{1,0:T(8,128)(2,1)S(1)}, u32[]{:S(2)}, u32[]{:S(2)}) collective-permute-start(bf16[64,1536]{1,0:T(8,128)(2,1)S(1)} %get-tuple-element.38.refs_0_), channel_id=1, source_target_pairs={{0,8},{1,9},{2,10},{3,11},{4,12},{5,13},{6,14},{7,15},{8,16},{9,17... | collective-permute-start | bytes 589832 | tf_op jit(solution)/shard_map/ppermute | solution.py:502
  44.9 2.6 %collective-permute-start.6 = (bf16[64,1536]{1,0:T(8,128)(2,1)S(1)}, bf16[64,1536]{1,0:T(8,128)(2,1)S(1)}, u32[]{:S(2)}, u32[]{:S(2)}) collective-permute-start(bf16[64,1536]{1,0:T(8,128)(2,1)S(1)} %get-tuple-element.38.refs_0_), channel_id=1, source_target_pairs={{0,16},{1,17},{2,18},{3,19},{4,20},{5,21},{6,22},{7,23},{8,24},{9,... | collective-permute-start | bytes 589832 | tf_op jit(solution)/shard_map/ppermute | solution.py:502
  48.8 12.8 %attend_rows.3 = (bf16[128,1536]{1,0:T(8,128)(2,1)}, bf16[128,1536]{1,0:T(8,128)(2,1)}, bf16[64,1536]{1,0:T(8,128)(2,1)S(1)}) custom-call(s32[2]{0:T(128)S(1)} %pad_add_fusion.place_ref, bf16[128,1536]{1,0:T(8,128)(2,1)S(1)} %get-tuple-element.29.q_ref, bf16[1,1024,512]{2,1,0:T(8,128)(2,1)S(1)} %copy-done.5, ...), custom_call_target="tpu_custom_call", output_to_operand_aliasing={{0}: (13, {}), {1}: (14, {})} | custom-call | flops 7247757312 | bytes 10000000 | tf_op jit(solution)/shard_map/attend_rows/pallas_call | solution.py:220
  65.6 3.0 %collective-permute-done.10.refs_3_ = bf16[64,1536]{1,0:T(8,128)(2,1)S(1)} collective-permute-done((bf16[64,1536]{1,0:T(8,128)(2,1)S(1)}, bf16[64,1536]{1,0:T(8,128)(2,1)S(1)}, u32[]{:S(2)}, u32[]{:S(2)}) %collective-permute-start.10) | collective-permute-done | bytes 196640 | tf_op jit(solution)/shard_map/ppermute | solution.py:502
  68.6 5.9 %collective-permute-done.8.refs_1_ = bf16[64,1536]{1,0:T(8,128)(2,1)S(1)} collective-permute-done((bf16[64,1536]{1,0:T(8,128)(2,1)S(1)}, bf16[64,1536]{1,0:T(8,128)(2,1)S(1)}, u32[]{:S(2)}, u32[]{:S(2)}) %collective-permute-start.8) | collective-permute-done | bytes 196640 | tf_op jit(solution)/shard_map/ppermute | solution.py:502
  74.5 14.5 %collective-permute-done.9.refs_2_ = bf16[64,1536]{1,0:T(8,128)(2,1)S(1)} collective-permute-done((bf16[64,1536]{1,0:T(8,128)(2,1)S(1)}, bf16[64,1536]{1,0:T(8,128)(2,1)S(1)}, u32[]{:S(2)}, u32[]{:S(2)}) %collective-permute-start.9) | collective-permute-done | bytes 196640 | tf_op jit(solution)/shard_map/ppermute | solution.py:502
  90.7 2.8 %collective-permute-start.13 = (bf16[4,64,1536]{2,1,0:T(8,128)(2,1)S(1)}, bf16[4,64,1536]{2,1,0:T(8,128)(2,1)}, u32[]{:S(2)}, u32[]{:S(2)}) collective-permute-start(bf16[4,64,1536]{2,1,0:T(8,128)(2,1)S(1)} %stack_rows.2.refs_0_), channel_id=1, source_target_pairs={{0,2},{1,5},{2,0},{3,7},{4,6},{5,1},{6,4},{7,3},{8,10},{9,13},{10,... | collective-permute-start | bytes 2359304 | tf_op jit(solution)/shard_map/ppermute | solution.py:502
  95.5 12.6 %collective-permute-done.12.refs_3_ = bf16[4,64,1536]{2,1,0:T(8,128)(2,1)S(1)} collective-permute-done((bf16[4,64,1536]{2,1,0:T(8,128)(2,1)S(1)}, bf16[4,64,1536]{2,1,0:T(8,128)(2,1)S(1)}, u32[]{:S(2)}, u32[]{:S(2)}) %collective-permute-start.12) | collective-permute-done | bytes 786464 | tf_op jit(solution)/shard_map/ppermute | solution.py:502
  108.1 3.5 %collective-permute-start.16 = (bf16[4,64,1536]{2,1,0:T(8,128)(2,1)S(1)}, bf16[4,64,1536]{2,1,0:T(8,128)(2,1)}, u32[]{:S(2)}, u32[]{:S(2)}) collective-permute-start(bf16[4,64,1536]{2,1,0:T(8,128)(2,1)S(1)} %collective-permute-done.12.refs_3_), channel_id=1, source_target_pairs={{0,2},{1,5},{2,0},{3,7},{4,6},{5,1},{6,4},{7,3},{8,10},{9,13},{10,... | collective-permute-start | bytes 2359304 | tf_op jit(solution)/shard_map/ppermute | solution.py:502
  114.1 12.6 %run_experts.2 = (bf16[4,64,1536]{2,1,0:T(8,128)(2,1)S(1)}, bf16[4,64,1536]{2,1,0:T(8,128)(2,1)S(1)}, bf16[4,64,1536]{2,1,0:T(8,128)(2,1)S(1)}, bf16[4,64,1536]{2,1,0:T(8,128)(2,1)S(1)}) custom-call(bf16[4,64,1536]{2,1,0:T(8,128)(2,1)S(1)} %stack_rows.2.refs_0_, bf16[4,64,1536]{2,1,0:T(8,128)(2,1)S(1)} %stack_rows.3.refs_1_, ...), custom_call_target="tpu_custom_call" | custom-call | flops 8053063680 | bytes 26000000 | tf_op jit(solution)/shard_map/run_experts/pallas_call | solution.py:422
  126.7 7.1 %collective-permute-done.16.refs_3_ = bf16[4,64,1536]{2,1,0:T(8,128)(2,1)} collective-permute-done((bf16[4,64,1536]{2,1,0:T(8,128)(2,1)S(1)}, bf16[4,64,1536]{2,1,0:T(8,128)(2,1)}, u32[]{:S(2)}, u32[]{:S(2)}) %collective-permute-start.16) | collective-permute-done | bytes 786464 | tf_op jit(solution)/shard_map/ppermute | solution.py:502
  133.8 13.4 %run_experts.3 = (bf16[4,64,1536]{2,1,0:T(8,128)(2,1)S(1)}, bf16[4,64,1536]{2,1,0:T(8,128)(2,1)S(1)}, bf16[4,64,1536]{2,1,0:T(8,128)(2,1)S(1)}, bf16[4,64,1536]{2,1,0:T(8,128)(2,1)S(1)}) custom-call(bf16[4,64,1536]{2,1,0:T(8,128)(2,1)} %collective-permute-done.13.refs_0_, bf16[4,64,1536]{2,1,0:T(8,128)(2,1)} %collective-permute-done.14.refs_1_, ...), custom_call_target="tpu_custom_call" | custom-call | flops 8053063680 | bytes 26000000 | tf_op jit(solution)/shard_map/run_experts/pallas_call | solution.py:422
  151.3 7.9 %collective-permute-done.17 = bf16[4,64,1536]{2,1,0:T(8,128)(2,1)S(1)} collective-permute-done((bf16[4,64,1536]{2,1,0:T(8,128)(2,1)S(1)}, bf16[4,64,1536]{2,1,0:T(8,128)(2,1)S(1)}, u32[]{:S(2)}, u32[]{:S(2)}) %collective-permute-start.17) | collective-permute-done | bytes 786464 | tf_op jit(solution)/shard_map/ppermute | solution.py:502
  159.4 2.6 %collective-permute-start.18 = (bf16[4,64,1536]{2,1,0:T(8,128)(2,1)S(1)}, bf16[4,64,1536]{2,1,0:T(8,128)(2,1)S(1)}, u32[]{:S(2)}, u32[]{:S(2)}) collective-permute-start(bf16[4,64,1536]{2,1,0:T(8,128)(2,1)S(1)} %add_convert_fusion.1), channel_id=1, source_target_pairs={{0,4},{1,3},{2,6},{3,1},{4,0},{5,7},{6,2},{7,5},{8,12},{9,11},{10,... | collective-permute-start | bytes 2359304 | tf_op jit(solution)/shard_map/ppermute | solution.py:502
  162.0 11.1 %collective-permute-done.23 = bf16[4,64,1536]{2,1,0:T(8,128)(2,1)S(1)} collective-permute-done((bf16[4,64,1536]{2,1,0:T(8,128)(2,1)S(1)}, bf16[4,64,1536]{2,1,0:T(8,128)(2,1)S(1)}, u32[]{:S(2)}, u32[]{:S(2)}) %collective-permute-start.23) | collective-permute-done | bytes 786464 | tf_op jit(solution)/shard_map/ppermute | solution.py:502
  173.3 3.4 %collective-permute-start.24 = (bf16[4,64,1536]{2,1,0:T(8,128)(2,1)S(1)}, bf16[4,64,1536]{2,1,0:T(8,128)(2,1)S(1)}, u32[]{:S(2)}, u32[]{:S(2)}) collective-permute-start(bf16[4,64,1536]{2,1,0:T(8,128)(2,1)S(1)} %add_convert_fusion), channel_id=1, source_target_pairs={{0,4},{1,3},{2,6},{3,1},{4,0},{5,7},{6,2},{7,5},{8,12},{9,11},{10,... | collective-permute-start | bytes 2359304 | tf_op jit(solution)/shard_map/ppermute | solution.py:502
  176.7 13.3 %collective-permute-done.19 = bf16[4,64,1536]{2,1,0:T(8,128)(2,1)S(1)} collective-permute-done((bf16[4,64,1536]{2,1,0:T(8,128)(2,1)S(1)}, bf16[4,64,1536]{2,1,0:T(8,128)(2,1)S(1)}, u32[]{:S(2)}, u32[]{:S(2)}) %collective-permute-start.19) | collective-permute-done | bytes 786464 | tf_op jit(solution)/shard_map/ppermute | solution.py:502
  192.3 9.1 %collective-permute-done.25 = bf16[4,64,1536]{2,1,0:T(8,128)(2,1)S(1)} collective-permute-done((bf16[4,64,1536]{2,1,0:T(8,128)(2,1)S(1)}, bf16[4,64,1536]{2,1,0:T(8,128)(2,1)S(1)}, u32[]{:S(2)}, u32[]{:S(2)}) %collective-permute-start.25) | collective-permute-done | bytes 786464 | tf_op jit(solution)/shard_map/ppermute | solution.py:502
  203.7 3.8 %collective-permute-done.21 = bf16[64,1536]{1,0:T(8,128)(2,1)S(1)} collective-permute-done((bf16[64,1536]{1,0:T(8,128)(2,1)S(1)}, bf16[64,1536]{1,0:T(8,128)(2,1)S(1)}, u32[]{:S(2)}, u32[]{:S(2)}) %collective-permute-start.21) | collective-permute-done | bytes 196640 | tf_op jit(solution)/shard_map/ppermute | solution.py:502
  207.7 3.8 %collective-permute-done.26 = bf16[64,1536]{1,0:T(8,128)(2,1)S(1)} collective-permute-done((bf16[64,1536]{1,0:T(8,128)(2,1)S(1)}, bf16[64,1536]{1,0:T(8,128)(2,1)S(1)}, u32[]{:S(2)}, u32[]{:S(2)}) %collective-permute-start.26) | collective-permute-done | bytes 196640 | tf_op jit(solution)/shard_map/ppermute | solution.py:502
  211.4 12.7 %collective-permute-done.27 = bf16[64,1536]{1,0:T(8,128)(2,1)S(1)} collective-permute-done((bf16[64,1536]{1,0:T(8,128)(2,1)S(1)}, bf16[64,1536]{1,0:T(8,128)(2,1)S(1)}, u32[]{:S(2)}, u32[]{:S(2)}) %collective-permute-start.27) | collective-permute-done | bytes 196640 | tf_op jit(solution)/shard_map/ppermute | solution.py:502
  (94 shorter events, 34.9 us)
Async XLA Ops:
  7.2 104.4 %all-gather.3.cloned.1.call-start = ((), (), s32[]{:S(2)}) async-start(), calls=%async_computation | async-start | bytes 1114112 | tf_op jit(solution)/shard_map/all_gather | solution.py:595
  22.1 26.7 %collective-permute-start.3 = (bf16[2,1536,1024]{2,1,0:T(8,128)(2,1)}, bf16[2,1536,1024]{2,1,0:T(8,128)(2,1)}, u32[]{:S(2)}, u32[]{:S(2)}) collective-permute-start(bf16[2,1536,1024]{2,1,0:T(8,128)(2,1)} %refs_7_.3), channel_id=1, source_target_pairs={{0,1},{1,0},{2,3},{3,2},{4,5},{5,4},{6,7},{7,6},{8,9},{9,8},{10,11... | collective-permute-start | bytes 18874376 | tf_op jit(solution)/shard_map/ppermute | solution.py:584
  22.5 26.3 %collective-permute-start.4 = (bf16[2,512,1536]{2,1,0:T(8,128)(2,1)}, bf16[2,512,1536]{2,1,0:T(8,128)(2,1)}, u32[]{:S(2)}, u32[]{:S(2)}) collective-permute-start(bf16[2,512,1536]{2,1,0:T(8,128)(2,1)} %refs_9_.3), channel_id=1, source_target_pairs={{0,1},{1,0},{2,3},{3,2},{4,5},{5,4},{6,7},{7,6},{8,9},{9,8},{10,11... | collective-permute-start | bytes 9437192 | tf_op jit(solution)/shard_map/ppermute | solution.py:584
  41.9 21.7 %collective-permute-start.5 = (bf16[64,1536]{1,0:T(8,128)(2,1)S(1)}, bf16[64,1536]{1,0:T(8,128)(2,1)S(1)}, u32[]{:S(2)}, u32[]{:S(2)}) collective-permute-start(bf16[64,1536]{1,0:T(8,128)(2,1)S(1)} %get-tuple-element.38.refs_0_), channel_id=1, source_target_pairs={{0,8},{1,9},{2,10},{3,11},{4,12},{5,13},{6,14},{7,15},{8,16},{9,17... | collective-permute-start | bytes 589832 | tf_op jit(solution)/shard_map/ppermute | solution.py:502
  44.9 19.1 %collective-permute-start.6 = (bf16[64,1536]{1,0:T(8,128)(2,1)S(1)}, bf16[64,1536]{1,0:T(8,128)(2,1)S(1)}, u32[]{:S(2)}, u32[]{:S(2)}) collective-permute-start(bf16[64,1536]{1,0:T(8,128)(2,1)S(1)} %get-tuple-element.38.refs_0_), channel_id=1, source_target_pairs={{0,16},{1,17},{2,18},{3,19},{4,20},{5,21},{6,22},{7,23},{8,24},{9,... | collective-permute-start | bytes 589832 | tf_op jit(solution)/shard_map/ppermute | solution.py:502
  47.5 16.5 %collective-permute-start.7 = (bf16[64,1536]{1,0:T(8,128)(2,1)S(1)}, bf16[64,1536]{1,0:T(8,128)(2,1)S(1)}, u32[]{:S(2)}, u32[]{:S(2)}) collective-permute-start(bf16[64,1536]{1,0:T(8,128)(2,1)S(1)} %get-tuple-element.38.refs_0_), channel_id=1, source_target_pairs={{0,24},{1,25},{2,26},{3,27},{4,28},{5,29},{6,30},{7,31},{8,0},{9,1... | collective-permute-start | bytes 589832 | tf_op jit(solution)/shard_map/ppermute | solution.py:502
  62.0 12.4 %collective-permute-start.8 = (bf16[64,1536]{1,0:T(8,128)(2,1)S(1)}, bf16[64,1536]{1,0:T(8,128)(2,1)S(1)}, u32[]{:S(2)}, u32[]{:S(2)}) collective-permute-start(bf16[64,1536]{1,0:T(8,128)(2,1)S(1)} %get-tuple-element.39.refs_4_.refs_0_), channel_id=1, source_target_pairs={{0,8},{1,9},{2,10},{3,11},{4,12},{5,13},{6,14},{7,15},{8,16},{9,17... | collective-permute-start | bytes 589832 | tf_op jit(solution)/shard_map/ppermute | solution.py:502
  63.6 25.3 %collective-permute-start.9 = (bf16[64,1536]{1,0:T(8,128)(2,1)S(1)}, bf16[64,1536]{1,0:T(8,128)(2,1)S(1)}, u32[]{:S(2)}, u32[]{:S(2)}) collective-permute-start(bf16[64,1536]{1,0:T(8,128)(2,1)S(1)} %get-tuple-element.39.refs_4_.refs_0_), channel_id=1, source_target_pairs={{0,16},{1,17},{2,18},{3,19},{4,20},{5,21},{6,22},{7,23},{8,24},{9,... | collective-permute-start | bytes 589832 | tf_op jit(solution)/shard_map/ppermute | solution.py:502
  64.0 29.5 %collective-permute-start.11 = (bf16[4,64,1536]{2,1,0:T(8,128)(2,1)S(1)}, bf16[4,64,1536]{2,1,0:T(8,128)(2,1)S(1)}, u32[]{:S(2)}, u32[]{:S(2)}) collective-permute-start(bf16[4,64,1536]{2,1,0:T(8,128)(2,1)S(1)} %stack_rows.2.refs_0_), channel_id=1, source_target_pairs={{0,4},{1,3},{2,6},{3,1},{4,0},{5,7},{6,2},{7,5},{8,12},{9,11},{10,... | collective-permute-start | bytes 2359304 | tf_op jit(solution)/shard_map/ppermute | solution.py:502
  89.0 19.1 %collective-permute-start.12 = (bf16[4,64,1536]{2,1,0:T(8,128)(2,1)S(1)}, bf16[4,64,1536]{2,1,0:T(8,128)(2,1)S(1)}, u32[]{:S(2)}, u32[]{:S(2)}) collective-permute-start(bf16[4,64,1536]{2,1,0:T(8,128)(2,1)S(1)} %stack_rows.3.refs_1_), channel_id=1, source_target_pairs={{0,4},{1,3},{2,6},{3,1},{4,0},{5,7},{6,2},{7,5},{8,12},{9,11},{10,... | collective-permute-start | bytes 2359304 | tf_op jit(solution)/shard_map/ppermute | solution.py:502
  90.7 36.0 %collective-permute-start.13 = (bf16[4,64,1536]{2,1,0:T(8,128)(2,1)S(1)}, bf16[4,64,1536]{2,1,0:T(8,128)(2,1)}, u32[]{:S(2)}, u32[]{:S(2)}) collective-permute-start(bf16[4,64,1536]{2,1,0:T(8,128)(2,1)S(1)} %stack_rows.2.refs_0_), channel_id=1, source_target_pairs={{0,2},{1,5},{2,0},{3,7},{4,6},{5,1},{6,4},{7,3},{8,10},{9,13},{10,... | collective-permute-start | bytes 2359304 | tf_op jit(solution)/shard_map/ppermute | solution.py:502
  93.5 33.2 %collective-permute-start.14 = (bf16[4,64,1536]{2,1,0:T(8,128)(2,1)S(1)}, bf16[4,64,1536]{2,1,0:T(8,128)(2,1)}, u32[]{:S(2)}, u32[]{:S(2)}) collective-permute-start(bf16[4,64,1536]{2,1,0:T(8,128)(2,1)S(1)} %stack_rows.3.refs_1_), channel_id=1, source_target_pairs={{0,2},{1,5},{2,0},{3,7},{4,6},{5,1},{6,4},{7,3},{8,10},{9,13},{10,... | collective-permute-start | bytes 2359304 | tf_op jit(solution)/shard_map/ppermute | solution.py:502
  93.5 33.1 %collective-permute-start.15 = (bf16[4,64,1536]{2,1,0:T(8,128)(2,1)S(1)}, bf16[4,64,1536]{2,1,0:T(8,128)(2,1)}, u32[]{:S(2)}, u32[]{:S(2)}) collective-permute-start(bf16[4,64,1536]{2,1,0:T(8,128)(2,1)S(1)} %collective-permute-done.11.refs_2_), channel_id=1, source_target_pairs={{0,2},{1,5},{2,0},{3,7},{4,6},{5,1},{6,4},{7,3},{8,10},{9,13},{10,... | collective-permute-start | bytes 2359304 | tf_op jit(solution)/shard_map/ppermute | solution.py:502
  108.1 25.7 %collective-permute-start.16 = (bf16[4,64,1536]{2,1,0:T(8,128)(2,1)S(1)}, bf16[4,64,1536]{2,1,0:T(8,128)(2,1)}, u32[]{:S(2)}, u32[]{:S(2)}) collective-permute-start(bf16[4,64,1536]{2,1,0:T(8,128)(2,1)S(1)} %collective-permute-done.12.refs_3_), channel_id=1, source_target_pairs={{0,2},{1,5},{2,0},{3,7},{4,6},{5,1},{6,4},{7,3},{8,10},{9,13},{10,... | collective-permute-start | bytes 2359304 | tf_op jit(solution)/shard_map/ppermute | solution.py:502
  148.8 24.3 %collective-permute-start.23 = (bf16[4,64,1536]{2,1,0:T(8,128)(2,1)S(1)}, bf16[4,64,1536]{2,1,0:T(8,128)(2,1)S(1)}, u32[]{:S(2)}, u32[]{:S(2)}) collective-permute-start(bf16[4,64,1536]{2,1,0:T(8,128)(2,1)S(1)} %get-tuple-element.51), channel_id=1, source_target_pairs={{0,2},{1,5},{2,0},{3,7},{4,6},{5,1},{6,4},{7,3},{8,10},{9,13},{10,... | collective-permute-start | bytes 2359304 | tf_op jit(solution)/shard_map/ppermute | solution.py:502
  149.3 40.7 %collective-permute-start.19 = (bf16[4,64,1536]{2,1,0:T(8,128)(2,1)S(1)}, bf16[4,64,1536]{2,1,0:T(8,128)(2,1)S(1)}, u32[]{:S(2)}, u32[]{:S(2)}) collective-permute-start(bf16[4,64,1536]{2,1,0:T(8,128)(2,1)S(1)} %get-tuple-element.49), channel_id=1, source_target_pairs={{0,2},{1,5},{2,0},{3,7},{4,6},{5,1},{6,4},{7,3},{8,10},{9,13},{10,... | collective-permute-start | bytes 2359304 | tf_op jit(solution)/shard_map/ppermute | solution.py:502
  150.8 50.6 %collective-permute-start.25 = (bf16[4,64,1536]{2,1,0:T(8,128)(2,1)S(1)}, bf16[4,64,1536]{2,1,0:T(8,128)(2,1)S(1)}, u32[]{:S(2)}, u32[]{:S(2)}) collective-permute-start(bf16[4,64,1536]{2,1,0:T(8,128)(2,1)S(1)} %get-tuple-element.53), channel_id=1, source_target_pairs={{0,2},{1,5},{2,0},{3,7},{4,6},{5,1},{6,4},{7,3},{8,10},{9,13},{10,... | collective-permute-start | bytes 2359304 | tf_op jit(solution)/shard_map/ppermute | solution.py:502
  159.4 30.5 %collective-permute-start.18 = (bf16[4,64,1536]{2,1,0:T(8,128)(2,1)S(1)}, bf16[4,64,1536]{2,1,0:T(8,128)(2,1)S(1)}, u32[]{:S(2)}, u32[]{:S(2)}) collective-permute-start(bf16[4,64,1536]{2,1,0:T(8,128)(2,1)S(1)} %add_convert_fusion.1), channel_id=1, source_target_pairs={{0,4},{1,3},{2,6},{3,1},{4,0},{5,7},{6,2},{7,5},{8,12},{9,11},{10,... | collective-permute-start | bytes 2359304 | tf_op jit(solution)/shard_map/ppermute | solution.py:502
  173.3 28.1 %collective-permute-start.24 = (bf16[4,64,1536]{2,1,0:T(8,128)(2,1)S(1)}, bf16[4,64,1536]{2,1,0:T(8,128)(2,1)S(1)}, u32[]{:S(2)}, u32[]{:S(2)}) collective-permute-start(bf16[4,64,1536]{2,1,0:T(8,128)(2,1)S(1)} %add_convert_fusion), channel_id=1, source_target_pairs={{0,4},{1,3},{2,6},{3,1},{4,0},{5,7},{6,2},{7,5},{8,12},{9,11},{10,... | collective-permute-start | bytes 2359304 | tf_op jit(solution)/shard_map/ppermute | solution.py:502
  190.2 12.1 %collective-permute-start.20 = (bf16[64,1536]{1,0:T(8,128)(2,1)S(1)}, bf16[64,1536]{1,0:T(8,128)(2,1)S(1)}, u32[]{:S(2)}, u32[]{:S(2)}) collective-permute-start(bf16[64,1536]{1,0:T(8,128)(2,1)S(1)} %get-tuple-element.54), channel_id=1, source_target_pairs={{0,24},{1,25},{2,26},{3,27},{4,28},{5,29},{6,30},{7,31},{8,0},{9,1... | collective-permute-start | bytes 589832 | tf_op jit(solution)/shard_map/ppermute | solution.py:502
  190.3 17.3 %collective-permute-start.21 = (bf16[64,1536]{1,0:T(8,128)(2,1)S(1)}, bf16[64,1536]{1,0:T(8,128)(2,1)S(1)}, u32[]{:S(2)}, u32[]{:S(2)}) collective-permute-start(bf16[64,1536]{1,0:T(8,128)(2,1)S(1)} %get-tuple-element.56), channel_id=1, source_target_pairs={{0,16},{1,17},{2,18},{3,19},{4,20},{5,21},{6,22},{7,23},{8,24},{9,... | collective-permute-start | bytes 589832 | tf_op jit(solution)/shard_map/ppermute | solution.py:502
  190.3 17.2 %collective-permute-start.22 = (bf16[64,1536]{1,0:T(8,128)(2,1)S(1)}, bf16[64,1536]{1,0:T(8,128)(2,1)S(1)}, u32[]{:S(2)}, u32[]{:S(2)}) collective-permute-start(bf16[64,1536]{1,0:T(8,128)(2,1)S(1)} %get-tuple-element.55), channel_id=1, source_target_pairs={{0,8},{1,9},{2,10},{3,11},{4,12},{5,13},{6,14},{7,15},{8,16},{9,17... | collective-permute-start | bytes 589832 | tf_op jit(solution)/shard_map/ppermute | solution.py:502
  202.3 21.9 %collective-permute-start.27 = (bf16[64,1536]{1,0:T(8,128)(2,1)S(1)}, bf16[64,1536]{1,0:T(8,128)(2,1)S(1)}, u32[]{:S(2)}, u32[]{:S(2)}) collective-permute-start(bf16[64,1536]{1,0:T(8,128)(2,1)S(1)} %get-tuple-element.59), channel_id=1, source_target_pairs={{0,16},{1,17},{2,18},{3,19},{4,20},{5,21},{6,22},{7,23},{8,24},{9,... | collective-permute-start | bytes 589832 | tf_op jit(solution)/shard_map/ppermute | solution.py:502
  202.3 21.9 %collective-permute-start.28 = (bf16[64,1536]{1,0:T(8,128)(2,1)S(1)}, bf16[64,1536]{1,0:T(8,128)(2,1)S(1)}, u32[]{:S(2)}, u32[]{:S(2)}) collective-permute-start(bf16[64,1536]{1,0:T(8,128)(2,1)S(1)} %get-tuple-element.58), channel_id=1, source_target_pairs={{0,8},{1,9},{2,10},{3,11},{4,12},{5,13},{6,14},{7,15},{8,16},{9,17... | collective-permute-start | bytes 589832 | tf_op jit(solution)/shard_map/ppermute | solution.py:502
  (19 other events, 91.2 us)
Sparse Core Ops, SparseCore 0:
  23.5 68.1 all-gather.2

commit v5 on v4

--- a/solution.py
+++ b/solution.py
@@ -98,7 +98,7 @@
             jax.ShapeDtypeStruct((rows, 2 * tile), jnp.bfloat16),
         ],
         scratch_shapes=[pltpu.VMEM((2 * rows, width), jnp.bfloat16)],
-        compiler_params=params(24),
+        compiler_params=params(58),
         cost_estimate=pl.CostEstimate(
             flops=2 * rows * width * 3584, bytes_accessed=9_500_000, transcendentals=0
         ),
@@ -106,8 +106,8 @@
     )(own, other, gain, cosine, sine, w_qkv, *after)
 
 
-def attend_kernel(first_row, extra, place_ref, q_ref, kc_ref, kco_ref, vc_ref, vco_ref, ks_ref, kso_ref, vs_ref, vso_ref, w_out_ref, tokens_ref, gain_ref, *refs):
-    attended_ref, stream_ref, expert_in_ref, keys, values, wide_q, total = refs[extra:]
+def attend_kernel(first_row, riders, extra, place_ref, q_ref, kc_ref, kco_ref, vc_ref, vco_ref, ks_ref, kso_ref, vs_ref, vso_ref, w_out_ref, tokens_ref, gain_ref, *refs):
+    attended_ref, stream_ref, expert_in_ref, keys, values, wide_q, total = refs[riders + extra :]
     step = pl.program_id(0)
     rows = q_ref.shape[0]
     cached = kc_ref.shape[1]
@@ -200,12 +200,14 @@
         stream_ref[...] = stream
         wide = stream.astype(jnp.float32)
         mean_square = jnp.mean(wide * wide, axis=-1, keepdims=True)
-        expert_in_ref[...] = (wide * lax.rsqrt(mean_square + epsilon) * gain_ref[...][None, :]).astype(
-            jnp.bfloat16
-        )
-
-
-def attend(place, queries, caches, spans, w_out, tokens, gain, first_row, rows, filled, after):
+        expert_in_ref[:rows] = (
+            wide * lax.rsqrt(mean_square + epsilon) * gain_ref[...][None, :]
+        ).astype(jnp.bfloat16)
+        if riders:
+            expert_in_ref[rows:] = refs[0][...]
+
+
+def attend(place, queries, caches, spans, w_out, tokens, gain, first_row, rows, riders, filled, after):
     k_cache, k_other, v_cache, v_other = caches
     own_span, other_span = spans
     cached = k_cache.shape[1]
@@ -217,8 +219,9 @@
     key_spec = pl.BlockSpec((span, LANES), lambda j: (0, j))
     value_spec = pl.BlockSpec((span, LANES), lambda j: (0, pairs + j))
     extra = [*filled, *after]
+    sent = rows + sum(r.shape[0] for r in riders)
     return pl.pallas_call(
-        functools.partial(attend_kernel, first_row, len(extra)),
+        functools.partial(attend_kernel, first_row, len(riders), len(extra)),
         grid=(pairs,),
         in_specs=[
             pl.BlockSpec(memory_space=pltpu.SMEM),
@@ -235,25 +238,26 @@
             pl.BlockSpec((rows, width), lambda j: (part, 0)),
             vmem_spec(),
         ]
+        + [vmem_spec()] * len(riders)
         + [pl.BlockSpec(memory_space=pl.ANY)] * len(extra),
         out_specs=[
             pl.BlockSpec((rows, PAIR), lambda j: (part, j)),
             pl.BlockSpec((rows, width), lambda j: (part, 0)),
-            pl.BlockSpec((rows, width), lambda j: (0, 0)),
+            pl.BlockSpec((sent, width), lambda j: (0, 0)),
         ],
         out_shape=[
             jax.ShapeDtypeStruct((span, HEADS * HEAD), jnp.bfloat16),
             jax.ShapeDtypeStruct((span, width), jnp.bfloat16),
-            jax.ShapeDtypeStruct((rows, width), jnp.bfloat16),
+            jax.ShapeDtypeStruct((sent, width), jnp.bfloat16),
         ],
-        input_output_aliases={13 + i: i for i in range(len(filled))},
+        input_output_aliases={13 + len(riders) + i: i for i in range(len(filled))},
         scratch_shapes=[
             pltpu.VMEM((key_count, 2 * LANES), jnp.bfloat16),
             pltpu.VMEM((key_count, 2 * LANES), jnp.bfloat16),
             pltpu.VMEM((2 * GROUP * rows, 2 * LANES), jnp.bfloat16),
             pltpu.VMEM((rows, width), jnp.float32),
         ],
-        compiler_params=params(40),
+        compiler_params=params(58),
         cost_estimate=pl.CostEstimate(
             flops=16 * HEADS * rows * key_count * LANES,
             bytes_accessed=10_000_000,
@@ -274,14 +278,16 @@
         w_out,
         tokens,
         gain,
+        *riders,
         *extra,
     )
 
 
-def plan_kernel(groups, capacity, top, slot_ref, chip_ref, table_ref, *out_refs):
+def plan_kernel(pieces, first, capacity, top, slot_ref, *refs):
+    pick_ref, back_ref, share_ref = refs[pieces:]
     slots = slot_ref.shape[0]
-    chips, _, tokens = table_ref.shape
-    in_group = chips // groups
+    sources, _, tokens = pick_ref.shape
+    deep = sources // pieces
     earlier = jnp.where(
         lax.broadcasted_iota(jnp.int32, (tokens, tokens), 0)
         < lax.broadcasted_iota(jnp.int32, (tokens, tokens), 1),
@@ -289,58 +295,60 @@
         0.0,
     ).astype(jnp.bfloat16)
     place = lax.broadcasted_iota(jnp.int32, (capacity, tokens), 0).astype(jnp.float32)
-    for group in range(groups):
-        pick_ref, back_ref, share_ref = out_refs[3 * group : 3 * group + 3]
-        hot_rows, share_lines = [], []
-        for source in range(in_group):
-            entry = table_ref[chip_ref[group * in_group + source]]
-            for slot in range(slots):
-                match = entry[:top] == slot_ref[slot].astype(jnp.float32)
-                hot_rows.append(jnp.max(jnp.where(match, 1.0, 0.0), axis=0, keepdims=True))
-                share_lines.append(
-                    jnp.sum(jnp.where(match, entry[top : 2 * top], 0.0), axis=0, keepdims=True)
-                )
-        hot = jnp.concatenate(hot_rows, axis=0)
-        rank = jnp.dot(hot.astype(jnp.bfloat16), earlier, preferred_element_type=jnp.float32)
-        rank = jnp.where(hot > 0.0, rank, -1.0)
-        for source in range(in_group):
-            picks = []
-            for slot in range(slots):
-                line = source * slots + slot
-                chosen = jnp.where(place == rank[line : line + 1], 1.0, 0.0)
-                share_ref[slot, source * capacity : (source + 1) * capacity] = jnp.sum(
-                    chosen * share_lines[line], axis=1, keepdims=True
-                )
-                picks.append(chosen)
-            picked = jnp.concatenate(picks, axis=0)
-            pick_ref[source] = picked.astype(jnp.bfloat16)
-            back_ref[source] = jnp.transpose(picked).astype(jnp.bfloat16)
-
-
-def plan_routes(slot_ids, chip_ids, tables, groups, capacity, top):
-    chips, _, tokens = tables.shape
+    hot_rows, share_lines = [], []
+    for source in range(sources):
+        packed = refs[source // deep][source % deep, first:].astype(jnp.float32)
+        across = packed.shape[1] // tokens
+        lines = [
+            packed[i // across : i // across + 1, i % across * tokens : (i % across + 1) * tokens]
+            for i in range(3 * top)
+        ]
+        ids = jnp.concatenate(lines[:top], axis=0)
+        shares = jnp.concatenate(lines[top : 2 * top], axis=0)
+        shares += jnp.concatenate(lines[2 * top :], axis=0)
+        for slot in range(slots):
+            match = ids == slot_ref[slot].astype(jnp.float32)
+            hot_rows.append(jnp.max(jnp.where(match, 1.0, 0.0), axis=0, keepdims=True))
+            share_lines.append(jnp.sum(jnp.where(match, shares, 0.0), axis=0, keepdims=True))
+    hot = jnp.concatenate(hot_rows, axis=0)
+    rank = jnp.dot(hot.astype(jnp.bfloat16), earlier, preferred_element_type=jnp.float32)
+    rank = jnp.where(hot > 0.0, rank, -1.0)
+    for source in range(sources):
+        picks = []
+        for slot in range(slots):
+            line = source * slots + slot
+            chosen = jnp.where(place == rank[line : line + 1], 1.0, 0.0)
+            share_ref[slot, source * capacity : (source + 1) * capacity] = jnp.sum(
+                chosen * share_lines[line], axis=1, keepdims=True
+            )
+            picks.append(chosen)
+        picked = jnp.concatenate(picks, axis=0)
+        pick_ref[source] = picked.astype(jnp.bfloat16)
+        back_ref[source] = jnp.transpose(picked).astype(jnp.bfloat16)
+
+
+def plan_routes(slot_ids, pieces, first, tokens, capacity, top):
     slots = slot_ids.shape[0]
-    in_group = chips // groups
-    flat = pl.pallas_call(
-        functools.partial(plan_kernel, groups, capacity, top),
-        in_specs=[pl.BlockSpec(memory_space=pltpu.SMEM)] * 2 + [vmem_spec()],
-        out_specs=[vmem_spec()] * (3 * groups),
+    sources = sum(p.shape[0] for p in pieces)
+    return pl.pallas_call(
+        functools.partial(plan_kernel, len(pieces), first, capacity, top),
+        in_specs=[pl.BlockSpec(memory_space=pltpu.SMEM)] + [vmem_spec()] * len(pieces),
+        out_specs=[vmem_spec()] * 3,
         out_shape=[
-            jax.ShapeDtypeStruct((in_group, slots * capacity, tokens), jnp.bfloat16),
-            jax.ShapeDtypeStruct((in_group, tokens, slots * capacity), jnp.bfloat16),
-            jax.ShapeDtypeStruct((slots, in_group * capacity, 1), jnp.float32),
-        ]
-        * groups,
+            jax.ShapeDtypeStruct((sources, slots * capacity, tokens), jnp.bfloat16),
+            jax.ShapeDtypeStruct((sources, tokens, slots * capacity), jnp.bfloat16),
+            jax.ShapeDtypeStruct((slots, sources * capacity, 1), jnp.float32),
+        ],
         compiler_params=params(24),
         cost_estimate=pl.CostEstimate(
-            flops=5_000_000_000, bytes_accessed=2_000_000, transcendentals=0
+            flops=1_000_000_000, bytes_accessed=2_000_000, transcendentals=0
         ),
         name="plan_routes",
-    )(slot_ids, chip_ids, tables)
-    return [flat[3 * i : 3 * i + 3] for i in range(groups)]
-
-
-def expert_kernel(pieces, halves, out_cuts, extra, *refs):
+    )(slot_ids, *pieces)
+
+
+def expert_kernel(pieces, in_cuts, out_cuts, extra, *refs):
+    halves = len(in_cuts)
     row_refs = refs[: pieces * halves]
     rest = refs[pieces * halves :]
     pick_ref, back_ref, share_ref, up_ref, up_other_ref, down_ref, down_other_ref = rest[:7]
@@ -359,7 +367,10 @@
         for source in range(sources):
             piece = source // deep
             rows = jnp.concatenate(
-                [ref[source % deep] for ref in row_refs[piece * halves : (piece + 1) * halves]],
+                [
+                    row_refs[piece * halves + index][source % deep, :count]
+                    for index, count in enumerate(in_cuts)
+                ],
                 axis=0,
             )
             rows = jnp.dot(
@@ -405,7 +416,7 @@
                 start += count
 
 
-def run_experts(rows, plan, ups, downs, out_cuts, after):
+def run_experts(rows, plan, ups, downs, in_cuts, out_cuts, after):
     pieces, halves = len(rows), len(rows[0])
     deep, _, width = rows[0][0].shape
     own_slots, _, double = ups[0].shape
@@ -420,7 +431,7 @@
         return (jnp.maximum(j - own_slots, 0), 0, 0)
 
     flat = pl.pallas_call(
-        functools.partial(expert_kernel, pieces, halves, tuple(out_cuts), len(after)),
+        functools.partial(expert_kernel, pieces, tuple(in_cuts), tuple(out_cuts), len(after)),
         grid=(slots,),
         in_specs=[vmem_spec()] * (pieces * halves + 3)
         + [
@@ -520,29 +531,24 @@
     return total.astype(terms[0].dtype)
 
 
-def scatter_planes(planes, shift, sizes):
+def scatter_chunks(chunks, shift, sizes):
     tall = sizes["a"]
-    arrived = {}
-    for j in range(tall - 1, -1, -1):
-        arrived[j] = [planes[0][j]] + [shift(planes[k][j], "b", -k) for k in range(1, sizes["b"])]
-    line = [shift(add_all(arrived[j]), "a", -j) for j in range(1, tall)] + arrived[0]
-    moved = [
-        shift(add_all([t[i] for t in line]), "z", -i) for i in range(1, sizes["z"])
-    ]
-    return add_all([t[0] for t in line] + moved)
-
-
-def source_chips(chip, core, chips):
-    depth, tall, wide = chip_shape(chips)
-    index = jnp.arange(chips, dtype=jnp.int32)
-    back_z, back_a, back_b = index % depth, index // depth % tall, index // (depth * tall)
-    back_y, back_x = back_a, back_b
-    if tall == wide:
-        back_y = jnp.where(core == 0, back_a, back_b)
-        back_x = jnp.where(core == 0, back_b, back_a)
-    z, y, x = chip // (tall * wide), chip // wide % tall, chip % wide
-    z, y, x = (z - back_z) % depth, (y - back_y) % tall, (x - back_x) % wide
-    return ((z * tall + y) * wide + x).astype(jnp.int32)
+    sums, before = [], []
+    for planes in chunks:
+        sending = planes[1:]
+        if before:
+            sending, _ = lax.optimization_barrier((sending, before))
+        arrived = {}
+        for j in range(tall - 1, -1, -1):
+            arrived[j] = [shift(plane[j], "b", -k - 1) for k, plane in enumerate(sending)]
+        before = [v for moved in arrived.values() for v in moved]
+        arrived = [[planes[0][j]] + arrived[j] for j in range(tall)]
+        line = [shift(add_all(arrived[j]), "a", -j) for j in range(1, tall)] + arrived[0]
+        moved = [
+            shift(add_all([t[i] for t in line]), "z", -i) for i in range(1, sizes["z"])
+        ]
+        sums.append(add_all([t[0] for t in line] + moved))
+    return jnp.concatenate(sums, axis=0)
 
 
 def rope_tables(positions):
@@ -590,9 +596,10 @@
         jnp.where(routes[:, :, None] == experts, replica_slot[:, None, :], 0), axis=2
     )
     shares = route_scores / jnp.sum(route_scores, axis=1, keepdims=True)
-    table = jnp.concatenate([slot_of.astype(jnp.float32), shares], axis=1).T
-    table = jnp.pad(table, ((0, row_count - table.shape[0]), (0, 0)))
-    tables = lax.all_gather(table, "req", axis=0)
+    coarse = lax.reduce_precision(shares, 8, 7)
+    table = jnp.concatenate([slot_of.astype(jnp.float32), coarse, shares - coarse], axis=1)
+    table = table.astype(jnp.bfloat16).T.reshape(-1, tokens.shape[1])
+    table = jnp.pad(table, ((0, 16 - table.shape[0]), (0, 0)))
     chip = lax.axis_index("req")
     chip_slots = jnp.arange(slots_dev, dtype=jnp.int32)
     slot_ids = jnp.concatenate(
@@ -601,7 +608,6 @@
             (chip * cores + 1 - seq_index) * slots_dev + chip_slots,
         ]
     ).astype(jnp.int32)
-    plans = plan_routes(slot_ids, source_chips(chip, seq_index, chips), tables, sizes["b"], capacity, top_count)
 
     row_index = jnp.arange(row_count, dtype=jnp.int32)
     cosine, sine = rope_tables(
@@ -629,31 +635,34 @@
             ffn_gain,
             index * half,
             half,
+            [] if index else [table],
             filled,
             [up_other, down_other] if index else [],
         )
         filled = [attended, stream]
         lines.append(gather_line(expert_in, shift, sizes))
-    halves = [gather_planes(stack_rows(line, [expert_in]), shift, sizes) for line in lines]
+    halves, after = [], [expert_in]
+    for line in lines:
+        planes = gather_planes(stack_rows(line, after), shift, sizes)
+        halves.append(planes)
+        after = [v for plane in planes[1:] for v in plane]
     cut = row_count // 2
     results = []
     for index in range(sizes["b"]):
+        plan = plan_routes(slot_ids, halves[0][index], half, row_count, capacity, top_count)
         results.append(
             run_experts(
                 [[planes[index][j] for planes in halves] for j in range(sizes["a"])],
-                plans[index],
+                plan,
                 (expert_up, up_other),
                 (expert_down, down_other),
+                (half, row_count - half),
                 (cut, row_count - cut),
                 results[-1][0][:1] if results else [],
             )
         )
-    expert_mix = jnp.concatenate(
-        [
-            scatter_planes([[piece[i] for piece in r] for r in results], shift, sizes)
-            for i in range(2)
-        ],
-        axis=0,
+    expert_mix = scatter_chunks(
+        [[[piece[i] for piece in r] for r in results] for i in range(2)], shift, sizes
     )
     return (attended, stream, expert_mix, appended)
 

time: 232 us -> 227 us (0.978)
  between operations: 14.9 us -> 1.53 us
  waiting for transfers between devices: 107 us -> 118 us
  local copies, waits for them, and re-layouts: 12.5 us -> 6.73 us
  Pallas kernels: 57.6 us -> 63.3 us
  starting transfers between devices: 36.5 us -> 32.8 us
    ppermute x24, waiting for transfers between devices: 105 us -> 117 us  [shift(): return lax.ppermute(value, BOTH, pairs(role, offset % sizes[role]))]
    unnamed x26 -> x24, local copies, waits for them, and re-layouts: 11.9 us -> 6.09 us
    ppermute x24, starting transfers between devices: 35 us -> 31.3 us  [shift(): return lax.ppermute(value, BOTH, pairs(role, offset % sizes[role]))]
    pallas_call x1, Pallas kernels: 4.87 us -> 7.38 us  [project(): pl.pallas_call(qkv_kernel, grid=(5,), in_specs=[vmem_spec()] * 5 + [pl.Bl...]
    pallas_call x5 -> x6, Pallas kernels: 52.7 us -> 54.9 us  [the longest x2 27.2 us: attend(): pl.pallas_call(functools.partial(attend_kernel, first_row, len(riders), l...]
  transfers between devices with their start and end apart: 30 -> 29, of which waited for: 13 -> 15; matrix products, arithmetic and copies ran while one was open for 1% -> 2% of each run, Pallas kernels for 17% -> 19%
where the time goes in v5:
time: 227 us
  waiting for transfers between devices  118 us (52%)
  Pallas kernels  63.3 us (28%)
  starting transfers between devices  32.8 us (14%)
  local copies, waits for them, and re-layouts  6.73 us (3%)
  other arithmetic  4.89 us (2%)
    ppermute x24, waiting for transfers between devices, shift(): return lax.ppermute(value, BOTH, pairs(role, offset % sizes[role]))  117 us
    ppermute x24, starting transfers between devices, shift(): return lax.ppermute(value, BOTH, pairs(role, offset % sizes[role]))  31.3 us
    pallas_call x2, Pallas kernels, attend(): pl.pallas_call(functools.partial(attend_kernel, first_row, len(riders), l...  27.2 us
    pallas_call x2, Pallas kernels, run_experts(): pl.pallas_call(functools.partial(expert_kernel, pieces, tuple(in_cuts), t...  25.6 us
    pallas_call x1, Pallas kernels, project(): pl.pallas_call(qkv_kernel, grid=(5,), in_specs=[vmem_spec()] * 5 + [pl.Bl...  7.38 us
    unnamed x24, local copies, waits for them, and re-layouts  6.09 us
  transfers between devices with their start and end apart: 29, of which 15 were waited for; matrix products, arithmetic and copies ran while one was open for 2% of the time, Pallas kernels for 19%

profile of v5, /device:TPU:0, one launch (start us, length us, event | category | flops | bytes accessed | tf_op | source)
XLA Modules:
  0.0 227.0 jit_solution(13974757764795664179)
XLA Ops:
  7.8 7.4 %project_rows.1 = (bf16[128,1536]{1,0:T(8,128)(2,1)}, bf16[128,1024]{1,0:T(8,128)(2,1)}, bf16[128,1024]{1,0:T(8,128)(2,1)}) custom-call(bf16[128,1536]{1,0:T(8,128)(2,1)} %tokens_ref.3, bf16[128,1536]{1,0:T(8,128)(2,1)} %copy-done.8, f32[1536]{0:T(1024)} %gain_ref.3, f32[256,128]{1,0:T(8,128)} %pad_maximum_fusion.1.cos_ref, ...), custom_call_target="tpu_custom_call" | custom-call | flops 1409286144 | bytes 9500000 | tf_op jit(solution)/shard_map/project_rows/pallas_call | solution.py:84
  17.1 13.6 %attend_rows.2 = (bf16[128,1536]{1,0:T(8,128)(2,1)}, bf16[128,1536]{1,0:T(8,128)(2,1)}, bf16[80,1536]{1,0:T(8,128)(2,1)}) custom-call(s32[2]{0:T(128)} %pad_add_fusion.place_ref, bf16[128,1536]{1,0:T(8,128)(2,1)} %get-tuple-element.31.q_ref, bf16[1,1024,512]{2,1,0:T(8,128)(2,1)} %kc_ref.3, bf16[1,1024,512]{2,1,0:T(8,128)(2,1)} %copy-done.6, ...), custom_call_target="tpu_custom_call" | custom-call | flops 7247757312 | bytes 10000000 | tf_op jit(solution)/shard_map/attend_rows/pallas_call | solution.py:223
  30.7 3.0 %collective-permute-start.5 = (bf16[80,1536]{1,0:T(8,128)(2,1)}, bf16[80,1536]{1,0:T(8,128)(2,1)S(1)}, u32[]{:S(2)}, u32[]{:S(2)}) collective-permute-start(bf16[80,1536]{1,0:T(8,128)(2,1)} %get-tuple-element.40.refs_0_), channel_id=1, source_target_pairs={{0,8},{1,9},{2,10},{3,11},{4,12},{5,13},{6,14},{7,15},{8,16},{9,17... | collective-permute-start | bytes 737288 | tf_op jit(solution)/shard_map/ppermute | solution.py:513
  33.7 2.6 %collective-permute-start.6 = (bf16[80,1536]{1,0:T(8,128)(2,1)}, bf16[80,1536]{1,0:T(8,128)(2,1)S(1)}, u32[]{:S(2)}, u32[]{:S(2)}) collective-permute-start(bf16[80,1536]{1,0:T(8,128)(2,1)} %get-tuple-element.40.refs_0_), channel_id=1, source_target_pairs={{0,16},{1,17},{2,18},{3,19},{4,20},{5,21},{6,22},{7,23},{8,24},{9,... | collective-permute-start | bytes 737288 | tf_op jit(solution)/shard_map/ppermute | solution.py:513
  37.6 13.6 %attend_rows.3 = (bf16[128,1536]{1,0:T(8,128)(2,1)}, bf16[128,1536]{1,0:T(8,128)(2,1)}, bf16[64,1536]{1,0:T(8,128)(2,1)}) custom-call(s32[2]{0:T(128)} %pad_add_fusion.place_ref, bf16[128,1536]{1,0:T(8,128)(2,1)} %get-tuple-element.31.q_ref, bf16[1,1024,512]{2,1,0:T(8,128)(2,1)} %kc_ref.3, ...), custom_call_target="tpu_custom_call", output_to_operand_aliasing={{0}: (13, {}), {1}: (14, {})} | custom-call | flops 7247757312 | bytes 10000000 | tf_op jit(solution)/shard_map/attend_rows/pallas_call | solution.py:223
  56.9 21.4 %collective-permute-done.12.refs_1_.refs_2_ = bf16[4,80,1536]{2,1,0:T(8,128)(2,1)S(1)} collective-permute-done((bf16[4,80,1536]{2,1,0:T(8,128)(2,1)S(1)}, bf16[4,80,1536]{2,1,0:T(8,128)(2,1)S(1)}, u32[]{:S(2)}, u32[]{:S(2)}) %collective-permute-start.12) | collective-permute-done | bytes 983072 | tf_op jit(solution)/shard_map/ppermute | solution.py:513
  80.2 6.2 %collective-permute-start.10 = (bf16[64,1536]{1,0:T(8,128)(2,1)S(1)}, bf16[64,1536]{1,0:T(8,128)(2,1)S(1)}, u32[]{:S(2)}, u32[]{:S(2)}) collective-permute-start(bf16[64,1536]{1,0:T(8,128)(2,1)S(1)} %copy-done), channel_id=1, source_target_pairs={{0,24},{1,25},{2,26},{3,27},{4,28},{5,29},{6,30},{7,31},{8,0},{9,1... | collective-permute-start | bytes 589832 | tf_op jit(solution)/shard_map/ppermute | solution.py:513
  87.5 5.5 %collective-permute-done.10.refs_3_ = bf16[64,1536]{1,0:T(8,128)(2,1)S(1)} collective-permute-done((bf16[64,1536]{1,0:T(8,128)(2,1)S(1)}, bf16[64,1536]{1,0:T(8,128)(2,1)S(1)}, u32[]{:S(2)}, u32[]{:S(2)}) %collective-permute-start.10) | collective-permute-done | bytes 196640 | tf_op jit(solution)/shard_map/ppermute | solution.py:513
  93.0 3.3 %collective-permute-done.8.refs_1_ = bf16[64,1536]{1,0:T(8,128)(2,1)S(1)} collective-permute-done((bf16[64,1536]{1,0:T(8,128)(2,1)S(1)}, bf16[64,1536]{1,0:T(8,128)(2,1)S(1)}, u32[]{:S(2)}, u32[]{:S(2)}) %collective-permute-start.8) | collective-permute-done | bytes 196640 | tf_op jit(solution)/shard_map/ppermute | solution.py:513
  96.2 6.7 %collective-permute-done.9.refs_2_ = bf16[64,1536]{1,0:T(8,128)(2,1)S(1)} collective-permute-done((bf16[64,1536]{1,0:T(8,128)(2,1)S(1)}, bf16[64,1536]{1,0:T(8,128)(2,1)S(1)}, u32[]{:S(2)}, u32[]{:S(2)}) %collective-permute-start.9) | collective-permute-done | bytes 196640 | tf_op jit(solution)/shard_map/ppermute | solution.py:513
  109.0 15.8 %collective-permute-done.14.refs_3_ = bf16[4,64,1536]{2,1,0:T(8,128)(2,1)} collective-permute-done((bf16[4,64,1536]{2,1,0:T(8,128)(2,1)}, bf16[4,64,1536]{2,1,0:T(8,128)(2,1)}, u32[]{:S(2)}, u32[]{:S(2)}) %collective-permute-start.14) | collective-permute-done | bytes 786464 | tf_op jit(solution)/shard_map/ppermute | solution.py:513
  124.8 2.1 collective-permute-start.16
  128.0 13.0 %run_experts.2 = (bf16[4,64,1536]{2,1,0:T(8,128)(2,1)S(1)}, bf16[4,64,1536]{2,1,0:T(8,128)(2,1)S(1)}, bf16[4,64,1536]{2,1,0:T(8,128)(2,1)S(1)}, bf16[4,64,1536]{2,1,0:T(8,128)(2,1)S(1)}) custom-call(bf16[4,80,1536]{2,1,0:T(8,128)(2,1)S(1)} %stack_rows.2.refs_0_, bf16[4,64,1536]{2,1,0:T(8,128)(2,1)} %stack_rows.3.refs_1_, bf16[4,80,1536]{2,1,0:T(8,128)(2,1)S(1)} %copy-done.5, ...), custom_call_target="tpu_custom_call" | custom-call | flops 8053063680 | bytes 26000000 | tf_op jit(solution)/shard_map/run_experts/pallas_call | solution.py:433
  141.0 12.6 %run_experts.3 = (bf16[4,64,1536]{2,1,0:T(8,128)(2,1)S(1)}, bf16[4,64,1536]{2,1,0:T(8,128)(2,1)S(1)}, bf16[4,64,1536]{2,1,0:T(8,128)(2,1)S(1)}, bf16[4,64,1536]{2,1,0:T(8,128)(2,1)S(1)}) custom-call(bf16[4,80,1536]{2,1,0:T(8,128)(2,1)S(1)} %collective-permute-done.11.refs_4_.refs_0_, bf16[4,64,1536]{2,1,0:T(8,128)(2,1)S(1)} %collective-permute-done.15.refs_1_, ...), custom_call_target="tpu_custom_call" | custom-call | flops 8053063680 | bytes 26000000 | tf_op jit(solution)/shard_map/run_experts/pallas_call | solution.py:433
  153.7 2.0 collective-permute-start.19
  155.7 10.0 %collective-permute-done.17 = bf16[4,64,1536]{2,1,0:T(8,128)(2,1)S(1)} collective-permute-done((bf16[4,64,1536]{2,1,0:T(8,128)(2,1)S(1)}, bf16[4,64,1536]{2,1,0:T(8,128)(2,1)S(1)}, u32[]{:S(2)}, u32[]{:S(2)}) %collective-permute-start.17) | collective-permute-done | bytes 786464 | tf_op jit(solution)/shard_map/ppermute | solution.py:513
  165.7 13.4 %collective-permute-done.19 = bf16[4,64,1536]{2,1,0:T(8,128)(2,1)S(1)} collective-permute-done((bf16[4,64,1536]{2,1,0:T(8,128)(2,1)S(1)}, bf16[4,64,1536]{2,1,0:T(8,128)(2,1)S(1)}, u32[]{:S(2)}, u32[]{:S(2)}) %collective-permute-start.19) | collective-permute-done | bytes 786464 | tf_op jit(solution)/shard_map/ppermute | solution.py:513
  179.4 2.1 collective-permute-start.25
  181.4 17.9 %collective-permute-done.23 = bf16[4,64,1536]{2,1,0:T(8,128)(2,1)S(1)} collective-permute-done((bf16[4,64,1536]{2,1,0:T(8,128)(2,1)S(1)}, bf16[4,64,1536]{2,1,0:T(8,128)(2,1)S(1)}, u32[]{:S(2)}, u32[]{:S(2)}) %collective-permute-start.23) | collective-permute-done | bytes 786464 | tf_op jit(solution)/shard_map/ppermute | solution.py:513
  202.3 5.5 %collective-permute-done.25 = bf16[4,64,1536]{2,1,0:T(8,128)(2,1)S(1)} collective-permute-done((bf16[4,64,1536]{2,1,0:T(8,128)(2,1)S(1)}, bf16[4,64,1536]{2,1,0:T(8,128)(2,1)S(1)}, u32[]{:S(2)}, u32[]{:S(2)}) %collective-permute-start.25) | collective-permute-done | bytes 786464 | tf_op jit(solution)/shard_map/ppermute | solution.py:513
  207.8 3.8 %collective-permute-done.24 = bf16[4,64,1536]{2,1,0:T(8,128)(2,1)S(1)} collective-permute-done((bf16[4,64,1536]{2,1,0:T(8,128)(2,1)S(1)}, bf16[4,64,1536]{2,1,0:T(8,128)(2,1)S(1)}, u32[]{:S(2)}, u32[]{:S(2)}) %collective-permute-start.24) | collective-permute-done | bytes 786464 | tf_op jit(solution)/shard_map/ppermute | solution.py:513
  214.3 3.4 %collective-permute-done.21 = bf16[64,1536]{1,0:T(8,128)(2,1)S(1)} collective-permute-done((bf16[64,1536]{1,0:T(8,128)(2,1)S(1)}, bf16[64,1536]{1,0:T(8,128)(2,1)S(1)}, u32[]{:S(2)}, u32[]{:S(2)}) %collective-permute-start.21) | collective-permute-done | bytes 196640 | tf_op jit(solution)/shard_map/ppermute | solution.py:513
  217.9 1.8 collective-permute-done.26
  219.7 6.4 %collective-permute-done.27 = bf16[64,1536]{1,0:T(8,128)(2,1)S(1)} collective-permute-done((bf16[64,1536]{1,0:T(8,128)(2,1)S(1)}, bf16[64,1536]{1,0:T(8,128)(2,1)S(1)}, u32[]{:S(2)}, u32[]{:S(2)}) %collective-permute-start.27) | collective-permute-done | bytes 196640 | tf_op jit(solution)/shard_map/ppermute | solution.py:513
  (90 shorter events, 32.3 us)
Async XLA Ops:
  15.2 22.4 %collective-permute-start.3 = (bf16[2,1536,1024]{2,1,0:T(8,128)(2,1)}, bf16[2,1536,1024]{2,1,0:T(8,128)(2,1)}, u32[]{:S(2)}, u32[]{:S(2)}) collective-permute-start(bf16[2,1536,1024]{2,1,0:T(8,128)(2,1)} %refs_7_.3), channel_id=1, source_target_pairs={{0,1},{1,0},{2,3},{3,2},{4,5},{5,4},{6,7},{7,6},{8,9},{9,8},{10,11... | collective-permute-start | bytes 18874376 | tf_op jit(solution)/shard_map/ppermute | solution.py:590
  15.5 22.0 %collective-permute-start.4 = (bf16[2,512,1536]{2,1,0:T(8,128)(2,1)}, bf16[2,512,1536]{2,1,0:T(8,128)(2,1)}, u32[]{:S(2)}, u32[]{:S(2)}) collective-permute-start(bf16[2,512,1536]{2,1,0:T(8,128)(2,1)} %refs_9_.3), channel_id=1, source_target_pairs={{0,1},{1,0},{2,3},{3,2},{4,5},{5,4},{6,7},{7,6},{8,9},{9,8},{10,11... | collective-permute-start | bytes 9437192 | tf_op jit(solution)/shard_map/ppermute | solution.py:590
  30.7 20.6 %collective-permute-start.5 = (bf16[80,1536]{1,0:T(8,128)(2,1)}, bf16[80,1536]{1,0:T(8,128)(2,1)S(1)}, u32[]{:S(2)}, u32[]{:S(2)}) collective-permute-start(bf16[80,1536]{1,0:T(8,128)(2,1)} %get-tuple-element.40.refs_0_), channel_id=1, source_target_pairs={{0,8},{1,9},{2,10},{3,11},{4,12},{5,13},{6,14},{7,15},{8,16},{9,17... | collective-permute-start | bytes 737288 | tf_op jit(solution)/shard_map/ppermute | solution.py:513
  33.7 19.2 %collective-permute-start.6 = (bf16[80,1536]{1,0:T(8,128)(2,1)}, bf16[80,1536]{1,0:T(8,128)(2,1)S(1)}, u32[]{:S(2)}, u32[]{:S(2)}) collective-permute-start(bf16[80,1536]{1,0:T(8,128)(2,1)} %get-tuple-element.40.refs_0_), channel_id=1, source_target_pairs={{0,16},{1,17},{2,18},{3,19},{4,20},{5,21},{6,22},{7,23},{8,24},{9,... | collective-permute-start | bytes 737288 | tf_op jit(solution)/shard_map/ppermute | solution.py:513
  36.2 16.6 %collective-permute-start.7 = (bf16[80,1536]{1,0:T(8,128)(2,1)}, bf16[80,1536]{1,0:T(8,128)(2,1)S(1)}, u32[]{:S(2)}, u32[]{:S(2)}) collective-permute-start(bf16[80,1536]{1,0:T(8,128)(2,1)} %get-tuple-element.40.refs_0_), channel_id=1, source_target_pairs={{0,24},{1,25},{2,26},{3,27},{4,28},{5,29},{6,30},{7,31},{8,0},{9,1... | collective-permute-start | bytes 737288 | tf_op jit(solution)/shard_map/ppermute | solution.py:513
  53.8 24.5 %collective-permute-start.12 = (bf16[4,80,1536]{2,1,0:T(8,128)(2,1)S(1)}, bf16[4,80,1536]{2,1,0:T(8,128)(2,1)S(1)}, u32[]{:S(2)}, u32[]{:S(2)}) collective-permute-start(bf16[4,80,1536]{2,1,0:T(8,128)(2,1)S(1)} %stack_rows.2.refs_0_), channel_id=1, source_target_pairs={{0,4},{1,3},{2,6},{3,1},{4,0},{5,7},{6,2},{7,5},{8,12},{9,11},{10,... | collective-permute-start | bytes 2949128 | tf_op jit(solution)/shard_map/ppermute | solution.py:513
  55.4 47.6 %collective-permute-start.11 = (bf16[4,80,1536]{2,1,0:T(8,128)(2,1)S(1)}, bf16[4,80,1536]{2,1,0:T(8,128)(2,1)S(1)}, u32[]{:S(2)}, u32[]{:S(2)}) collective-permute-start(bf16[4,80,1536]{2,1,0:T(8,128)(2,1)S(1)} %stack_rows.2.refs_0_), channel_id=1, source_target_pairs={{0,2},{1,5},{2,0},{3,7},{4,6},{5,1},{6,4},{7,3},{8,10},{9,13},{10,... | collective-permute-start | bytes 2949128 | tf_op jit(solution)/shard_map/ppermute | solution.py:513
  78.3 24.6 %collective-permute-start.13 = (bf16[4,80,1536]{2,1,0:T(8,128)(2,1)S(1)}, bf16[4,80,1536]{2,1,0:T(8,128)(2,1)S(1)}, u32[]{:S(2)}, u32[]{:S(2)}) collective-permute-start(bf16[4,80,1536]{2,1,0:T(8,128)(2,1)S(1)} %collective-permute-done.12.refs_1_.refs_2_), channel_id=1, source_target_pairs={{0,2},{1,5},{2,0},{3,7},{4,6},{5,1},{6,4},{7,3},{8,10},{9,13},{10,... | collective-permute-start | bytes 2949128 | tf_op jit(solution)/shard_map/ppermute | solution.py:513
  80.2 12.8 %collective-permute-start.10 = (bf16[64,1536]{1,0:T(8,128)(2,1)S(1)}, bf16[64,1536]{1,0:T(8,128)(2,1)S(1)}, u32[]{:S(2)}, u32[]{:S(2)}) collective-permute-start(bf16[64,1536]{1,0:T(8,128)(2,1)S(1)} %copy-done), channel_id=1, source_target_pairs={{0,24},{1,25},{2,26},{3,27},{4,28},{5,29},{6,30},{7,31},{8,0},{9,1... | collective-permute-start | bytes 589832 | tf_op jit(solution)/shard_map/ppermute | solution.py:513
  86.3 16.7 %collective-permute-start.9 = (bf16[64,1536]{1,0:T(8,128)(2,1)S(1)}, bf16[64,1536]{1,0:T(8,128)(2,1)S(1)}, u32[]{:S(2)}, u32[]{:S(2)}) collective-permute-start(bf16[64,1536]{1,0:T(8,128)(2,1)S(1)} %copy-done), channel_id=1, source_target_pairs={{0,16},{1,17},{2,18},{3,19},{4,20},{5,21},{6,22},{7,23},{8,24},{9,... | collective-permute-start | bytes 589832 | tf_op jit(solution)/shard_map/ppermute | solution.py:513
  104.8 20.0 %collective-permute-start.14 = (bf16[4,64,1536]{2,1,0:T(8,128)(2,1)}, bf16[4,64,1536]{2,1,0:T(8,128)(2,1)}, u32[]{:S(2)}, u32[]{:S(2)}) collective-permute-start(bf16[4,64,1536]{2,1,0:T(8,128)(2,1)} %stack_rows.3.refs_1_), channel_id=1, source_target_pairs={{0,4},{1,3},{2,6},{3,1},{4,0},{5,7},{6,2},{7,5},{8,12},{9,11},{10,... | collective-permute-start | bytes 2359304 | tf_op jit(solution)/shard_map/ppermute | solution.py:513
  107.5 33.5 %collective-permute-start.15 = (bf16[4,64,1536]{2,1,0:T(8,128)(2,1)}, bf16[4,64,1536]{2,1,0:T(8,128)(2,1)S(1)}, u32[]{:S(2)}, u32[]{:S(2)}) collective-permute-start(bf16[4,64,1536]{2,1,0:T(8,128)(2,1)} %stack_rows.3.refs_1_), channel_id=1, source_target_pairs={{0,2},{1,5},{2,0},{3,7},{4,6},{5,1},{6,4},{7,3},{8,10},{9,13},{10,... | collective-permute-start | bytes 2359304 | tf_op jit(solution)/shard_map/ppermute | solution.py:513
  124.8 16.2 %collective-permute-start.16 = (bf16[4,64,1536]{2,1,0:T(8,128)(2,1)}, bf16[4,64,1536]{2,1,0:T(8,128)(2,1)S(1)}, u32[]{:S(2)}, u32[]{:S(2)}) collective-permute-start(bf16[4,64,1536]{2,1,0:T(8,128)(2,1)} %collective-permute-done.14.refs_3_), channel_id=1, source_target_pairs={{0,2},{1,5},{2,0},{3,7},{4,6},{5,1},{6,4},{7,3},{8,10},{9,13},{10,... | collective-permute-start | bytes 2359304 | tf_op jit(solution)/shard_map/ppermute | solution.py:513
  153.6 12.1 %collective-permute-start.17 = (bf16[4,64,1536]{2,1,0:T(8,128)(2,1)S(1)}, bf16[4,64,1536]{2,1,0:T(8,128)(2,1)S(1)}, u32[]{:S(2)}, u32[]{:S(2)}) collective-permute-start(bf16[4,64,1536]{2,1,0:T(8,128)(2,1)S(1)} %get-tuple-element.50), channel_id=1, source_target_pairs={{0,2},{1,5},{2,0},{3,7},{4,6},{5,1},{6,4},{7,3},{8,10},{9,13},{10,... | collective-permute-start | bytes 2359304 | tf_op jit(solution)/shard_map/ppermute | solution.py:513
  153.7 25.4 %collective-permute-start.19 = (bf16[4,64,1536]{2,1,0:T(8,128)(2,1)S(1)}, bf16[4,64,1536]{2,1,0:T(8,128)(2,1)S(1)}, u32[]{:S(2)}, u32[]{:S(2)}) collective-permute-start(bf16[4,64,1536]{2,1,0:T(8,128)(2,1)S(1)} %get-tuple-element.51), channel_id=1, source_target_pairs={{0,2},{1,5},{2,0},{3,7},{4,6},{5,1},{6,4},{7,3},{8,10},{9,13},{10,... | collective-permute-start | bytes 2359304 | tf_op jit(solution)/shard_map/ppermute | solution.py:513
  179.1 20.3 %collective-permute-start.23 = (bf16[4,64,1536]{2,1,0:T(8,128)(2,1)S(1)}, bf16[4,64,1536]{2,1,0:T(8,128)(2,1)S(1)}, u32[]{:S(2)}, u32[]{:S(2)}) collective-permute-start(bf16[4,64,1536]{2,1,0:T(8,128)(2,1)S(1)} %get-tuple-element.55), channel_id=1, source_target_pairs={{0,2},{1,5},{2,0},{3,7},{4,6},{5,1},{6,4},{7,3},{8,10},{9,13},{10,... | collective-permute-start | bytes 2359304 | tf_op jit(solution)/shard_map/ppermute | solution.py:513
  179.3 20.4 %collective-permute-start.18 = (bf16[4,64,1536]{2,1,0:T(8,128)(2,1)S(1)}, bf16[4,64,1536]{2,1,0:T(8,128)(2,1)S(1)}, u32[]{:S(2)}, u32[]{:S(2)}) collective-permute-start(bf16[4,64,1536]{2,1,0:T(8,128)(2,1)S(1)} %add_convert_fusion.1), channel_id=1, source_target_pairs={{0,4},{1,3},{2,6},{3,1},{4,0},{5,7},{6,2},{7,5},{8,12},{9,11},{10,... | collective-permute-start | bytes 2359304 | tf_op jit(solution)/shard_map/ppermute | solution.py:513
  179.4 28.5 %collective-permute-start.25 = (bf16[4,64,1536]{2,1,0:T(8,128)(2,1)S(1)}, bf16[4,64,1536]{2,1,0:T(8,128)(2,1)S(1)}, u32[]{:S(2)}, u32[]{:S(2)}) collective-permute-start(bf16[4,64,1536]{2,1,0:T(8,128)(2,1)S(1)} %get-tuple-element.57), channel_id=1, source_target_pairs={{0,2},{1,5},{2,0},{3,7},{4,6},{5,1},{6,4},{7,3},{8,10},{9,13},{10,... | collective-permute-start | bytes 2359304 | tf_op jit(solution)/shard_map/ppermute | solution.py:513
  199.6 12.1 %collective-permute-start.24 = (bf16[4,64,1536]{2,1,0:T(8,128)(2,1)S(1)}, bf16[4,64,1536]{2,1,0:T(8,128)(2,1)S(1)}, u32[]{:S(2)}, u32[]{:S(2)}) collective-permute-start(bf16[4,64,1536]{2,1,0:T(8,128)(2,1)S(1)} %add_convert_fusion), channel_id=1, source_target_pairs={{0,4},{1,3},{2,6},{3,1},{4,0},{5,7},{6,2},{7,5},{8,12},{9,11},{10,... | collective-permute-start | bytes 2359304 | tf_op jit(solution)/shard_map/ppermute | solution.py:513
  199.9 13.7 %collective-permute-start.20 = (bf16[64,1536]{1,0:T(8,128)(2,1)S(1)}, bf16[64,1536]{1,0:T(8,128)(2,1)S(1)}, u32[]{:S(2)}, u32[]{:S(2)}) collective-permute-start(bf16[64,1536]{1,0:T(8,128)(2,1)S(1)} %get-tuple-element.58), channel_id=1, source_target_pairs={{0,24},{1,25},{2,26},{3,27},{4,28},{5,29},{6,30},{7,31},{8,0},{9,1... | collective-permute-start | bytes 589832 | tf_op jit(solution)/shard_map/ppermute | solution.py:513
  201.7 16.0 %collective-permute-start.21 = (bf16[64,1536]{1,0:T(8,128)(2,1)S(1)}, bf16[64,1536]{1,0:T(8,128)(2,1)S(1)}, u32[]{:S(2)}, u32[]{:S(2)}) collective-permute-start(bf16[64,1536]{1,0:T(8,128)(2,1)S(1)} %get-tuple-element.60), channel_id=1, source_target_pairs={{0,16},{1,17},{2,18},{3,19},{4,20},{5,21},{6,22},{7,23},{8,24},{9,... | collective-permute-start | bytes 589832 | tf_op jit(solution)/shard_map/ppermute | solution.py:513
  201.7 16.0 %collective-permute-start.22 = (bf16[64,1536]{1,0:T(8,128)(2,1)S(1)}, bf16[64,1536]{1,0:T(8,128)(2,1)S(1)}, u32[]{:S(2)}, u32[]{:S(2)}) collective-permute-start(bf16[64,1536]{1,0:T(8,128)(2,1)S(1)} %get-tuple-element.59), channel_id=1, source_target_pairs={{0,8},{1,9},{2,10},{3,11},{4,12},{5,13},{6,14},{7,15},{8,16},{9,17... | collective-permute-start | bytes 589832 | tf_op jit(solution)/shard_map/ppermute | solution.py:513
  213.6 12.4 %collective-permute-start.27 = (bf16[64,1536]{1,0:T(8,128)(2,1)S(1)}, bf16[64,1536]{1,0:T(8,128)(2,1)S(1)}, u32[]{:S(2)}, u32[]{:S(2)}) collective-permute-start(bf16[64,1536]{1,0:T(8,128)(2,1)S(1)} %get-tuple-element.63), channel_id=1, source_target_pairs={{0,16},{1,17},{2,18},{3,19},{4,20},{5,21},{6,22},{7,23},{8,24},{9,... | collective-permute-start | bytes 589832 | tf_op jit(solution)/shard_map/ppermute | solution.py:513
  213.6 12.4 %collective-permute-start.28 = (bf16[64,1536]{1,0:T(8,128)(2,1)S(1)}, bf16[64,1536]{1,0:T(8,128)(2,1)S(1)}, u32[]{:S(2)}, u32[]{:S(2)}) collective-permute-start(bf16[64,1536]{1,0:T(8,128)(2,1)S(1)} %get-tuple-element.62), channel_id=1, source_target_pairs={{0,8},{1,9},{2,10},{3,11},{4,12},{5,13},{6,14},{7,15},{8,16},{9,17... | collective-permute-start | bytes 589832 | tf_op jit(solution)/shard_map/ppermute | solution.py:513
  (17 other events, 109.0 us)

commit v6 on v5

--- a/solution.py
+++ b/solution.py
@@ -200,11 +200,10 @@
         stream_ref[...] = stream
         wide = stream.astype(jnp.float32)
         mean_square = jnp.mean(wide * wide, axis=-1, keepdims=True)
-        expert_in_ref[:rows] = (
-            wide * lax.rsqrt(mean_square + epsilon) * gain_ref[...][None, :]
-        ).astype(jnp.bfloat16)
-        if riders:
-            expert_in_ref[rows:] = refs[0][...]
+        sent = (wide * lax.rsqrt(mean_square + epsilon) * gain_ref[...][None, :]).astype(
+            jnp.bfloat16
+        )
+        expert_in_ref[...] = jnp.concatenate([sent, *[r[...] for r in refs[:riders]]], axis=0)
 
 
 def attend(place, queries, caches, spans, w_out, tokens, gain, first_row, rows, riders, filled, after):
@@ -297,7 +296,7 @@
     place = lax.broadcasted_iota(jnp.int32, (capacity, tokens), 0).astype(jnp.float32)
     hot_rows, share_lines = [], []
     for source in range(sources):
-        packed = refs[source // deep][source % deep, first:].astype(jnp.float32)
+        packed = refs[source // deep][source % deep][first:].astype(jnp.float32)
         across = packed.shape[1] // tokens
         lines = [
             packed[i // across : i // across + 1, i % across * tokens : (i % across + 1) * tokens]
@@ -347,13 +346,13 @@
     )(slot_ids, *pieces)
 
 
-def expert_kernel(pieces, in_cuts, out_cuts, extra, *refs):
+def expert_kernel(pieces, in_cuts, extra, *refs):
     halves = len(in_cuts)
     row_refs = refs[: pieces * halves]
-    rest = refs[pieces * halves :]
-    pick_ref, back_ref, share_ref, up_ref, up_other_ref, down_ref, down_other_ref = rest[:7]
-    out_refs = rest[7 + extra : 7 + extra + pieces * len(out_cuts)]
-    held = rest[-1]
+    pick_ref, share_ref, up_ref, up_other_ref, down_ref, down_other_ref = refs[
+        pieces * halves : pieces * halves + 6
+    ]
+    out_ref, held = refs[-2:]
     step = pl.program_id(0)
     slots = held.shape[0]
     own_slots = slots // 2
@@ -386,7 +385,7 @@
         active = (
             jax.nn.silu(gate_up[:, :hidden]) * gate_up[:, hidden:] * share_ref[step]
         ).astype(jnp.bfloat16)
-        held[step] = jnp.dot(active, down[0], preferred_element_type=jnp.float32).astype(
+        out_ref[step] = jnp.dot(active, down[0], preferred_element_type=jnp.float32).astype(
             jnp.bfloat16
         )
 
@@ -398,31 +397,14 @@
     def _():
         run(up_other_ref, down_other_ref)
 
-    @pl.when(step == slots - 1)
-    def _():
-        for source in range(sources):
-            rows = jnp.concatenate(
-                [
-                    held[slot, source * capacity : (source + 1) * capacity]
-                    for slot in range(slots)
-                ],
-                axis=0,
-            )
-            mixed = jnp.dot(back_ref[source], rows, preferred_element_type=jnp.float32)
-            start = 0
-            for index, count in enumerate(out_cuts):
-                ref = out_refs[source // deep * len(out_cuts) + index]
-                ref[source % deep] = mixed[start : start + count].astype(jnp.bfloat16)
-                start += count
-
-
-def run_experts(rows, plan, ups, downs, in_cuts, out_cuts, after):
+
+def run_experts(rows, pick, share, ups, downs, in_cuts, after):
     pieces, halves = len(rows), len(rows[0])
-    deep, _, width = rows[0][0].shape
+    width = rows[0][0].shape[2]
     own_slots, _, double = ups[0].shape
     hidden = double // 2
     slots = 2 * own_slots
-    places = plan[2].shape[1]
+    places = share.shape[1]
 
     def own(j):
         return (jnp.minimum(j, own_slots - 1), 0, 0)
@@ -430,10 +412,10 @@
     def other(j):
         return (jnp.maximum(j - own_slots, 0), 0, 0)
 
-    flat = pl.pallas_call(
-        functools.partial(expert_kernel, pieces, tuple(in_cuts), tuple(out_cuts), len(after)),
+    return pl.pallas_call(
+        functools.partial(expert_kernel, pieces, tuple(in_cuts), len(after)),
         grid=(slots,),
-        in_specs=[vmem_spec()] * (pieces * halves + 3)
+        in_specs=[vmem_spec()] * (pieces * halves + 2)
         + [
             pl.BlockSpec((1, width, double), own),
             pl.BlockSpec((1, width, double), other),
@@ -441,9 +423,8 @@
             pl.BlockSpec((1, hidden, width), other),
         ]
         + [pl.BlockSpec(memory_space=pl.ANY)] * len(after),
-        out_specs=[vmem_spec()] * (pieces * len(out_cuts)),
-        out_shape=[jax.ShapeDtypeStruct((deep, c, width), jnp.bfloat16) for c in out_cuts]
-        * pieces,
+        out_specs=vmem_spec(),
+        out_shape=jax.ShapeDtypeStruct((slots, places, width), jnp.bfloat16),
         scratch_shapes=[pltpu.VMEM((slots, places, width), jnp.bfloat16)],
         compiler_params=params(44),
         cost_estimate=pl.CostEstimate(
@@ -452,7 +433,47 @@
             transcendentals=slots * places * hidden,
         ),
         name="run_experts",
-    )(*[r for piece in rows for r in piece], *plan, ups[0], ups[1], downs[0], downs[1], *after)
+    )(*[r for piece in rows for r in piece], pick, share, ups[0], ups[1], downs[0], downs[1], *after)
+
+
+def mix_kernel(pieces, out_cuts, held_ref, back_ref, *refs):
+    count = len(out_cuts)
+    out_refs = refs[-pieces * count :]
+    slots, places, _ = held_ref.shape
+    sources = back_ref.shape[0]
+    deep = sources // pieces
+    capacity = places // sources
+    for source in range(sources):
+        rows = jnp.concatenate(
+            [
+                held_ref[slot, source * capacity : (source + 1) * capacity]
+                for slot in range(slots)
+            ],
+            axis=0,
+        )
+        mixed = jnp.dot(back_ref[source], rows, preferred_element_type=jnp.float32)
+        start = 0
+        for index, cut in enumerate(out_cuts):
+            ref = out_refs[source // deep * count + index]
+            ref[source % deep] = mixed[start : start + cut].astype(jnp.bfloat16)
+            start += cut
+
+
+def mix_rows(held, back, pieces, out_cuts, after):
+    width = held.shape[2]
+    deep = back.shape[0] // pieces
+    flat = pl.pallas_call(
+        functools.partial(mix_kernel, pieces, tuple(out_cuts)),
+        in_specs=[vmem_spec()] * 2 + [pl.BlockSpec(memory_space=pl.ANY)] * len(after),
+        out_specs=[vmem_spec()] * (pieces * len(out_cuts)),
+        out_shape=[jax.ShapeDtypeStruct((deep, c, width), jnp.bfloat16) for c in out_cuts]
+        * pieces,
+        compiler_params=params(24),
+        cost_estimate=pl.CostEstimate(
+            flops=2_000_000_000, bytes_accessed=6_000_000, transcendentals=0
+        ),
+        name="mix_rows",
+    )(held, back, *after)
     count = len(out_cuts)
     return [flat[i * count : (i + 1) * count] for i in range(pieces)]
 
@@ -519,9 +540,14 @@
     return [value] + [shift(value, "z", k) for k in range(1, sizes["z"])]
 
 
-def gather_planes(line, shift, sizes):
+def gather_planes(line, shift, sizes, before):
     plane = [line] + [shift(line, "a", j) for j in range(1, sizes["a"])]
-    return [plane] + [[shift(v, "b", k) for v in plane] for k in range(1, sizes["b"])]
+    forwarded = plane[1:]
+    if before:
+        forwarded, _ = lax.optimization_barrier((forwarded, before))
+    return [plane] + [
+        [shift(v, "b", k) for v in [line, *forwarded]] for k in range(1, sizes["b"])
+    ]
 
 
 def add_all(terms):
@@ -531,19 +557,18 @@
     return total.astype(terms[0].dtype)
 
 
-def scatter_chunks(chunks, shift, sizes):
-    tall = sizes["a"]
+def leave_along_a(plane, shift):
+    return [plane[0]] + [shift(v, "a", -j) for j, v in enumerate(plane) if j]
+
+
+def scatter_chunks(own, others, shift, sizes):
     sums, before = [], []
-    for planes in chunks:
-        sending = planes[1:]
+    for line, sending in zip(own, others):
         if before:
             sending, _ = lax.optimization_barrier((sending, before))
-        arrived = {}
-        for j in range(tall - 1, -1, -1):
-            arrived[j] = [shift(plane[j], "b", -k - 1) for k, plane in enumerate(sending)]
-        before = [v for moved in arrived.values() for v in moved]
-        arrived = [[planes[0][j]] + arrived[j] for j in range(tall)]
-        line = [shift(add_all(arrived[j]), "a", -j) for j in range(1, tall)] + arrived[0]
+        terms = [leave_along_a(plane, shift) for plane in sending]
+        before = [v for moved in terms for v in moved[1:]]
+        line = line + [shift(add_all(t), "b", -k - 1) for k, t in enumerate(terms)]
         moved = [
             shift(add_all([t[i] for t in line]), "z", -i) for i in range(1, sizes["z"])
         ]
@@ -599,7 +624,7 @@
     coarse = lax.reduce_precision(shares, 8, 7)
     table = jnp.concatenate([slot_of.astype(jnp.float32), coarse, shares - coarse], axis=1)
     table = table.astype(jnp.bfloat16).T.reshape(-1, tokens.shape[1])
-    table = jnp.pad(table, ((0, 16 - table.shape[0]), (0, 0)))
+    table = jnp.pad(table, ((0, -table.shape[0] % 8), (0, 0)))
     chip = lax.axis_index("req")
     chip_slots = jnp.arange(slots_dev, dtype=jnp.int32)
     slot_ids = jnp.concatenate(
@@ -641,29 +666,33 @@
         )
         filled = [attended, stream]
         lines.append(gather_line(expert_in, shift, sizes))
-    halves, after = [], [expert_in]
-    for line in lines:
-        planes = gather_planes(stack_rows(line, after), shift, sizes)
-        halves.append(planes)
-        after = [v for plane in planes[1:] for v in plane]
-    cut = row_count // 2
-    results = []
+    first, second = lines
+    planes = gather_planes(stack_rows(first, [expert_in]), shift, sizes, second[1:])
+    stacked = stack_rows(second, [plane[0] for plane in planes[1:]])
+    halves = [planes, gather_planes(stacked, shift, sizes, [])]
+    cuts = (row_count // 2, row_count - row_count // 2)
+    own, others, held = [], [], None
     for index in range(sizes["b"]):
-        plan = plan_routes(slot_ids, halves[0][index], half, row_count, capacity, top_count)
-        results.append(
-            run_experts(
-                [[planes[index][j] for planes in halves] for j in range(sizes["a"])],
-                plan,
-                (expert_up, up_other),
-                (expert_down, down_other),
-                (half, row_count - half),
-                (cut, row_count - cut),
-                results[-1][0][:1] if results else [],
-            )
-        )
-    expert_mix = scatter_chunks(
-        [[[piece[i] for piece in r] for r in results] for i in range(2)], shift, sizes
-    )
+        pick, back, share = plan_routes(
+            slot_ids, halves[0][index], half, row_count, capacity, top_count
+        )
+        held = run_experts(
+            [[planes[index][j] for planes in halves] for j in range(sizes["a"])],
+            pick,
+            share,
+            (expert_up, up_other),
+            (expert_down, down_other),
+            (half, row_count - half),
+            [] if index == 0 else [held],
+        )
+        mixed = mix_rows(held, back, sizes["a"], cuts, [v for line in own for v in line[1:]])
+        chunks = [[piece[i] for piece in mixed] for i in range(len(cuts))]
+        if index == 0:
+            own = [leave_along_a(plane, shift) for plane in chunks]
+        else:
+            others.append(chunks)
+    others = [[planes[i] for planes in others] for i in range(len(cuts))]
+    expert_mix = scatter_chunks(own, others, shift, sizes)
     return (attended, stream, expert_mix, appended)
 
 

time: 227 us -> 200 us (0.88)
  waiting for transfers between devices: 118 us -> 89.9 us
  starting transfers between devices: 32.8 us -> 38.6 us
  local copies, waits for them, and re-layouts: 6.73 us -> 3.23 us
    ppermute x24, waiting for transfers between devices: 117 us -> 88.6 us  [shift(): return lax.ppermute(value, BOTH, pairs(role, offset % sizes[role]))]
    ppermute x24, starting transfers between devices: 31.3 us -> 37.1 us  [shift(): return lax.ppermute(value, BOTH, pairs(role, offset % sizes[role]))]
    unnamed x24 -> x18, local copies, waits for them, and re-layouts: 6.09 us -> 2.61 us
    pallas_call x2 -> x4, Pallas kernels: 25.6 us -> 24.3 us  [the longest x2 22.4 us: run_experts(): pl.pallas_call(functools.partial(expert_kernel, pieces, tuple(in_cuts), l...]
  transfers between devices with their start and end apart: 29 -> 29, of which waited for: 15 -> 13; matrix products, arithmetic and copies ran while one was open for 2% -> 3% of each run, Pallas kernels for 19% -> 26%
where the time goes in v6:
time: 200 us
  waiting for transfers between devices  89.9 us (45%)
  Pallas kernels  61.2 us (31%)
  starting transfers between devices  38.6 us (19%)
  other arithmetic  5.61 us (3%)
  local copies, waits for them, and re-layouts  3.23 us (2%)
    ppermute x24, waiting for transfers between devices, shift(): return lax.ppermute(value, BOTH, pairs(role, offset % sizes[role]))  88.6 us
    ppermute x24, starting transfers between devices, shift(): return lax.ppermute(value, BOTH, pairs(role, offset % sizes[role]))  37.1 us
    pallas_call x2, Pallas kernels, attend(): pl.pallas_call(functools.partial(attend_kernel, first_row, len(riders), l...  27.2 us
    pallas_call x2, Pallas kernels, run_experts(): pl.pallas_call(functools.partial(expert_kernel, pieces, tuple(in_cuts), l...  22.4 us
    pallas_call x1, Pallas kernels, project(): pl.pallas_call(qkv_kernel, grid=(5,), in_specs=[vmem_spec()] * 5 + [pl.Bl...  7.38 us
  transfers between devices with their start and end apart: 29, of which 13 were waited for; matrix products, arithmetic and copies ran while one was open for 3% of the time, Pallas kernels for 26%

profile of v6, /device:TPU:0, one launch (start us, length us, event | category | flops | bytes accessed | tf_op | source)
XLA Modules:
  0.0 200.0 jit_solution(14263809376666411550)
XLA Ops:
  5.8 7.4 %project_rows.1 = (bf16[128,1536]{1,0:T(8,128)(2,1)}, bf16[128,1024]{1,0:T(8,128)(2,1)}, bf16[128,1024]{1,0:T(8,128)(2,1)}) custom-call(bf16[128,1536]{1,0:T(8,128)(2,1)} %tokens_ref.3, bf16[128,1536]{1,0:T(8,128)(2,1)} %copy-done.6, f32[1536]{0:T(1024)} %gain_ref.3, f32[256,128]{1,0:T(8,128)} %pad_maximum_fusion.1.cos_ref, ...), custom_call_target="tpu_custom_call" | custom-call | flops 1409286144 | bytes 9500000 | tf_op jit(solution)/shard_map/project_rows/pallas_call | solution.py:84
  15.8 13.6 %attend_rows.2 = (bf16[128,1536]{1,0:T(8,128)(2,1)}, bf16[128,1536]{1,0:T(8,128)(2,1)}, bf16[72,1536]{1,0:T(8,128)(2,1)}) custom-call(s32[2]{0:T(128)} %pad_add_fusion.place_ref, bf16[128,1536]{1,0:T(8,128)(2,1)} %get-tuple-element.32.q_ref, bf16[1,1024,512]{2,1,0:T(8,128)(2,1)} %kc_ref.3, bf16[1,1024,512]{2,1,0:T(8,128)(2,1)} %collective-permute-done.1.refs_0_.kco_ref, ...), custom_call_target="tpu_custom_call" | custom-call | flops 7247757312 | bytes 10000000 | tf_op jit(solution)/shard_map/attend_rows/pallas_call | solution.py:222
  29.4 5.1 %collective-permute-start.7 = (bf16[72,1536]{1,0:T(8,128)(2,1)}, bf16[72,1536]{1,0:T(8,128)(2,1)S(1)}, u32[]{:S(2)}, u32[]{:S(2)}) collective-permute-start(bf16[72,1536]{1,0:T(8,128)(2,1)} %get-tuple-element.41.refs_0_), channel_id=1, source_target_pairs={{0,24},{1,25},{2,26},{3,27},{4,28},{5,29},{6,30},{7,31},{8,0},{9,1... | collective-permute-start | bytes 663560 | tf_op jit(solution)/shard_map/ppermute | solution.py:534
  35.5 13.6 %attend_rows.3 = (bf16[128,1536]{1,0:T(8,128)(2,1)}, bf16[128,1536]{1,0:T(8,128)(2,1)}, bf16[64,1536]{1,0:T(8,128)(2,1)}) custom-call(s32[2]{0:T(128)} %pad_add_fusion.place_ref, bf16[128,1536]{1,0:T(8,128)(2,1)} %get-tuple-element.32.q_ref, bf16[1,1024,512]{2,1,0:T(8,128)(2,1)} %kc_ref.3, ...), custom_call_target="tpu_custom_call", output_to_operand_aliasing={{0}: (13, {}), {1}: (14, {})} | custom-call | flops 7247757312 | bytes 10000000 | tf_op jit(solution)/shard_map/attend_rows/pallas_call | solution.py:222
  49.1 4.6 %collective-permute-done.6.refs_2_ = bf16[72,1536]{1,0:T(8,128)(2,1)S(1)} collective-permute-done((bf16[72,1536]{1,0:T(8,128)(2,1)}, bf16[72,1536]{1,0:T(8,128)(2,1)S(1)}, u32[]{:S(2)}, u32[]{:S(2)}) %collective-permute-start.6) | collective-permute-done | bytes 221216 | tf_op jit(solution)/shard_map/ppermute | solution.py:534
  54.7 1.6 collective-permute-start.11
  56.3 2.8 %collective-permute-start.9 = (bf16[64,1536]{1,0:T(8,128)(2,1)S(1)}, bf16[64,1536]{1,0:T(8,128)(2,1)S(1)}, u32[]{:S(2)}, u32[]{:S(2)}) collective-permute-start(bf16[64,1536]{1,0:T(8,128)(2,1)S(1)} %copy-done), channel_id=1, source_target_pairs={{0,16},{1,17},{2,18},{3,19},{4,20},{5,21},{6,22},{7,23},{8,24},{9,... | collective-permute-start | bytes 589832 | tf_op jit(solution)/shard_map/ppermute | solution.py:534
  59.1 2.0 %collective-permute-start.8 = (bf16[64,1536]{1,0:T(8,128)(2,1)S(1)}, bf16[64,1536]{1,0:T(8,128)(2,1)S(1)}, u32[]{:S(2)}, u32[]{:S(2)}) collective-permute-start(bf16[64,1536]{1,0:T(8,128)(2,1)S(1)} %copy-done), channel_id=1, source_target_pairs={{0,8},{1,9},{2,10},{3,11},{4,12},{5,13},{6,14},{7,15},{8,16},{9,17... | collective-permute-start | bytes 589832 | tf_op jit(solution)/shard_map/ppermute | solution.py:534
  62.6 13.2 %collective-permute-done.9.refs_2_ = bf16[64,1536]{1,0:T(8,128)(2,1)S(1)} collective-permute-done((bf16[64,1536]{1,0:T(8,128)(2,1)S(1)}, bf16[64,1536]{1,0:T(8,128)(2,1)S(1)}, u32[]{:S(2)}, u32[]{:S(2)}) %collective-permute-start.9) | collective-permute-done | bytes 196640 | tf_op jit(solution)/shard_map/ppermute | solution.py:534
  80.5 16.8 %collective-permute-done.13.refs_3_ = bf16[4,64,1536]{2,1,0:T(8,128)(2,1)} collective-permute-done((bf16[4,64,1536]{2,1,0:T(8,128)(2,1)S(1)}, bf16[4,64,1536]{2,1,0:T(8,128)(2,1)}, u32[]{:S(2)}, u32[]{:S(2)}) %collective-permute-start.13) | collective-permute-done | bytes 786464 | tf_op jit(solution)/shard_map/ppermute | solution.py:534
  98.9 11.3 %run_experts.2.held_ref.refs_10_ = bf16[4,256,1536]{2,1,0:T(8,128)(2,1)S(1)} custom-call(bf16[4,72,1536]{2,1,0:T(8,128)(2,1)S(1)} %stack_rows.2.refs_0_, bf16[4,64,1536]{2,1,0:T(8,128)(2,1)S(1)} %stack_rows.3.refs_1_, bf16[4,72,1536]{2,1,0:T(8,128)(2,1)S(1)} %collective-permute-done.12.refs_1_.refs_2_, bf16[4,64,1536]{2,1,0:T(8,128)(2,1)} %collective-permute-done.13.refs_3_, ...), custom_call_target="tpu_custom_call" | custom-call | flops 8053063680 | bytes 26000000 | tf_op jit(solution)/shard_map/run_experts/pallas_call | solution.py:415
  115.1 2.5 %collective-permute-done.17.refs_3_ = bf16[4,64,1536]{2,1,0:T(8,128)(2,1)S(1)} collective-permute-done((bf16[4,64,1536]{2,1,0:T(8,128)(2,1)}, bf16[4,64,1536]{2,1,0:T(8,128)(2,1)S(1)}, u32[]{:S(2)}, u32[]{:S(2)}) %collective-permute-start.17) | collective-permute-done | bytes 786464 | tf_op jit(solution)/shard_map/ppermute | solution.py:534
  117.6 11.1 %run_experts.3.held_ref = bf16[4,256,1536]{2,1,0:T(8,128)(2,1)S(1)} custom-call(bf16[4,72,1536]{2,1,0:T(8,128)(2,1)S(1)} %collective-permute-done.11.refs_4_.refs_0_, bf16[4,64,1536]{2,1,0:T(8,128)(2,1)S(1)} %collective-permute-done.15.refs_1_, bf16[4,72,1536]{2,1,0:T(8,128)(2,1)S(1)} %collective-permute-done.16.refs_1_.refs_2_, ...), custom_call_target="tpu_custom_call" | custom-call | flops 8053063680 | bytes 26000000 | tf_op jit(solution)/shard_map/run_experts/pallas_call | solution.py:415
  128.7 3.6 %collective-permute-done.18.refs_1_ = bf16[4,64,1536]{2,1,0:T(8,128)(2,1)S(1)} collective-permute-done((bf16[4,64,1536]{2,1,0:T(8,128)(2,1)S(1)}, bf16[4,64,1536]{2,1,0:T(8,128)(2,1)S(1)}, u32[]{:S(2)}, u32[]{:S(2)}) %collective-permute-start.18) | collective-permute-done | bytes 786464 | tf_op jit(solution)/shard_map/ppermute | solution.py:534
  133.9 11.5 %collective-permute-done.19 = bf16[4,64,1536]{2,1,0:T(8,128)(2,1)S(1)} collective-permute-done((bf16[4,64,1536]{2,1,0:T(8,128)(2,1)S(1)}, bf16[4,64,1536]{2,1,0:T(8,128)(2,1)S(1)}, u32[]{:S(2)}, u32[]{:S(2)}) %collective-permute-start.19) | collective-permute-done | bytes 786464 | tf_op jit(solution)/shard_map/ppermute | solution.py:534
  146.5 19.3 %collective-permute-done.24 = bf16[4,64,1536]{2,1,0:T(8,128)(2,1)S(1)} collective-permute-done((bf16[4,64,1536]{2,1,0:T(8,128)(2,1)S(1)}, bf16[4,64,1536]{2,1,0:T(8,128)(2,1)S(1)}, u32[]{:S(2)}, u32[]{:S(2)}) %collective-permute-start.24) | collective-permute-done | bytes 786464 | tf_op jit(solution)/shard_map/ppermute | solution.py:534
  166.4 2.0 %collective-permute-start.23 = (bf16[64,1536]{1,0:T(8,128)(2,1)S(1)}, bf16[64,1536]{1,0:T(8,128)(2,1)S(1)}, u32[]{:S(2)}, u32[]{:S(2)}) collective-permute-start(bf16[64,1536]{1,0:T(8,128)(2,1)S(1)} %get-tuple-element.61), channel_id=1, source_target_pairs={{0,8},{1,9},{2,10},{3,11},{4,12},{5,13},{6,14},{7,15},{8,16},{9,17... | collective-permute-start | bytes 589832 | tf_op jit(solution)/shard_map/ppermute | solution.py:534
  168.5 5.9 %collective-permute-start.22 = (bf16[64,1536]{1,0:T(8,128)(2,1)S(1)}, bf16[64,1536]{1,0:T(8,128)(2,1)S(1)}, u32[]{:S(2)}, u32[]{:S(2)}) collective-permute-start(bf16[64,1536]{1,0:T(8,128)(2,1)S(1)} %get-tuple-element.62), channel_id=1, source_target_pairs={{0,16},{1,17},{2,18},{3,19},{4,20},{5,21},{6,22},{7,23},{8,24},{9,... | collective-permute-start | bytes 589832 | tf_op jit(solution)/shard_map/ppermute | solution.py:534
  174.3 3.8 %collective-permute-done.25 = bf16[4,64,1536]{2,1,0:T(8,128)(2,1)S(1)} collective-permute-done((bf16[4,64,1536]{2,1,0:T(8,128)(2,1)S(1)}, bf16[4,64,1536]{2,1,0:T(8,128)(2,1)S(1)}, u32[]{:S(2)}, u32[]{:S(2)}) %collective-permute-start.25) | collective-permute-done | bytes 786464 | tf_op jit(solution)/shard_map/ppermute | solution.py:534
  178.4 2.0 %collective-permute-start.28 = (bf16[64,1536]{1,0:T(8,128)(2,1)S(1)}, bf16[64,1536]{1,0:T(8,128)(2,1)S(1)}, u32[]{:S(2)}, u32[]{:S(2)}) collective-permute-start(bf16[64,1536]{1,0:T(8,128)(2,1)S(1)} %get-tuple-element.64), channel_id=1, source_target_pairs={{0,8},{1,9},{2,10},{3,11},{4,12},{5,13},{6,14},{7,15},{8,16},{9,17... | collective-permute-start | bytes 589832 | tf_op jit(solution)/shard_map/ppermute | solution.py:534
  180.4 5.4 %collective-permute-start.27 = (bf16[64,1536]{1,0:T(8,128)(2,1)S(1)}, bf16[64,1536]{1,0:T(8,128)(2,1)S(1)}, u32[]{:S(2)}, u32[]{:S(2)}) collective-permute-start(bf16[64,1536]{1,0:T(8,128)(2,1)S(1)} %get-tuple-element.65), channel_id=1, source_target_pairs={{0,16},{1,17},{2,18},{3,19},{4,20},{5,21},{6,22},{7,23},{8,24},{9,... | collective-permute-start | bytes 589832 | tf_op jit(solution)/shard_map/ppermute | solution.py:534
  185.8 3.1 %collective-permute-done.22 = bf16[64,1536]{1,0:T(8,128)(2,1)S(1)} collective-permute-done((bf16[64,1536]{1,0:T(8,128)(2,1)S(1)}, bf16[64,1536]{1,0:T(8,128)(2,1)S(1)}, u32[]{:S(2)}, u32[]{:S(2)}) %collective-permute-start.22) | collective-permute-done | bytes 196640 | tf_op jit(solution)/shard_map/ppermute | solution.py:534
  189.1 3.2 %collective-permute-done.28 = bf16[64,1536]{1,0:T(8,128)(2,1)S(1)} collective-permute-done((bf16[64,1536]{1,0:T(8,128)(2,1)S(1)}, bf16[64,1536]{1,0:T(8,128)(2,1)S(1)}, u32[]{:S(2)}, u32[]{:S(2)}) %collective-permute-start.28) | collective-permute-done | bytes 196640 | tf_op jit(solution)/shard_map/ppermute | solution.py:534
  192.3 6.8 %collective-permute-done.27 = bf16[64,1536]{1,0:T(8,128)(2,1)S(1)} collective-permute-done((bf16[64,1536]{1,0:T(8,128)(2,1)S(1)}, bf16[64,1536]{1,0:T(8,128)(2,1)S(1)}, u32[]{:S(2)}, u32[]{:S(2)}) %collective-permute-start.27) | collective-permute-done | bytes 196640 | tf_op jit(solution)/shard_map/ppermute | solution.py:534
  (86 shorter events, 26.3 us)
Async XLA Ops:
  13.2 22.3 %collective-permute-start.3 = (bf16[2,1536,1024]{2,1,0:T(8,128)(2,1)}, bf16[2,1536,1024]{2,1,0:T(8,128)(2,1)}, u32[]{:S(2)}, u32[]{:S(2)}) collective-permute-start(bf16[2,1536,1024]{2,1,0:T(8,128)(2,1)} %refs_6_.3), channel_id=1, source_target_pairs={{0,1},{1,0},{2,3},{3,2},{4,5},{5,4},{6,7},{7,6},{8,9},{9,8},{10,11... | collective-permute-start | bytes 18874376 | tf_op jit(solution)/shard_map/ppermute | solution.py:615
  13.6 21.9 %collective-permute-start.4 = (bf16[2,512,1536]{2,1,0:T(8,128)(2,1)S(1)}, bf16[2,512,1536]{2,1,0:T(8,128)(2,1)}, u32[]{:S(2)}, u32[]{:S(2)}) collective-permute-start(bf16[2,512,1536]{2,1,0:T(8,128)(2,1)S(1)} %copy-done.3), channel_id=1, source_target_pairs={{0,1},{1,0},{2,3},{3,2},{4,5},{5,4},{6,7},{7,6},{8,9},{9,8},{10,11... | collective-permute-start | bytes 9437192 | tf_op jit(solution)/shard_map/ppermute | solution.py:615
  29.4 19.7 %collective-permute-start.7 = (bf16[72,1536]{1,0:T(8,128)(2,1)}, bf16[72,1536]{1,0:T(8,128)(2,1)S(1)}, u32[]{:S(2)}, u32[]{:S(2)}) collective-permute-start(bf16[72,1536]{1,0:T(8,128)(2,1)} %get-tuple-element.41.refs_0_), channel_id=1, source_target_pairs={{0,24},{1,25},{2,26},{3,27},{4,28},{5,29},{6,30},{7,31},{8,0},{9,1... | collective-permute-start | bytes 663560 | tf_op jit(solution)/shard_map/ppermute | solution.py:534
  34.5 19.3 %collective-permute-start.6 = (bf16[72,1536]{1,0:T(8,128)(2,1)}, bf16[72,1536]{1,0:T(8,128)(2,1)S(1)}, u32[]{:S(2)}, u32[]{:S(2)}) collective-permute-start(bf16[72,1536]{1,0:T(8,128)(2,1)} %get-tuple-element.41.refs_0_), channel_id=1, source_target_pairs={{0,16},{1,17},{2,18},{3,19},{4,20},{5,21},{6,22},{7,23},{8,24},{9,... | collective-permute-start | bytes 663560 | tf_op jit(solution)/shard_map/ppermute | solution.py:534
  34.5 19.3 %collective-permute-start.5 = (bf16[72,1536]{1,0:T(8,128)(2,1)}, bf16[72,1536]{1,0:T(8,128)(2,1)S(1)}, u32[]{:S(2)}, u32[]{:S(2)}) collective-permute-start(bf16[72,1536]{1,0:T(8,128)(2,1)} %get-tuple-element.41.refs_0_), channel_id=1, source_target_pairs={{0,8},{1,9},{2,10},{3,11},{4,12},{5,13},{6,14},{7,15},{8,16},{9,17... | collective-permute-start | bytes 663560 | tf_op jit(solution)/shard_map/ppermute | solution.py:534
  54.7 21.1 %collective-permute-start.11 = (bf16[4,72,1536]{2,1,0:T(8,128)(2,1)S(1)}, bf16[4,72,1536]{2,1,0:T(8,128)(2,1)S(1)}, u32[]{:S(2)}, u32[]{:S(2)}) collective-permute-start(bf16[4,72,1536]{2,1,0:T(8,128)(2,1)S(1)} %stack_rows.2.refs_0_), channel_id=1, source_target_pairs={{0,2},{1,5},{2,0},{3,7},{4,6},{5,1},{6,4},{7,3},{8,10},{9,13},{10,... | collective-permute-start | bytes 2654216 | tf_op jit(solution)/shard_map/ppermute | solution.py:534
  56.3 19.5 %collective-permute-start.9 = (bf16[64,1536]{1,0:T(8,128)(2,1)S(1)}, bf16[64,1536]{1,0:T(8,128)(2,1)S(1)}, u32[]{:S(2)}, u32[]{:S(2)}) collective-permute-start(bf16[64,1536]{1,0:T(8,128)(2,1)S(1)} %copy-done), channel_id=1, source_target_pairs={{0,16},{1,17},{2,18},{3,19},{4,20},{5,21},{6,22},{7,23},{8,24},{9,... | collective-permute-start | bytes 589832 | tf_op jit(solution)/shard_map/ppermute | solution.py:534
  59.1 16.7 %collective-permute-start.8 = (bf16[64,1536]{1,0:T(8,128)(2,1)S(1)}, bf16[64,1536]{1,0:T(8,128)(2,1)S(1)}, u32[]{:S(2)}, u32[]{:S(2)}) collective-permute-start(bf16[64,1536]{1,0:T(8,128)(2,1)S(1)} %copy-done), channel_id=1, source_target_pairs={{0,8},{1,9},{2,10},{3,11},{4,12},{5,13},{6,14},{7,15},{8,16},{9,17... | collective-permute-start | bytes 589832 | tf_op jit(solution)/shard_map/ppermute | solution.py:534
  61.1 17.8 %collective-permute-start.12 = (bf16[4,72,1536]{2,1,0:T(8,128)(2,1)S(1)}, bf16[4,72,1536]{2,1,0:T(8,128)(2,1)S(1)}, u32[]{:S(2)}, u32[]{:S(2)}) collective-permute-start(bf16[4,72,1536]{2,1,0:T(8,128)(2,1)S(1)} %stack_rows.2.refs_0_), channel_id=1, source_target_pairs={{0,4},{1,3},{2,6},{3,1},{4,0},{5,7},{6,2},{7,5},{8,12},{9,11},{10,... | collective-permute-start | bytes 2654216 | tf_op jit(solution)/shard_map/ppermute | solution.py:534
  76.8 20.6 %collective-permute-start.13 = (bf16[4,64,1536]{2,1,0:T(8,128)(2,1)S(1)}, bf16[4,64,1536]{2,1,0:T(8,128)(2,1)}, u32[]{:S(2)}, u32[]{:S(2)}) collective-permute-start(bf16[4,64,1536]{2,1,0:T(8,128)(2,1)S(1)} %stack_rows.3.refs_1_), channel_id=1, source_target_pairs={{0,4},{1,3},{2,6},{3,1},{4,0},{5,7},{6,2},{7,5},{8,12},{9,11},{10,... | collective-permute-start | bytes 2359304 | tf_op jit(solution)/shard_map/ppermute | solution.py:534
  77.4 37.6 %collective-permute-start.15 = (bf16[4,64,1536]{2,1,0:T(8,128)(2,1)S(1)}, bf16[4,64,1536]{2,1,0:T(8,128)(2,1)S(1)}, u32[]{:S(2)}, u32[]{:S(2)}) collective-permute-start(bf16[4,64,1536]{2,1,0:T(8,128)(2,1)S(1)} %stack_rows.3.refs_1_), channel_id=1, source_target_pairs={{0,2},{1,5},{2,0},{3,7},{4,6},{5,1},{6,4},{7,3},{8,10},{9,13},{10,... | collective-permute-start | bytes 2359304 | tf_op jit(solution)/shard_map/ppermute | solution.py:534
  78.9 35.0 %collective-permute-start.16 = (bf16[4,72,1536]{2,1,0:T(8,128)(2,1)S(1)}, bf16[4,72,1536]{2,1,0:T(8,128)(2,1)S(1)}, u32[]{:S(2)}, u32[]{:S(2)}) collective-permute-start(bf16[4,72,1536]{2,1,0:T(8,128)(2,1)S(1)} %collective-permute-done.12.refs_1_.refs_2_), channel_id=1, source_target_pairs={{0,2},{1,5},{2,0},{3,7},{4,6},{5,1},{6,4},{7,3},{8,10},{9,13},{10,... | collective-permute-start | bytes 2654216 | tf_op jit(solution)/shard_map/ppermute | solution.py:534
  97.4 20.2 %collective-permute-start.17 = (bf16[4,64,1536]{2,1,0:T(8,128)(2,1)}, bf16[4,64,1536]{2,1,0:T(8,128)(2,1)S(1)}, u32[]{:S(2)}, u32[]{:S(2)}) collective-permute-start(bf16[4,64,1536]{2,1,0:T(8,128)(2,1)} %collective-permute-done.13.refs_3_), channel_id=1, source_target_pairs={{0,2},{1,5},{2,0},{3,7},{4,6},{5,1},{6,4},{7,3},{8,10},{9,13},{10,... | collective-permute-start | bytes 2359304 | tf_op jit(solution)/shard_map/ppermute | solution.py:534
  111.9 16.8 %collective-permute-start.14 = (bf16[4,64,1536]{2,1,0:T(8,128)(2,1)S(1)}, bf16[4,64,1536]{2,1,0:T(8,128)(2,1)S(1)}, u32[]{:S(2)}, u32[]{:S(2)}) collective-permute-start(bf16[4,64,1536]{2,1,0:T(8,128)(2,1)S(1)} %get-tuple-element.47), channel_id=1, source_target_pairs={{0,4},{1,3},{2,6},{3,1},{4,0},{5,7},{6,2},{7,5},{8,12},{9,11},{10,... | collective-permute-start | bytes 2359304 | tf_op jit(solution)/shard_map/ppermute | solution.py:534
  112.4 19.9 %collective-permute-start.18 = (bf16[4,64,1536]{2,1,0:T(8,128)(2,1)S(1)}, bf16[4,64,1536]{2,1,0:T(8,128)(2,1)S(1)}, u32[]{:S(2)}, u32[]{:S(2)}) collective-permute-start(bf16[4,64,1536]{2,1,0:T(8,128)(2,1)S(1)} %get-tuple-element.52), channel_id=1, source_target_pairs={{0,4},{1,3},{2,6},{3,1},{4,0},{5,7},{6,2},{7,5},{8,12},{9,11},{10,... | collective-permute-start | bytes 2359304 | tf_op jit(solution)/shard_map/ppermute | solution.py:534
  133.3 12.1 %collective-permute-start.19 = (bf16[4,64,1536]{2,1,0:T(8,128)(2,1)S(1)}, bf16[4,64,1536]{2,1,0:T(8,128)(2,1)S(1)}, u32[]{:S(2)}, u32[]{:S(2)}) collective-permute-start(bf16[4,64,1536]{2,1,0:T(8,128)(2,1)S(1)} %get-tuple-element.54), channel_id=1, source_target_pairs={{0,4},{1,3},{2,6},{3,1},{4,0},{5,7},{6,2},{7,5},{8,12},{9,11},{10,... | collective-permute-start | bytes 2359304 | tf_op jit(solution)/shard_map/ppermute | solution.py:534
  145.4 20.5 %collective-permute-start.24 = (bf16[4,64,1536]{2,1,0:T(8,128)(2,1)S(1)}, bf16[4,64,1536]{2,1,0:T(8,128)(2,1)S(1)}, u32[]{:S(2)}, u32[]{:S(2)}) collective-permute-start(bf16[4,64,1536]{2,1,0:T(8,128)(2,1)S(1)} %get-tuple-element.59), channel_id=1, source_target_pairs={{0,4},{1,3},{2,6},{3,1},{4,0},{5,7},{6,2},{7,5},{8,12},{9,11},{10,... | collective-permute-start | bytes 2359304 | tf_op jit(solution)/shard_map/ppermute | solution.py:534
  146.1 20.1 %collective-permute-start.20 = (bf16[4,64,1536]{2,1,0:T(8,128)(2,1)S(1)}, bf16[4,64,1536]{2,1,0:T(8,128)(2,1)S(1)}, u32[]{:S(2)}, u32[]{:S(2)}) collective-permute-start(bf16[4,64,1536]{2,1,0:T(8,128)(2,1)S(1)} %add_convert_fusion.1), channel_id=1, source_target_pairs={{0,2},{1,5},{2,0},{3,7},{4,6},{5,1},{6,4},{7,3},{8,10},{9,13},{10,... | collective-permute-start | bytes 2359304 | tf_op jit(solution)/shard_map/ppermute | solution.py:534
  166.1 12.1 %collective-permute-start.25 = (bf16[4,64,1536]{2,1,0:T(8,128)(2,1)S(1)}, bf16[4,64,1536]{2,1,0:T(8,128)(2,1)S(1)}, u32[]{:S(2)}, u32[]{:S(2)}) collective-permute-start(bf16[4,64,1536]{2,1,0:T(8,128)(2,1)S(1)} %add_convert_fusion), channel_id=1, source_target_pairs={{0,2},{1,5},{2,0},{3,7},{4,6},{5,1},{6,4},{7,3},{8,10},{9,13},{10,... | collective-permute-start | bytes 2359304 | tf_op jit(solution)/shard_map/ppermute | solution.py:534
  166.4 14.0 %collective-permute-start.21 = (bf16[64,1536]{1,0:T(8,128)(2,1)S(1)}, bf16[64,1536]{1,0:T(8,128)(2,1)S(1)}, u32[]{:S(2)}, u32[]{:S(2)}) collective-permute-start(bf16[64,1536]{1,0:T(8,128)(2,1)S(1)} %get-tuple-element.60), channel_id=1, source_target_pairs={{0,24},{1,25},{2,26},{3,27},{4,28},{5,29},{6,30},{7,31},{8,0},{9,1... | collective-permute-start | bytes 589832 | tf_op jit(solution)/shard_map/ppermute | solution.py:534
  166.4 19.3 %collective-permute-start.23 = (bf16[64,1536]{1,0:T(8,128)(2,1)S(1)}, bf16[64,1536]{1,0:T(8,128)(2,1)S(1)}, u32[]{:S(2)}, u32[]{:S(2)}) collective-permute-start(bf16[64,1536]{1,0:T(8,128)(2,1)S(1)} %get-tuple-element.61), channel_id=1, source_target_pairs={{0,8},{1,9},{2,10},{3,11},{4,12},{5,13},{6,14},{7,15},{8,16},{9,17... | collective-permute-start | bytes 589832 | tf_op jit(solution)/shard_map/ppermute | solution.py:534
  168.5 20.5 %collective-permute-start.22 = (bf16[64,1536]{1,0:T(8,128)(2,1)S(1)}, bf16[64,1536]{1,0:T(8,128)(2,1)S(1)}, u32[]{:S(2)}, u32[]{:S(2)}) collective-permute-start(bf16[64,1536]{1,0:T(8,128)(2,1)S(1)} %get-tuple-element.62), channel_id=1, source_target_pairs={{0,16},{1,17},{2,18},{3,19},{4,20},{5,21},{6,22},{7,23},{8,24},{9,... | collective-permute-start | bytes 589832 | tf_op jit(solution)/shard_map/ppermute | solution.py:534
  178.4 13.9 %collective-permute-start.28 = (bf16[64,1536]{1,0:T(8,128)(2,1)S(1)}, bf16[64,1536]{1,0:T(8,128)(2,1)S(1)}, u32[]{:S(2)}, u32[]{:S(2)}) collective-permute-start(bf16[64,1536]{1,0:T(8,128)(2,1)S(1)} %get-tuple-element.64), channel_id=1, source_target_pairs={{0,8},{1,9},{2,10},{3,11},{4,12},{5,13},{6,14},{7,15},{8,16},{9,17... | collective-permute-start | bytes 589832 | tf_op jit(solution)/shard_map/ppermute | solution.py:534
  180.4 18.7 %collective-permute-start.27 = (bf16[64,1536]{1,0:T(8,128)(2,1)S(1)}, bf16[64,1536]{1,0:T(8,128)(2,1)S(1)}, u32[]{:S(2)}, u32[]{:S(2)}) collective-permute-start(bf16[64,1536]{1,0:T(8,128)(2,1)S(1)} %get-tuple-element.65), channel_id=1, source_target_pairs={{0,16},{1,17},{2,18},{3,19},{4,20},{5,21},{6,22},{7,23},{8,24},{9,... | collective-permute-start | bytes 589832 | tf_op jit(solution)/shard_map/ppermute | solution.py:534
  (14 other events, 101.4 us)

commit v7 on v6

--- a/solution.py
+++ b/solution.py
@@ -20,6 +20,7 @@
 score_scale = 0.015625
 rope_base = 10000.0
 neg_big = -1e30
+log2_e = math.log2(math.e)
 
 BOTH = ("req", "seq")
 
@@ -112,8 +113,8 @@
     rows = q_ref.shape[0]
     cached = kc_ref.shape[1]
     span = ks_ref.shape[0]
-    seq_index = place_ref[0]
-    length = place_ref[1]
+    seq_index = lax.axis_index("seq")
+    length = place_ref[0]
 
     @pl.when(step == 0)
     def _():
@@ -169,7 +170,7 @@
             preferred_element_type=jnp.float32,
         )
         best = jnp.max(scores, axis=-1, keepdims=True)
-        weights = jnp.exp(scores - best).astype(jnp.bfloat16)
+        weights = jnp.exp2(((scores - best) * log2_e).astype(jnp.bfloat16))
         sums = jnp.dot(weights, values[...], preferred_element_type=jnp.float32)
         mean = sums[:, :LANES] / sums[:, LANES:]
         heads += [mean[i : i + rows] for i in range(0, batch, rows)]
@@ -520,7 +521,7 @@
                             axis = {"z": "z", "a": "b", "b": "a"}[role]
                         to_z, to_y, to_x = z, y, x
                         if axis == "z":
-                            to_z = (z + offset) % depth
+                            to_z = z ^ offset
                         elif axis == "a":
                             to_y = (y + offset) % tall
                         else:
@@ -531,13 +532,43 @@
         return out
 
     def shift(value, role, offset):
-        return lax.ppermute(value, BOTH, pairs(role, offset % sizes[role]))
+        if role != "z":
+            offset %= sizes[role]
+        return lax.ppermute(value, BOTH, pairs(role, offset))
 
     return shift, sizes
 
 
 def gather_line(value, shift, sizes):
     return [value] + [shift(value, "z", k) for k in range(1, sizes["z"])]
+
+
+def gather_line_doubling(value, shift, sizes):
+    line, step = {0: value}, sizes["z"] // 2
+    while step:
+        known = sorted(line)
+        if len(known) == 1:
+            arrived = [shift(line[0], "z", step)]
+        else:
+            arrived = shift(jnp.stack([line[k] for k in known]), "z", step)
+        for place, k in enumerate(known):
+            line[k ^ step] = arrived[place]
+        step //= 2
+    return [line[k] for k in range(sizes["z"])]
+
+
+def scatter_line(line, shift, sizes):
+    step = 1
+    while step < sizes["z"]:
+        kept = [k for k in range(0, sizes["z"], step) if not k & step]
+        if len(kept) == 1:
+            arrived = [shift(add_all(line[step]), "z", step)]
+        else:
+            arrived = shift(jnp.stack([add_all(line[k | step]) for k in kept]), "z", step)
+        for place, k in enumerate(kept):
+            line[k] = line[k] + [arrived[place]]
+        step *= 2
+    return add_all(line[0])
 
 
 def gather_planes(line, shift, sizes, before):
@@ -569,11 +600,14 @@
         terms = [leave_along_a(plane, shift) for plane in sending]
         before = [v for moved in terms for v in moved[1:]]
         line = line + [shift(add_all(t), "b", -k - 1) for k, t in enumerate(terms)]
-        moved = [
-            shift(add_all([t[i] for t in line]), "z", -i) for i in range(1, sizes["z"])
-        ]
-        sums.append(add_all([t[0] for t in line] + moved))
-    return jnp.concatenate(sums, axis=0)
+        parts = {i: [t[i] for t in line] for i in range(sizes["z"])}
+        sums.append(scatter_line(parts, shift, sizes))
+    total = jnp.zeros((sum(v.shape[0] for v in sums), sums[0].shape[1]), sums[0].dtype)
+    first = 0
+    for value in sums:
+        total = lax.dynamic_update_slice(total, value, (first, 0))
+        first += value.shape[0]
+    return total
 
 
 def rope_tables(positions):
@@ -644,14 +678,13 @@
     queries, appended, other_span = project(
         tokens, other_tokens, attn_gain, cosine, sine, w_qkv, [k_other, v_other]
     )
-    place = jnp.stack([seq_index, length]).astype(jnp.int32)
     later_up, later_down, _ = lax.optimization_barrier((expert_up, expert_down, appended))
     up_other, down_other = swap(later_up), swap(later_down)
     half = row_count // 2
     filled, lines = [], []
     for index in range(2):
         attended, stream, expert_in = attend(
-            place,
+            cache_len,
             queries,
             (k_cache, k_other, v_cache, v_other),
             (appended, other_span),
@@ -665,7 +698,8 @@
             [up_other, down_other] if index else [],
         )
         filled = [attended, stream]
-        lines.append(gather_line(expert_in, shift, sizes))
+        gather = gather_line_doubling if index else gather_line
+        lines.append(gather(expert_in, shift, sizes))
     first, second = lines
     planes = gather_planes(stack_rows(first, [expert_in]), shift, sizes, second[1:])
     stacked = stack_rows(second, [plane[0] for plane in planes[1:]])

time: 200 us -> 203 us (1.015)
  waiting for transfers between devices: 89.9 us -> 105 us
  starting transfers between devices: 38.6 us -> 26 us
    ppermute x24 -> x21, waiting for transfers between devices: 88.6 us -> 104 us  [shift(): return lax.ppermute(value, BOTH, pairs(role, offset))]
    ppermute x24 -> x21, starting transfers between devices: 37.1 us -> 24.5 us  [shift(): return lax.ppermute(value, BOTH, pairs(role, offset))]
  transfers between devices with their start and end apart: 29 -> 26, of which waited for: 13 -> 15; matrix products, arithmetic and copies ran while one was open for 3% -> 2% of each run, Pallas kernels for 26% -> 27%
where the time goes in v7:
time: 203 us; the launch traced here: 202 us
  waiting for transfers between devices  105 us (52%)
  Pallas kernels  62.2 us (31%)
  starting transfers between devices  26 us (13%)
  other arithmetic  5.1 us (3%)
  local copies, waits for them, and re-layouts  2.33 us (1%)
    ppermute x21, waiting for transfers between devices, shift(): return lax.ppermute(value, BOTH, pairs(role, offset))  104 us
    pallas_call x2, Pallas kernels, attend(): pl.pallas_call(functools.partial(attend_kernel, first_row, len(riders), l...  28.1 us
    ppermute x21, starting transfers between devices, shift(): return lax.ppermute(value, BOTH, pairs(role, offset))  24.5 us
    pallas_call x2, Pallas kernels, run_experts(): pl.pallas_call(functools.partial(expert_kernel, pieces, tuple(in_cuts), l...  22.6 us
    pallas_call x1, Pallas kernels, project(): pl.pallas_call(qkv_kernel, grid=(5,), in_specs=[vmem_spec()] * 5 + [pl.Bl...  7.39 us
  transfers between devices with their start and end apart: 26, of which 15 were waited for; matrix products, arithmetic and copies ran while one was open for 2% of the time, Pallas kernels for 27%

profile of v7, /device:TPU:0, one launch (start us, length us, event | category | flops | bytes accessed | tf_op | source)
XLA Modules:
  0.0 202.3 jit_solution(5394913970154733955)
XLA Ops:
  5.8 7.4 %project_rows.1 = (bf16[128,1536]{1,0:T(8,128)(2,1)}, bf16[128,1024]{1,0:T(8,128)(2,1)}, bf16[128,1024]{1,0:T(8,128)(2,1)}) custom-call(bf16[128,1536]{1,0:T(8,128)(2,1)} %tokens_ref.3, bf16[128,1536]{1,0:T(8,128)(2,1)} %copy-done.6, f32[1536]{0:T(1024)} %gain_ref.3, f32[256,128]{1,0:T(8,128)} %pad_maximum_fusion.4.cos_ref, ...), custom_call_target="tpu_custom_call" | custom-call | flops 1409286144 | bytes 9500000 | tf_op jit(solution)/shard_map/project_rows/pallas_call | solution.py:85
  15.2 14.0 %attend_rows.2 = (bf16[128,1536]{1,0:T(8,128)(2,1)}, bf16[128,1536]{1,0:T(8,128)(2,1)}, bf16[72,1536]{1,0:T(8,128)(2,1)}) custom-call(s32[1]{0:T(128)} %copy.24.place_ref, bf16[128,1536]{1,0:T(8,128)(2,1)} %get-tuple-element.32.q_ref, bf16[1,1024,512]{2,1,0:T(8,128)(2,1)} %kc_ref.3, bf16[1,1024,512]{2,1,0:T(8,128)(2,1)} %collective-permute-done.1.refs_0_.kco_ref, ...), custom_call_target="tpu_custom_call" | custom-call | flops 7247757312 | bytes 10000000 | tf_op jit(solution)/shard_map/attend_rows/pallas_call | solution.py:223
  29.2 5.1 %collective-permute-start.7 = (bf16[72,1536]{1,0:T(8,128)(2,1)}, bf16[72,1536]{1,0:T(8,128)(2,1)S(1)}, u32[]{:S(2)}, u32[]{:S(2)}) collective-permute-start(bf16[72,1536]{1,0:T(8,128)(2,1)} %get-tuple-element.41.refs_0_), channel_id=1, source_target_pairs={{0,24},{1,25},{2,26},{3,27},{4,28},{5,29},{6,30},{7,31},{8,16},{9,... | collective-permute-start | bytes 663560 | tf_op jit(solution)/shard_map/ppermute | solution.py:537
  34.9 14.1 %attend_rows.3 = (bf16[128,1536]{1,0:T(8,128)(2,1)}, bf16[128,1536]{1,0:T(8,128)(2,1)}, bf16[64,1536]{1,0:T(8,128)(2,1)}) custom-call(s32[1]{0:T(128)} %copy.24.place_ref, bf16[128,1536]{1,0:T(8,128)(2,1)} %get-tuple-element.32.q_ref, bf16[1,1024,512]{2,1,0:T(8,128)(2,1)} %kc_ref.3, ...), custom_call_target="tpu_custom_call", output_to_operand_aliasing={{0}: (13, {}), {1}: (14, {})} | custom-call | flops 7247757312 | bytes 10000000 | tf_op jit(solution)/shard_map/attend_rows/pallas_call | solution.py:223
  49.0 2.4 %collective-permute-start.8 = (bf16[64,1536]{1,0:T(8,128)(2,1)}, bf16[64,1536]{1,0:T(8,128)(2,1)S(1)}, u32[]{:S(2)}, u32[]{:S(2)}) collective-permute-start(bf16[64,1536]{1,0:T(8,128)(2,1)} %get-tuple-element.42.refs_4_.refs_0_), channel_id=1, source_target_pairs={{0,16},{1,17},{2,18},{3,19},{4,20},{5,21},{6,22},{7,23},{8,24},{9,... | collective-permute-start | bytes 589832 | tf_op jit(solution)/shard_map/ppermute | solution.py:537
  51.4 7.2 %collective-permute-done.6.refs_2_ = bf16[72,1536]{1,0:T(8,128)(2,1)S(1)} collective-permute-done((bf16[72,1536]{1,0:T(8,128)(2,1)}, bf16[72,1536]{1,0:T(8,128)(2,1)S(1)}, u32[]{:S(2)}, u32[]{:S(2)}) %collective-permute-start.6) | collective-permute-done | bytes 221216 | tf_op jit(solution)/shard_map/ppermute | solution.py:537
  59.6 1.6 collective-permute-start.10
  62.1 1.6 collective-permute-start.11
  63.7 8.7 %collective-permute-done.9 = bf16[2,64,1536]{2,1,0:T(8,128)(2,1)S(1)} collective-permute-done((bf16[2,64,1536]{2,1,0:T(8,128)(2,1)S(1)}, bf16[2,64,1536]{2,1,0:T(8,128)(2,1)S(1)}, u32[]{:S(2)}, u32[]{:S(2)}) %collective-permute-start.9) | collective-permute-done | bytes 393248 | tf_op jit(solution)/shard_map/ppermute | solution.py:537
  72.4 9.0 %collective-permute-done.10.refs_4_.refs_0_ = bf16[4,72,1536]{2,1,0:T(8,128)(2,1)S(1)} collective-permute-done((bf16[4,72,1536]{2,1,0:T(8,128)(2,1)S(1)}, bf16[4,72,1536]{2,1,0:T(8,128)(2,1)S(1)}, u32[]{:S(2)}, u32[]{:S(2)}) %collective-permute-start.10) | collective-permute-done | bytes 884768 | tf_op jit(solution)/shard_map/ppermute | solution.py:537
  81.5 1.6 collective-permute-start.12
  86.2 15.7 %collective-permute-done.12.refs_3_ = bf16[4,64,1536]{2,1,0:T(8,128)(2,1)} collective-permute-done((bf16[4,64,1536]{2,1,0:T(8,128)(2,1)S(1)}, bf16[4,64,1536]{2,1,0:T(8,128)(2,1)}, u32[]{:S(2)}, u32[]{:S(2)}) %collective-permute-start.12) | collective-permute-done | bytes 786464 | tf_op jit(solution)/shard_map/ppermute | solution.py:537
  102.0 1.5 collective-permute-start.16
  103.5 11.5 %run_experts.2.held_ref.refs_10_ = bf16[4,256,1536]{2,1,0:T(8,128)(2,1)S(1)} custom-call(bf16[4,72,1536]{2,1,0:T(8,128)(2,1)S(1)} %stack_rows.2.refs_0_, bf16[4,64,1536]{2,1,0:T(8,128)(2,1)S(1)} %stack_rows.3.refs_1_, bf16[4,72,1536]{2,1,0:T(8,128)(2,1)S(1)} %collective-permute-done.11.refs_1_.refs_2_, bf16[4,64,1536]{2,1,0:T(8,128)(2,1)} %collective-permute-done.12.refs_3_, ...), custom_call_target="tpu_custom_call" | custom-call | flops 8053063680 | bytes 26000000 | tf_op jit(solution)/shard_map/run_experts/pallas_call | solution.py:416
  121.1 11.1 %run_experts.3.held_ref = bf16[4,256,1536]{2,1,0:T(8,128)(2,1)S(1)} custom-call(bf16[4,72,1536]{2,1,0:T(8,128)(2,1)S(1)} %collective-permute-done.10.refs_4_.refs_0_, bf16[4,64,1536]{2,1,0:T(8,128)(2,1)S(1)} %collective-permute-done.14.refs_1_, bf16[4,72,1536]{2,1,0:T(8,128)(2,1)S(1)} %collective-permute-done.15.refs_1_.refs_2_, ...), custom_call_target="tpu_custom_call" | custom-call | flops 8053063680 | bytes 26000000 | tf_op jit(solution)/shard_map/run_experts/pallas_call | solution.py:416
  132.2 4.8 %collective-permute-done.17.refs_1_ = bf16[4,64,1536]{2,1,0:T(8,128)(2,1)S(1)} collective-permute-done((bf16[4,64,1536]{2,1,0:T(8,128)(2,1)S(1)}, bf16[4,64,1536]{2,1,0:T(8,128)(2,1)S(1)}, u32[]{:S(2)}, u32[]{:S(2)}) %collective-permute-start.17) | collective-permute-done | bytes 786464 | tf_op jit(solution)/shard_map/ppermute | solution.py:537
  138.0 1.5 collective-permute-start.18
  139.5 10.5 %collective-permute-done.18 = bf16[4,64,1536]{2,1,0:T(8,128)(2,1)S(1)} collective-permute-done((bf16[4,64,1536]{2,1,0:T(8,128)(2,1)S(1)}, bf16[4,64,1536]{2,1,0:T(8,128)(2,1)S(1)}, u32[]{:S(2)}, u32[]{:S(2)}) %collective-permute-start.18) | collective-permute-done | bytes 786464 | tf_op jit(solution)/shard_map/ppermute | solution.py:537
  152.4 18.1 %collective-permute-done.22 = bf16[4,64,1536]{2,1,0:T(8,128)(2,1)S(1)} collective-permute-done((bf16[4,64,1536]{2,1,0:T(8,128)(2,1)S(1)}, bf16[4,64,1536]{2,1,0:T(8,128)(2,1)S(1)}, u32[]{:S(2)}, u32[]{:S(2)}) %collective-permute-start.22) | collective-permute-done | bytes 786464 | tf_op jit(solution)/shard_map/ppermute | solution.py:537
  171.1 11.7 %collective-permute-done.23 = bf16[4,64,1536]{2,1,0:T(8,128)(2,1)S(1)} collective-permute-done((bf16[4,64,1536]{2,1,0:T(8,128)(2,1)S(1)}, bf16[4,64,1536]{2,1,0:T(8,128)(2,1)S(1)}, u32[]{:S(2)}, u32[]{:S(2)}) %collective-permute-start.23) | collective-permute-done | bytes 786464 | tf_op jit(solution)/shard_map/ppermute | solution.py:537
  183.2 1.7 collective-permute-start.21
  184.9 8.2 %collective-permute-done.24 = bf16[2,64,1536]{2,1,0:T(8,128)(2,1)S(1)} collective-permute-done((bf16[2,64,1536]{2,1,0:T(8,128)(2,1)S(1)}, bf16[2,64,1536]{2,1,0:T(8,128)(2,1)S(1)}, u32[]{:S(2)}, u32[]{:S(2)}) %collective-permute-start.24) | collective-permute-done | bytes 393248 | tf_op jit(solution)/shard_map/ppermute | solution.py:537
  193.8 1.8 collective-permute-done.21
  195.7 5.8 %collective-permute-done.25 = bf16[64,1536]{1,0:T(8,128)(2,1)S(1)} collective-permute-done((bf16[64,1536]{1,0:T(8,128)(2,1)S(1)}, bf16[64,1536]{1,0:T(8,128)(2,1)S(1)}, u32[]{:S(2)}, u32[]{:S(2)}) %collective-permute-start.25) | collective-permute-done | bytes 196640 | tf_op jit(solution)/shard_map/ppermute | solution.py:537
  (85 shorter events, 24.3 us)
Async XLA Ops:
  1.1 4.7 %collective-permute-start.2 = (bf16[1,1024,512]{2,1,0:T(8,128)(2,1)}, bf16[1,1024,512]{2,1,0:T(8,128)(2,1)}, u32[]{:S(2)}, u32[]{:S(2)}) collective-permute-start(bf16[1,1024,512]{2,1,0:T(8,128)(2,1)} %vc_ref.3), channel_id=1, source_target_pairs={{0,1},{1,0},{2,3},{3,2},{4,5},{5,4},{6,7},{7,6},{8,9},{9,8},{10,11... | collective-permute-start | bytes 3145736 | tf_op jit(solution)/shard_map/ppermute | solution.py:649
  13.2 21.7 %collective-permute-start.3 = (bf16[2,1536,1024]{2,1,0:T(8,128)(2,1)}, bf16[2,1536,1024]{2,1,0:T(8,128)(2,1)}, u32[]{:S(2)}, u32[]{:S(2)}) collective-permute-start(bf16[2,1536,1024]{2,1,0:T(8,128)(2,1)} %refs_6_.3), channel_id=1, source_target_pairs={{0,1},{1,0},{2,3},{3,2},{4,5},{5,4},{6,7},{7,6},{8,9},{9,8},{10,11... | collective-permute-start | bytes 18874376 | tf_op jit(solution)/shard_map/ppermute | solution.py:649
  13.6 21.3 %collective-permute-start.4 = (bf16[2,512,1536]{2,1,0:T(8,128)(2,1)S(1)}, bf16[2,512,1536]{2,1,0:T(8,128)(2,1)}, u32[]{:S(2)}, u32[]{:S(2)}) collective-permute-start(bf16[2,512,1536]{2,1,0:T(8,128)(2,1)S(1)} %copy-done.3), channel_id=1, source_target_pairs={{0,1},{1,0},{2,3},{3,2},{4,5},{5,4},{6,7},{7,6},{8,9},{9,8},{10,11... | collective-permute-start | bytes 9437192 | tf_op jit(solution)/shard_map/ppermute | solution.py:649
  29.2 22.1 %collective-permute-start.7 = (bf16[72,1536]{1,0:T(8,128)(2,1)}, bf16[72,1536]{1,0:T(8,128)(2,1)S(1)}, u32[]{:S(2)}, u32[]{:S(2)}) collective-permute-start(bf16[72,1536]{1,0:T(8,128)(2,1)} %get-tuple-element.41.refs_0_), channel_id=1, source_target_pairs={{0,24},{1,25},{2,26},{3,27},{4,28},{5,29},{6,30},{7,31},{8,16},{9,... | collective-permute-start | bytes 663560 | tf_op jit(solution)/shard_map/ppermute | solution.py:537
  34.3 24.3 %collective-permute-start.6 = (bf16[72,1536]{1,0:T(8,128)(2,1)}, bf16[72,1536]{1,0:T(8,128)(2,1)S(1)}, u32[]{:S(2)}, u32[]{:S(2)}) collective-permute-start(bf16[72,1536]{1,0:T(8,128)(2,1)} %get-tuple-element.41.refs_0_), channel_id=1, source_target_pairs={{0,16},{1,17},{2,18},{3,19},{4,20},{5,21},{6,22},{7,23},{8,24},{9,... | collective-permute-start | bytes 663560 | tf_op jit(solution)/shard_map/ppermute | solution.py:537
  34.3 24.3 %collective-permute-start.5 = (bf16[72,1536]{1,0:T(8,128)(2,1)}, bf16[72,1536]{1,0:T(8,128)(2,1)S(1)}, u32[]{:S(2)}, u32[]{:S(2)}) collective-permute-start(bf16[72,1536]{1,0:T(8,128)(2,1)} %get-tuple-element.41.refs_0_), channel_id=1, source_target_pairs={{0,8},{1,9},{2,10},{3,11},{4,12},{5,13},{6,14},{7,15},{8,0},{9,1},... | collective-permute-start | bytes 663560 | tf_op jit(solution)/shard_map/ppermute | solution.py:537
  49.0 13.0 %collective-permute-start.8 = (bf16[64,1536]{1,0:T(8,128)(2,1)}, bf16[64,1536]{1,0:T(8,128)(2,1)S(1)}, u32[]{:S(2)}, u32[]{:S(2)}) collective-permute-start(bf16[64,1536]{1,0:T(8,128)(2,1)} %get-tuple-element.42.refs_4_.refs_0_), channel_id=1, source_target_pairs={{0,16},{1,17},{2,18},{3,19},{4,20},{5,21},{6,22},{7,23},{8,24},{9,... | collective-permute-start | bytes 589832 | tf_op jit(solution)/shard_map/ppermute | solution.py:537
  59.6 21.8 %collective-permute-start.10 = (bf16[4,72,1536]{2,1,0:T(8,128)(2,1)S(1)}, bf16[4,72,1536]{2,1,0:T(8,128)(2,1)S(1)}, u32[]{:S(2)}, u32[]{:S(2)}) collective-permute-start(bf16[4,72,1536]{2,1,0:T(8,128)(2,1)S(1)} %stack_rows.2.refs_0_), channel_id=1, source_target_pairs={{0,2},{1,5},{2,0},{3,7},{4,6},{5,1},{6,4},{7,3},{8,10},{9,13},{10,... | collective-permute-start | bytes 2654216 | tf_op jit(solution)/shard_map/ppermute | solution.py:537
  62.0 10.4 %collective-permute-start.9 = (bf16[2,64,1536]{2,1,0:T(8,128)(2,1)S(1)}, bf16[2,64,1536]{2,1,0:T(8,128)(2,1)S(1)}, u32[]{:S(2)}, u32[]{:S(2)}) collective-permute-start(bf16[2,64,1536]{2,1,0:T(8,128)(2,1)S(1)} %pad_maximum_fusion), channel_id=1, source_target_pairs={{0,8},{1,9},{2,10},{3,11},{4,12},{5,13},{6,14},{7,15},{8,0},{9,1},... | collective-permute-start | bytes 1179656 | tf_op jit(solution)/shard_map/ppermute | solution.py:537
  62.1 22.5 %collective-permute-start.11 = (bf16[4,72,1536]{2,1,0:T(8,128)(2,1)S(1)}, bf16[4,72,1536]{2,1,0:T(8,128)(2,1)S(1)}, u32[]{:S(2)}, u32[]{:S(2)}) collective-permute-start(bf16[4,72,1536]{2,1,0:T(8,128)(2,1)S(1)} %stack_rows.2.refs_0_), channel_id=1, source_target_pairs={{0,4},{1,3},{2,6},{3,1},{4,0},{5,7},{6,2},{7,5},{8,12},{9,11},{10,... | collective-permute-start | bytes 2654216 | tf_op jit(solution)/shard_map/ppermute | solution.py:537
  81.5 20.5 %collective-permute-start.12 = (bf16[4,64,1536]{2,1,0:T(8,128)(2,1)S(1)}, bf16[4,64,1536]{2,1,0:T(8,128)(2,1)}, u32[]{:S(2)}, u32[]{:S(2)}) collective-permute-start(bf16[4,64,1536]{2,1,0:T(8,128)(2,1)S(1)} %stack_rows.3.refs_1_), channel_id=1, source_target_pairs={{0,4},{1,3},{2,6},{3,1},{4,0},{5,7},{6,2},{7,5},{8,12},{9,11},{10,... | collective-permute-start | bytes 2359304 | tf_op jit(solution)/shard_map/ppermute | solution.py:537
  83.1 36.6 %collective-permute-start.14 = (bf16[4,64,1536]{2,1,0:T(8,128)(2,1)S(1)}, bf16[4,64,1536]{2,1,0:T(8,128)(2,1)S(1)}, u32[]{:S(2)}, u32[]{:S(2)}) collective-permute-start(bf16[4,64,1536]{2,1,0:T(8,128)(2,1)S(1)} %stack_rows.3.refs_1_), channel_id=1, source_target_pairs={{0,2},{1,5},{2,0},{3,7},{4,6},{5,1},{6,4},{7,3},{8,10},{9,13},{10,... | collective-permute-start | bytes 2359304 | tf_op jit(solution)/shard_map/ppermute | solution.py:537
  84.6 34.1 %collective-permute-start.15 = (bf16[4,72,1536]{2,1,0:T(8,128)(2,1)S(1)}, bf16[4,72,1536]{2,1,0:T(8,128)(2,1)S(1)}, u32[]{:S(2)}, u32[]{:S(2)}) collective-permute-start(bf16[4,72,1536]{2,1,0:T(8,128)(2,1)S(1)} %collective-permute-done.11.refs_1_.refs_2_), channel_id=1, source_target_pairs={{0,2},{1,5},{2,0},{3,7},{4,6},{5,1},{6,4},{7,3},{8,10},{9,13},{10,... | collective-permute-start | bytes 2654216 | tf_op jit(solution)/shard_map/ppermute | solution.py:537
  102.0 19.1 %collective-permute-start.16 = (bf16[4,64,1536]{2,1,0:T(8,128)(2,1)}, bf16[4,64,1536]{2,1,0:T(8,128)(2,1)S(1)}, u32[]{:S(2)}, u32[]{:S(2)}) collective-permute-start(bf16[4,64,1536]{2,1,0:T(8,128)(2,1)} %collective-permute-done.12.refs_3_), channel_id=1, source_target_pairs={{0,2},{1,5},{2,0},{3,7},{4,6},{5,1},{6,4},{7,3},{8,10},{9,13},{10,... | collective-permute-start | bytes 2359304 | tf_op jit(solution)/shard_map/ppermute | solution.py:537
  116.6 15.6 %collective-permute-start.13 = (bf16[4,64,1536]{2,1,0:T(8,128)(2,1)S(1)}, bf16[4,64,1536]{2,1,0:T(8,128)(2,1)S(1)}, u32[]{:S(2)}, u32[]{:S(2)}) collective-permute-start(bf16[4,64,1536]{2,1,0:T(8,128)(2,1)S(1)} %get-tuple-element.47), channel_id=1, source_target_pairs={{0,4},{1,3},{2,6},{3,1},{4,0},{5,7},{6,2},{7,5},{8,12},{9,11},{10,... | collective-permute-start | bytes 2359304 | tf_op jit(solution)/shard_map/ppermute | solution.py:537
  118.1 19.0 %collective-permute-start.17 = (bf16[4,64,1536]{2,1,0:T(8,128)(2,1)S(1)}, bf16[4,64,1536]{2,1,0:T(8,128)(2,1)S(1)}, u32[]{:S(2)}, u32[]{:S(2)}) collective-permute-start(bf16[4,64,1536]{2,1,0:T(8,128)(2,1)S(1)} %get-tuple-element.52), channel_id=1, source_target_pairs={{0,4},{1,3},{2,6},{3,1},{4,0},{5,7},{6,2},{7,5},{8,12},{9,11},{10,... | collective-permute-start | bytes 2359304 | tf_op jit(solution)/shard_map/ppermute | solution.py:537
  138.0 12.1 %collective-permute-start.18 = (bf16[4,64,1536]{2,1,0:T(8,128)(2,1)S(1)}, bf16[4,64,1536]{2,1,0:T(8,128)(2,1)S(1)}, u32[]{:S(2)}, u32[]{:S(2)}) collective-permute-start(bf16[4,64,1536]{2,1,0:T(8,128)(2,1)S(1)} %get-tuple-element.54), channel_id=1, source_target_pairs={{0,4},{1,3},{2,6},{3,1},{4,0},{5,7},{6,2},{7,5},{8,12},{9,11},{10,... | collective-permute-start | bytes 2359304 | tf_op jit(solution)/shard_map/ppermute | solution.py:537
  150.1 20.5 %collective-permute-start.22 = (bf16[4,64,1536]{2,1,0:T(8,128)(2,1)S(1)}, bf16[4,64,1536]{2,1,0:T(8,128)(2,1)S(1)}, u32[]{:S(2)}, u32[]{:S(2)}) collective-permute-start(bf16[4,64,1536]{2,1,0:T(8,128)(2,1)S(1)} %get-tuple-element.59), channel_id=1, source_target_pairs={{0,4},{1,3},{2,6},{3,1},{4,0},{5,7},{6,2},{7,5},{8,12},{9,11},{10,... | collective-permute-start | bytes 2359304 | tf_op jit(solution)/shard_map/ppermute | solution.py:537
  151.7 19.1 %collective-permute-start.19 = (bf16[4,64,1536]{2,1,0:T(8,128)(2,1)S(1)}, bf16[4,64,1536]{2,1,0:T(8,128)(2,1)S(1)}, u32[]{:S(2)}, u32[]{:S(2)}) collective-permute-start(bf16[4,64,1536]{2,1,0:T(8,128)(2,1)S(1)} %add_convert_fusion.1), channel_id=1, source_target_pairs={{0,2},{1,5},{2,0},{3,7},{4,6},{5,1},{6,4},{7,3},{8,10},{9,13},{10,... | collective-permute-start | bytes 2359304 | tf_op jit(solution)/shard_map/ppermute | solution.py:537
  170.8 12.1 %collective-permute-start.23 = (bf16[4,64,1536]{2,1,0:T(8,128)(2,1)S(1)}, bf16[4,64,1536]{2,1,0:T(8,128)(2,1)S(1)}, u32[]{:S(2)}, u32[]{:S(2)}) collective-permute-start(bf16[4,64,1536]{2,1,0:T(8,128)(2,1)S(1)} %add_convert_fusion), channel_id=1, source_target_pairs={{0,2},{1,5},{2,0},{3,7},{4,6},{5,1},{6,4},{7,3},{8,10},{9,13},{10,... | collective-permute-start | bytes 2359304 | tf_op jit(solution)/shard_map/ppermute | solution.py:537
  171.0 12.0 %collective-permute-start.20 = (bf16[2,64,1536]{2,1,0:T(8,128)(2,1)S(1)}, bf16[2,64,1536]{2,1,0:T(8,128)(2,1)S(1)}, u32[]{:S(2)}, u32[]{:S(2)}) collective-permute-start(bf16[2,64,1536]{2,1,0:T(8,128)(2,1)S(1)} %pad_maximum_fusion.1), channel_id=1, source_target_pairs={{0,8},{1,9},{2,10},{3,11},{4,12},{5,13},{6,14},{7,15},{8,0},{9,1},... | collective-permute-start | bytes 1179656 | tf_op jit(solution)/shard_map/ppermute | solution.py:537
  183.0 10.1 %collective-permute-start.24 = (bf16[2,64,1536]{2,1,0:T(8,128)(2,1)S(1)}, bf16[2,64,1536]{2,1,0:T(8,128)(2,1)S(1)}, u32[]{:S(2)}, u32[]{:S(2)}) collective-permute-start(bf16[2,64,1536]{2,1,0:T(8,128)(2,1)S(1)} %pad_maximum_fusion.2), channel_id=1, source_target_pairs={{0,8},{1,9},{2,10},{3,11},{4,12},{5,13},{6,14},{7,15},{8,0},{9,1},... | collective-permute-start | bytes 1179656 | tf_op jit(solution)/shard_map/ppermute | solution.py:537
  183.2 12.3 %collective-permute-start.21 = (bf16[64,1536]{1,0:T(8,128)(2,1)S(1)}, bf16[64,1536]{1,0:T(8,128)(2,1)S(1)}, u32[]{:S(2)}, u32[]{:S(2)}) collective-permute-start(bf16[64,1536]{1,0:T(8,128)(2,1)S(1)} %fusion.2), channel_id=1, source_target_pairs={{0,16},{1,17},{2,18},{3,19},{4,20},{5,21},{6,22},{7,23},{8,24},{9,... | collective-permute-start | bytes 589832 | tf_op jit(solution)/shard_map/ppermute | solution.py:537
  193.2 8.2 %collective-permute-start.25 = (bf16[64,1536]{1,0:T(8,128)(2,1)S(1)}, bf16[64,1536]{1,0:T(8,128)(2,1)S(1)}, u32[]{:S(2)}, u32[]{:S(2)}) collective-permute-start(bf16[64,1536]{1,0:T(8,128)(2,1)S(1)} %fusion.3), channel_id=1, source_target_pairs={{0,16},{1,17},{2,18},{3,19},{4,20},{5,21},{6,22},{7,23},{8,24},{9,... | collective-permute-start | bytes 589832 | tf_op jit(solution)/shard_map/ppermute | solution.py:537
  (11 other events, 104.8 us)

commit v8 on v7

--- a/solution.py
+++ b/solution.py
@@ -20,7 +20,6 @@
 score_scale = 0.015625
 rope_base = 10000.0
 neg_big = -1e30
-log2_e = math.log2(math.e)
 
 BOTH = ("req", "seq")
 
@@ -170,7 +169,7 @@
             preferred_element_type=jnp.float32,
         )
         best = jnp.max(scores, axis=-1, keepdims=True)
-        weights = jnp.exp2(((scores - best) * log2_e).astype(jnp.bfloat16))
+        weights = jnp.exp(scores - best).astype(jnp.bfloat16)
         sums = jnp.dot(weights, values[...], preferred_element_type=jnp.float32)
         mean = sums[:, :LANES] / sums[:, LANES:]
         heads += [mean[i : i + rows] for i in range(0, batch, rows)]
@@ -543,20 +542,6 @@
     return [value] + [shift(value, "z", k) for k in range(1, sizes["z"])]
 
 
-def gather_line_doubling(value, shift, sizes):
-    line, step = {0: value}, sizes["z"] // 2
-    while step:
-        known = sorted(line)
-        if len(known) == 1:
-            arrived = [shift(line[0], "z", step)]
-        else:
-            arrived = shift(jnp.stack([line[k] for k in known]), "z", step)
-        for place, k in enumerate(known):
-            line[k ^ step] = arrived[place]
-        step //= 2
-    return [line[k] for k in range(sizes["z"])]
-
-
 def scatter_line(line, shift, sizes):
     step = 1
     while step < sizes["z"]:
@@ -568,7 +553,7 @@
         for place, k in enumerate(kept):
             line[k] = line[k] + [arrived[place]]
         step *= 2
-    return add_all(line[0])
+    return line[0]
 
 
 def gather_planes(line, shift, sizes, before):
@@ -592,16 +577,18 @@
     return [plane[0]] + [shift(v, "a", -j) for j, v in enumerate(plane) if j]
 
 
+def scatter_plane(terms, shift, sizes):
+    return scatter_line({i: [t[i] for t in terms] for i in range(sizes["z"])}, shift, sizes)
+
+
 def scatter_chunks(own, others, shift, sizes):
-    sums, before = [], []
-    for line, sending in zip(own, others):
-        if before:
-            sending, _ = lax.optimization_barrier((sending, before))
-        terms = [leave_along_a(plane, shift) for plane in sending]
-        before = [v for moved in terms for v in moved[1:]]
-        line = line + [shift(add_all(t), "b", -k - 1) for k, t in enumerate(terms)]
-        parts = {i: [t[i] for t in line] for i in range(sizes["z"])}
-        sums.append(scatter_line(parts, shift, sizes))
+    sums = []
+    for terms, sending in zip(own, others):
+        found = scatter_plane(terms, shift, sizes)
+        for k, plane in enumerate(sending):
+            part = scatter_plane(leave_along_a(plane, shift), shift, sizes)
+            found = found + [shift(add_all(part), "b", -k - 1)]
+        sums.append(add_all(found))
     total = jnp.zeros((sum(v.shape[0] for v in sums), sums[0].shape[1]), sums[0].dtype)
     first = 0
     for value in sums:
@@ -698,8 +685,10 @@
             [up_other, down_other] if index else [],
         )
         filled = [attended, stream]
-        gather = gather_line_doubling if index else gather_line
-        lines.append(gather(expert_in, shift, sizes))
+        sent = expert_in
+        if index:
+            sent, _ = lax.optimization_barrier((sent, lines[0][1:]))
+        lines.append(gather_line(sent, shift, sizes))
     first, second = lines
     planes = gather_planes(stack_rows(first, [expert_in]), shift, sizes, second[1:])
     stacked = stack_rows(second, [plane[0] for plane in planes[1:]])
@@ -722,6 +711,7 @@
         mixed = mix_rows(held, back, sizes["a"], cuts, [v for line in own for v in line[1:]])
         chunks = [[piece[i] for piece in mixed] for i in range(len(cuts))]
         if index == 0:
+            chunks, _ = lax.optimization_barrier((chunks, halves[1][1:]))
             own = [leave_along_a(plane, shift) for plane in chunks]
         else:
             others.append(chunks)

time: 203 us -> 194 us (0.956)
  waiting for transfers between devices: 105 us -> 88.5 us
  starting transfers between devices: 26 us -> 32.2 us
  local copies, waits for them, and re-layouts: 2.33 us -> 4.39 us
    ppermute x21 -> x26, waiting for transfers between devices: 104 us -> 87.2 us  [shift(): return lax.ppermute(value, BOTH, pairs(role, offset))]
    ppermute x21 -> x26, starting transfers between devices: 24.5 us -> 30.7 us  [shift(): return lax.ppermute(value, BOTH, pairs(role, offset))]
    unnamed x18 -> x20, local copies, waits for them, and re-layouts: 1.67 us -> 3.77 us
  transfers between devices with their start and end apart: 26 -> 31, of which waited for: 15 -> 17; matrix products, arithmetic and copies ran while one was open for 2% -> 3% of each run, Pallas kernels for 27% -> 28%
where the time goes in v8:
time: 194 us; the launch traced here: 193 us
  waiting for transfers between devices  88.5 us (46%)
  Pallas kernels  61.3 us (32%)
  starting transfers between devices  32.2 us (17%)
  other arithmetic  5.14 us (3%)
  local copies, waits for them, and re-layouts  4.39 us (2%)
    ppermute x26, waiting for transfers between devices, shift(): return lax.ppermute(value, BOTH, pairs(role, offset))  87.2 us
    ppermute x26, starting transfers between devices, shift(): return lax.ppermute(value, BOTH, pairs(role, offset))  30.7 us
    pallas_call x2, Pallas kernels, attend(): pl.pallas_call(functools.partial(attend_kernel, first_row, len(riders), l...  27.2 us
    pallas_call x2, Pallas kernels, run_experts(): pl.pallas_call(functools.partial(expert_kernel, pieces, tuple(in_cuts), l...  22.6 us
    pallas_call x1, Pallas kernels, project(): pl.pallas_call(qkv_kernel, grid=(5,), in_specs=[vmem_spec()] * 5 + [pl.Bl...  7.4 us
  transfers between devices with their start and end apart: 31, of which 17 were waited for; matrix products, arithmetic and copies ran while one was open for 3% of the time, Pallas kernels for 28%

profile of v8, /device:TPU:0, one launch (start us, length us, event | category | flops | bytes accessed | tf_op | source)
XLA Modules:
  0.0 193.2 jit_solution(5105646400001459988)
XLA Ops:
  5.8 7.4 %project_rows.1 = (bf16[128,1536]{1,0:T(8,128)(2,1)}, bf16[128,1024]{1,0:T(8,128)(2,1)}, bf16[128,1024]{1,0:T(8,128)(2,1)}) custom-call(bf16[128,1536]{1,0:T(8,128)(2,1)} %tokens_ref.3, bf16[128,1536]{1,0:T(8,128)(2,1)} %copy-done.7, f32[1536]{0:T(1024)} %gain_ref.3, f32[256,128]{1,0:T(8,128)} %pad_maximum_fusion.5.cos_ref, ...), custom_call_target="tpu_custom_call" | custom-call | flops 1409286144 | bytes 9500000 | tf_op jit(solution)/shard_map/project_rows/pallas_call | solution.py:84
  15.2 13.6 %attend_rows.2 = (bf16[128,1536]{1,0:T(8,128)(2,1)}, bf16[128,1536]{1,0:T(8,128)(2,1)}, bf16[72,1536]{1,0:T(8,128)(2,1)}) custom-call(s32[1]{0:T(128)} %copy.24.place_ref, bf16[128,1536]{1,0:T(8,128)(2,1)} %get-tuple-element.35.q_ref, bf16[1,1024,512]{2,1,0:T(8,128)(2,1)} %kc_ref.3, bf16[1,1024,512]{2,1,0:T(8,128)(2,1)} %collective-permute-done.1.refs_0_.kco_ref, ...), custom_call_target="tpu_custom_call" | custom-call | flops 7247757312 | bytes 10000000 | tf_op jit(solution)/shard_map/attend_rows/pallas_call | solution.py:222
  28.8 5.1 %collective-permute-start.7 = (bf16[72,1536]{1,0:T(8,128)(2,1)}, bf16[72,1536]{1,0:T(8,128)(2,1)S(1)}, u32[]{:S(2)}, u32[]{:S(2)}) collective-permute-start(bf16[72,1536]{1,0:T(8,128)(2,1)} %get-tuple-element.44.refs_0_), channel_id=1, source_target_pairs={{0,24},{1,25},{2,26},{3,27},{4,28},{5,29},{6,30},{7,31},{8,16},{9,... | collective-permute-start | bytes 663560 | tf_op jit(solution)/shard_map/ppermute | solution.py:536
  34.5 13.6 %attend_rows.3 = (bf16[128,1536]{1,0:T(8,128)(2,1)}, bf16[128,1536]{1,0:T(8,128)(2,1)}, bf16[64,1536]{1,0:T(8,128)(2,1)}) custom-call(s32[1]{0:T(128)} %copy.24.place_ref, bf16[128,1536]{1,0:T(8,128)(2,1)} %get-tuple-element.35.q_ref, bf16[1,1024,512]{2,1,0:T(8,128)(2,1)} %kc_ref.3, ...), custom_call_target="tpu_custom_call", output_to_operand_aliasing={{0}: (13, {}), {1}: (14, {})} | custom-call | flops 7247757312 | bytes 10000000 | tf_op jit(solution)/shard_map/attend_rows/pallas_call | solution.py:222
  48.1 5.0 %collective-permute-done.6.refs_2_ = bf16[72,1536]{1,0:T(8,128)(2,1)S(1)} collective-permute-done((bf16[72,1536]{1,0:T(8,128)(2,1)}, bf16[72,1536]{1,0:T(8,128)(2,1)S(1)}, u32[]{:S(2)}, u32[]{:S(2)}) %collective-permute-start.6) | collective-permute-done | bytes 221216 | tf_op jit(solution)/shard_map/ppermute | solution.py:536
  55.7 2.5 %collective-permute-start.10 = (bf16[64,1536]{1,0:T(8,128)(2,1)S(1)}, bf16[64,1536]{1,0:T(8,128)(2,1)S(1)}, u32[]{:S(2)}, u32[]{:S(2)}) collective-permute-start(bf16[64,1536]{1,0:T(8,128)(2,1)S(1)} %copy-done), channel_id=1, source_target_pairs={{0,24},{1,25},{2,26},{3,27},{4,28},{5,29},{6,30},{7,31},{8,16},{9,... | collective-permute-start | bytes 589832 | tf_op jit(solution)/shard_map/ppermute | solution.py:536
  61.6 3.8 %collective-permute-done.10.refs_3_ = bf16[64,1536]{1,0:T(8,128)(2,1)S(1)} collective-permute-done((bf16[64,1536]{1,0:T(8,128)(2,1)S(1)}, bf16[64,1536]{1,0:T(8,128)(2,1)S(1)}, u32[]{:S(2)}, u32[]{:S(2)}) %collective-permute-start.10) | collective-permute-done | bytes 196640 | tf_op jit(solution)/shard_map/ppermute | solution.py:536
  65.4 7.9 %collective-permute-done.9.refs_2_ = bf16[64,1536]{1,0:T(8,128)(2,1)S(1)} collective-permute-done((bf16[64,1536]{1,0:T(8,128)(2,1)S(1)}, bf16[64,1536]{1,0:T(8,128)(2,1)S(1)}, u32[]{:S(2)}, u32[]{:S(2)}) %collective-permute-start.9) | collective-permute-done | bytes 196640 | tf_op jit(solution)/shard_map/ppermute | solution.py:536
  74.5 2.6 %collective-permute-start.13 = (bf16[4,64,1536]{2,1,0:T(8,128)(2,1)S(1)}, bf16[4,64,1536]{2,1,0:T(8,128)(2,1)}, u32[]{:S(2)}, u32[]{:S(2)}) collective-permute-start(bf16[4,64,1536]{2,1,0:T(8,128)(2,1)S(1)} %stack_rows.3.refs_1_), channel_id=1, source_target_pairs={{0,4},{1,3},{2,6},{3,1},{4,0},{5,7},{6,2},{7,5},{8,12},{9,11},{10,... | collective-permute-start | bytes 2359304 | tf_op jit(solution)/shard_map/ppermute | solution.py:536
  80.3 15.4 %collective-permute-done.13.refs_3_ = bf16[4,64,1536]{2,1,0:T(8,128)(2,1)} collective-permute-done((bf16[4,64,1536]{2,1,0:T(8,128)(2,1)S(1)}, bf16[4,64,1536]{2,1,0:T(8,128)(2,1)}, u32[]{:S(2)}, u32[]{:S(2)}) %collective-permute-start.13) | collective-permute-done | bytes 786464 | tf_op jit(solution)/shard_map/ppermute | solution.py:536
  99.1 11.5 %run_experts.2.held_ref.refs_10_ = bf16[4,256,1536]{2,1,0:T(8,128)(2,1)S(1)} custom-call(bf16[4,72,1536]{2,1,0:T(8,128)(2,1)S(1)} %stack_rows.2.refs_0_, bf16[4,64,1536]{2,1,0:T(8,128)(2,1)S(1)} %stack_rows.3.refs_1_, bf16[4,72,1536]{2,1,0:T(8,128)(2,1)S(1)} %collective-permute-done.12.refs_1_.refs_2_, bf16[4,64,1536]{2,1,0:T(8,128)(2,1)} %collective-permute-done.13.refs_3_, ...), custom_call_target="tpu_custom_call" | custom-call | flops 8053063680 | bytes 26000000 | tf_op jit(solution)/shard_map/run_experts/pallas_call | solution.py:415
  111.6 2.1 %collective-permute-start.16 = (bf16[4,64,1536]{2,1,0:T(8,128)(2,1)S(1)}, bf16[4,64,1536]{2,1,0:T(8,128)(2,1)S(1)}, u32[]{:S(2)}, u32[]{:S(2)}) collective-permute-start(bf16[4,64,1536]{2,1,0:T(8,128)(2,1)S(1)} %get-tuple-element.55), channel_id=1, source_target_pairs={{0,4},{1,3},{2,6},{3,1},{4,0},{5,7},{6,2},{7,5},{8,12},{9,11},{10,... | collective-permute-start | bytes 2359304 | tf_op jit(solution)/shard_map/ppermute | solution.py:536
  114.8 11.1 %run_experts.3.held_ref = bf16[4,256,1536]{2,1,0:T(8,128)(2,1)S(1)} custom-call(bf16[4,72,1536]{2,1,0:T(8,128)(2,1)S(1)} %collective-permute-done.11.refs_4_.refs_0_, bf16[4,64,1536]{2,1,0:T(8,128)(2,1)S(1)} %collective-permute-done.14.refs_1_, bf16[4,72,1536]{2,1,0:T(8,128)(2,1)S(1)} %collective-permute-done.19.refs_1_.refs_2_, ...), custom_call_target="tpu_custom_call" | custom-call | flops 8053063680 | bytes 26000000 | tf_op jit(solution)/shard_map/run_experts/pallas_call | solution.py:415
  126.2 5.9 %collective-permute-done.20.refs_1_ = bf16[4,64,1536]{2,1,0:T(8,128)(2,1)S(1)} collective-permute-done((bf16[4,64,1536]{2,1,0:T(8,128)(2,1)S(1)}, bf16[4,64,1536]{2,1,0:T(8,128)(2,1)S(1)}, u32[]{:S(2)}, u32[]{:S(2)}) %collective-permute-start.20) | collective-permute-done | bytes 786464 | tf_op jit(solution)/shard_map/ppermute | solution.py:536
  133.3 2.1 %collective-permute-start.21 = (bf16[4,64,1536]{2,1,0:T(8,128)(2,1)S(1)}, bf16[4,64,1536]{2,1,0:T(8,128)(2,1)S(1)}, u32[]{:S(2)}, u32[]{:S(2)}) collective-permute-start(bf16[4,64,1536]{2,1,0:T(8,128)(2,1)S(1)} %get-tuple-element.62), channel_id=1, source_target_pairs={{0,4},{1,3},{2,6},{3,1},{4,0},{5,7},{6,2},{7,5},{8,12},{9,11},{10,... | collective-permute-start | bytes 2359304 | tf_op jit(solution)/shard_map/ppermute | solution.py:536
  135.4 2.8 %collective-permute-done.17 = bf16[2,64,1536]{2,1,0:T(8,128)(2,1)S(1)} collective-permute-done((bf16[2,64,1536]{2,1,0:T(8,128)(2,1)S(1)}, bf16[2,64,1536]{2,1,0:T(8,128)(2,1)S(1)}, u32[]{:S(2)}, u32[]{:S(2)}) %collective-permute-start.17) | collective-permute-done | bytes 393248 | tf_op jit(solution)/shard_map/ppermute | solution.py:536
  139.4 10.2 %collective-permute-done.25 = bf16[2,64,1536]{2,1,0:T(8,128)(2,1)S(1)} collective-permute-done((bf16[2,64,1536]{2,1,0:T(8,128)(2,1)S(1)}, bf16[2,64,1536]{2,1,0:T(8,128)(2,1)S(1)}, u32[]{:S(2)}, u32[]{:S(2)}) %collective-permute-start.25) | collective-permute-done | bytes 393248 | tf_op jit(solution)/shard_map/ppermute | solution.py:536
  150.0 2.5 %collective-permute-start.22 = (bf16[2,64,1536]{2,1,0:T(8,128)(2,1)S(1)}, bf16[2,64,1536]{2,1,0:T(8,128)(2,1)S(1)}, u32[]{:S(2)}, u32[]{:S(2)}) collective-permute-start(bf16[2,64,1536]{2,1,0:T(8,128)(2,1)S(1)} %pad_maximum_fusion.1), channel_id=1, source_target_pairs={{0,8},{1,9},{2,10},{3,11},{4,12},{5,13},{6,14},{7,15},{8,0},{9,1},... | collective-permute-start | bytes 1179656 | tf_op jit(solution)/shard_map/ppermute | solution.py:536
  156.0 12.5 %collective-permute-done.22 = bf16[2,64,1536]{2,1,0:T(8,128)(2,1)S(1)} collective-permute-done((bf16[2,64,1536]{2,1,0:T(8,128)(2,1)S(1)}, bf16[2,64,1536]{2,1,0:T(8,128)(2,1)S(1)}, u32[]{:S(2)}, u32[]{:S(2)}) %collective-permute-start.22) | collective-permute-done | bytes 393248 | tf_op jit(solution)/shard_map/ppermute | solution.py:536
  168.6 6.9 %collective-permute-done.28 = bf16[2,64,1536]{2,1,0:T(8,128)(2,1)S(1)} collective-permute-done((bf16[2,64,1536]{2,1,0:T(8,128)(2,1)S(1)}, bf16[2,64,1536]{2,1,0:T(8,128)(2,1)S(1)}, u32[]{:S(2)}, u32[]{:S(2)}) %collective-permute-start.28) | collective-permute-done | bytes 393248 | tf_op jit(solution)/shard_map/ppermute | solution.py:536
  175.9 7.6 %collective-permute-done.23 = bf16[64,1536]{1,0:T(8,128)(2,1)S(1)} collective-permute-done((bf16[64,1536]{1,0:T(8,128)(2,1)S(1)}, bf16[64,1536]{1,0:T(8,128)(2,1)S(1)}, u32[]{:S(2)}, u32[]{:S(2)}) %collective-permute-start.23) | collective-permute-done | bytes 196640 | tf_op jit(solution)/shard_map/ppermute | solution.py:536
  184.1 2.4 %collective-permute-done.29 = bf16[64,1536]{1,0:T(8,128)(2,1)S(1)} collective-permute-done((bf16[64,1536]{1,0:T(8,128)(2,1)S(1)}, bf16[64,1536]{1,0:T(8,128)(2,1)S(1)}, u32[]{:S(2)}, u32[]{:S(2)}) %collective-permute-start.29) | collective-permute-done | bytes 196640 | tf_op jit(solution)/shard_map/ppermute | solution.py:536
  186.7 2.8 %collective-permute-done.24 = bf16[64,1536]{1,0:T(8,128)(2,1)S(1)} collective-permute-done((bf16[64,1536]{1,0:T(8,128)(2,1)S(1)}, bf16[64,1536]{1,0:T(8,128)(2,1)S(1)}, u32[]{:S(2)}, u32[]{:S(2)}) %collective-permute-start.24) | collective-permute-done | bytes 196640 | tf_op jit(solution)/shard_map/ppermute | solution.py:536
  189.6 2.7 %collective-permute-done.30 = bf16[64,1536]{1,0:T(8,128)(2,1)S(1)} collective-permute-done((bf16[64,1536]{1,0:T(8,128)(2,1)S(1)}, bf16[64,1536]{1,0:T(8,128)(2,1)S(1)}, u32[]{:S(2)}, u32[]{:S(2)}) %collective-permute-start.30) | collective-permute-done | bytes 196640 | tf_op jit(solution)/shard_map/ppermute | solution.py:536
  (101 shorter events, 31.7 us)
Async XLA Ops:
  13.2 21.2 %collective-permute-start.3 = (bf16[2,1536,1024]{2,1,0:T(8,128)(2,1)}, bf16[2,1536,1024]{2,1,0:T(8,128)(2,1)}, u32[]{:S(2)}, u32[]{:S(2)}) collective-permute-start(bf16[2,1536,1024]{2,1,0:T(8,128)(2,1)} %refs_6_.3), channel_id=1, source_target_pairs={{0,1},{1,0},{2,3},{3,2},{4,5},{5,4},{6,7},{7,6},{8,9},{9,8},{10,11... | collective-permute-start | bytes 18874376 | tf_op jit(solution)/shard_map/ppermute | solution.py:636
  13.6 20.8 %collective-permute-start.4 = (bf16[2,512,1536]{2,1,0:T(8,128)(2,1)S(1)}, bf16[2,512,1536]{2,1,0:T(8,128)(2,1)}, u32[]{:S(2)}, u32[]{:S(2)}) collective-permute-start(bf16[2,512,1536]{2,1,0:T(8,128)(2,1)S(1)} %copy-done.3), channel_id=1, source_target_pairs={{0,1},{1,0},{2,3},{3,2},{4,5},{5,4},{6,7},{7,6},{8,9},{9,8},{10,11... | collective-permute-start | bytes 9437192 | tf_op jit(solution)/shard_map/ppermute | solution.py:636
  28.8 19.3 %collective-permute-start.7 = (bf16[72,1536]{1,0:T(8,128)(2,1)}, bf16[72,1536]{1,0:T(8,128)(2,1)S(1)}, u32[]{:S(2)}, u32[]{:S(2)}) collective-permute-start(bf16[72,1536]{1,0:T(8,128)(2,1)} %get-tuple-element.44.refs_0_), channel_id=1, source_target_pairs={{0,24},{1,25},{2,26},{3,27},{4,28},{5,29},{6,30},{7,31},{8,16},{9,... | collective-permute-start | bytes 663560 | tf_op jit(solution)/shard_map/ppermute | solution.py:536
  33.8 19.3 %collective-permute-start.6 = (bf16[72,1536]{1,0:T(8,128)(2,1)}, bf16[72,1536]{1,0:T(8,128)(2,1)S(1)}, u32[]{:S(2)}, u32[]{:S(2)}) collective-permute-start(bf16[72,1536]{1,0:T(8,128)(2,1)} %get-tuple-element.44.refs_0_), channel_id=1, source_target_pairs={{0,16},{1,17},{2,18},{3,19},{4,20},{5,21},{6,22},{7,23},{8,24},{9,... | collective-permute-start | bytes 663560 | tf_op jit(solution)/shard_map/ppermute | solution.py:536
  33.8 19.3 %collective-permute-start.5 = (bf16[72,1536]{1,0:T(8,128)(2,1)}, bf16[72,1536]{1,0:T(8,128)(2,1)S(1)}, u32[]{:S(2)}, u32[]{:S(2)}) collective-permute-start(bf16[72,1536]{1,0:T(8,128)(2,1)} %get-tuple-element.44.refs_0_), channel_id=1, source_target_pairs={{0,8},{1,9},{2,10},{3,11},{4,12},{5,13},{6,14},{7,15},{8,0},{9,1},... | collective-permute-start | bytes 663560 | tf_op jit(solution)/shard_map/ppermute | solution.py:536
  54.1 19.4 %collective-permute-start.11 = (bf16[4,72,1536]{2,1,0:T(8,128)(2,1)S(1)}, bf16[4,72,1536]{2,1,0:T(8,128)(2,1)S(1)}, u32[]{:S(2)}, u32[]{:S(2)}) collective-permute-start(bf16[4,72,1536]{2,1,0:T(8,128)(2,1)S(1)} %stack_rows.2.refs_0_), channel_id=1, source_target_pairs={{0,2},{1,5},{2,0},{3,7},{4,6},{5,1},{6,4},{7,3},{8,10},{9,13},{10,... | collective-permute-start | bytes 2654216 | tf_op jit(solution)/shard_map/ppermute | solution.py:536
  58.2 15.2 %collective-permute-start.9 = (bf16[64,1536]{1,0:T(8,128)(2,1)S(1)}, bf16[64,1536]{1,0:T(8,128)(2,1)S(1)}, u32[]{:S(2)}, u32[]{:S(2)}) collective-permute-start(bf16[64,1536]{1,0:T(8,128)(2,1)S(1)} %copy-done), channel_id=1, source_target_pairs={{0,16},{1,17},{2,18},{3,19},{4,20},{5,21},{6,22},{7,23},{8,24},{9,... | collective-permute-start | bytes 589832 | tf_op jit(solution)/shard_map/ppermute | solution.py:536
  58.2 15.2 %collective-permute-start.8 = (bf16[64,1536]{1,0:T(8,128)(2,1)S(1)}, bf16[64,1536]{1,0:T(8,128)(2,1)S(1)}, u32[]{:S(2)}, u32[]{:S(2)}) collective-permute-start(bf16[64,1536]{1,0:T(8,128)(2,1)S(1)} %copy-done), channel_id=1, source_target_pairs={{0,8},{1,9},{2,10},{3,11},{4,12},{5,13},{6,14},{7,15},{8,0},{9,1},... | collective-permute-start | bytes 589832 | tf_op jit(solution)/shard_map/ppermute | solution.py:536
  60.1 18.7 %collective-permute-start.12 = (bf16[4,72,1536]{2,1,0:T(8,128)(2,1)S(1)}, bf16[4,72,1536]{2,1,0:T(8,128)(2,1)S(1)}, u32[]{:S(2)}, u32[]{:S(2)}) collective-permute-start(bf16[4,72,1536]{2,1,0:T(8,128)(2,1)S(1)} %stack_rows.2.refs_0_), channel_id=1, source_target_pairs={{0,4},{1,3},{2,6},{3,1},{4,0},{5,7},{6,2},{7,5},{8,12},{9,11},{10,... | collective-permute-start | bytes 2654216 | tf_op jit(solution)/shard_map/ppermute | solution.py:536
  74.5 21.1 %collective-permute-start.13 = (bf16[4,64,1536]{2,1,0:T(8,128)(2,1)S(1)}, bf16[4,64,1536]{2,1,0:T(8,128)(2,1)}, u32[]{:S(2)}, u32[]{:S(2)}) collective-permute-start(bf16[4,64,1536]{2,1,0:T(8,128)(2,1)S(1)} %stack_rows.3.refs_1_), channel_id=1, source_target_pairs={{0,4},{1,3},{2,6},{3,1},{4,0},{5,7},{6,2},{7,5},{8,12},{9,11},{10,... | collective-permute-start | bytes 2359304 | tf_op jit(solution)/shard_map/ppermute | solution.py:536
  77.2 34.4 %collective-permute-start.14 = (bf16[4,64,1536]{2,1,0:T(8,128)(2,1)S(1)}, bf16[4,64,1536]{2,1,0:T(8,128)(2,1)S(1)}, u32[]{:S(2)}, u32[]{:S(2)}) collective-permute-start(bf16[4,64,1536]{2,1,0:T(8,128)(2,1)S(1)} %stack_rows.3.refs_1_), channel_id=1, source_target_pairs={{0,2},{1,5},{2,0},{3,7},{4,6},{5,1},{6,4},{7,3},{8,10},{9,13},{10,... | collective-permute-start | bytes 2359304 | tf_op jit(solution)/shard_map/ppermute | solution.py:536
  78.7 34.9 %collective-permute-start.19 = (bf16[4,72,1536]{2,1,0:T(8,128)(2,1)S(1)}, bf16[4,72,1536]{2,1,0:T(8,128)(2,1)S(1)}, u32[]{:S(2)}, u32[]{:S(2)}) collective-permute-start(bf16[4,72,1536]{2,1,0:T(8,128)(2,1)S(1)} %collective-permute-done.12.refs_1_.refs_2_), channel_id=1, source_target_pairs={{0,2},{1,5},{2,0},{3,7},{4,6},{5,1},{6,4},{7,3},{8,10},{9,13},{10,... | collective-permute-start | bytes 2654216 | tf_op jit(solution)/shard_map/ppermute | solution.py:536
  95.7 15.9 %collective-permute-start.15 = (bf16[4,64,1536]{2,1,0:T(8,128)(2,1)}, bf16[4,64,1536]{2,1,0:T(8,128)(2,1)S(1)}, u32[]{:S(2)}, u32[]{:S(2)}) collective-permute-start(bf16[4,64,1536]{2,1,0:T(8,128)(2,1)} %collective-permute-done.13.refs_3_), channel_id=1, source_target_pairs={{0,2},{1,5},{2,0},{3,7},{4,6},{5,1},{6,4},{7,3},{8,10},{9,13},{10,... | collective-permute-start | bytes 2359304 | tf_op jit(solution)/shard_map/ppermute | solution.py:536
  111.6 14.4 %collective-permute-start.16 = (bf16[4,64,1536]{2,1,0:T(8,128)(2,1)S(1)}, bf16[4,64,1536]{2,1,0:T(8,128)(2,1)S(1)}, u32[]{:S(2)}, u32[]{:S(2)}) collective-permute-start(bf16[4,64,1536]{2,1,0:T(8,128)(2,1)S(1)} %get-tuple-element.55), channel_id=1, source_target_pairs={{0,4},{1,3},{2,6},{3,1},{4,0},{5,7},{6,2},{7,5},{8,12},{9,11},{10,... | collective-permute-start | bytes 2359304 | tf_op jit(solution)/shard_map/ppermute | solution.py:536
  114.8 17.3 %collective-permute-start.20 = (bf16[4,64,1536]{2,1,0:T(8,128)(2,1)S(1)}, bf16[4,64,1536]{2,1,0:T(8,128)(2,1)S(1)}, u32[]{:S(2)}, u32[]{:S(2)}) collective-permute-start(bf16[4,64,1536]{2,1,0:T(8,128)(2,1)S(1)} %get-tuple-element.60), channel_id=1, source_target_pairs={{0,4},{1,3},{2,6},{3,1},{4,0},{5,7},{6,2},{7,5},{8,12},{9,11},{10,... | collective-permute-start | bytes 2359304 | tf_op jit(solution)/shard_map/ppermute | solution.py:536
  126.1 12.1 %collective-permute-start.17 = (bf16[2,64,1536]{2,1,0:T(8,128)(2,1)S(1)}, bf16[2,64,1536]{2,1,0:T(8,128)(2,1)S(1)}, u32[]{:S(2)}, u32[]{:S(2)}) collective-permute-start(bf16[2,64,1536]{2,1,0:T(8,128)(2,1)S(1)} %pad_maximum_fusion), channel_id=1, source_target_pairs={{0,8},{1,9},{2,10},{3,11},{4,12},{5,13},{6,14},{7,15},{8,0},{9,1},... | collective-permute-start | bytes 1179656 | tf_op jit(solution)/shard_map/ppermute | solution.py:536
  132.2 17.4 %collective-permute-start.25 = (bf16[2,64,1536]{2,1,0:T(8,128)(2,1)S(1)}, bf16[2,64,1536]{2,1,0:T(8,128)(2,1)S(1)}, u32[]{:S(2)}, u32[]{:S(2)}) collective-permute-start(bf16[2,64,1536]{2,1,0:T(8,128)(2,1)S(1)} %pad_maximum_fusion.2), channel_id=1, source_target_pairs={{0,8},{1,9},{2,10},{3,11},{4,12},{5,13},{6,14},{7,15},{8,0},{9,1},... | collective-permute-start | bytes 1179656 | tf_op jit(solution)/shard_map/ppermute | solution.py:536
  133.3 16.6 %collective-permute-start.21 = (bf16[4,64,1536]{2,1,0:T(8,128)(2,1)S(1)}, bf16[4,64,1536]{2,1,0:T(8,128)(2,1)S(1)}, u32[]{:S(2)}, u32[]{:S(2)}) collective-permute-start(bf16[4,64,1536]{2,1,0:T(8,128)(2,1)S(1)} %get-tuple-element.62), channel_id=1, source_target_pairs={{0,4},{1,3},{2,6},{3,1},{4,0},{5,7},{6,2},{7,5},{8,12},{9,11},{10,... | collective-permute-start | bytes 2359304 | tf_op jit(solution)/shard_map/ppermute | solution.py:536
  135.3 18.4 %collective-permute-start.27 = (bf16[4,64,1536]{2,1,0:T(8,128)(2,1)S(1)}, bf16[4,64,1536]{2,1,0:T(8,128)(2,1)S(1)}, u32[]{:S(2)}, u32[]{:S(2)}) collective-permute-start(bf16[4,64,1536]{2,1,0:T(8,128)(2,1)S(1)} %get-tuple-element.65), channel_id=1, source_target_pairs={{0,4},{1,3},{2,6},{3,1},{4,0},{5,7},{6,2},{7,5},{8,12},{9,11},{10,... | collective-permute-start | bytes 2359304 | tf_op jit(solution)/shard_map/ppermute | solution.py:536
  138.3 48.4 %collective-permute-start.18 = (bf16[64,1536]{1,0:T(8,128)(2,1)S(1)}, bf16[64,1536]{1,0:T(8,128)(2,1)S(1)}, u32[]{:S(2)}, u32[]{:S(2)}) collective-permute-start(bf16[64,1536]{1,0:T(8,128)(2,1)S(1)} %fusion.6), channel_id=1, source_target_pairs={{0,16},{1,17},{2,18},{3,19},{4,20},{5,21},{6,22},{7,23},{8,24},{9,... | collective-permute-start | bytes 589832 | tf_op jit(solution)/shard_map/ppermute | solution.py:536
  149.7 39.9 %collective-permute-start.26 = (bf16[64,1536]{1,0:T(8,128)(2,1)S(1)}, bf16[64,1536]{1,0:T(8,128)(2,1)S(1)}, u32[]{:S(2)}, u32[]{:S(2)}) collective-permute-start(bf16[64,1536]{1,0:T(8,128)(2,1)S(1)} %fusion.8), channel_id=1, source_target_pairs={{0,16},{1,17},{2,18},{3,19},{4,20},{5,21},{6,22},{7,23},{8,24},{9,... | collective-permute-start | bytes 589832 | tf_op jit(solution)/shard_map/ppermute | solution.py:536
  150.0 18.4 %collective-permute-start.22 = (bf16[2,64,1536]{2,1,0:T(8,128)(2,1)S(1)}, bf16[2,64,1536]{2,1,0:T(8,128)(2,1)S(1)}, u32[]{:S(2)}, u32[]{:S(2)}) collective-permute-start(bf16[2,64,1536]{2,1,0:T(8,128)(2,1)S(1)} %pad_maximum_fusion.1), channel_id=1, source_target_pairs={{0,8},{1,9},{2,10},{3,11},{4,12},{5,13},{6,14},{7,15},{8,0},{9,1},... | collective-permute-start | bytes 1179656 | tf_op jit(solution)/shard_map/ppermute | solution.py:536
  153.9 21.6 %collective-permute-start.28 = (bf16[2,64,1536]{2,1,0:T(8,128)(2,1)S(1)}, bf16[2,64,1536]{2,1,0:T(8,128)(2,1)S(1)}, u32[]{:S(2)}, u32[]{:S(2)}) collective-permute-start(bf16[2,64,1536]{2,1,0:T(8,128)(2,1)S(1)} %pad_maximum_fusion.3), channel_id=1, source_target_pairs={{0,8},{1,9},{2,10},{3,11},{4,12},{5,13},{6,14},{7,15},{8,0},{9,1},... | collective-permute-start | bytes 1179656 | tf_op jit(solution)/shard_map/ppermute | solution.py:536
  168.6 15.0 %collective-permute-start.23 = (bf16[64,1536]{1,0:T(8,128)(2,1)S(1)}, bf16[64,1536]{1,0:T(8,128)(2,1)S(1)}, u32[]{:S(2)}, u32[]{:S(2)}) collective-permute-start(bf16[64,1536]{1,0:T(8,128)(2,1)S(1)} %fusion.7), channel_id=1, source_target_pairs={{0,16},{1,17},{2,18},{3,19},{4,20},{5,21},{6,22},{7,23},{8,24},{9,... | collective-permute-start | bytes 589832 | tf_op jit(solution)/shard_map/ppermute | solution.py:536
  (17 other events, 103.9 us)

commit v9 on v8

--- a/solution.py
+++ b/solution.py
@@ -160,7 +160,7 @@
         wide_q[head * rows : (head + 1) * rows, :LANES] = part.astype(jnp.bfloat16)
 
     heads = []
-    batch = GROUP * rows
+    batch = 2 * GROUP * rows
     for first in range(0, 2 * GROUP * rows, batch):
         scores = lax.dot_general(
             wide_q[first : first + batch],
@@ -583,11 +583,17 @@
 
 def scatter_chunks(own, others, shift, sizes):
     sums = []
-    for terms, sending in zip(own, others):
-        found = scatter_plane(terms, shift, sizes)
-        for k, plane in enumerate(sending):
-            part = scatter_plane(leave_along_a(plane, shift), shift, sizes)
-            found = found + [shift(add_all(part), "b", -k - 1)]
+    for index, (terms, sending) in enumerate(zip(own, others)):
+        planes = [leave_along_a(plane, shift) for plane in sending]
+        if index == len(own) - 1:
+            for k, part in enumerate(planes):
+                terms = terms + [shift(add_all(part), "b", -k - 1)]
+            found = scatter_plane(terms, shift, sizes)
+        else:
+            found = scatter_plane(terms, shift, sizes)
+            for k, part in enumerate(planes):
+                total = add_all(scatter_plane(part, shift, sizes))
+                found = found + [shift(total, "b", -k - 1)]
         sums.append(add_all(found))
     total = jnp.zeros((sum(v.shape[0] for v in sums), sums[0].shape[1]), sums[0].dtype)
     first = 0
@@ -693,7 +699,7 @@
     planes = gather_planes(stack_rows(first, [expert_in]), shift, sizes, second[1:])
     stacked = stack_rows(second, [plane[0] for plane in planes[1:]])
     halves = [planes, gather_planes(stacked, shift, sizes, [])]
-    cuts = (row_count // 2, row_count - row_count // 2)
+    cuts = (5 * row_count // 8, row_count - 5 * row_count // 8)
     own, others, held = [], [], None
     for index in range(sizes["b"]):
         pick, back, share = plan_routes(
@@ -706,7 +712,7 @@
             (expert_up, up_other),
             (expert_down, down_other),
             (half, row_count - half),
-            [] if index == 0 else [held],
+            [held] if index else [v for plane in halves[0][1:] for v in plane],
         )
         mixed = mix_rows(held, back, sizes["a"], cuts, [v for line in own for v in line[1:]])
         chunks = [[piece[i] for piece in mixed] for i in range(len(cuts))]
@@ -716,6 +722,7 @@
         else:
             others.append(chunks)
     others = [[planes[i] for planes in others] for i in range(len(cuts))]
+    own, _ = lax.optimization_barrier((own, held))
     expert_mix = scatter_chunks(own, others, shift, sizes)
     return (attended, stream, expert_mix, appended)
 

time: 194 us -> 194 us (level)
    ppermute x26 -> x24, waiting for transfers between devices: 87.2 us -> 88.1 us  [shift(): return lax.ppermute(value, BOTH, pairs(role, offset))]
    ppermute x26 -> x24, starting transfers between devices: 30.7 us -> 30.6 us  [shift(): return lax.ppermute(value, BOTH, pairs(role, offset))]
  transfers between devices with their start and end apart: 31 -> 29, of which waited for: 17 -> 17; matrix products, arithmetic and copies ran while one was open for 3% -> 2% of each run, Pallas kernels for 28% -> 28%
where the time goes in v9:
time: 194 us
  waiting for transfers between devices  89.4 us (46%)
  Pallas kernels  62.2 us (32%)
  starting transfers between devices  32.1 us (17%)
  other arithmetic  5.1 us (3%)
  local copies, waits for them, and re-layouts  3.25 us (2%)
    ppermute x24, waiting for transfers between devices, shift(): return lax.ppermute(value, BOTH, pairs(role, offset))  88.1 us
    ppermute x24, starting transfers between devices, shift(): return lax.ppermute(value, BOTH, pairs(role, offset))  30.6 us
    pallas_call x2, Pallas kernels, attend(): pl.pallas_call(functools.partial(attend_kernel, first_row, len(riders), l...  26.7 us
    pallas_call x2, Pallas kernels, run_experts(): pl.pallas_call(functools.partial(expert_kernel, pieces, tuple(in_cuts), l...  23.3 us
    pallas_call x1, Pallas kernels, project(): pl.pallas_call(qkv_kernel, grid=(5,), in_specs=[vmem_spec()] * 5 + [pl.Bl...  7.4 us
  transfers between devices with their start and end apart: 29, of which 17 were waited for; matrix products, arithmetic and copies ran while one was open for 2% of the time, Pallas kernels for 28%

profile of v9, /device:TPU:0, one launch (start us, length us, event | category | flops | bytes accessed | tf_op | source)
XLA Modules:
  0.0 193.7 jit_solution(276586153046600886)
XLA Ops:
  5.8 7.4 %project_rows.1 = (bf16[128,1536]{1,0:T(8,128)(2,1)}, bf16[128,1024]{1,0:T(8,128)(2,1)}, bf16[128,1024]{1,0:T(8,128)(2,1)}) custom-call(bf16[128,1536]{1,0:T(8,128)(2,1)} %tokens_ref.3, bf16[128,1536]{1,0:T(8,128)(2,1)} %copy-done.6, f32[1536]{0:T(1024)} %gain_ref.3, f32[256,128]{1,0:T(8,128)} %pad_maximum_fusion.4.cos_ref, ...), custom_call_target="tpu_custom_call" | custom-call | flops 1409286144 | bytes 9500000 | tf_op jit(solution)/shard_map/project_rows/pallas_call | solution.py:84
  15.2 13.3 %attend_rows.2 = (bf16[128,1536]{1,0:T(8,128)(2,1)}, bf16[128,1536]{1,0:T(8,128)(2,1)}, bf16[72,1536]{1,0:T(8,128)(2,1)}) custom-call(s32[1]{0:T(128)} %copy.24.place_ref, bf16[128,1536]{1,0:T(8,128)(2,1)} %get-tuple-element.39.q_ref, bf16[1,1024,512]{2,1,0:T(8,128)(2,1)} %kc_ref.3, bf16[1,1024,512]{2,1,0:T(8,128)(2,1)} %collective-permute-done.1.refs_0_.kco_ref, ...), custom_call_target="tpu_custom_call" | custom-call | flops 7247757312 | bytes 10000000 | tf_op jit(solution)/shard_map/attend_rows/pallas_call | solution.py:222
  28.6 5.1 %collective-permute-start.7 = (bf16[72,1536]{1,0:T(8,128)(2,1)}, bf16[72,1536]{1,0:T(8,128)(2,1)S(1)}, u32[]{:S(2)}, u32[]{:S(2)}) collective-permute-start(bf16[72,1536]{1,0:T(8,128)(2,1)} %get-tuple-element.48.refs_0_), channel_id=1, source_target_pairs={{0,24},{1,25},{2,26},{3,27},{4,28},{5,29},{6,30},{7,31},{8,16},{9,... | collective-permute-start | bytes 663560 | tf_op jit(solution)/shard_map/ppermute | solution.py:536
  34.3 13.4 %attend_rows.3 = (bf16[128,1536]{1,0:T(8,128)(2,1)}, bf16[128,1536]{1,0:T(8,128)(2,1)}, bf16[64,1536]{1,0:T(8,128)(2,1)}) custom-call(s32[1]{0:T(128)} %copy.24.place_ref, bf16[128,1536]{1,0:T(8,128)(2,1)} %get-tuple-element.39.q_ref, bf16[1,1024,512]{2,1,0:T(8,128)(2,1)} %kc_ref.3, ...), custom_call_target="tpu_custom_call", output_to_operand_aliasing={{0}: (13, {}), {1}: (14, {})} | custom-call | flops 7247757312 | bytes 10000000 | tf_op jit(solution)/shard_map/attend_rows/pallas_call | solution.py:222
  47.7 5.2 %collective-permute-done.6.refs_2_ = bf16[72,1536]{1,0:T(8,128)(2,1)S(1)} collective-permute-done((bf16[72,1536]{1,0:T(8,128)(2,1)}, bf16[72,1536]{1,0:T(8,128)(2,1)S(1)}, u32[]{:S(2)}, u32[]{:S(2)}) %collective-permute-start.6) | collective-permute-done | bytes 221216 | tf_op jit(solution)/shard_map/ppermute | solution.py:536
  57.0 2.5 %collective-permute-start.10 = (bf16[64,1536]{1,0:T(8,128)(2,1)S(1)}, bf16[64,1536]{1,0:T(8,128)(2,1)S(1)}, u32[]{:S(2)}, u32[]{:S(2)}) collective-permute-start(bf16[64,1536]{1,0:T(8,128)(2,1)S(1)} %copy-done), channel_id=1, source_target_pairs={{0,24},{1,25},{2,26},{3,27},{4,28},{5,29},{6,30},{7,31},{8,16},{9,... | collective-permute-start | bytes 589832 | tf_op jit(solution)/shard_map/ppermute | solution.py:536
  59.5 1.9 collective-permute-start.8
  61.4 5.3 %collective-permute-done.10.refs_3_ = bf16[64,1536]{1,0:T(8,128)(2,1)S(1)} collective-permute-done((bf16[64,1536]{1,0:T(8,128)(2,1)S(1)}, bf16[64,1536]{1,0:T(8,128)(2,1)S(1)}, u32[]{:S(2)}, u32[]{:S(2)}) %collective-permute-start.10) | collective-permute-done | bytes 196640 | tf_op jit(solution)/shard_map/ppermute | solution.py:536
  66.7 7.8 %collective-permute-done.9.refs_2_ = bf16[64,1536]{1,0:T(8,128)(2,1)S(1)} collective-permute-done((bf16[64,1536]{1,0:T(8,128)(2,1)S(1)}, bf16[64,1536]{1,0:T(8,128)(2,1)S(1)}, u32[]{:S(2)}, u32[]{:S(2)}) %collective-permute-start.9) | collective-permute-done | bytes 196640 | tf_op jit(solution)/shard_map/ppermute | solution.py:536
  74.5 1.7 collective-permute-done.12.refs_1_.refs_2_
  79.3 1.9 collective-permute-start.15
  82.9 15.4 %collective-permute-done.13.refs_3_ = bf16[4,64,1536]{2,1,0:T(8,128)(2,1)} collective-permute-done((bf16[4,64,1536]{2,1,0:T(8,128)(2,1)S(1)}, bf16[4,64,1536]{2,1,0:T(8,128)(2,1)}, u32[]{:S(2)}, u32[]{:S(2)}) %collective-permute-start.13) | collective-permute-done | bytes 786464 | tf_op jit(solution)/shard_map/ppermute | solution.py:536
  99.9 12.2 %run_experts.2.held_ref.refs_10_ = bf16[4,256,1536]{2,1,0:T(8,128)(2,1)S(1)} custom-call(bf16[4,72,1536]{2,1,0:T(8,128)(2,1)S(1)} %stack_rows.2.refs_0_, bf16[4,64,1536]{2,1,0:T(8,128)(2,1)S(1)} %stack_rows.3.refs_1_, bf16[4,72,1536]{2,1,0:T(8,128)(2,1)} %collective-permute-done.12.refs_1_.refs_2_, bf16[4,64,1536]{2,1,0:T(8,128)(2,1)} %collective-permute-done.13.refs_3_, ...), custom_call_target="tpu_custom_call" | custom-call | flops 8053063680 | bytes 26000000 | tf_op jit(solution)/shard_map/run_experts/pallas_call | solution.py:415
  114.6 1.9 collective-permute-start.17
  117.8 11.1 %run_experts.3.held_ref = bf16[4,256,1536]{2,1,0:T(8,128)(2,1)S(1)} custom-call(bf16[4,72,1536]{2,1,0:T(8,128)(2,1)S(1)} %collective-permute-done.11.refs_4_.refs_10_.refs_0_, bf16[4,64,1536]{2,1,0:T(8,128)(2,1)S(1)} %collective-permute-done.15.refs_1_, bf16[4,72,1536]{2,1,0:T(8,128)(2,1)S(1)} %collective-permute-done.14.refs_11_.refs_1_.refs_2_, ...), custom_call_target="tpu_custom_call" | custom-call | flops 8053063680 | bytes 26000000 | tf_op jit(solution)/shard_map/run_experts/pallas_call | solution.py:415
  128.9 6.1 %collective-permute-done.18.refs_1_ = bf16[4,48,1536]{2,1,0:T(8,128)(2,1)S(1)} collective-permute-done((bf16[4,48,1536]{2,1,0:T(8,128)(2,1)S(1)}, bf16[4,48,1536]{2,1,0:T(8,128)(2,1)S(1)}, u32[]{:S(2)}, u32[]{:S(2)}) %collective-permute-start.18) | collective-permute-done | bytes 589856 | tf_op jit(solution)/shard_map/ppermute | solution.py:536
  136.3 2.0 %collective-permute-start.25 = (bf16[4,48,1536]{2,1,0:T(8,128)(2,1)S(1)}, bf16[4,48,1536]{2,1,0:T(8,128)(2,1)S(1)}, u32[]{:S(2)}, u32[]{:S(2)}) collective-permute-start(bf16[4,48,1536]{2,1,0:T(8,128)(2,1)S(1)} %get-tuple-element.73), channel_id=1, source_target_pairs={{0,4},{1,3},{2,6},{3,1},{4,0},{5,7},{6,2},{7,5},{8,12},{9,11},{10,... | collective-permute-start | bytes 1769480 | tf_op jit(solution)/shard_map/ppermute | solution.py:536
  138.4 7.4 %collective-permute-done.19 = bf16[2,80,1536]{2,1,0:T(8,128)(2,1)S(1)} collective-permute-done((bf16[2,80,1536]{2,1,0:T(8,128)(2,1)S(1)}, bf16[2,80,1536]{2,1,0:T(8,128)(2,1)S(1)}, u32[]{:S(2)}, u32[]{:S(2)}) %collective-permute-start.19) | collective-permute-done | bytes 491552 | tf_op jit(solution)/shard_map/ppermute | solution.py:536
  145.9 1.9 collective-permute-start.20
  148.3 14.8 %collective-permute-done.21 = bf16[4,80,1536]{2,1,0:T(8,128)(2,1)S(1)} collective-permute-done((bf16[4,80,1536]{2,1,0:T(8,128)(2,1)S(1)}, bf16[4,80,1536]{2,1,0:T(8,128)(2,1)S(1)}, u32[]{:S(2)}, u32[]{:S(2)}) %collective-permute-start.21) | collective-permute-done | bytes 983072 | tf_op jit(solution)/shard_map/ppermute | solution.py:536
  163.2 2.1 %collective-permute-start.22 = (bf16[2,80,1536]{2,1,0:T(8,128)(2,1)S(1)}, bf16[2,80,1536]{2,1,0:T(8,128)(2,1)S(1)}, u32[]{:S(2)}, u32[]{:S(2)}) collective-permute-start(bf16[2,80,1536]{2,1,0:T(8,128)(2,1)S(1)} %pad_maximum_fusion.1), channel_id=1, source_target_pairs={{0,8},{1,9},{2,10},{3,11},{4,12},{5,13},{6,14},{7,15},{8,0},{9,1},... | collective-permute-start | bytes 1474568 | tf_op jit(solution)/shard_map/ppermute | solution.py:536
  165.6 9.3 %collective-permute-done.22 = bf16[2,80,1536]{2,1,0:T(8,128)(2,1)S(1)} collective-permute-done((bf16[2,80,1536]{2,1,0:T(8,128)(2,1)S(1)}, bf16[2,80,1536]{2,1,0:T(8,128)(2,1)S(1)}, u32[]{:S(2)}, u32[]{:S(2)}) %collective-permute-start.22) | collective-permute-done | bytes 491552 | tf_op jit(solution)/shard_map/ppermute | solution.py:536
  179.7 6.6 %collective-permute-done.23 = bf16[80,1536]{1,0:T(8,128)(2,1)S(1)} collective-permute-done((bf16[80,1536]{1,0:T(8,128)(2,1)S(1)}, bf16[80,1536]{1,0:T(8,128)(2,1)S(1)}, u32[]{:S(2)}, u32[]{:S(2)}) %collective-permute-start.23) | collective-permute-done | bytes 245792 | tf_op jit(solution)/shard_map/ppermute | solution.py:536
  188.0 4.7 %collective-permute-done.24 = bf16[80,1536]{1,0:T(8,128)(2,1)S(1)} collective-permute-done((bf16[80,1536]{1,0:T(8,128)(2,1)S(1)}, bf16[80,1536]{1,0:T(8,128)(2,1)S(1)}, u32[]{:S(2)}, u32[]{:S(2)}) %collective-permute-start.24) | collective-permute-done | bytes 245792 | tf_op jit(solution)/shard_map/ppermute | solution.py:536
  (92 shorter events, 31.1 us)
Async XLA Ops:
  13.2 21.0 %collective-permute-start.3 = (bf16[2,1536,1024]{2,1,0:T(8,128)(2,1)}, bf16[2,1536,1024]{2,1,0:T(8,128)(2,1)}, u32[]{:S(2)}, u32[]{:S(2)}) collective-permute-start(bf16[2,1536,1024]{2,1,0:T(8,128)(2,1)} %refs_6_.3), channel_id=1, source_target_pairs={{0,1},{1,0},{2,3},{3,2},{4,5},{5,4},{6,7},{7,6},{8,9},{9,8},{10,11... | collective-permute-start | bytes 18874376 | tf_op jit(solution)/shard_map/ppermute | solution.py:642
  13.6 20.6 %collective-permute-start.4 = (bf16[2,512,1536]{2,1,0:T(8,128)(2,1)S(1)}, bf16[2,512,1536]{2,1,0:T(8,128)(2,1)}, u32[]{:S(2)}, u32[]{:S(2)}) collective-permute-start(bf16[2,512,1536]{2,1,0:T(8,128)(2,1)S(1)} %copy-done.3), channel_id=1, source_target_pairs={{0,1},{1,0},{2,3},{3,2},{4,5},{5,4},{6,7},{7,6},{8,9},{9,8},{10,11... | collective-permute-start | bytes 9437192 | tf_op jit(solution)/shard_map/ppermute | solution.py:642
  28.6 19.1 %collective-permute-start.7 = (bf16[72,1536]{1,0:T(8,128)(2,1)}, bf16[72,1536]{1,0:T(8,128)(2,1)S(1)}, u32[]{:S(2)}, u32[]{:S(2)}) collective-permute-start(bf16[72,1536]{1,0:T(8,128)(2,1)} %get-tuple-element.48.refs_0_), channel_id=1, source_target_pairs={{0,24},{1,25},{2,26},{3,27},{4,28},{5,29},{6,30},{7,31},{8,16},{9,... | collective-permute-start | bytes 663560 | tf_op jit(solution)/shard_map/ppermute | solution.py:536
  33.6 19.3 %collective-permute-start.6 = (bf16[72,1536]{1,0:T(8,128)(2,1)}, bf16[72,1536]{1,0:T(8,128)(2,1)S(1)}, u32[]{:S(2)}, u32[]{:S(2)}) collective-permute-start(bf16[72,1536]{1,0:T(8,128)(2,1)} %get-tuple-element.48.refs_0_), channel_id=1, source_target_pairs={{0,16},{1,17},{2,18},{3,19},{4,20},{5,21},{6,22},{7,23},{8,24},{9,... | collective-permute-start | bytes 663560 | tf_op jit(solution)/shard_map/ppermute | solution.py:536
  33.6 19.3 %collective-permute-start.5 = (bf16[72,1536]{1,0:T(8,128)(2,1)}, bf16[72,1536]{1,0:T(8,128)(2,1)S(1)}, u32[]{:S(2)}, u32[]{:S(2)}) collective-permute-start(bf16[72,1536]{1,0:T(8,128)(2,1)} %get-tuple-element.48.refs_0_), channel_id=1, source_target_pairs={{0,8},{1,9},{2,10},{3,11},{4,12},{5,13},{6,14},{7,15},{8,0},{9,1},... | collective-permute-start | bytes 663560 | tf_op jit(solution)/shard_map/ppermute | solution.py:536
  53.9 22.3 %collective-permute-start.12 = (bf16[4,72,1536]{2,1,0:T(8,128)(2,1)S(1)}, bf16[4,72,1536]{2,1,0:T(8,128)(2,1)}, u32[]{:S(2)}, u32[]{:S(2)}) collective-permute-start(bf16[4,72,1536]{2,1,0:T(8,128)(2,1)S(1)} %stack_rows.2.refs_0_), channel_id=1, source_target_pairs={{0,4},{1,3},{2,6},{3,1},{4,0},{5,7},{6,2},{7,5},{8,12},{9,11},{10,... | collective-permute-start | bytes 2654216 | tf_op jit(solution)/shard_map/ppermute | solution.py:536
  55.5 21.2 %collective-permute-start.11 = (bf16[4,72,1536]{2,1,0:T(8,128)(2,1)S(1)}, bf16[4,72,1536]{2,1,0:T(8,128)(2,1)S(1)}, u32[]{:S(2)}, u32[]{:S(2)}) collective-permute-start(bf16[4,72,1536]{2,1,0:T(8,128)(2,1)S(1)} %stack_rows.2.refs_0_), channel_id=1, source_target_pairs={{0,2},{1,5},{2,0},{3,7},{4,6},{5,1},{6,4},{7,3},{8,10},{9,13},{10,... | collective-permute-start | bytes 2654216 | tf_op jit(solution)/shard_map/ppermute | solution.py:536
  59.5 15.0 %collective-permute-start.9 = (bf16[64,1536]{1,0:T(8,128)(2,1)S(1)}, bf16[64,1536]{1,0:T(8,128)(2,1)S(1)}, u32[]{:S(2)}, u32[]{:S(2)}) collective-permute-start(bf16[64,1536]{1,0:T(8,128)(2,1)S(1)} %copy-done), channel_id=1, source_target_pairs={{0,16},{1,17},{2,18},{3,19},{4,20},{5,21},{6,22},{7,23},{8,24},{9,... | collective-permute-start | bytes 589832 | tf_op jit(solution)/shard_map/ppermute | solution.py:536
  59.5 15.0 %collective-permute-start.8 = (bf16[64,1536]{1,0:T(8,128)(2,1)S(1)}, bf16[64,1536]{1,0:T(8,128)(2,1)S(1)}, u32[]{:S(2)}, u32[]{:S(2)}) collective-permute-start(bf16[64,1536]{1,0:T(8,128)(2,1)S(1)} %copy-done), channel_id=1, source_target_pairs={{0,8},{1,9},{2,10},{3,11},{4,12},{5,13},{6,14},{7,15},{8,0},{9,1},... | collective-permute-start | bytes 589832 | tf_op jit(solution)/shard_map/ppermute | solution.py:536
  76.2 23.7 %collective-permute-start.14 = (bf16[4,72,1536]{2,1,0:T(8,128)(2,1)}, bf16[4,72,1536]{2,1,0:T(8,128)(2,1)S(1)}, u32[]{:S(2)}, u32[]{:S(2)}) collective-permute-start(bf16[4,72,1536]{2,1,0:T(8,128)(2,1)} %collective-permute-done.12.refs_1_.refs_2_), channel_id=1, source_target_pairs={{0,2},{1,5},{2,0},{3,7},{4,6},{5,1},{6,4},{7,3},{8,10},{9,13},{10,... | collective-permute-start | bytes 2654216 | tf_op jit(solution)/shard_map/ppermute | solution.py:536
  77.6 20.7 %collective-permute-start.13 = (bf16[4,64,1536]{2,1,0:T(8,128)(2,1)S(1)}, bf16[4,64,1536]{2,1,0:T(8,128)(2,1)}, u32[]{:S(2)}, u32[]{:S(2)}) collective-permute-start(bf16[4,64,1536]{2,1,0:T(8,128)(2,1)S(1)} %stack_rows.3.refs_1_), channel_id=1, source_target_pairs={{0,4},{1,3},{2,6},{3,1},{4,0},{5,7},{6,2},{7,5},{8,12},{9,11},{10,... | collective-permute-start | bytes 2359304 | tf_op jit(solution)/shard_map/ppermute | solution.py:536
  79.3 34.5 %collective-permute-start.15 = (bf16[4,64,1536]{2,1,0:T(8,128)(2,1)S(1)}, bf16[4,64,1536]{2,1,0:T(8,128)(2,1)S(1)}, u32[]{:S(2)}, u32[]{:S(2)}) collective-permute-start(bf16[4,64,1536]{2,1,0:T(8,128)(2,1)S(1)} %stack_rows.3.refs_1_), channel_id=1, source_target_pairs={{0,2},{1,5},{2,0},{3,7},{4,6},{5,1},{6,4},{7,3},{8,10},{9,13},{10,... | collective-permute-start | bytes 2359304 | tf_op jit(solution)/shard_map/ppermute | solution.py:536
  98.3 16.3 %collective-permute-start.16 = (bf16[4,64,1536]{2,1,0:T(8,128)(2,1)}, bf16[4,64,1536]{2,1,0:T(8,128)(2,1)S(1)}, u32[]{:S(2)}, u32[]{:S(2)}) collective-permute-start(bf16[4,64,1536]{2,1,0:T(8,128)(2,1)} %collective-permute-done.13.refs_3_), channel_id=1, source_target_pairs={{0,2},{1,5},{2,0},{3,7},{4,6},{5,1},{6,4},{7,3},{8,10},{9,13},{10,... | collective-permute-start | bytes 2359304 | tf_op jit(solution)/shard_map/ppermute | solution.py:536
  114.6 20.4 %collective-permute-start.17 = (bf16[4,80,1536]{2,1,0:T(8,128)(2,1)S(1)}, bf16[4,80,1536]{2,1,0:T(8,128)(2,1)S(1)}, u32[]{:S(2)}, u32[]{:S(2)}) collective-permute-start(bf16[4,80,1536]{2,1,0:T(8,128)(2,1)S(1)} %get-tuple-element.60), channel_id=1, source_target_pairs={{0,4},{1,3},{2,6},{3,1},{4,0},{5,7},{6,2},{7,5},{8,12},{9,11},{10,... | collective-permute-start | bytes 2949128 | tf_op jit(solution)/shard_map/ppermute | solution.py:536
  117.6 17.4 %collective-permute-start.18 = (bf16[4,48,1536]{2,1,0:T(8,128)(2,1)S(1)}, bf16[4,48,1536]{2,1,0:T(8,128)(2,1)S(1)}, u32[]{:S(2)}, u32[]{:S(2)}) collective-permute-start(bf16[4,48,1536]{2,1,0:T(8,128)(2,1)S(1)} %get-tuple-element.62), channel_id=1, source_target_pairs={{0,4},{1,3},{2,6},{3,1},{4,0},{5,7},{6,2},{7,5},{8,12},{9,11},{10,... | collective-permute-start | bytes 1769480 | tf_op jit(solution)/shard_map/ppermute | solution.py:536
  135.2 10.5 %collective-permute-start.19 = (bf16[2,80,1536]{2,1,0:T(8,128)(2,1)S(1)}, bf16[2,80,1536]{2,1,0:T(8,128)(2,1)S(1)}, u32[]{:S(2)}, u32[]{:S(2)}) collective-permute-start(bf16[2,80,1536]{2,1,0:T(8,128)(2,1)S(1)} %pad_maximum_fusion), channel_id=1, source_target_pairs={{0,8},{1,9},{2,10},{3,11},{4,12},{5,13},{6,14},{7,15},{8,0},{9,1},... | collective-permute-start | bytes 1474568 | tf_op jit(solution)/shard_map/ppermute | solution.py:536
  136.3 11.8 %collective-permute-start.25 = (bf16[4,48,1536]{2,1,0:T(8,128)(2,1)S(1)}, bf16[4,48,1536]{2,1,0:T(8,128)(2,1)S(1)}, u32[]{:S(2)}, u32[]{:S(2)}) collective-permute-start(bf16[4,48,1536]{2,1,0:T(8,128)(2,1)S(1)} %get-tuple-element.73), channel_id=1, source_target_pairs={{0,4},{1,3},{2,6},{3,1},{4,0},{5,7},{6,2},{7,5},{8,12},{9,11},{10,... | collective-permute-start | bytes 1769480 | tf_op jit(solution)/shard_map/ppermute | solution.py:536
  138.3 24.8 %collective-permute-start.21 = (bf16[4,80,1536]{2,1,0:T(8,128)(2,1)S(1)}, bf16[4,80,1536]{2,1,0:T(8,128)(2,1)S(1)}, u32[]{:S(2)}, u32[]{:S(2)}) collective-permute-start(bf16[4,80,1536]{2,1,0:T(8,128)(2,1)S(1)} %get-tuple-element.69), channel_id=1, source_target_pairs={{0,4},{1,3},{2,6},{3,1},{4,0},{5,7},{6,2},{7,5},{8,12},{9,11},{10,... | collective-permute-start | bytes 2949128 | tf_op jit(solution)/shard_map/ppermute | solution.py:536
  145.9 42.2 %collective-permute-start.20 = (bf16[80,1536]{1,0:T(8,128)(2,1)S(1)}, bf16[80,1536]{1,0:T(8,128)(2,1)S(1)}, u32[]{:S(2)}, u32[]{:S(2)}) collective-permute-start(bf16[80,1536]{1,0:T(8,128)(2,1)S(1)} %fusion.4), channel_id=1, source_target_pairs={{0,16},{1,17},{2,18},{3,19},{4,20},{5,21},{6,22},{7,23},{8,24},{9,... | collective-permute-start | bytes 737288 | tf_op jit(solution)/shard_map/ppermute | solution.py:536
  148.2 17.1 %collective-permute-start.26 = (bf16[4,48,1536]{2,1,0:T(8,128)(2,1)S(1)}, bf16[4,48,1536]{2,1,0:T(8,128)(2,1)S(1)}, u32[]{:S(2)}, u32[]{:S(2)}) collective-permute-start(bf16[4,48,1536]{2,1,0:T(8,128)(2,1)S(1)} %add_convert_fusion), channel_id=1, source_target_pairs={{0,2},{1,5},{2,0},{3,7},{4,6},{5,1},{6,4},{7,3},{8,10},{9,13},{10,... | collective-permute-start | bytes 1769480 | tf_op jit(solution)/shard_map/ppermute | solution.py:536
  163.2 11.6 %collective-permute-start.22 = (bf16[2,80,1536]{2,1,0:T(8,128)(2,1)S(1)}, bf16[2,80,1536]{2,1,0:T(8,128)(2,1)S(1)}, u32[]{:S(2)}, u32[]{:S(2)}) collective-permute-start(bf16[2,80,1536]{2,1,0:T(8,128)(2,1)S(1)} %pad_maximum_fusion.1), channel_id=1, source_target_pairs={{0,8},{1,9},{2,10},{3,11},{4,12},{5,13},{6,14},{7,15},{8,0},{9,1},... | collective-permute-start | bytes 1474568 | tf_op jit(solution)/shard_map/ppermute | solution.py:536
  165.5 12.6 %collective-permute-start.27 = (bf16[2,48,1536]{2,1,0:T(8,128)(2,1)S(1)}, bf16[2,48,1536]{2,1,0:T(8,128)(2,1)S(1)}, u32[]{:S(2)}, u32[]{:S(2)}) collective-permute-start(bf16[2,48,1536]{2,1,0:T(8,128)(2,1)S(1)} %pad_maximum_fusion.3), channel_id=1, source_target_pairs={{0,8},{1,9},{2,10},{3,11},{4,12},{5,13},{6,14},{7,15},{8,0},{9,1},... | collective-permute-start | bytes 884744 | tf_op jit(solution)/shard_map/ppermute | solution.py:536
  175.0 11.4 %collective-permute-start.23 = (bf16[80,1536]{1,0:T(8,128)(2,1)S(1)}, bf16[80,1536]{1,0:T(8,128)(2,1)S(1)}, u32[]{:S(2)}, u32[]{:S(2)}) collective-permute-start(bf16[80,1536]{1,0:T(8,128)(2,1)S(1)} %fusion.5), channel_id=1, source_target_pairs={{0,16},{1,17},{2,18},{3,19},{4,20},{5,21},{6,22},{7,23},{8,24},{9,... | collective-permute-start | bytes 737288 | tf_op jit(solution)/shard_map/ppermute | solution.py:536
  178.1 9.8 %collective-permute-start.28 = (bf16[48,1536]{1,0:T(8,128)(2,1)S(1)}, bf16[48,1536]{1,0:T(8,128)(2,1)S(1)}, u32[]{:S(2)}, u32[]{:S(2)}) collective-permute-start(bf16[48,1536]{1,0:T(8,128)(2,1)S(1)} %fusion.6), channel_id=1, source_target_pairs={{0,16},{1,17},{2,18},{3,19},{4,20},{5,21},{6,22},{7,23},{8,24},{9,... | collective-permute-start | bytes 442376 | tf_op jit(solution)/shard_map/ppermute | solution.py:536
  (14 other events, 83.1 us)

commit v10 on v9

--- a/solution.py
+++ b/solution.py
@@ -582,8 +582,10 @@
 
 
 def scatter_chunks(own, others, shift, sizes):
-    sums = []
+    sums, before = [], []
     for index, (terms, sending) in enumerate(zip(own, others)):
+        if before:
+            sending, _ = lax.optimization_barrier((sending, before))
         planes = [leave_along_a(plane, shift) for plane in sending]
         if index == len(own) - 1:
             for k, part in enumerate(planes):
@@ -591,6 +593,7 @@
             found = scatter_plane(terms, shift, sizes)
         else:
             found = scatter_plane(terms, shift, sizes)
+            before = [v for part in planes for v in part[1:]]
             for k, part in enumerate(planes):
                 total = add_all(scatter_plane(part, shift, sizes))
                 found = found + [shift(total, "b", -k - 1)]
@@ -712,7 +715,7 @@
             (expert_up, up_other),
             (expert_down, down_other),
             (half, row_count - half),
-            [held] if index else [v for plane in halves[0][1:] for v in plane],
+            [held] if index else [],
         )
         mixed = mix_rows(held, back, sizes["a"], cuts, [v for line in own for v in line[1:]])
         chunks = [[piece[i] for piece in mixed] for i in range(len(cuts))]

time: 194 us -> 191 us (0.985)
  transfers between devices with their start and end apart: 29 -> 29, of which waited for: 17 -> 17; matrix products, arithmetic and copies ran while one was open for 2% -> 3% of each run, Pallas kernels for 28% -> 27%
where the time goes in v10:
time: 191 us
  waiting for transfers between devices  89 us (47%)
  Pallas kernels  60.9 us (32%)
  starting transfers between devices  31.3 us (16%)
  other arithmetic  5.1 us (3%)
  local copies, waits for them, and re-layouts  3.25 us (2%)
    ppermute x24, waiting for transfers between devices, shift(): return lax.ppermute(value, BOTH, pairs(role, offset))  87.7 us
    ppermute x24, starting transfers between devices, shift(): return lax.ppermute(value, BOTH, pairs(role, offset))  29.7 us
    pallas_call x2, Pallas kernels, attend(): pl.pallas_call(functools.partial(attend_kernel, first_row, len(riders), l...  26.7 us
    pallas_call x2, Pallas kernels, run_experts(): pl.pallas_call(functools.partial(expert_kernel, pieces, tuple(in_cuts), l...  22.6 us
    pallas_call x1, Pallas kernels, project(): pl.pallas_call(qkv_kernel, grid=(5,), in_specs=[vmem_spec()] * 5 + [pl.Bl...  7.4 us
  transfers between devices with their start and end apart: 29, of which 17 were waited for; matrix products, arithmetic and copies ran while one was open for 3% of the time, Pallas kernels for 27%

profile of v10, /device:TPU:0, one launch (start us, length us, event | category | flops | bytes accessed | tf_op | source)
XLA Modules:
  0.0 191.0 jit_solution(8347572619116084433)
XLA Ops:
  5.8 7.4 %project_rows.1 = (bf16[128,1536]{1,0:T(8,128)(2,1)}, bf16[128,1024]{1,0:T(8,128)(2,1)}, bf16[128,1024]{1,0:T(8,128)(2,1)}) custom-call(bf16[128,1536]{1,0:T(8,128)(2,1)} %tokens_ref.3, bf16[128,1536]{1,0:T(8,128)(2,1)} %copy-done.6, f32[1536]{0:T(1024)} %gain_ref.3, f32[256,128]{1,0:T(8,128)} %pad_maximum_fusion.4.cos_ref, ...), custom_call_target="tpu_custom_call" | custom-call | flops 1409286144 | bytes 9500000 | tf_op jit(solution)/shard_map/project_rows/pallas_call | solution.py:84
  15.2 13.3 %attend_rows.2 = (bf16[128,1536]{1,0:T(8,128)(2,1)}, bf16[128,1536]{1,0:T(8,128)(2,1)}, bf16[72,1536]{1,0:T(8,128)(2,1)}) custom-call(s32[1]{0:T(128)} %copy.24.place_ref, bf16[128,1536]{1,0:T(8,128)(2,1)} %get-tuple-element.41.q_ref, bf16[1,1024,512]{2,1,0:T(8,128)(2,1)} %kc_ref.3, bf16[1,1024,512]{2,1,0:T(8,128)(2,1)} %collective-permute-done.1.refs_0_.kco_ref, ...), custom_call_target="tpu_custom_call" | custom-call | flops 7247757312 | bytes 10000000 | tf_op jit(solution)/shard_map/attend_rows/pallas_call | solution.py:222
  28.6 5.1 %collective-permute-start.7 = (bf16[72,1536]{1,0:T(8,128)(2,1)}, bf16[72,1536]{1,0:T(8,128)(2,1)S(1)}, u32[]{:S(2)}, u32[]{:S(2)}) collective-permute-start(bf16[72,1536]{1,0:T(8,128)(2,1)} %get-tuple-element.50.refs_0_), channel_id=1, source_target_pairs={{0,24},{1,25},{2,26},{3,27},{4,28},{5,29},{6,30},{7,31},{8,16},{9,... | collective-permute-start | bytes 663560 | tf_op jit(solution)/shard_map/ppermute | solution.py:536
  34.3 13.4 %attend_rows.3 = (bf16[128,1536]{1,0:T(8,128)(2,1)}, bf16[128,1536]{1,0:T(8,128)(2,1)}, bf16[64,1536]{1,0:T(8,128)(2,1)}) custom-call(s32[1]{0:T(128)} %copy.24.place_ref, bf16[128,1536]{1,0:T(8,128)(2,1)} %get-tuple-element.41.q_ref, bf16[1,1024,512]{2,1,0:T(8,128)(2,1)} %kc_ref.3, ...), custom_call_target="tpu_custom_call", output_to_operand_aliasing={{0}: (13, {}), {1}: (14, {})} | custom-call | flops 7247757312 | bytes 10000000 | tf_op jit(solution)/shard_map/attend_rows/pallas_call | solution.py:222
  47.7 5.2 %collective-permute-done.6.refs_2_ = bf16[72,1536]{1,0:T(8,128)(2,1)S(1)} collective-permute-done((bf16[72,1536]{1,0:T(8,128)(2,1)}, bf16[72,1536]{1,0:T(8,128)(2,1)S(1)}, u32[]{:S(2)}, u32[]{:S(2)}) %collective-permute-start.6) | collective-permute-done | bytes 221216 | tf_op jit(solution)/shard_map/ppermute | solution.py:536
  55.5 2.5 %collective-permute-start.10 = (bf16[64,1536]{1,0:T(8,128)(2,1)S(1)}, bf16[64,1536]{1,0:T(8,128)(2,1)S(1)}, u32[]{:S(2)}, u32[]{:S(2)}) collective-permute-start(bf16[64,1536]{1,0:T(8,128)(2,1)S(1)} %copy-done), channel_id=1, source_target_pairs={{0,24},{1,25},{2,26},{3,27},{4,28},{5,29},{6,30},{7,31},{8,16},{9,... | collective-permute-start | bytes 589832 | tf_op jit(solution)/shard_map/ppermute | solution.py:536
  57.9 1.9 %collective-permute-start.8 = (bf16[64,1536]{1,0:T(8,128)(2,1)S(1)}, bf16[64,1536]{1,0:T(8,128)(2,1)S(1)}, u32[]{:S(2)}, u32[]{:S(2)}) collective-permute-start(bf16[64,1536]{1,0:T(8,128)(2,1)S(1)} %copy-done), channel_id=1, source_target_pairs={{0,8},{1,9},{2,10},{3,11},{4,12},{5,13},{6,14},{7,15},{8,0},{9,1},... | collective-permute-start | bytes 589832 | tf_op jit(solution)/shard_map/ppermute | solution.py:536
  61.4 3.8 %collective-permute-done.10.refs_3_ = bf16[64,1536]{1,0:T(8,128)(2,1)S(1)} collective-permute-done((bf16[64,1536]{1,0:T(8,128)(2,1)S(1)}, bf16[64,1536]{1,0:T(8,128)(2,1)S(1)}, u32[]{:S(2)}, u32[]{:S(2)}) %collective-permute-start.10) | collective-permute-done | bytes 196640 | tf_op jit(solution)/shard_map/ppermute | solution.py:536
  65.2 7.9 %collective-permute-done.9.refs_2_ = bf16[64,1536]{1,0:T(8,128)(2,1)S(1)} collective-permute-done((bf16[64,1536]{1,0:T(8,128)(2,1)S(1)}, bf16[64,1536]{1,0:T(8,128)(2,1)S(1)}, u32[]{:S(2)}, u32[]{:S(2)}) %collective-permute-start.9) | collective-permute-done | bytes 196640 | tf_op jit(solution)/shard_map/ppermute | solution.py:536
  74.3 2.6 %collective-permute-start.13 = (bf16[4,64,1536]{2,1,0:T(8,128)(2,1)S(1)}, bf16[4,64,1536]{2,1,0:T(8,128)(2,1)}, u32[]{:S(2)}, u32[]{:S(2)}) collective-permute-start(bf16[4,64,1536]{2,1,0:T(8,128)(2,1)S(1)} %stack_rows.3.refs_1_), channel_id=1, source_target_pairs={{0,4},{1,3},{2,6},{3,1},{4,0},{5,7},{6,2},{7,5},{8,12},{9,11},{10,... | collective-permute-start | bytes 2359304 | tf_op jit(solution)/shard_map/ppermute | solution.py:536
  80.1 15.4 %collective-permute-done.13.refs_3_ = bf16[4,64,1536]{2,1,0:T(8,128)(2,1)} collective-permute-done((bf16[4,64,1536]{2,1,0:T(8,128)(2,1)S(1)}, bf16[4,64,1536]{2,1,0:T(8,128)(2,1)}, u32[]{:S(2)}, u32[]{:S(2)}) %collective-permute-start.13) | collective-permute-done | bytes 786464 | tf_op jit(solution)/shard_map/ppermute | solution.py:536
  97.0 11.5 %run_experts.2.held_ref.refs_10_ = bf16[4,256,1536]{2,1,0:T(8,128)(2,1)S(1)} custom-call(bf16[4,72,1536]{2,1,0:T(8,128)(2,1)S(1)} %stack_rows.2.refs_0_, bf16[4,64,1536]{2,1,0:T(8,128)(2,1)S(1)} %stack_rows.3.refs_1_, bf16[4,72,1536]{2,1,0:T(8,128)(2,1)S(1)} %collective-permute-done.12.refs_1_.refs_2_, bf16[4,64,1536]{2,1,0:T(8,128)(2,1)} %collective-permute-done.13.refs_3_, ...), custom_call_target="tpu_custom_call" | custom-call | flops 8053063680 | bytes 26000000 | tf_op jit(solution)/shard_map/run_experts/pallas_call | solution.py:415
  114.4 11.1 %run_experts.3.held_ref = bf16[4,256,1536]{2,1,0:T(8,128)(2,1)S(1)} custom-call(bf16[4,72,1536]{2,1,0:T(8,128)(2,1)S(1)} %collective-permute-done.11.refs_4_.refs_0_, bf16[4,64,1536]{2,1,0:T(8,128)(2,1)S(1)} %collective-permute-done.14.refs_1_, bf16[4,72,1536]{2,1,0:T(8,128)(2,1)S(1)} %collective-permute-done.18.refs_1_.refs_2_, ...), custom_call_target="tpu_custom_call" | custom-call | flops 8053063680 | bytes 26000000 | tf_op jit(solution)/shard_map/run_experts/pallas_call | solution.py:415
  125.5 6.1 %collective-permute-done.17.refs_1_ = bf16[4,48,1536]{2,1,0:T(8,128)(2,1)S(1)} collective-permute-done((bf16[4,48,1536]{2,1,0:T(8,128)(2,1)S(1)}, bf16[4,48,1536]{2,1,0:T(8,128)(2,1)S(1)}, u32[]{:S(2)}, u32[]{:S(2)}) %collective-permute-start.17) | collective-permute-done | bytes 589856 | tf_op jit(solution)/shard_map/ppermute | solution.py:536
  132.6 1.6 collective-permute-start.21
  134.5 12.3 %collective-permute-done.21 = bf16[4,80,1536]{2,1,0:T(8,128)(2,1)S(1)} collective-permute-done((bf16[4,80,1536]{2,1,0:T(8,128)(2,1)S(1)}, bf16[4,80,1536]{2,1,0:T(8,128)(2,1)S(1)}, u32[]{:S(2)}, u32[]{:S(2)}) %collective-permute-start.21) | collective-permute-done | bytes 983072 | tf_op jit(solution)/shard_map/ppermute | solution.py:536
  148.6 8.1 %collective-permute-done.25 = bf16[4,48,1536]{2,1,0:T(8,128)(2,1)S(1)} collective-permute-done((bf16[4,48,1536]{2,1,0:T(8,128)(2,1)S(1)}, bf16[4,48,1536]{2,1,0:T(8,128)(2,1)S(1)}, u32[]{:S(2)}, u32[]{:S(2)}) %collective-permute-start.25) | collective-permute-done | bytes 589856 | tf_op jit(solution)/shard_map/ppermute | solution.py:536
  156.8 1.9 collective-permute-start.26
  159.9 2.0 %collective-permute-start.23 = (bf16[80,1536]{1,0:T(8,128)(2,1)S(1)}, bf16[80,1536]{1,0:T(8,128)(2,1)S(1)}, u32[]{:S(2)}, u32[]{:S(2)}) collective-permute-start(bf16[80,1536]{1,0:T(8,128)(2,1)S(1)} %fusion.5), channel_id=1, source_target_pairs={{0,16},{1,17},{2,18},{3,19},{4,20},{5,21},{6,22},{7,23},{8,24},{9,... | collective-permute-start | bytes 737288 | tf_op jit(solution)/shard_map/ppermute | solution.py:536
  161.9 4.8 %collective-permute-done.26 = bf16[4,48,1536]{2,1,0:T(8,128)(2,1)S(1)} collective-permute-done((bf16[4,48,1536]{2,1,0:T(8,128)(2,1)S(1)}, bf16[4,48,1536]{2,1,0:T(8,128)(2,1)S(1)}, u32[]{:S(2)}, u32[]{:S(2)}) %collective-permute-start.26) | collective-permute-done | bytes 589856 | tf_op jit(solution)/shard_map/ppermute | solution.py:536
  167.0 12.8 %collective-permute-done.23 = bf16[80,1536]{1,0:T(8,128)(2,1)S(1)} collective-permute-done((bf16[80,1536]{1,0:T(8,128)(2,1)S(1)}, bf16[80,1536]{1,0:T(8,128)(2,1)S(1)}, u32[]{:S(2)}, u32[]{:S(2)}) %collective-permute-start.23) | collective-permute-done | bytes 245792 | tf_op jit(solution)/shard_map/ppermute | solution.py:536
  180.5 1.8 collective-permute-done.27
  182.9 3.3 %collective-permute-done.24 = bf16[80,1536]{1,0:T(8,128)(2,1)S(1)} collective-permute-done((bf16[80,1536]{1,0:T(8,128)(2,1)S(1)}, bf16[80,1536]{1,0:T(8,128)(2,1)S(1)}, u32[]{:S(2)}, u32[]{:S(2)}) %collective-permute-start.24) | collective-permute-done | bytes 245792 | tf_op jit(solution)/shard_map/ppermute | solution.py:536
  186.4 3.7 %collective-permute-done.28 = bf16[48,1536]{1,0:T(8,128)(2,1)S(1)} collective-permute-done((bf16[48,1536]{1,0:T(8,128)(2,1)S(1)}, bf16[48,1536]{1,0:T(8,128)(2,1)S(1)}, u32[]{:S(2)}, u32[]{:S(2)}) %collective-permute-start.28) | collective-permute-done | bytes 147488 | tf_op jit(solution)/shard_map/ppermute | solution.py:536
  (92 shorter events, 29.8 us)
Async XLA Ops:
  13.2 21.0 %collective-permute-start.3 = (bf16[2,1536,1024]{2,1,0:T(8,128)(2,1)}, bf16[2,1536,1024]{2,1,0:T(8,128)(2,1)}, u32[]{:S(2)}, u32[]{:S(2)}) collective-permute-start(bf16[2,1536,1024]{2,1,0:T(8,128)(2,1)} %refs_6_.3), channel_id=1, source_target_pairs={{0,1},{1,0},{2,3},{3,2},{4,5},{5,4},{6,7},{7,6},{8,9},{9,8},{10,11... | collective-permute-start | bytes 18874376 | tf_op jit(solution)/shard_map/ppermute | solution.py:645
  13.6 20.6 %collective-permute-start.4 = (bf16[2,512,1536]{2,1,0:T(8,128)(2,1)S(1)}, bf16[2,512,1536]{2,1,0:T(8,128)(2,1)}, u32[]{:S(2)}, u32[]{:S(2)}) collective-permute-start(bf16[2,512,1536]{2,1,0:T(8,128)(2,1)S(1)} %copy-done.3), channel_id=1, source_target_pairs={{0,1},{1,0},{2,3},{3,2},{4,5},{5,4},{6,7},{7,6},{8,9},{9,8},{10,11... | collective-permute-start | bytes 9437192 | tf_op jit(solution)/shard_map/ppermute | solution.py:645
  28.6 19.1 %collective-permute-start.7 = (bf16[72,1536]{1,0:T(8,128)(2,1)}, bf16[72,1536]{1,0:T(8,128)(2,1)S(1)}, u32[]{:S(2)}, u32[]{:S(2)}) collective-permute-start(bf16[72,1536]{1,0:T(8,128)(2,1)} %get-tuple-element.50.refs_0_), channel_id=1, source_target_pairs={{0,24},{1,25},{2,26},{3,27},{4,28},{5,29},{6,30},{7,31},{8,16},{9,... | collective-permute-start | bytes 663560 | tf_op jit(solution)/shard_map/ppermute | solution.py:536
  33.6 19.3 %collective-permute-start.6 = (bf16[72,1536]{1,0:T(8,128)(2,1)}, bf16[72,1536]{1,0:T(8,128)(2,1)S(1)}, u32[]{:S(2)}, u32[]{:S(2)}) collective-permute-start(bf16[72,1536]{1,0:T(8,128)(2,1)} %get-tuple-element.50.refs_0_), channel_id=1, source_target_pairs={{0,16},{1,17},{2,18},{3,19},{4,20},{5,21},{6,22},{7,23},{8,24},{9,... | collective-permute-start | bytes 663560 | tf_op jit(solution)/shard_map/ppermute | solution.py:536
  33.6 19.3 %collective-permute-start.5 = (bf16[72,1536]{1,0:T(8,128)(2,1)}, bf16[72,1536]{1,0:T(8,128)(2,1)S(1)}, u32[]{:S(2)}, u32[]{:S(2)}) collective-permute-start(bf16[72,1536]{1,0:T(8,128)(2,1)} %get-tuple-element.50.refs_0_), channel_id=1, source_target_pairs={{0,8},{1,9},{2,10},{3,11},{4,12},{5,13},{6,14},{7,15},{8,0},{9,1},... | collective-permute-start | bytes 663560 | tf_op jit(solution)/shard_map/ppermute | solution.py:536
  53.9 19.4 %collective-permute-start.11 = (bf16[4,72,1536]{2,1,0:T(8,128)(2,1)S(1)}, bf16[4,72,1536]{2,1,0:T(8,128)(2,1)S(1)}, u32[]{:S(2)}, u32[]{:S(2)}) collective-permute-start(bf16[4,72,1536]{2,1,0:T(8,128)(2,1)S(1)} %stack_rows.2.refs_0_), channel_id=1, source_target_pairs={{0,2},{1,5},{2,0},{3,7},{4,6},{5,1},{6,4},{7,3},{8,10},{9,13},{10,... | collective-permute-start | bytes 2654216 | tf_op jit(solution)/shard_map/ppermute | solution.py:536
  55.5 9.7 %collective-permute-start.10 = (bf16[64,1536]{1,0:T(8,128)(2,1)S(1)}, bf16[64,1536]{1,0:T(8,128)(2,1)S(1)}, u32[]{:S(2)}, u32[]{:S(2)}) collective-permute-start(bf16[64,1536]{1,0:T(8,128)(2,1)S(1)} %copy-done), channel_id=1, source_target_pairs={{0,24},{1,25},{2,26},{3,27},{4,28},{5,29},{6,30},{7,31},{8,16},{9,... | collective-permute-start | bytes 589832 | tf_op jit(solution)/shard_map/ppermute | solution.py:536
  57.9 15.2 %collective-permute-start.9 = (bf16[64,1536]{1,0:T(8,128)(2,1)S(1)}, bf16[64,1536]{1,0:T(8,128)(2,1)S(1)}, u32[]{:S(2)}, u32[]{:S(2)}) collective-permute-start(bf16[64,1536]{1,0:T(8,128)(2,1)S(1)} %copy-done), channel_id=1, source_target_pairs={{0,16},{1,17},{2,18},{3,19},{4,20},{5,21},{6,22},{7,23},{8,24},{9,... | collective-permute-start | bytes 589832 | tf_op jit(solution)/shard_map/ppermute | solution.py:536
  57.9 15.2 %collective-permute-start.8 = (bf16[64,1536]{1,0:T(8,128)(2,1)S(1)}, bf16[64,1536]{1,0:T(8,128)(2,1)S(1)}, u32[]{:S(2)}, u32[]{:S(2)}) collective-permute-start(bf16[64,1536]{1,0:T(8,128)(2,1)S(1)} %copy-done), channel_id=1, source_target_pairs={{0,8},{1,9},{2,10},{3,11},{4,12},{5,13},{6,14},{7,15},{8,0},{9,1},... | collective-permute-start | bytes 589832 | tf_op jit(solution)/shard_map/ppermute | solution.py:536
  59.9 18.7 %collective-permute-start.12 = (bf16[4,72,1536]{2,1,0:T(8,128)(2,1)S(1)}, bf16[4,72,1536]{2,1,0:T(8,128)(2,1)S(1)}, u32[]{:S(2)}, u32[]{:S(2)}) collective-permute-start(bf16[4,72,1536]{2,1,0:T(8,128)(2,1)S(1)} %stack_rows.2.refs_0_), channel_id=1, source_target_pairs={{0,4},{1,3},{2,6},{3,1},{4,0},{5,7},{6,2},{7,5},{8,12},{9,11},{10,... | collective-permute-start | bytes 2654216 | tf_op jit(solution)/shard_map/ppermute | solution.py:536
  74.3 21.1 %collective-permute-start.13 = (bf16[4,64,1536]{2,1,0:T(8,128)(2,1)S(1)}, bf16[4,64,1536]{2,1,0:T(8,128)(2,1)}, u32[]{:S(2)}, u32[]{:S(2)}) collective-permute-start(bf16[4,64,1536]{2,1,0:T(8,128)(2,1)S(1)} %stack_rows.3.refs_1_), channel_id=1, source_target_pairs={{0,4},{1,3},{2,6},{3,1},{4,0},{5,7},{6,2},{7,5},{8,12},{9,11},{10,... | collective-permute-start | bytes 2359304 | tf_op jit(solution)/shard_map/ppermute | solution.py:536
  77.0 33.2 %collective-permute-start.14 = (bf16[4,64,1536]{2,1,0:T(8,128)(2,1)S(1)}, bf16[4,64,1536]{2,1,0:T(8,128)(2,1)S(1)}, u32[]{:S(2)}, u32[]{:S(2)}) collective-permute-start(bf16[4,64,1536]{2,1,0:T(8,128)(2,1)S(1)} %stack_rows.3.refs_1_), channel_id=1, source_target_pairs={{0,2},{1,5},{2,0},{3,7},{4,6},{5,1},{6,4},{7,3},{8,10},{9,13},{10,... | collective-permute-start | bytes 2359304 | tf_op jit(solution)/shard_map/ppermute | solution.py:536
  78.5 34.3 %collective-permute-start.18 = (bf16[4,72,1536]{2,1,0:T(8,128)(2,1)S(1)}, bf16[4,72,1536]{2,1,0:T(8,128)(2,1)S(1)}, u32[]{:S(2)}, u32[]{:S(2)}) collective-permute-start(bf16[4,72,1536]{2,1,0:T(8,128)(2,1)S(1)} %collective-permute-done.12.refs_1_.refs_2_), channel_id=1, source_target_pairs={{0,2},{1,5},{2,0},{3,7},{4,6},{5,1},{6,4},{7,3},{8,10},{9,13},{10,... | collective-permute-start | bytes 2654216 | tf_op jit(solution)/shard_map/ppermute | solution.py:536
  95.5 15.8 %collective-permute-start.15 = (bf16[4,64,1536]{2,1,0:T(8,128)(2,1)}, bf16[4,64,1536]{2,1,0:T(8,128)(2,1)S(1)}, u32[]{:S(2)}, u32[]{:S(2)}) collective-permute-start(bf16[4,64,1536]{2,1,0:T(8,128)(2,1)} %collective-permute-done.13.refs_3_), channel_id=1, source_target_pairs={{0,2},{1,5},{2,0},{3,7},{4,6},{5,1},{6,4},{7,3},{8,10},{9,13},{10,... | collective-permute-start | bytes 2359304 | tf_op jit(solution)/shard_map/ppermute | solution.py:536
  111.3 20.4 %collective-permute-start.16 = (bf16[4,80,1536]{2,1,0:T(8,128)(2,1)S(1)}, bf16[4,80,1536]{2,1,0:T(8,128)(2,1)S(1)}, u32[]{:S(2)}, u32[]{:S(2)}) collective-permute-start(bf16[4,80,1536]{2,1,0:T(8,128)(2,1)S(1)} %get-tuple-element.61), channel_id=1, source_target_pairs={{0,4},{1,3},{2,6},{3,1},{4,0},{5,7},{6,2},{7,5},{8,12},{9,11},{10,... | collective-permute-start | bytes 2949128 | tf_op jit(solution)/shard_map/ppermute | solution.py:536
  113.8 17.8 %collective-permute-start.17 = (bf16[4,48,1536]{2,1,0:T(8,128)(2,1)S(1)}, bf16[4,48,1536]{2,1,0:T(8,128)(2,1)S(1)}, u32[]{:S(2)}, u32[]{:S(2)}) collective-permute-start(bf16[4,48,1536]{2,1,0:T(8,128)(2,1)S(1)} %get-tuple-element.63), channel_id=1, source_target_pairs={{0,4},{1,3},{2,6},{3,1},{4,0},{5,7},{6,2},{7,5},{8,12},{9,11},{10,... | collective-permute-start | bytes 1769480 | tf_op jit(solution)/shard_map/ppermute | solution.py:536
  132.6 14.2 %collective-permute-start.21 = (bf16[4,80,1536]{2,1,0:T(8,128)(2,1)S(1)}, bf16[4,80,1536]{2,1,0:T(8,128)(2,1)S(1)}, u32[]{:S(2)}, u32[]{:S(2)}) collective-permute-start(bf16[4,80,1536]{2,1,0:T(8,128)(2,1)S(1)} %get-tuple-element.71), channel_id=1, source_target_pairs={{0,4},{1,3},{2,6},{3,1},{4,0},{5,7},{6,2},{7,5},{8,12},{9,11},{10,... | collective-permute-start | bytes 2949128 | tf_op jit(solution)/shard_map/ppermute | solution.py:536
  134.4 24.3 %collective-permute-start.19 = (bf16[2,80,1536]{2,1,0:T(8,128)(2,1)S(1)}, bf16[2,80,1536]{2,1,0:T(8,128)(2,1)S(1)}, u32[]{:S(2)}, u32[]{:S(2)}) collective-permute-start(bf16[2,80,1536]{2,1,0:T(8,128)(2,1)S(1)} %pad_maximum_fusion), channel_id=1, source_target_pairs={{0,8},{1,9},{2,10},{3,11},{4,12},{5,13},{6,14},{7,15},{8,0},{9,1},... | collective-permute-start | bytes 1474568 | tf_op jit(solution)/shard_map/ppermute | solution.py:536
  146.8 9.9 %collective-permute-start.25 = (bf16[4,48,1536]{2,1,0:T(8,128)(2,1)S(1)}, bf16[4,48,1536]{2,1,0:T(8,128)(2,1)S(1)}, u32[]{:S(2)}, u32[]{:S(2)}) collective-permute-start(bf16[4,48,1536]{2,1,0:T(8,128)(2,1)S(1)} %get-tuple-element.77), channel_id=1, source_target_pairs={{0,4},{1,3},{2,6},{3,1},{4,0},{5,7},{6,2},{7,5},{8,12},{9,11},{10,... | collective-permute-start | bytes 1769480 | tf_op jit(solution)/shard_map/ppermute | solution.py:536
  148.5 11.4 %collective-permute-start.22 = (bf16[2,80,1536]{2,1,0:T(8,128)(2,1)S(1)}, bf16[2,80,1536]{2,1,0:T(8,128)(2,1)S(1)}, u32[]{:S(2)}, u32[]{:S(2)}) collective-permute-start(bf16[2,80,1536]{2,1,0:T(8,128)(2,1)S(1)} %pad_maximum_fusion.1), channel_id=1, source_target_pairs={{0,8},{1,9},{2,10},{3,11},{4,12},{5,13},{6,14},{7,15},{8,0},{9,1},... | collective-permute-start | bytes 1474568 | tf_op jit(solution)/shard_map/ppermute | solution.py:536
  156.8 9.9 %collective-permute-start.26 = (bf16[4,48,1536]{2,1,0:T(8,128)(2,1)S(1)}, bf16[4,48,1536]{2,1,0:T(8,128)(2,1)S(1)}, u32[]{:S(2)}, u32[]{:S(2)}) collective-permute-start(bf16[4,48,1536]{2,1,0:T(8,128)(2,1)S(1)} %add_convert_fusion), channel_id=1, source_target_pairs={{0,2},{1,5},{2,0},{3,7},{4,6},{5,1},{6,4},{7,3},{8,10},{9,13},{10,... | collective-permute-start | bytes 1769480 | tf_op jit(solution)/shard_map/ppermute | solution.py:536
  158.8 24.1 %collective-permute-start.20 = (bf16[80,1536]{1,0:T(8,128)(2,1)S(1)}, bf16[80,1536]{1,0:T(8,128)(2,1)S(1)}, u32[]{:S(2)}, u32[]{:S(2)}) collective-permute-start(bf16[80,1536]{1,0:T(8,128)(2,1)S(1)} %fusion.4), channel_id=1, source_target_pairs={{0,16},{1,17},{2,18},{3,19},{4,20},{5,21},{6,22},{7,23},{8,24},{9,... | collective-permute-start | bytes 737288 | tf_op jit(solution)/shard_map/ppermute | solution.py:536
  159.9 19.9 %collective-permute-start.23 = (bf16[80,1536]{1,0:T(8,128)(2,1)S(1)}, bf16[80,1536]{1,0:T(8,128)(2,1)S(1)}, u32[]{:S(2)}, u32[]{:S(2)}) collective-permute-start(bf16[80,1536]{1,0:T(8,128)(2,1)S(1)} %fusion.5), channel_id=1, source_target_pairs={{0,16},{1,17},{2,18},{3,19},{4,20},{5,21},{6,22},{7,23},{8,24},{9,... | collective-permute-start | bytes 737288 | tf_op jit(solution)/shard_map/ppermute | solution.py:536
  166.9 15.4 %collective-permute-start.27 = (bf16[2,48,1536]{2,1,0:T(8,128)(2,1)S(1)}, bf16[2,48,1536]{2,1,0:T(8,128)(2,1)S(1)}, u32[]{:S(2)}, u32[]{:S(2)}) collective-permute-start(bf16[2,48,1536]{2,1,0:T(8,128)(2,1)S(1)} %pad_maximum_fusion.3), channel_id=1, source_target_pairs={{0,8},{1,9},{2,10},{3,11},{4,12},{5,13},{6,14},{7,15},{8,0},{9,1},... | collective-permute-start | bytes 884744 | tf_op jit(solution)/shard_map/ppermute | solution.py:536
  (14 other events, 97.2 us)

commit v11 on v10

--- a/solution.py
+++ b/solution.py
@@ -582,18 +582,22 @@
 
 
 def scatter_chunks(own, others, shift, sizes):
-    sums, before = [], []
+    sums, before, early = [], [], []
     for index, (terms, sending) in enumerate(zip(own, others)):
         if before:
             sending, _ = lax.optimization_barrier((sending, before))
         planes = [leave_along_a(plane, shift) for plane in sending]
         if index == len(own) - 1:
             for k, part in enumerate(planes):
-                terms = terms + [shift(add_all(part), "b", -k - 1)]
+                total = add_all(part)
+                if early:
+                    total, _ = lax.optimization_barrier((total, early))
+                terms = terms + [shift(total, "b", -k - 1)]
             found = scatter_plane(terms, shift, sizes)
         else:
             found = scatter_plane(terms, shift, sizes)
             before = [v for part in planes for v in part[1:]]
+            early = found[-1:]
             for k, part in enumerate(planes):
                 total = add_all(scatter_plane(part, shift, sizes))
                 found = found + [shift(total, "b", -k - 1)]

time: 191 us -> 189 us (0.990)
  waiting for transfers between devices: 89 us -> 85.7 us
    ppermute x24, waiting for transfers between devices: 87.7 us -> 84.5 us  [shift(): return lax.ppermute(value, BOTH, pairs(role, offset))]
  transfers between devices with their start and end apart: 29 -> 29, of which waited for: 17 -> 18; matrix products, arithmetic and copies ran while one was open for 3% -> 3% of each run, Pallas kernels for 27% -> 28%
where the time goes in v11:
time: 189 us
  waiting for transfers between devices  85.7 us (45%)
  Pallas kernels  60.9 us (32%)
  starting transfers between devices  32.7 us (17%)
  other arithmetic  5.1 us (3%)
  local copies, waits for them, and re-layouts  3.25 us (2%)
    ppermute x24, waiting for transfers between devices, shift(): return lax.ppermute(value, BOTH, pairs(role, offset))  84.5 us
    ppermute x24, starting transfers between devices, shift(): return lax.ppermute(value, BOTH, pairs(role, offset))  31.2 us
    pallas_call x2, Pallas kernels, attend(): pl.pallas_call(functools.partial(attend_kernel, first_row, len(riders), l...  26.7 us
    pallas_call x2, Pallas kernels, run_experts(): pl.pallas_call(functools.partial(expert_kernel, pieces, tuple(in_cuts), l...  22.6 us
    pallas_call x1, Pallas kernels, project(): pl.pallas_call(qkv_kernel, grid=(5,), in_specs=[vmem_spec()] * 5 + [pl.Bl...  7.4 us
  transfers between devices with their start and end apart: 29, of which 18 were waited for; matrix products, arithmetic and copies ran while one was open for 3% of the time, Pallas kernels for 28%

profile of v11, /device:TPU:0, one launch (start us, length us, event | category | flops | bytes accessed | tf_op | source)
XLA Modules:
  0.0 189.2 jit_solution(3162614225112344044)
XLA Ops:
  5.8 7.4 %project_rows.1 = (bf16[128,1536]{1,0:T(8,128)(2,1)}, bf16[128,1024]{1,0:T(8,128)(2,1)}, bf16[128,1024]{1,0:T(8,128)(2,1)}) custom-call(bf16[128,1536]{1,0:T(8,128)(2,1)} %tokens_ref.3, bf16[128,1536]{1,0:T(8,128)(2,1)} %copy-done.6, f32[1536]{0:T(1024)} %gain_ref.3, f32[256,128]{1,0:T(8,128)} %pad_maximum_fusion.4.cos_ref, ...), custom_call_target="tpu_custom_call" | custom-call | flops 1409286144 | bytes 9500000 | tf_op jit(solution)/shard_map/project_rows/pallas_call | solution.py:84
  15.2 13.3 %attend_rows.2 = (bf16[128,1536]{1,0:T(8,128)(2,1)}, bf16[128,1536]{1,0:T(8,128)(2,1)}, bf16[72,1536]{1,0:T(8,128)(2,1)}) custom-call(s32[1]{0:T(128)} %copy.24.place_ref, bf16[128,1536]{1,0:T(8,128)(2,1)} %get-tuple-element.42.q_ref, bf16[1,1024,512]{2,1,0:T(8,128)(2,1)} %kc_ref.3, bf16[1,1024,512]{2,1,0:T(8,128)(2,1)} %collective-permute-done.1.refs_0_.kco_ref, ...), custom_call_target="tpu_custom_call" | custom-call | flops 7247757312 | bytes 10000000 | tf_op jit(solution)/shard_map/attend_rows/pallas_call | solution.py:222
  28.6 5.1 %collective-permute-start.7 = (bf16[72,1536]{1,0:T(8,128)(2,1)}, bf16[72,1536]{1,0:T(8,128)(2,1)S(1)}, u32[]{:S(2)}, u32[]{:S(2)}) collective-permute-start(bf16[72,1536]{1,0:T(8,128)(2,1)} %get-tuple-element.51.refs_0_), channel_id=1, source_target_pairs={{0,24},{1,25},{2,26},{3,27},{4,28},{5,29},{6,30},{7,31},{8,16},{9,... | collective-permute-start | bytes 663560 | tf_op jit(solution)/shard_map/ppermute | solution.py:536
  34.3 13.4 %attend_rows.3 = (bf16[128,1536]{1,0:T(8,128)(2,1)}, bf16[128,1536]{1,0:T(8,128)(2,1)}, bf16[64,1536]{1,0:T(8,128)(2,1)}) custom-call(s32[1]{0:T(128)} %copy.24.place_ref, bf16[128,1536]{1,0:T(8,128)(2,1)} %get-tuple-element.42.q_ref, bf16[1,1024,512]{2,1,0:T(8,128)(2,1)} %kc_ref.3, ...), custom_call_target="tpu_custom_call", output_to_operand_aliasing={{0}: (13, {}), {1}: (14, {})} | custom-call | flops 7247757312 | bytes 10000000 | tf_op jit(solution)/shard_map/attend_rows/pallas_call | solution.py:222
  47.7 5.2 %collective-permute-done.6.refs_2_ = bf16[72,1536]{1,0:T(8,128)(2,1)S(1)} collective-permute-done((bf16[72,1536]{1,0:T(8,128)(2,1)}, bf16[72,1536]{1,0:T(8,128)(2,1)S(1)}, u32[]{:S(2)}, u32[]{:S(2)}) %collective-permute-start.6) | collective-permute-done | bytes 221216 | tf_op jit(solution)/shard_map/ppermute | solution.py:536
  53.9 1.6 collective-permute-start.11
  55.5 2.5 %collective-permute-start.10 = (bf16[64,1536]{1,0:T(8,128)(2,1)S(1)}, bf16[64,1536]{1,0:T(8,128)(2,1)S(1)}, u32[]{:S(2)}, u32[]{:S(2)}) collective-permute-start(bf16[64,1536]{1,0:T(8,128)(2,1)S(1)} %copy-done), channel_id=1, source_target_pairs={{0,24},{1,25},{2,26},{3,27},{4,28},{5,29},{6,30},{7,31},{8,16},{9,... | collective-permute-start | bytes 589832 | tf_op jit(solution)/shard_map/ppermute | solution.py:536
  57.9 1.9 %collective-permute-start.8 = (bf16[64,1536]{1,0:T(8,128)(2,1)S(1)}, bf16[64,1536]{1,0:T(8,128)(2,1)S(1)}, u32[]{:S(2)}, u32[]{:S(2)}) collective-permute-start(bf16[64,1536]{1,0:T(8,128)(2,1)S(1)} %copy-done), channel_id=1, source_target_pairs={{0,8},{1,9},{2,10},{3,11},{4,12},{5,13},{6,14},{7,15},{8,0},{9,1},... | collective-permute-start | bytes 589832 | tf_op jit(solution)/shard_map/ppermute | solution.py:536
  61.4 3.8 %collective-permute-done.10.refs_3_ = bf16[64,1536]{1,0:T(8,128)(2,1)S(1)} collective-permute-done((bf16[64,1536]{1,0:T(8,128)(2,1)S(1)}, bf16[64,1536]{1,0:T(8,128)(2,1)S(1)}, u32[]{:S(2)}, u32[]{:S(2)}) %collective-permute-start.10) | collective-permute-done | bytes 196640 | tf_op jit(solution)/shard_map/ppermute | solution.py:536
  65.2 7.9 %collective-permute-done.9.refs_2_ = bf16[64,1536]{1,0:T(8,128)(2,1)S(1)} collective-permute-done((bf16[64,1536]{1,0:T(8,128)(2,1)S(1)}, bf16[64,1536]{1,0:T(8,128)(2,1)S(1)}, u32[]{:S(2)}, u32[]{:S(2)}) %collective-permute-start.9) | collective-permute-done | bytes 196640 | tf_op jit(solution)/shard_map/ppermute | solution.py:536
  74.3 2.6 %collective-permute-start.13 = (bf16[4,64,1536]{2,1,0:T(8,128)(2,1)S(1)}, bf16[4,64,1536]{2,1,0:T(8,128)(2,1)}, u32[]{:S(2)}, u32[]{:S(2)}) collective-permute-start(bf16[4,64,1536]{2,1,0:T(8,128)(2,1)S(1)} %stack_rows.3.refs_1_), channel_id=1, source_target_pairs={{0,4},{1,3},{2,6},{3,1},{4,0},{5,7},{6,2},{7,5},{8,12},{9,11},{10,... | collective-permute-start | bytes 2359304 | tf_op jit(solution)/shard_map/ppermute | solution.py:536
  80.1 15.4 %collective-permute-done.13.refs_3_ = bf16[4,64,1536]{2,1,0:T(8,128)(2,1)} collective-permute-done((bf16[4,64,1536]{2,1,0:T(8,128)(2,1)S(1)}, bf16[4,64,1536]{2,1,0:T(8,128)(2,1)}, u32[]{:S(2)}, u32[]{:S(2)}) %collective-permute-start.13) | collective-permute-done | bytes 786464 | tf_op jit(solution)/shard_map/ppermute | solution.py:536
  97.0 11.5 %run_experts.2.held_ref.refs_10_ = bf16[4,256,1536]{2,1,0:T(8,128)(2,1)S(1)} custom-call(bf16[4,72,1536]{2,1,0:T(8,128)(2,1)S(1)} %stack_rows.2.refs_0_, bf16[4,64,1536]{2,1,0:T(8,128)(2,1)S(1)} %stack_rows.3.refs_1_, bf16[4,72,1536]{2,1,0:T(8,128)(2,1)S(1)} %collective-permute-done.12.refs_1_.refs_2_, bf16[4,64,1536]{2,1,0:T(8,128)(2,1)} %collective-permute-done.13.refs_3_, ...), custom_call_target="tpu_custom_call" | custom-call | flops 8053063680 | bytes 26000000 | tf_op jit(solution)/shard_map/run_experts/pallas_call | solution.py:415
  114.4 11.1 %run_experts.3.held_ref = bf16[4,256,1536]{2,1,0:T(8,128)(2,1)S(1)} custom-call(bf16[4,72,1536]{2,1,0:T(8,128)(2,1)S(1)} %collective-permute-done.11.refs_4_.refs_0_, bf16[4,64,1536]{2,1,0:T(8,128)(2,1)S(1)} %collective-permute-done.14.refs_1_, bf16[4,72,1536]{2,1,0:T(8,128)(2,1)S(1)} %collective-permute-done.18.refs_1_.refs_2_, ...), custom_call_target="tpu_custom_call" | custom-call | flops 8053063680 | bytes 26000000 | tf_op jit(solution)/shard_map/run_experts/pallas_call | solution.py:415
  125.5 6.1 %collective-permute-done.17.refs_1_ = bf16[4,48,1536]{2,1,0:T(8,128)(2,1)S(1)} collective-permute-done((bf16[4,48,1536]{2,1,0:T(8,128)(2,1)S(1)}, bf16[4,48,1536]{2,1,0:T(8,128)(2,1)S(1)}, u32[]{:S(2)}, u32[]{:S(2)}) %collective-permute-start.17) | collective-permute-done | bytes 589856 | tf_op jit(solution)/shard_map/ppermute | solution.py:536
  132.6 1.6 collective-permute-start.21
  134.5 11.6 %collective-permute-done.19 = bf16[2,80,1536]{2,1,0:T(8,128)(2,1)S(1)} collective-permute-done((bf16[2,80,1536]{2,1,0:T(8,128)(2,1)S(1)}, bf16[2,80,1536]{2,1,0:T(8,128)(2,1)S(1)}, u32[]{:S(2)}, u32[]{:S(2)}) %collective-permute-start.19) | collective-permute-done | bytes 491552 | tf_op jit(solution)/shard_map/ppermute | solution.py:536
  149.8 7.4 %collective-permute-done.25 = bf16[4,48,1536]{2,1,0:T(8,128)(2,1)S(1)} collective-permute-done((bf16[4,48,1536]{2,1,0:T(8,128)(2,1)S(1)}, bf16[4,48,1536]{2,1,0:T(8,128)(2,1)S(1)}, u32[]{:S(2)}, u32[]{:S(2)}) %collective-permute-start.25) | collective-permute-done | bytes 589856 | tf_op jit(solution)/shard_map/ppermute | solution.py:536
  159.2 5.3 %collective-permute-done.22 = bf16[2,80,1536]{2,1,0:T(8,128)(2,1)S(1)} collective-permute-done((bf16[2,80,1536]{2,1,0:T(8,128)(2,1)S(1)}, bf16[2,80,1536]{2,1,0:T(8,128)(2,1)S(1)}, u32[]{:S(2)}, u32[]{:S(2)}) %collective-permute-start.22) | collective-permute-done | bytes 491552 | tf_op jit(solution)/shard_map/ppermute | solution.py:536
  164.9 2.8 %collective-permute-done.26 = bf16[4,48,1536]{2,1,0:T(8,128)(2,1)S(1)} collective-permute-done((bf16[4,48,1536]{2,1,0:T(8,128)(2,1)S(1)}, bf16[4,48,1536]{2,1,0:T(8,128)(2,1)S(1)}, u32[]{:S(2)}, u32[]{:S(2)}) %collective-permute-start.26) | collective-permute-done | bytes 589856 | tf_op jit(solution)/shard_map/ppermute | solution.py:536
  169.4 7.1 %collective-permute-done.23 = bf16[80,1536]{1,0:T(8,128)(2,1)S(1)} collective-permute-done((bf16[80,1536]{1,0:T(8,128)(2,1)S(1)}, bf16[80,1536]{1,0:T(8,128)(2,1)S(1)}, u32[]{:S(2)}, u32[]{:S(2)}) %collective-permute-start.23) | collective-permute-done | bytes 245792 | tf_op jit(solution)/shard_map/ppermute | solution.py:536
  178.0 2.5 %collective-permute-done.27 = bf16[2,48,1536]{2,1,0:T(8,128)(2,1)S(1)} collective-permute-done((bf16[2,48,1536]{2,1,0:T(8,128)(2,1)S(1)}, bf16[2,48,1536]{2,1,0:T(8,128)(2,1)S(1)}, u32[]{:S(2)}, u32[]{:S(2)}) %collective-permute-start.27) | collective-permute-done | bytes 294944 | tf_op jit(solution)/shard_map/ppermute | solution.py:536
  180.7 2.1 %collective-permute-done.24 = bf16[80,1536]{1,0:T(8,128)(2,1)S(1)} collective-permute-done((bf16[80,1536]{1,0:T(8,128)(2,1)S(1)}, bf16[80,1536]{1,0:T(8,128)(2,1)S(1)}, u32[]{:S(2)}, u32[]{:S(2)}) %collective-permute-start.24) | collective-permute-done | bytes 245792 | tf_op jit(solution)/shard_map/ppermute | solution.py:536
  183.0 5.3 %collective-permute-done.28 = bf16[48,1536]{1,0:T(8,128)(2,1)S(1)} collective-permute-done((bf16[48,1536]{1,0:T(8,128)(2,1)S(1)}, bf16[48,1536]{1,0:T(8,128)(2,1)S(1)}, u32[]{:S(2)}, u32[]{:S(2)}) %collective-permute-start.28) | collective-permute-done | bytes 147488 | tf_op jit(solution)/shard_map/ppermute | solution.py:536
  (92 shorter events, 33.1 us)
Async XLA Ops:
  13.2 21.0 %collective-permute-start.3 = (bf16[2,1536,1024]{2,1,0:T(8,128)(2,1)}, bf16[2,1536,1024]{2,1,0:T(8,128)(2,1)}, u32[]{:S(2)}, u32[]{:S(2)}) collective-permute-start(bf16[2,1536,1024]{2,1,0:T(8,128)(2,1)} %refs_6_.3), channel_id=1, source_target_pairs={{0,1},{1,0},{2,3},{3,2},{4,5},{5,4},{6,7},{7,6},{8,9},{9,8},{10,11... | collective-permute-start | bytes 18874376 | tf_op jit(solution)/shard_map/ppermute | solution.py:649
  13.6 20.6 %collective-permute-start.4 = (bf16[2,512,1536]{2,1,0:T(8,128)(2,1)S(1)}, bf16[2,512,1536]{2,1,0:T(8,128)(2,1)}, u32[]{:S(2)}, u32[]{:S(2)}) collective-permute-start(bf16[2,512,1536]{2,1,0:T(8,128)(2,1)S(1)} %copy-done.3), channel_id=1, source_target_pairs={{0,1},{1,0},{2,3},{3,2},{4,5},{5,4},{6,7},{7,6},{8,9},{9,8},{10,11... | collective-permute-start | bytes 9437192 | tf_op jit(solution)/shard_map/ppermute | solution.py:649
  28.6 19.1 %collective-permute-start.7 = (bf16[72,1536]{1,0:T(8,128)(2,1)}, bf16[72,1536]{1,0:T(8,128)(2,1)S(1)}, u32[]{:S(2)}, u32[]{:S(2)}) collective-permute-start(bf16[72,1536]{1,0:T(8,128)(2,1)} %get-tuple-element.51.refs_0_), channel_id=1, source_target_pairs={{0,24},{1,25},{2,26},{3,27},{4,28},{5,29},{6,30},{7,31},{8,16},{9,... | collective-permute-start | bytes 663560 | tf_op jit(solution)/shard_map/ppermute | solution.py:536
  33.6 19.3 %collective-permute-start.6 = (bf16[72,1536]{1,0:T(8,128)(2,1)}, bf16[72,1536]{1,0:T(8,128)(2,1)S(1)}, u32[]{:S(2)}, u32[]{:S(2)}) collective-permute-start(bf16[72,1536]{1,0:T(8,128)(2,1)} %get-tuple-element.51.refs_0_), channel_id=1, source_target_pairs={{0,16},{1,17},{2,18},{3,19},{4,20},{5,21},{6,22},{7,23},{8,24},{9,... | collective-permute-start | bytes 663560 | tf_op jit(solution)/shard_map/ppermute | solution.py:536
  33.6 19.3 %collective-permute-start.5 = (bf16[72,1536]{1,0:T(8,128)(2,1)}, bf16[72,1536]{1,0:T(8,128)(2,1)S(1)}, u32[]{:S(2)}, u32[]{:S(2)}) collective-permute-start(bf16[72,1536]{1,0:T(8,128)(2,1)} %get-tuple-element.51.refs_0_), channel_id=1, source_target_pairs={{0,8},{1,9},{2,10},{3,11},{4,12},{5,13},{6,14},{7,15},{8,0},{9,1},... | collective-permute-start | bytes 663560 | tf_op jit(solution)/shard_map/ppermute | solution.py:536
  53.9 19.4 %collective-permute-start.11 = (bf16[4,72,1536]{2,1,0:T(8,128)(2,1)S(1)}, bf16[4,72,1536]{2,1,0:T(8,128)(2,1)S(1)}, u32[]{:S(2)}, u32[]{:S(2)}) collective-permute-start(bf16[4,72,1536]{2,1,0:T(8,128)(2,1)S(1)} %stack_rows.2.refs_0_), channel_id=1, source_target_pairs={{0,2},{1,5},{2,0},{3,7},{4,6},{5,1},{6,4},{7,3},{8,10},{9,13},{10,... | collective-permute-start | bytes 2654216 | tf_op jit(solution)/shard_map/ppermute | solution.py:536
  55.5 9.7 %collective-permute-start.10 = (bf16[64,1536]{1,0:T(8,128)(2,1)S(1)}, bf16[64,1536]{1,0:T(8,128)(2,1)S(1)}, u32[]{:S(2)}, u32[]{:S(2)}) collective-permute-start(bf16[64,1536]{1,0:T(8,128)(2,1)S(1)} %copy-done), channel_id=1, source_target_pairs={{0,24},{1,25},{2,26},{3,27},{4,28},{5,29},{6,30},{7,31},{8,16},{9,... | collective-permute-start | bytes 589832 | tf_op jit(solution)/shard_map/ppermute | solution.py:536
  57.9 15.2 %collective-permute-start.9 = (bf16[64,1536]{1,0:T(8,128)(2,1)S(1)}, bf16[64,1536]{1,0:T(8,128)(2,1)S(1)}, u32[]{:S(2)}, u32[]{:S(2)}) collective-permute-start(bf16[64,1536]{1,0:T(8,128)(2,1)S(1)} %copy-done), channel_id=1, source_target_pairs={{0,16},{1,17},{2,18},{3,19},{4,20},{5,21},{6,22},{7,23},{8,24},{9,... | collective-permute-start | bytes 589832 | tf_op jit(solution)/shard_map/ppermute | solution.py:536
  57.9 15.2 %collective-permute-start.8 = (bf16[64,1536]{1,0:T(8,128)(2,1)S(1)}, bf16[64,1536]{1,0:T(8,128)(2,1)S(1)}, u32[]{:S(2)}, u32[]{:S(2)}) collective-permute-start(bf16[64,1536]{1,0:T(8,128)(2,1)S(1)} %copy-done), channel_id=1, source_target_pairs={{0,8},{1,9},{2,10},{3,11},{4,12},{5,13},{6,14},{7,15},{8,0},{9,1},... | collective-permute-start | bytes 589832 | tf_op jit(solution)/shard_map/ppermute | solution.py:536
  59.9 18.7 %collective-permute-start.12 = (bf16[4,72,1536]{2,1,0:T(8,128)(2,1)S(1)}, bf16[4,72,1536]{2,1,0:T(8,128)(2,1)S(1)}, u32[]{:S(2)}, u32[]{:S(2)}) collective-permute-start(bf16[4,72,1536]{2,1,0:T(8,128)(2,1)S(1)} %stack_rows.2.refs_0_), channel_id=1, source_target_pairs={{0,4},{1,3},{2,6},{3,1},{4,0},{5,7},{6,2},{7,5},{8,12},{9,11},{10,... | collective-permute-start | bytes 2654216 | tf_op jit(solution)/shard_map/ppermute | solution.py:536
  74.3 21.1 %collective-permute-start.13 = (bf16[4,64,1536]{2,1,0:T(8,128)(2,1)S(1)}, bf16[4,64,1536]{2,1,0:T(8,128)(2,1)}, u32[]{:S(2)}, u32[]{:S(2)}) collective-permute-start(bf16[4,64,1536]{2,1,0:T(8,128)(2,1)S(1)} %stack_rows.3.refs_1_), channel_id=1, source_target_pairs={{0,4},{1,3},{2,6},{3,1},{4,0},{5,7},{6,2},{7,5},{8,12},{9,11},{10,... | collective-permute-start | bytes 2359304 | tf_op jit(solution)/shard_map/ppermute | solution.py:536
  77.0 33.2 %collective-permute-start.14 = (bf16[4,64,1536]{2,1,0:T(8,128)(2,1)S(1)}, bf16[4,64,1536]{2,1,0:T(8,128)(2,1)S(1)}, u32[]{:S(2)}, u32[]{:S(2)}) collective-permute-start(bf16[4,64,1536]{2,1,0:T(8,128)(2,1)S(1)} %stack_rows.3.refs_1_), channel_id=1, source_target_pairs={{0,2},{1,5},{2,0},{3,7},{4,6},{5,1},{6,4},{7,3},{8,10},{9,13},{10,... | collective-permute-start | bytes 2359304 | tf_op jit(solution)/shard_map/ppermute | solution.py:536
  78.5 34.3 %collective-permute-start.18 = (bf16[4,72,1536]{2,1,0:T(8,128)(2,1)S(1)}, bf16[4,72,1536]{2,1,0:T(8,128)(2,1)S(1)}, u32[]{:S(2)}, u32[]{:S(2)}) collective-permute-start(bf16[4,72,1536]{2,1,0:T(8,128)(2,1)S(1)} %collective-permute-done.12.refs_1_.refs_2_), channel_id=1, source_target_pairs={{0,2},{1,5},{2,0},{3,7},{4,6},{5,1},{6,4},{7,3},{8,10},{9,13},{10,... | collective-permute-start | bytes 2654216 | tf_op jit(solution)/shard_map/ppermute | solution.py:536
  95.5 15.8 %collective-permute-start.15 = (bf16[4,64,1536]{2,1,0:T(8,128)(2,1)}, bf16[4,64,1536]{2,1,0:T(8,128)(2,1)S(1)}, u32[]{:S(2)}, u32[]{:S(2)}) collective-permute-start(bf16[4,64,1536]{2,1,0:T(8,128)(2,1)} %collective-permute-done.13.refs_3_), channel_id=1, source_target_pairs={{0,2},{1,5},{2,0},{3,7},{4,6},{5,1},{6,4},{7,3},{8,10},{9,13},{10,... | collective-permute-start | bytes 2359304 | tf_op jit(solution)/shard_map/ppermute | solution.py:536
  111.3 20.4 %collective-permute-start.16 = (bf16[4,80,1536]{2,1,0:T(8,128)(2,1)S(1)}, bf16[4,80,1536]{2,1,0:T(8,128)(2,1)S(1)}, u32[]{:S(2)}, u32[]{:S(2)}) collective-permute-start(bf16[4,80,1536]{2,1,0:T(8,128)(2,1)S(1)} %get-tuple-element.62), channel_id=1, source_target_pairs={{0,4},{1,3},{2,6},{3,1},{4,0},{5,7},{6,2},{7,5},{8,12},{9,11},{10,... | collective-permute-start | bytes 2949128 | tf_op jit(solution)/shard_map/ppermute | solution.py:536
  113.8 17.8 %collective-permute-start.17 = (bf16[4,48,1536]{2,1,0:T(8,128)(2,1)S(1)}, bf16[4,48,1536]{2,1,0:T(8,128)(2,1)S(1)}, u32[]{:S(2)}, u32[]{:S(2)}) collective-permute-start(bf16[4,48,1536]{2,1,0:T(8,128)(2,1)S(1)} %get-tuple-element.64), channel_id=1, source_target_pairs={{0,4},{1,3},{2,6},{3,1},{4,0},{5,7},{6,2},{7,5},{8,12},{9,11},{10,... | collective-permute-start | bytes 1769480 | tf_op jit(solution)/shard_map/ppermute | solution.py:536
  132.6 14.6 %collective-permute-start.21 = (bf16[4,80,1536]{2,1,0:T(8,128)(2,1)S(1)}, bf16[4,80,1536]{2,1,0:T(8,128)(2,1)S(1)}, u32[]{:S(2)}, u32[]{:S(2)}) collective-permute-start(bf16[4,80,1536]{2,1,0:T(8,128)(2,1)S(1)} %get-tuple-element.72), channel_id=1, source_target_pairs={{0,4},{1,3},{2,6},{3,1},{4,0},{5,7},{6,2},{7,5},{8,12},{9,11},{10,... | collective-permute-start | bytes 2949128 | tf_op jit(solution)/shard_map/ppermute | solution.py:536
  134.4 11.7 %collective-permute-start.19 = (bf16[2,80,1536]{2,1,0:T(8,128)(2,1)S(1)}, bf16[2,80,1536]{2,1,0:T(8,128)(2,1)S(1)}, u32[]{:S(2)}, u32[]{:S(2)}) collective-permute-start(bf16[2,80,1536]{2,1,0:T(8,128)(2,1)S(1)} %pad_maximum_fusion), channel_id=1, source_target_pairs={{0,8},{1,9},{2,10},{3,11},{4,12},{5,13},{6,14},{7,15},{8,0},{9,1},... | collective-permute-start | bytes 1474568 | tf_op jit(solution)/shard_map/ppermute | solution.py:536
  146.2 11.7 %collective-permute-start.20 = (bf16[80,1536]{1,0:T(8,128)(2,1)S(1)}, bf16[80,1536]{1,0:T(8,128)(2,1)S(1)}, u32[]{:S(2)}, u32[]{:S(2)}) collective-permute-start(bf16[80,1536]{1,0:T(8,128)(2,1)S(1)} %fusion.4), channel_id=1, source_target_pairs={{0,16},{1,17},{2,18},{3,19},{4,20},{5,21},{6,22},{7,23},{8,24},{9,... | collective-permute-start | bytes 737288 | tf_op jit(solution)/shard_map/ppermute | solution.py:536
  147.3 9.9 %collective-permute-start.25 = (bf16[4,48,1536]{2,1,0:T(8,128)(2,1)S(1)}, bf16[4,48,1536]{2,1,0:T(8,128)(2,1)S(1)}, u32[]{:S(2)}, u32[]{:S(2)}) collective-permute-start(bf16[4,48,1536]{2,1,0:T(8,128)(2,1)S(1)} %get-tuple-element.78), channel_id=1, source_target_pairs={{0,4},{1,3},{2,6},{3,1},{4,0},{5,7},{6,2},{7,5},{8,12},{9,11},{10,... | collective-permute-start | bytes 1769480 | tf_op jit(solution)/shard_map/ppermute | solution.py:536
  148.5 16.0 %collective-permute-start.22 = (bf16[2,80,1536]{2,1,0:T(8,128)(2,1)S(1)}, bf16[2,80,1536]{2,1,0:T(8,128)(2,1)S(1)}, u32[]{:S(2)}, u32[]{:S(2)}) collective-permute-start(bf16[2,80,1536]{2,1,0:T(8,128)(2,1)S(1)} %pad_maximum_fusion.1), channel_id=1, source_target_pairs={{0,8},{1,9},{2,10},{3,11},{4,12},{5,13},{6,14},{7,15},{8,0},{9,1},... | collective-permute-start | bytes 1474568 | tf_op jit(solution)/shard_map/ppermute | solution.py:536
  157.9 9.9 %collective-permute-start.26 = (bf16[4,48,1536]{2,1,0:T(8,128)(2,1)S(1)}, bf16[4,48,1536]{2,1,0:T(8,128)(2,1)S(1)}, u32[]{:S(2)}, u32[]{:S(2)}) collective-permute-start(bf16[4,48,1536]{2,1,0:T(8,128)(2,1)S(1)} %add_convert_fusion), channel_id=1, source_target_pairs={{0,2},{1,5},{2,0},{3,7},{4,6},{5,1},{6,4},{7,3},{8,10},{9,13},{10,... | collective-permute-start | bytes 1769480 | tf_op jit(solution)/shard_map/ppermute | solution.py:536
  164.6 11.9 %collective-permute-start.23 = (bf16[80,1536]{1,0:T(8,128)(2,1)S(1)}, bf16[80,1536]{1,0:T(8,128)(2,1)S(1)}, u32[]{:S(2)}, u32[]{:S(2)}) collective-permute-start(bf16[80,1536]{1,0:T(8,128)(2,1)S(1)} %fusion.5), channel_id=1, source_target_pairs={{0,16},{1,17},{2,18},{3,19},{4,20},{5,21},{6,22},{7,23},{8,24},{9,... | collective-permute-start | bytes 737288 | tf_op jit(solution)/shard_map/ppermute | solution.py:536
  167.9 12.6 %collective-permute-start.27 = (bf16[2,48,1536]{2,1,0:T(8,128)(2,1)S(1)}, bf16[2,48,1536]{2,1,0:T(8,128)(2,1)S(1)}, u32[]{:S(2)}, u32[]{:S(2)}) collective-permute-start(bf16[2,48,1536]{2,1,0:T(8,128)(2,1)S(1)} %pad_maximum_fusion.3), channel_id=1, source_target_pairs={{0,8},{1,9},{2,10},{3,11},{4,12},{5,13},{6,14},{7,15},{8,0},{9,1},... | collective-permute-start | bytes 884744 | tf_op jit(solution)/shard_map/ppermute | solution.py:536
  (14 other events, 97.2 us)

commit v12 on v11

--- a/solution.py
+++ b/solution.py
@@ -721,7 +721,7 @@
             (half, row_count - half),
             [held] if index else [],
         )
-        mixed = mix_rows(held, back, sizes["a"], cuts, [v for line in own for v in line[1:]])
+        mixed = mix_rows(held, back, sizes["a"], cuts, [v for line in own[:1] for v in line[1:]])
         chunks = [[piece[i] for piece in mixed] for i in range(len(cuts))]
         if index == 0:
             chunks, _ = lax.optimization_barrier((chunks, halves[1][1:]))
@@ -729,7 +729,7 @@
         else:
             others.append(chunks)
     others = [[planes[i] for planes in others] for i in range(len(cuts))]
-    own, _ = lax.optimization_barrier((own, held))
+    own, _ = lax.optimization_barrier((own, others))
     expert_mix = scatter_chunks(own, others, shift, sizes)
     return (attended, stream, expert_mix, appended)
 

time: 189 us -> 190 us (level)
  no operation moved by 1% of the time
where the time goes in v12:
time: 190 us
  waiting for transfers between devices  86.5 us (46%)
  Pallas kernels  60.9 us (32%)
  starting transfers between devices  32.5 us (17%)
  other arithmetic  5.1 us (3%)
  local copies, waits for them, and re-layouts  3.25 us (2%)
    ppermute x24, waiting for transfers between devices, shift(): return lax.ppermute(value, BOTH, pairs(role, offset))  85.2 us
    ppermute x24, starting transfers between devices, shift(): return lax.ppermute(value, BOTH, pairs(role, offset))  30.9 us
    pallas_call x2, Pallas kernels, attend(): pl.pallas_call(functools.partial(attend_kernel, first_row, len(riders), l...  26.7 us
    pallas_call x2, Pallas kernels, run_experts(): pl.pallas_call(functools.partial(expert_kernel, pieces, tuple(in_cuts), l...  22.6 us
    pallas_call x1, Pallas kernels, project(): pl.pallas_call(qkv_kernel, grid=(5,), in_specs=[vmem_spec()] * 5 + [pl.Bl...  7.4 us
  transfers between devices with their start and end apart: 29, of which 18 were waited for; matrix products, arithmetic and copies ran while one was open for 3% of the time, Pallas kernels for 28%

profile of v12, /device:TPU:0, one launch (start us, length us, event | category | flops | bytes accessed | tf_op | source)
XLA Modules:
  0.0 189.7 jit_solution(6464320565416626172)
XLA Ops:
  5.8 7.4 %project_rows.1 = (bf16[128,1536]{1,0:T(8,128)(2,1)}, bf16[128,1024]{1,0:T(8,128)(2,1)}, bf16[128,1024]{1,0:T(8,128)(2,1)}) custom-call(bf16[128,1536]{1,0:T(8,128)(2,1)} %tokens_ref.3, bf16[128,1536]{1,0:T(8,128)(2,1)} %copy-done.6, f32[1536]{0:T(1024)} %gain_ref.3, f32[256,128]{1,0:T(8,128)} %pad_maximum_fusion.4.cos_ref, ...), custom_call_target="tpu_custom_call" | custom-call | flops 1409286144 | bytes 9500000 | tf_op jit(solution)/shard_map/project_rows/pallas_call | solution.py:84
  15.2 13.3 %attend_rows.2 = (bf16[128,1536]{1,0:T(8,128)(2,1)}, bf16[128,1536]{1,0:T(8,128)(2,1)}, bf16[72,1536]{1,0:T(8,128)(2,1)}) custom-call(s32[1]{0:T(128)} %copy.24.place_ref, bf16[128,1536]{1,0:T(8,128)(2,1)} %get-tuple-element.42.q_ref, bf16[1,1024,512]{2,1,0:T(8,128)(2,1)} %kc_ref.3, bf16[1,1024,512]{2,1,0:T(8,128)(2,1)} %collective-permute-done.1.refs_0_.kco_ref, ...), custom_call_target="tpu_custom_call" | custom-call | flops 7247757312 | bytes 10000000 | tf_op jit(solution)/shard_map/attend_rows/pallas_call | solution.py:222
  28.6 5.1 %collective-permute-start.7 = (bf16[72,1536]{1,0:T(8,128)(2,1)}, bf16[72,1536]{1,0:T(8,128)(2,1)S(1)}, u32[]{:S(2)}, u32[]{:S(2)}) collective-permute-start(bf16[72,1536]{1,0:T(8,128)(2,1)} %get-tuple-element.51.refs_0_), channel_id=1, source_target_pairs={{0,24},{1,25},{2,26},{3,27},{4,28},{5,29},{6,30},{7,31},{8,16},{9,... | collective-permute-start | bytes 663560 | tf_op jit(solution)/shard_map/ppermute | solution.py:536
  34.3 13.4 %attend_rows.3 = (bf16[128,1536]{1,0:T(8,128)(2,1)}, bf16[128,1536]{1,0:T(8,128)(2,1)}, bf16[64,1536]{1,0:T(8,128)(2,1)}) custom-call(s32[1]{0:T(128)} %copy.24.place_ref, bf16[128,1536]{1,0:T(8,128)(2,1)} %get-tuple-element.42.q_ref, bf16[1,1024,512]{2,1,0:T(8,128)(2,1)} %kc_ref.3, ...), custom_call_target="tpu_custom_call", output_to_operand_aliasing={{0}: (13, {}), {1}: (14, {})} | custom-call | flops 7247757312 | bytes 10000000 | tf_op jit(solution)/shard_map/attend_rows/pallas_call | solution.py:222
  47.7 5.2 %collective-permute-done.6.refs_2_ = bf16[72,1536]{1,0:T(8,128)(2,1)S(1)} collective-permute-done((bf16[72,1536]{1,0:T(8,128)(2,1)}, bf16[72,1536]{1,0:T(8,128)(2,1)S(1)}, u32[]{:S(2)}, u32[]{:S(2)}) %collective-permute-start.6) | collective-permute-done | bytes 221216 | tf_op jit(solution)/shard_map/ppermute | solution.py:536
  55.5 2.5 %collective-permute-start.10 = (bf16[64,1536]{1,0:T(8,128)(2,1)S(1)}, bf16[64,1536]{1,0:T(8,128)(2,1)S(1)}, u32[]{:S(2)}, u32[]{:S(2)}) collective-permute-start(bf16[64,1536]{1,0:T(8,128)(2,1)S(1)} %copy-done), channel_id=1, source_target_pairs={{0,24},{1,25},{2,26},{3,27},{4,28},{5,29},{6,30},{7,31},{8,16},{9,... | collective-permute-start | bytes 589832 | tf_op jit(solution)/shard_map/ppermute | solution.py:536
  57.9 1.9 %collective-permute-start.8 = (bf16[64,1536]{1,0:T(8,128)(2,1)S(1)}, bf16[64,1536]{1,0:T(8,128)(2,1)S(1)}, u32[]{:S(2)}, u32[]{:S(2)}) collective-permute-start(bf16[64,1536]{1,0:T(8,128)(2,1)S(1)} %copy-done), channel_id=1, source_target_pairs={{0,8},{1,9},{2,10},{3,11},{4,12},{5,13},{6,14},{7,15},{8,0},{9,1},... | collective-permute-start | bytes 589832 | tf_op jit(solution)/shard_map/ppermute | solution.py:536
  61.4 3.8 %collective-permute-done.10.refs_3_ = bf16[64,1536]{1,0:T(8,128)(2,1)S(1)} collective-permute-done((bf16[64,1536]{1,0:T(8,128)(2,1)S(1)}, bf16[64,1536]{1,0:T(8,128)(2,1)S(1)}, u32[]{:S(2)}, u32[]{:S(2)}) %collective-permute-start.10) | collective-permute-done | bytes 196640 | tf_op jit(solution)/shard_map/ppermute | solution.py:536
  65.2 7.9 %collective-permute-done.9.refs_2_ = bf16[64,1536]{1,0:T(8,128)(2,1)S(1)} collective-permute-done((bf16[64,1536]{1,0:T(8,128)(2,1)S(1)}, bf16[64,1536]{1,0:T(8,128)(2,1)S(1)}, u32[]{:S(2)}, u32[]{:S(2)}) %collective-permute-start.9) | collective-permute-done | bytes 196640 | tf_op jit(solution)/shard_map/ppermute | solution.py:536
  74.3 2.6 %collective-permute-start.13 = (bf16[4,64,1536]{2,1,0:T(8,128)(2,1)S(1)}, bf16[4,64,1536]{2,1,0:T(8,128)(2,1)}, u32[]{:S(2)}, u32[]{:S(2)}) collective-permute-start(bf16[4,64,1536]{2,1,0:T(8,128)(2,1)S(1)} %stack_rows.3.refs_1_), channel_id=1, source_target_pairs={{0,4},{1,3},{2,6},{3,1},{4,0},{5,7},{6,2},{7,5},{8,12},{9,11},{10,... | collective-permute-start | bytes 2359304 | tf_op jit(solution)/shard_map/ppermute | solution.py:536
  80.1 15.4 %collective-permute-done.13.refs_3_ = bf16[4,64,1536]{2,1,0:T(8,128)(2,1)} collective-permute-done((bf16[4,64,1536]{2,1,0:T(8,128)(2,1)S(1)}, bf16[4,64,1536]{2,1,0:T(8,128)(2,1)}, u32[]{:S(2)}, u32[]{:S(2)}) %collective-permute-start.13) | collective-permute-done | bytes 786464 | tf_op jit(solution)/shard_map/ppermute | solution.py:536
  97.0 11.5 %run_experts.2.held_ref.refs_10_ = bf16[4,256,1536]{2,1,0:T(8,128)(2,1)S(1)} custom-call(bf16[4,72,1536]{2,1,0:T(8,128)(2,1)S(1)} %stack_rows.2.refs_0_, bf16[4,64,1536]{2,1,0:T(8,128)(2,1)S(1)} %stack_rows.3.refs_1_, bf16[4,72,1536]{2,1,0:T(8,128)(2,1)S(1)} %collective-permute-done.12.refs_1_.refs_2_, bf16[4,64,1536]{2,1,0:T(8,128)(2,1)} %collective-permute-done.13.refs_3_, ...), custom_call_target="tpu_custom_call" | custom-call | flops 8053063680 | bytes 26000000 | tf_op jit(solution)/shard_map/run_experts/pallas_call | solution.py:415
  114.4 11.1 %run_experts.3.held_ref = bf16[4,256,1536]{2,1,0:T(8,128)(2,1)S(1)} custom-call(bf16[4,72,1536]{2,1,0:T(8,128)(2,1)S(1)} %collective-permute-done.11.refs_4_.refs_0_, bf16[4,64,1536]{2,1,0:T(8,128)(2,1)S(1)} %collective-permute-done.14.refs_1_, bf16[4,72,1536]{2,1,0:T(8,128)(2,1)S(1)} %collective-permute-done.18.refs_1_.refs_2_, ...), custom_call_target="tpu_custom_call" | custom-call | flops 8053063680 | bytes 26000000 | tf_op jit(solution)/shard_map/run_experts/pallas_call | solution.py:415
  128.1 3.6 %collective-permute-done.17 = bf16[4,48,1536]{2,1,0:T(8,128)(2,1)S(1)} collective-permute-done((bf16[4,48,1536]{2,1,0:T(8,128)(2,1)S(1)}, bf16[4,48,1536]{2,1,0:T(8,128)(2,1)S(1)}, u32[]{:S(2)}, u32[]{:S(2)}) %collective-permute-start.17) | collective-permute-done | bytes 589856 | tf_op jit(solution)/shard_map/ppermute | solution.py:536
  131.9 12.8 %collective-permute-done.19 = bf16[2,80,1536]{2,1,0:T(8,128)(2,1)S(1)} collective-permute-done((bf16[2,80,1536]{2,1,0:T(8,128)(2,1)S(1)}, bf16[2,80,1536]{2,1,0:T(8,128)(2,1)S(1)}, u32[]{:S(2)}, u32[]{:S(2)}) %collective-permute-start.19) | collective-permute-done | bytes 491552 | tf_op jit(solution)/shard_map/ppermute | solution.py:536
  146.7 1.8 collective-permute-start.22
  148.5 7.2 %collective-permute-done.25 = bf16[4,48,1536]{2,1,0:T(8,128)(2,1)S(1)} collective-permute-done((bf16[4,48,1536]{2,1,0:T(8,128)(2,1)S(1)}, bf16[4,48,1536]{2,1,0:T(8,128)(2,1)S(1)}, u32[]{:S(2)}, u32[]{:S(2)}) %collective-permute-start.25) | collective-permute-done | bytes 589856 | tf_op jit(solution)/shard_map/ppermute | solution.py:536
  155.8 2.0 %collective-permute-done.20 = bf16[80,1536]{1,0:T(8,128)(2,1)S(1)} collective-permute-done((bf16[80,1536]{1,0:T(8,128)(2,1)S(1)}, bf16[80,1536]{1,0:T(8,128)(2,1)S(1)}, u32[]{:S(2)}, u32[]{:S(2)}) %collective-permute-start.20) | collective-permute-done | bytes 245792 | tf_op jit(solution)/shard_map/ppermute | solution.py:536
  157.8 4.9 %collective-permute-done.22 = bf16[2,80,1536]{2,1,0:T(8,128)(2,1)S(1)} collective-permute-done((bf16[2,80,1536]{2,1,0:T(8,128)(2,1)S(1)}, bf16[2,80,1536]{2,1,0:T(8,128)(2,1)S(1)}, u32[]{:S(2)}, u32[]{:S(2)}) %collective-permute-start.22) | collective-permute-done | bytes 491552 | tf_op jit(solution)/shard_map/ppermute | solution.py:536
  163.8 3.9 %collective-permute-done.26 = bf16[4,48,1536]{2,1,0:T(8,128)(2,1)S(1)} collective-permute-done((bf16[4,48,1536]{2,1,0:T(8,128)(2,1)S(1)}, bf16[4,48,1536]{2,1,0:T(8,128)(2,1)S(1)}, u32[]{:S(2)}, u32[]{:S(2)}) %collective-permute-start.26) | collective-permute-done | bytes 589856 | tf_op jit(solution)/shard_map/ppermute | solution.py:536
  167.9 5.9 %collective-permute-done.23 = bf16[80,1536]{1,0:T(8,128)(2,1)S(1)} collective-permute-done((bf16[80,1536]{1,0:T(8,128)(2,1)S(1)}, bf16[80,1536]{1,0:T(8,128)(2,1)S(1)}, u32[]{:S(2)}, u32[]{:S(2)}) %collective-permute-start.23) | collective-permute-done | bytes 245792 | tf_op jit(solution)/shard_map/ppermute | solution.py:536
  174.0 3.0 %collective-permute-start.24 = (bf16[80,1536]{1,0:T(8,128)(2,1)S(1)}, bf16[80,1536]{1,0:T(8,128)(2,1)S(1)}, u32[]{:S(2)}, u32[]{:S(2)}) collective-permute-start(bf16[80,1536]{1,0:T(8,128)(2,1)S(1)} %fusion), channel_id=1, source_target_pairs={{0,2},{1,5},{2,0},{3,7},{4,6},{5,1},{6,4},{7,3},{8,10},{9,13},{10,... | collective-permute-start | bytes 737288 | tf_op jit(solution)/shard_map/ppermute | solution.py:536
  176.9 3.0 %collective-permute-done.27 = bf16[2,48,1536]{2,1,0:T(8,128)(2,1)S(1)} collective-permute-done((bf16[2,48,1536]{2,1,0:T(8,128)(2,1)S(1)}, bf16[2,48,1536]{2,1,0:T(8,128)(2,1)S(1)}, u32[]{:S(2)}, u32[]{:S(2)}) %collective-permute-start.27) | collective-permute-done | bytes 294944 | tf_op jit(solution)/shard_map/ppermute | solution.py:536
  181.3 7.6 %collective-permute-done.28 = bf16[48,1536]{1,0:T(8,128)(2,1)S(1)} collective-permute-done((bf16[48,1536]{1,0:T(8,128)(2,1)S(1)}, bf16[48,1536]{1,0:T(8,128)(2,1)S(1)}, u32[]{:S(2)}, u32[]{:S(2)}) %collective-permute-start.28) | collective-permute-done | bytes 147488 | tf_op jit(solution)/shard_map/ppermute | solution.py:536
  (92 shorter events, 31.4 us)
Async XLA Ops:
  13.2 21.0 %collective-permute-start.3 = (bf16[2,1536,1024]{2,1,0:T(8,128)(2,1)}, bf16[2,1536,1024]{2,1,0:T(8,128)(2,1)}, u32[]{:S(2)}, u32[]{:S(2)}) collective-permute-start(bf16[2,1536,1024]{2,1,0:T(8,128)(2,1)} %refs_6_.3), channel_id=1, source_target_pairs={{0,1},{1,0},{2,3},{3,2},{4,5},{5,4},{6,7},{7,6},{8,9},{9,8},{10,11... | collective-permute-start | bytes 18874376 | tf_op jit(solution)/shard_map/ppermute | solution.py:649
  13.6 20.6 %collective-permute-start.4 = (bf16[2,512,1536]{2,1,0:T(8,128)(2,1)S(1)}, bf16[2,512,1536]{2,1,0:T(8,128)(2,1)}, u32[]{:S(2)}, u32[]{:S(2)}) collective-permute-start(bf16[2,512,1536]{2,1,0:T(8,128)(2,1)S(1)} %copy-done.3), channel_id=1, source_target_pairs={{0,1},{1,0},{2,3},{3,2},{4,5},{5,4},{6,7},{7,6},{8,9},{9,8},{10,11... | collective-permute-start | bytes 9437192 | tf_op jit(solution)/shard_map/ppermute | solution.py:649
  28.6 19.1 %collective-permute-start.7 = (bf16[72,1536]{1,0:T(8,128)(2,1)}, bf16[72,1536]{1,0:T(8,128)(2,1)S(1)}, u32[]{:S(2)}, u32[]{:S(2)}) collective-permute-start(bf16[72,1536]{1,0:T(8,128)(2,1)} %get-tuple-element.51.refs_0_), channel_id=1, source_target_pairs={{0,24},{1,25},{2,26},{3,27},{4,28},{5,29},{6,30},{7,31},{8,16},{9,... | collective-permute-start | bytes 663560 | tf_op jit(solution)/shard_map/ppermute | solution.py:536
  33.6 19.3 %collective-permute-start.6 = (bf16[72,1536]{1,0:T(8,128)(2,1)}, bf16[72,1536]{1,0:T(8,128)(2,1)S(1)}, u32[]{:S(2)}, u32[]{:S(2)}) collective-permute-start(bf16[72,1536]{1,0:T(8,128)(2,1)} %get-tuple-element.51.refs_0_), channel_id=1, source_target_pairs={{0,16},{1,17},{2,18},{3,19},{4,20},{5,21},{6,22},{7,23},{8,24},{9,... | collective-permute-start | bytes 663560 | tf_op jit(solution)/shard_map/ppermute | solution.py:536
  33.6 19.3 %collective-permute-start.5 = (bf16[72,1536]{1,0:T(8,128)(2,1)}, bf16[72,1536]{1,0:T(8,128)(2,1)S(1)}, u32[]{:S(2)}, u32[]{:S(2)}) collective-permute-start(bf16[72,1536]{1,0:T(8,128)(2,1)} %get-tuple-element.51.refs_0_), channel_id=1, source_target_pairs={{0,8},{1,9},{2,10},{3,11},{4,12},{5,13},{6,14},{7,15},{8,0},{9,1},... | collective-permute-start | bytes 663560 | tf_op jit(solution)/shard_map/ppermute | solution.py:536
  53.9 19.4 %collective-permute-start.11 = (bf16[4,72,1536]{2,1,0:T(8,128)(2,1)S(1)}, bf16[4,72,1536]{2,1,0:T(8,128)(2,1)S(1)}, u32[]{:S(2)}, u32[]{:S(2)}) collective-permute-start(bf16[4,72,1536]{2,1,0:T(8,128)(2,1)S(1)} %stack_rows.2.refs_0_), channel_id=1, source_target_pairs={{0,2},{1,5},{2,0},{3,7},{4,6},{5,1},{6,4},{7,3},{8,10},{9,13},{10,... | collective-permute-start | bytes 2654216 | tf_op jit(solution)/shard_map/ppermute | solution.py:536
  55.5 9.7 %collective-permute-start.10 = (bf16[64,1536]{1,0:T(8,128)(2,1)S(1)}, bf16[64,1536]{1,0:T(8,128)(2,1)S(1)}, u32[]{:S(2)}, u32[]{:S(2)}) collective-permute-start(bf16[64,1536]{1,0:T(8,128)(2,1)S(1)} %copy-done), channel_id=1, source_target_pairs={{0,24},{1,25},{2,26},{3,27},{4,28},{5,29},{6,30},{7,31},{8,16},{9,... | collective-permute-start | bytes 589832 | tf_op jit(solution)/shard_map/ppermute | solution.py:536
  57.9 15.2 %collective-permute-start.9 = (bf16[64,1536]{1,0:T(8,128)(2,1)S(1)}, bf16[64,1536]{1,0:T(8,128)(2,1)S(1)}, u32[]{:S(2)}, u32[]{:S(2)}) collective-permute-start(bf16[64,1536]{1,0:T(8,128)(2,1)S(1)} %copy-done), channel_id=1, source_target_pairs={{0,16},{1,17},{2,18},{3,19},{4,20},{5,21},{6,22},{7,23},{8,24},{9,... | collective-permute-start | bytes 589832 | tf_op jit(solution)/shard_map/ppermute | solution.py:536
  57.9 15.2 %collective-permute-start.8 = (bf16[64,1536]{1,0:T(8,128)(2,1)S(1)}, bf16[64,1536]{1,0:T(8,128)(2,1)S(1)}, u32[]{:S(2)}, u32[]{:S(2)}) collective-permute-start(bf16[64,1536]{1,0:T(8,128)(2,1)S(1)} %copy-done), channel_id=1, source_target_pairs={{0,8},{1,9},{2,10},{3,11},{4,12},{5,13},{6,14},{7,15},{8,0},{9,1},... | collective-permute-start | bytes 589832 | tf_op jit(solution)/shard_map/ppermute | solution.py:536
  59.9 18.7 %collective-permute-start.12 = (bf16[4,72,1536]{2,1,0:T(8,128)(2,1)S(1)}, bf16[4,72,1536]{2,1,0:T(8,128)(2,1)S(1)}, u32[]{:S(2)}, u32[]{:S(2)}) collective-permute-start(bf16[4,72,1536]{2,1,0:T(8,128)(2,1)S(1)} %stack_rows.2.refs_0_), channel_id=1, source_target_pairs={{0,4},{1,3},{2,6},{3,1},{4,0},{5,7},{6,2},{7,5},{8,12},{9,11},{10,... | collective-permute-start | bytes 2654216 | tf_op jit(solution)/shard_map/ppermute | solution.py:536
  74.3 21.1 %collective-permute-start.13 = (bf16[4,64,1536]{2,1,0:T(8,128)(2,1)S(1)}, bf16[4,64,1536]{2,1,0:T(8,128)(2,1)}, u32[]{:S(2)}, u32[]{:S(2)}) collective-permute-start(bf16[4,64,1536]{2,1,0:T(8,128)(2,1)S(1)} %stack_rows.3.refs_1_), channel_id=1, source_target_pairs={{0,4},{1,3},{2,6},{3,1},{4,0},{5,7},{6,2},{7,5},{8,12},{9,11},{10,... | collective-permute-start | bytes 2359304 | tf_op jit(solution)/shard_map/ppermute | solution.py:536
  77.0 33.2 %collective-permute-start.14 = (bf16[4,64,1536]{2,1,0:T(8,128)(2,1)S(1)}, bf16[4,64,1536]{2,1,0:T(8,128)(2,1)S(1)}, u32[]{:S(2)}, u32[]{:S(2)}) collective-permute-start(bf16[4,64,1536]{2,1,0:T(8,128)(2,1)S(1)} %stack_rows.3.refs_1_), channel_id=1, source_target_pairs={{0,2},{1,5},{2,0},{3,7},{4,6},{5,1},{6,4},{7,3},{8,10},{9,13},{10,... | collective-permute-start | bytes 2359304 | tf_op jit(solution)/shard_map/ppermute | solution.py:536
  78.5 34.3 %collective-permute-start.18 = (bf16[4,72,1536]{2,1,0:T(8,128)(2,1)S(1)}, bf16[4,72,1536]{2,1,0:T(8,128)(2,1)S(1)}, u32[]{:S(2)}, u32[]{:S(2)}) collective-permute-start(bf16[4,72,1536]{2,1,0:T(8,128)(2,1)S(1)} %collective-permute-done.12.refs_1_.refs_2_), channel_id=1, source_target_pairs={{0,2},{1,5},{2,0},{3,7},{4,6},{5,1},{6,4},{7,3},{8,10},{9,13},{10,... | collective-permute-start | bytes 2654216 | tf_op jit(solution)/shard_map/ppermute | solution.py:536
  95.5 15.8 %collective-permute-start.15 = (bf16[4,64,1536]{2,1,0:T(8,128)(2,1)}, bf16[4,64,1536]{2,1,0:T(8,128)(2,1)S(1)}, u32[]{:S(2)}, u32[]{:S(2)}) collective-permute-start(bf16[4,64,1536]{2,1,0:T(8,128)(2,1)} %collective-permute-done.13.refs_3_), channel_id=1, source_target_pairs={{0,2},{1,5},{2,0},{3,7},{4,6},{5,1},{6,4},{7,3},{8,10},{9,13},{10,... | collective-permute-start | bytes 2359304 | tf_op jit(solution)/shard_map/ppermute | solution.py:536
  111.3 14.3 %collective-permute-start.16 = (bf16[4,80,1536]{2,1,0:T(8,128)(2,1)S(1)}, bf16[4,80,1536]{2,1,0:T(8,128)(2,1)S(1)}, u32[]{:S(2)}, u32[]{:S(2)}) collective-permute-start(bf16[4,80,1536]{2,1,0:T(8,128)(2,1)S(1)} %get-tuple-element.62), channel_id=1, source_target_pairs={{0,4},{1,3},{2,6},{3,1},{4,0},{5,7},{6,2},{7,5},{8,12},{9,11},{10,... | collective-permute-start | bytes 2949128 | tf_op jit(solution)/shard_map/ppermute | solution.py:536
  113.8 17.8 %collective-permute-start.17 = (bf16[4,48,1536]{2,1,0:T(8,128)(2,1)S(1)}, bf16[4,48,1536]{2,1,0:T(8,128)(2,1)S(1)}, u32[]{:S(2)}, u32[]{:S(2)}) collective-permute-start(bf16[4,48,1536]{2,1,0:T(8,128)(2,1)S(1)} %get-tuple-element.64), channel_id=1, source_target_pairs={{0,4},{1,3},{2,6},{3,1},{4,0},{5,7},{6,2},{7,5},{8,12},{9,11},{10,... | collective-permute-start | bytes 1769480 | tf_op jit(solution)/shard_map/ppermute | solution.py:536
  126.5 19.2 %collective-permute-start.21 = (bf16[4,80,1536]{2,1,0:T(8,128)(2,1)S(1)}, bf16[4,80,1536]{2,1,0:T(8,128)(2,1)S(1)}, u32[]{:S(2)}, u32[]{:S(2)}) collective-permute-start(bf16[4,80,1536]{2,1,0:T(8,128)(2,1)S(1)} %get-tuple-element.70), channel_id=1, source_target_pairs={{0,4},{1,3},{2,6},{3,1},{4,0},{5,7},{6,2},{7,5},{8,12},{9,11},{10,... | collective-permute-start | bytes 2949128 | tf_op jit(solution)/shard_map/ppermute | solution.py:536
  131.8 12.9 %collective-permute-start.19 = (bf16[2,80,1536]{2,1,0:T(8,128)(2,1)S(1)}, bf16[2,80,1536]{2,1,0:T(8,128)(2,1)S(1)}, u32[]{:S(2)}, u32[]{:S(2)}) collective-permute-start(bf16[2,80,1536]{2,1,0:T(8,128)(2,1)S(1)} %pad_maximum_fusion), channel_id=1, source_target_pairs={{0,8},{1,9},{2,10},{3,11},{4,12},{5,13},{6,14},{7,15},{8,0},{9,1},... | collective-permute-start | bytes 1474568 | tf_op jit(solution)/shard_map/ppermute | solution.py:536
  144.8 13.0 %collective-permute-start.20 = (bf16[80,1536]{1,0:T(8,128)(2,1)S(1)}, bf16[80,1536]{1,0:T(8,128)(2,1)S(1)}, u32[]{:S(2)}, u32[]{:S(2)}) collective-permute-start(bf16[80,1536]{1,0:T(8,128)(2,1)S(1)} %fusion.4), channel_id=1, source_target_pairs={{0,16},{1,17},{2,18},{3,19},{4,20},{5,21},{6,22},{7,23},{8,24},{9,... | collective-permute-start | bytes 737288 | tf_op jit(solution)/shard_map/ppermute | solution.py:536
  145.8 9.9 %collective-permute-start.25 = (bf16[4,48,1536]{2,1,0:T(8,128)(2,1)S(1)}, bf16[4,48,1536]{2,1,0:T(8,128)(2,1)S(1)}, u32[]{:S(2)}, u32[]{:S(2)}) collective-permute-start(bf16[4,48,1536]{2,1,0:T(8,128)(2,1)S(1)} %get-tuple-element.78), channel_id=1, source_target_pairs={{0,4},{1,3},{2,6},{3,1},{4,0},{5,7},{6,2},{7,5},{8,12},{9,11},{10,... | collective-permute-start | bytes 1769480 | tf_op jit(solution)/shard_map/ppermute | solution.py:536
  146.7 16.1 %collective-permute-start.22 = (bf16[2,80,1536]{2,1,0:T(8,128)(2,1)S(1)}, bf16[2,80,1536]{2,1,0:T(8,128)(2,1)S(1)}, u32[]{:S(2)}, u32[]{:S(2)}) collective-permute-start(bf16[2,80,1536]{2,1,0:T(8,128)(2,1)S(1)} %pad_maximum_fusion.1), channel_id=1, source_target_pairs={{0,8},{1,9},{2,10},{3,11},{4,12},{5,13},{6,14},{7,15},{8,0},{9,1},... | collective-permute-start | bytes 1474568 | tf_op jit(solution)/shard_map/ppermute | solution.py:536
  157.8 9.9 %collective-permute-start.26 = (bf16[4,48,1536]{2,1,0:T(8,128)(2,1)S(1)}, bf16[4,48,1536]{2,1,0:T(8,128)(2,1)S(1)}, u32[]{:S(2)}, u32[]{:S(2)}) collective-permute-start(bf16[4,48,1536]{2,1,0:T(8,128)(2,1)S(1)} %add_convert_fusion), channel_id=1, source_target_pairs={{0,2},{1,5},{2,0},{3,7},{4,6},{5,1},{6,4},{7,3},{8,10},{9,13},{10,... | collective-permute-start | bytes 1769480 | tf_op jit(solution)/shard_map/ppermute | solution.py:536
  162.8 11.0 %collective-permute-start.23 = (bf16[80,1536]{1,0:T(8,128)(2,1)S(1)}, bf16[80,1536]{1,0:T(8,128)(2,1)S(1)}, u32[]{:S(2)}, u32[]{:S(2)}) collective-permute-start(bf16[80,1536]{1,0:T(8,128)(2,1)S(1)} %fusion.5), channel_id=1, source_target_pairs={{0,16},{1,17},{2,18},{3,19},{4,20},{5,21},{6,22},{7,23},{8,24},{9,... | collective-permute-start | bytes 737288 | tf_op jit(solution)/shard_map/ppermute | solution.py:536
  167.8 12.2 %collective-permute-start.27 = (bf16[2,48,1536]{2,1,0:T(8,128)(2,1)S(1)}, bf16[2,48,1536]{2,1,0:T(8,128)(2,1)S(1)}, u32[]{:S(2)}, u32[]{:S(2)}) collective-permute-start(bf16[2,48,1536]{2,1,0:T(8,128)(2,1)S(1)} %pad_maximum_fusion.3), channel_id=1, source_target_pairs={{0,8},{1,9},{2,10},{3,11},{4,12},{5,13},{6,14},{7,15},{8,0},{9,1},... | collective-permute-start | bytes 884744 | tf_op jit(solution)/shard_map/ppermute | solution.py:536
  (14 other events, 99.2 us)
